TPU v7x, 256 devices: a whole 4x4x8 slice. The times are simulated.
256 devices in a mesh: rep: 32 (over y, z), voc: 8 (over x, core).
Axes of the slice: x: 4, y: 4, z: 8, core: 2. Of those that a mesh axis runs over, the one named last changes fastest.
Arguments:
- log_hidden: bfloat16 [2048, 8192], P('rep'), may hold values from -6 to 6
- positions: int32 [256], P('rep'), may hold values from 0 to 59
- offsets: int32 [256], P('rep'), may hold values from 1 to 4
- head_weight: bfloat16 [8192, 8192], P('voc', 'rep'), may hold values from -0.0625 to 0.0625
- head_bias: float32 [8192], P('rep'), may hold values from -3 to 3
- vocab_head: bfloat16 [128256, 8192], P(('rep', 'voc')), may hold values from -0.4375 to 0.4375
Outputs:
- loss: float32 [], replicated
- grad_weight: float32 [8192, 8192], P('voc', 'rep')
- grad_bias: float32 [8192], P('rep')
Inputs may be any that keep to these rules, and one draw needn't show every extreme that they name: `positions`: a row within the replica's own block of 64 log rows, leaving room for the offset.
All inputs are finite; a program needn't handle non-finite values.
Results may differ from a plain program's by a relative error of at most 0.008.
Values may be sent and summed in bfloat16 or wider, within the bound.
No kernel may reach another device: no remote copies, remote signals or barrier semaphores. Data moves between devices by JAX's collectives and lax.ppermute only.
A program may use at most 128 MiB of HBM per device.

v0:
```python
import jax
import jax.numpy as jnp
from jax import lax
from jax.sharding import PartitionSpec as P


def silu_slope(preact):
    sigma = jax.nn.sigmoid(preact)
    return sigma * (1.0 + preact * (1.0 - sigma))


def shards(log_hidden, positions, offsets, head_weight, head_bias, vocab_head):
    in_width = head_weight.shape[0]
    voc_index = lax.axis_index("voc")
    inputs = jnp.take(log_hidden, positions, axis=0)
    targets = jnp.take(log_hidden, positions + offsets, axis=0)
    input_block = lax.dynamic_slice_in_dim(inputs, voc_index * in_width, in_width, 1)
    input_rows = lax.all_gather(input_block, "rep", axis=0, tiled=True)
    input_cols = lax.all_to_all(inputs, "rep", split_axis=1, concat_axis=0, tiled=True)
    partial_pre = jnp.dot(input_rows, head_weight, preferred_element_type=jnp.float32)
    preact = lax.psum(partial_pre, "voc") + head_bias
    heads = (input_cols.astype(jnp.float32) + jax.nn.silu(preact)).astype(jnp.bfloat16)
    count_rows = heads.shape[0]
    contract = (((1,), (1,)), ((), ()))
    teacher = lax.dot_general(
        vocab_head,
        lax.all_gather(targets, "rep", axis=0, tiled=True),
        contract,
        preferred_element_type=jnp.float32,
    )
    columns = vocab_head
    student = lax.dot_general(
        columns,
        lax.all_gather(heads, "rep", axis=1, tiled=True),
        contract,
        preferred_element_type=jnp.float32,
    )
    exp_teacher = jnp.exp(teacher)
    exp_student = jnp.exp(student)
    total_teacher, total_student = lax.psum(
        (jnp.sum(exp_teacher, axis=0), jnp.sum(exp_student, axis=0)), ("rep", "voc")
    )
    log_target = teacher - jnp.log(total_teacher)
    log_student = student - jnp.log(total_student)
    target_prob = jnp.exp(log_target)
    student_prob = jnp.exp(log_student)
    loss = lax.psum(jnp.sum(target_prob * (log_target - log_student)), ("rep", "voc")) / count_rows
    grad_logits = (student_prob - target_prob).astype(jnp.bfloat16)
    outer = (((0,), (0,)), ((), ()))
    columns = vocab_head
    grad_part = lax.psum_scatter(
        lax.dot_general(columns, grad_logits, outer, preferred_element_type=jnp.float32),
        "rep",
        scatter_dimension=0,
        tiled=True,
    )
    grad_heads = lax.psum(grad_part, "voc")
    grad_pre = grad_heads.T * silu_slope(preact)
    grad_bias = jnp.sum(grad_pre, axis=0)
    grad_weight = jnp.dot(
        input_rows.T, grad_pre.astype(jnp.bfloat16), preferred_element_type=jnp.float32
    )
    return (loss, grad_weight, grad_bias)


def solution(mesh):
    return jax.shard_map(
        shards,
        mesh=mesh,
        in_specs=(
            P("rep", None),
            P("rep"),
            P("rep"),
            P("voc", "rep"),
            P("rep"),
            P(("rep", "voc"), None),
        ),
        out_specs=(P(), P("voc", "rep"), P("rep")),
        check_vma=False,
    )
```

profile of v0, /device:TPU:1, one launch (start us, length us, event | category | flops | bytes accessed | tf_op | source)
XLA Modules:
  0.0 638.5 jit_solution(10808661493541748195)
XLA Ops:
  8.1 0.7 compare_select_fusion
  8.8 0.7 compare_and_fusion.1
  9.5 0.6 gather_fusion.1
  10.1 0.7 broadcast_select_fusion
  10.9 0.7 constant_dynamic-slice_fusion
  11.6 42.3 %all_gather.10 = bf16[256,1024]{1,0:T(8,128)(2,1)S(1)} all-gather(bf16[8,1024]{1,0:T(8,128)(2,1)S(1)} %constant_dynamic-slice_fusion), channel_id=1, replica_groups=mesh['rep'=32,'voc'=8] {'rep'}, dimensions={0}, use_global_device_ids=true | all-gather | bytes 540672 | tf_op jit(solution)/shard_map/all_gather | solution.py:18
  53.9 2.0 fusion.6
  56.0 0.6 gather_fusion
  56.7 0.7 broadcast_select_fusion.1
  57.4 5.0 all-to-all-start
  62.5 0.0 all-gather.5.cloned.1.call-start
  62.5 66.3 %all-reduce.4.cloned.1.call-done = f32[256,256]{1,0:T(8,128)} async-done(((f32[256,256]{1,0:T(8,128)}), f32[256,256]{1,0:T(8,128)}) %all-reduce.4.cloned.1.call-update) | async-done | bytes 262160 | tf_op jit(solution)/shard_map/psum | solution.py:21
  128.8 1.7 fusion
  130.6 15.9 %all-gather.3.cloned.1.call-done = bf16[256,8192]{1,0:T(8,128)(2,1)} async-done(((bf16[8,8192]{1,0:T(8,128)(2,1)}), bf16[256,8192]{1,0:T(8,128)(2,1)}) %all-gather.3.cloned.1.call-update) | async-done | bytes 4194320 | tf_op jit(solution)/shard_map/all_gather | solution.py:27
  146.6 6.3 exponential_reduce_fusion.1
  152.8 78.1 %all-gather.5.cloned.1.call-done = bf16[256,8192]{1,0:T(8,128)(2,1)} async-done(((bf16[256,256]{1,0:T(8,128)(2,1)}), bf16[256,8192]{1,0:T(8,128)(2,1)}) %all-gather.5.cloned.1.call-update) | async-done | bytes 4194320 | tf_op jit(solution)/shard_map/all_gather | solution.py:34
  231.0 6.3 exponential_reduce_fusion
  237.3 79.2 %all-reduce = (f32[256]{0:T(256)S(1)}, f32[256]{0:T(256)S(1)}) all-reduce(f32[256]{0:T(256)S(1)} %get-tuple-element.11, f32[256]{0:T(256)S(1)} %get-tuple-element.13), channel_id=1, replica_groups=mesh['rep'=32,'voc'=8] {'rep','voc'}, use_global_device_ids=true, to_apply=%region_4.6 | all-reduce | flops 512 | bytes 4096 | tf_op jit(solution)/shard_map/psum | solution.py:40
  316.5 9.1 %convolution_bitcast_fusion = f32[8192,256]{0,1:T(8,128)} fusion(bf16[501,8192]{1,0:T(8,128)(2,1)} %param.13, f32[256,501]{0,1:T(8,128)S(1)} %get-tuple-element.12, f32[256,501]{0,1:T(8,128)S(1)} %get-tuple-element.14, f32[256]{0:T(256)S(1)} %log.7, f32[256]{0:T(256)S(1)} %log.6), kind=kOutput, calls=%fused_computation.2 | convolution fusion | flops 2101859328 | bytes 17625088 | tf_op jit(solution)/shard_map/dot_general | solution.py:52
  325.7 221.0 %reduce-scatter.2.cloned.1.call-done = f32[256,256]{0,1:T(8,128)} async-done(((f32[8192,256]{0,1:T(8,128)}), f32[256,256]{0,1:T(8,128)}) %reduce-scatter.2.cloned.1.call-update) | async-done | bytes 262160 | tf_op jit(solution)/shard_map/reduce_scatter | solution.py:51
  546.7 0.8 multiply_reduce_fusion
  547.5 78.7 %psum.38 = f32[]{:T(128)} all-reduce(f32[]{:T(128)} %multiply_reduce_fusion), channel_id=1, replica_groups=mesh['rep'=32,'voc'=8] {'rep','voc'}, use_global_device_ids=true, to_apply=%region_6.8 | all-reduce | flops 1 | bytes 8 | tf_op jit(solution)/shard_map/psum | solution.py:47
  626.8 1.6 fusion.5
  628.5 1.3 fusion.3
  (21 shorter events, 0.3 us)
Async XLA Ops:
  8.0 1.5 copy-start
  8.0 120.8 %all-reduce.4.cloned.1.call-start = ((), (), s32[]{:S(2)}) async-start(), calls=%async_computation.3 | async-start | bytes 524288 | tf_op jit(solution)/shard_map/psum | solution.py:21
  56.0 90.6 %all-gather.3.cloned.1.call-start = ((), (), s32[]{:S(2)}) async-start(), calls=%async_computation.2 | async-start | bytes 4325376 | tf_op jit(solution)/shard_map/all_gather | solution.py:27
  57.4 71.4 %all-to-all-start = ((bf16[8,32,256]{2,0,1:T(8,128)(2,1)}), bf16[8,32,256]{2,0,1:T(8,128)(2,1)S(1)}, u32[]{:S(2)}, u32[]{:S(2)}) async-start(bf16[8,32,256]{2,0,1:T(8,128)(2,1)} %bitcast), calls=%async_computation | async-start | bytes 262144 | tf_op jit(solution)/shard_map/all_to_all | solution.py:19
  62.5 168.5 %all-gather.5.cloned.1.call-start = ((), (), s32[]{:S(2)}) async-start(), calls=%async_computation.4 | async-start | bytes 4325376 | tf_op jit(solution)/shard_map/all_gather | solution.py:34
  130.6 416.1 %reduce-scatter.2.cloned.1.call-start = ((), (), s32[]{:S(2)}) async-start(), calls=%async_computation.5 | async-start | bytes 8650752 | tf_op jit(solution)/shard_map/reduce_scatter | solution.py:51
  325.6 301.2 %copy-start.1 = (f32[256,256]{1,0:T(8,128)S(1)}, f32[256,256]{1,0:T(8,128)}, u32[]{:S(2)}) copy-start(f32[256,256]{1,0:T(8,128)} %all-reduce.4.cloned.1.call-done) | copy-start | bytes 786436
  325.6 301.2 %copy-start.2 = (f32[256]{0:T(256)S(1)}, f32[256]{0:T(256)}, u32[]{:S(2)}) copy-start(f32[256]{0:T(256)} %param.12) | copy-start | bytes 3076
  325.6 301.2 %all-reduce.6.cloned.1.call-start = ((), (), s32[]{:S(2)}) async-start(), calls=%async_computation.6 | async-start | bytes 524288 | tf_op jit(solution)/shard_map/psum | solution.py:57
Sparse Core Ops, SparseCore 0:
  56.1 72.7 all-reduce.3
  546.8 65.1 all-reduce.5
Sparse Core Ops, SparseCore 1:
  59.0 87.5 all-gather.2
  149.8 81.2 all-gather.4
  325.7 220.9 reduce-scatter.1
where the time goes:
time: 639 us
  waiting for transfers between devices  382 us (60%)
  blocking collectives  200 us (31%)
  matrix products  25 us (4%)
  between operations  17.5 us (3%)
  other arithmetic  6.98 us (1%)
    reduce_scatter x1, waiting for transfers between devices, shards(): lax.psum_scatter(lax.dot_general(columns, grad_logits, outer, preferred_e...  221 us
    psum x1, blocking collectives, shards(): lax.psum((jnp.sum(exp_teacher, axis=0), jnp.sum(exp_student, axis=0)), ('...  79.2 us
    psum x1, blocking collectives, shards(): lax.psum(jnp.sum(target_prob * (log_target - log_student)), ('rep', 'voc'))  78.7 us
    all_gather x1, waiting for transfers between devices, shards(): lax.all_gather(heads, 'rep', axis=1, tiled=True)  78.1 us
    psum x1, waiting for transfers between devices, shards(): preact = lax.psum(partial_pre, 'voc') + head_bias  66.3 us
    all_gather x1, blocking collectives, shards(): input_rows = lax.all_gather(input_block, 'rep', axis=0, tiled=True)  42.3 us
    all_gather x1, waiting for transfers between devices, shards(): lax.all_gather(targets, 'rep', axis=0, tiled=True)  15.9 us
  transfers between devices with their start and end apart: 6, of which 4 were waited for; matrix products, arithmetic and copies ran while one was open for 2% of the time, Pallas kernels for 0%

commit v1 on v0

v1 whole, which is shorter than its diff:
```python
import jax
import jax.numpy as jnp
from jax import lax
from jax.sharding import PartitionSpec as P

BF16 = jnp.bfloat16
F32 = jnp.float32


def exchange(blocks, axis):
    return lax.all_to_all(blocks, axis, split_axis=0, concat_axis=0, tiled=True)


def gathered(block, axis, count):
    return exchange(jnp.broadcast_to(block[None], (count, *block.shape)), axis)


def thirds(value):
    high = lax.reduce_precision(value, 8, 7)
    middle = lax.reduce_precision(value - high, 8, 7)
    return jnp.stack([high, middle, value - high - middle])


def shards(reps, vocs, log_hidden, positions, offsets, head_weight, head_bias, vocab_head):
    in_width, out_width = head_weight.shape
    own = positions.shape[0]
    count = own * reps
    rows = count // vocs
    voc_index = lax.axis_index("voc")
    inputs = jnp.take(log_hidden, positions, axis=0, mode="clip")
    targets = jnp.take(log_hidden, positions + offsets, axis=0, mode="clip")
    with jax.named_scope("gather_inputs"):
        input_block = lax.dynamic_slice_in_dim(inputs, voc_index * in_width, in_width, 1)
        input_cols = inputs.reshape(own, reps, out_width).transpose(1, 0, 2)
        sent = jnp.concatenate(
            [jnp.broadcast_to(input_block[None], (reps, own, in_width)), input_cols], axis=2
        )
        got = exchange(sent, "rep")
        input_rows = got[:, :, :in_width].reshape(count, in_width)
        residual = got[:, :, in_width:].reshape(count, out_width)
        residual = lax.dynamic_slice_in_dim(residual, voc_index * rows, rows, 0)
    with jax.named_scope("gather_targets"):
        target_block = lax.dynamic_slice_in_dim(targets, voc_index * in_width, in_width, 1)
        target_rows = gathered(target_block, "rep", reps).reshape(count, in_width)
        target_all = lax.all_gather(target_rows, "voc", axis=1, tiled=True)
    with jax.named_scope("head"):
        partial_pre = jnp.dot(input_rows, head_weight, preferred_element_type=F32)
        parts = exchange(partial_pre.reshape(vocs, rows, out_width), "voc")
        preact = jnp.sum(parts, axis=0) + head_bias
        heads = (residual.astype(F32) + jax.nn.silu(preact)).astype(BF16)
    with jax.named_scope("gather_heads"):
        head_rows = gathered(heads, "rep", reps).transpose(1, 0, 2).reshape(rows, -1)
        head_all = lax.all_gather(head_rows, "voc", axis=0, tiled=True)
    contract = (((1,), (1,)), ((), ()))
    with jax.named_scope("logits"):
        teacher = lax.dot_general(vocab_head, target_all, contract, preferred_element_type=F32)
        student = lax.dot_general(vocab_head, head_all, contract, preferred_element_type=F32)
        exp_teacher = jnp.exp(teacher)
        sums = jnp.stack(
            [
                jnp.sum(exp_teacher, axis=0),
                jnp.sum(jnp.exp(student), axis=0),
                jnp.sum(exp_teacher * (teacher - student), axis=0),
                jnp.zeros((count,), F32),
            ]
        ).reshape(8, -1)
    with jax.named_scope("totals"):
        sums = jnp.sum(gathered(sums, "voc", vocs), axis=0)
        sums = jnp.sum(gathered(sums, "rep", reps), axis=0).reshape(4, count)
        log_teacher, log_student = jnp.log(sums[0]), jnp.log(sums[1])
        loss = jnp.sum(sums[2] / sums[0] - log_teacher + log_student) / count
    with jax.named_scope("grad"):
        grad_logits = (jnp.exp(student - log_student) - jnp.exp(teacher - log_teacher)).astype(BF16)
        outer = (((0,), (0,)), ((), ()))
        grad_part = lax.dot_general(
            grad_logits, vocab_head, outer, preferred_element_type=F32
        ).astype(BF16)
    with jax.named_scope("reduce_grad"):
        grad_rows = lax.psum_scatter(grad_part, "voc", scatter_dimension=0, tiled=True)
        sent = grad_rows.reshape(rows, reps, out_width).transpose(1, 0, 2)
        grad_heads = jnp.sum(exchange(sent, "rep").astype(F32), axis=0)
    with jax.named_scope("finish"):
        sigma = jax.nn.sigmoid(preact)
        grad_pre = grad_heads * (sigma * (1.0 + preact * (1.0 - sigma)))
        bias_part = thirds(jnp.sum(grad_pre, axis=0))
        sent = jnp.concatenate(
            [grad_pre, bias_part, jnp.zeros((13, out_width), F32)], axis=0
        ).astype(BF16)
        got = gathered(sent, "voc", vocs)
        grad_all = got[:, :rows].reshape(count, out_width)
        grad_bias = jnp.sum(got[:, rows : rows + 3].astype(F32), axis=(0, 1))
        grad_weight = lax.dot_general(
            input_rows, grad_all, (((0,), (0,)), ((), ())), preferred_element_type=F32
        )
    return (loss, grad_weight, grad_bias)


def solution(mesh):
    reps, vocs = mesh.shape["rep"], mesh.shape["voc"]

    def body(*args):
        return shards(reps, vocs, *args)

    return jax.shard_map(
        body,
        mesh=mesh,
        in_specs=(
            P("rep", None),
            P("rep"),
            P("rep"),
            P("voc", "rep"),
            P("rep"),
            P(("rep", "voc"), None),
        ),
        out_specs=(P(), P("voc", "rep"), P("rep")),
        check_vma=False,
    )
```

time: 639 us -> 268 us (0.42)
  waiting for transfers between devices: 382 us -> 102 us
  blocking collectives: 200 us -> 87.3 us
  starting transfers between devices: 5.25 us -> 31.9 us
    reduce_scatter x1, waiting for transfers between devices: 221 us -> 32.5 us  [shards(): lax.psum_scatter(grad_part, 'voc', scatter_dimension=0, tiled=True)]
    psum x2 -> x0, blocking collectives: 158 us -> none  [the longest x1 79.2 us: shards(): lax.psum((jnp.sum(exp_teacher, axis=0), jnp.sum(exp_student, axis=0)), ('...]
    all_to_all x0 -> x5, blocking collectives: none -> 87.3 us  [exchange(): return lax.all_to_all(blocks, axis, split_axis=0, concat_axis=0, tiled=True)]
    psum x2 -> x0, waiting for transfers between devices: 66.3 us -> none  [the longest x1 66.3 us: shards(): preact = lax.psum(partial_pre, 'voc') + head_bias]
    all_gather x2, waiting for transfers between devices: 94.1 us -> 41.3 us  [the longest x1 30.3 us: shards(): target_all = lax.all_gather(target_rows, 'voc', axis=1, tiled=True)]
    all_gather x1 -> x0, blocking collectives: 42.3 us -> none  [shards(): input_rows = lax.all_gather(input_block, 'rep', axis=0, tiled=True)]
    all_to_all x1 -> x3, waiting for transfers between devices: 0.01 us -> 28.1 us  [exchange(): return lax.all_to_all(blocks, axis, split_axis=0, concat_axis=0, tiled=True)]
    all_to_all x1 -> x3, starting transfers between devices: 5.04 us -> 31.8 us  [exchange(): return lax.all_to_all(blocks, axis, split_axis=0, concat_axis=0, tiled=True)]
  transfers between devices with their start and end apart: 6 -> 6, of which waited for: 4 -> 6; matrix products, arithmetic and copies ran while one was open for 2% -> 3% of each run, Pallas kernels for 0% -> 0%
where the time goes in v1:
time: 268 us; the launch traced here: 267 us
  waiting for transfers between devices  102 us (38%)
  blocking collectives  87.3 us (33%)
  starting transfers between devices  31.9 us (12%)
  matrix products  22.6 us (8%)
  between operations  15.7 us (6%)
  local copies, waits for them, and re-layouts  4.83 us (2%)
  other arithmetic  3.16 us (1%)
    all_to_all x5, blocking collectives, exchange(): return lax.all_to_all(blocks, axis, split_axis=0, concat_axis=0, tiled=True)  87.3 us
    reduce_scatter x1, waiting for transfers between devices, shards(): lax.psum_scatter(grad_part, 'voc', scatter_dimension=0, tiled=True)  32.5 us
    all_to_all x3, starting transfers between devices, exchange(): return lax.all_to_all(blocks, axis, split_axis=0, concat_axis=0, tiled=True)  31.8 us
    all_gather x1, waiting for transfers between devices, shards(): target_all = lax.all_gather(target_rows, 'voc', axis=1, tiled=True)  30.3 us
    all_to_all x3, waiting for transfers between devices, exchange(): return lax.all_to_all(blocks, axis, split_axis=0, concat_axis=0, tiled=True)  28.1 us
    all_gather x1, waiting for transfers between devices, shards(): head_all = lax.all_gather(head_rows, 'voc', axis=0, tiled=True)  11 us
    dot_general x1, matrix products, shards(): lax.dot_general(grad_logits, vocab_head, outer, preferred_element_type=F32)  7.79 us
    dot_general x1, matrix products, shards(): lax.dot_general(vocab_head, target_all, contract, preferred_element_type=...  6.29 us
  transfers between devices with their start and end apart: 6, of which 6 were waited for; matrix products, arithmetic and copies ran while one was open for 3% of the time, Pallas kernels for 0%

profile of v1, /device:TPU:1, one launch (start us, length us, event | category | flops | bytes accessed | tf_op | source)
XLA Modules:
  0.0 267.5 jit_solution(848773953378702488)
XLA Ops:
  7.2 0.8 pad_clamp_fusion
  9.1 0.9 pad_maximum_fusion
  10.0 12.2 %all-to-all-start.1 = ((bf16[32,8,1280]{2,1,0:T(8,128)(2,1)}), bf16[32,8,1280]{2,1,0:T(8,128)(2,1)S(1)}, u32[]{:S(2)}, u32[]{:S(2)}) async-start(bf16[32,8,1280]{2,1,0:T(8,128)(2,1)} %pad_maximum_fusion), calls=%async_computation.1 | async-start | bytes 1310720 | tf_op jit(solution)/shard_map/gather_inputs/all_to_all | solution.py:11
  22.2 16.4 %all-to-all-done.1 = bf16[32,8,1280]{2,1,0:T(8,128)(2,1)S(1)} async-done(((bf16[32,8,1280]{2,1,0:T(8,128)(2,1)}), bf16[32,8,1280]{2,1,0:T(8,128)(2,1)S(1)}, u32[]{:S(2)}, u32[]{:S(2)}) %all-to-all-start.1) | async-done | bytes 655392 | tf_op jit(solution)/shard_map/gather_inputs/all_to_all | solution.py:11
  38.6 1.0 fusion.2
  39.6 9.3 %all-to-all-start.2 = ((f32[8,32,256]{2,1,0:T(8,128)}), f32[8,32,256]{2,1,0:T(8,128)S(1)}, u32[]{:S(2)}, u32[]{:S(2)}) async-start(f32[8,32,256]{2,1,0:T(8,128)} %fusion.2), calls=%async_computation.2 | async-start | bytes 524288 | tf_op jit(solution)/shard_map/head/all_to_all | solution.py:11
  49.0 6.5 %all-to-all-done.2 = f32[8,32,256]{2,1,0:T(8,128)S(1)} async-done(((f32[8,32,256]{2,1,0:T(8,128)}), f32[8,32,256]{2,1,0:T(8,128)S(1)}, u32[]{:S(2)}, u32[]{:S(2)}) %all-to-all-start.2) | async-done | bytes 262176 | tf_op jit(solution)/shard_map/head/all_to_all | solution.py:11
  55.6 18.4 %all_to_all.40 = bf16[32,32,256]{2,1,0:T(8,128)(2,1)S(1)} all-to-all(bf16[32,32,256]{2,1,0:T(8,128)(2,1)S(1)} %broadcast_in_dim.29), channel_id=1, replica_groups=mesh['rep'=32,'voc'=8] {'rep'}, dimensions={0} | all-to-all | bytes 1048576 | tf_op jit(solution)/shard_map/gather_heads/all_to_all | solution.py:11
  74.0 0.8 copy.24
  75.6 21.6 %all_to_all.41 = bf16[32,8,1024]{2,1,0:T(8,128)(2,1)} all-to-all(bf16[32,8,1024]{2,1,0:T(8,128)(2,1)S(1)} %broadcast_in_dim.26), channel_id=1, replica_groups=mesh['rep'=32,'voc'=8] {'rep'}, dimensions={0} | all-to-all | bytes 1048576 | tf_op jit(solution)/shard_map/gather_targets/all_to_all | solution.py:11
  97.4 11.0 %all-gather.5.cloned.1.call-done = bf16[256,8192]{1,0:T(8,128)(2,1)} async-done(((bf16[32,8192]{1,0:T(8,128)(2,1)}), bf16[256,8192]{1,0:T(8,128)(2,1)}) %all-gather.5.cloned.1.call-update) | async-done | bytes 4194320 | tf_op jit(solution)/shard_map/gather_heads/all_gather | solution.py:53
  108.4 6.2 %fusion.10 = f32[256,501]{0,1:T(8,128)S(1)} fusion(bf16[256,8192]{1,0:T(8,128)(2,1)} %all-gather.5.cloned.1.call-done, bf16[501,8192]{1,0:T(8,128)(2,1)} %param.11), kind=kOutput, calls=%fused_computation.37 | convolution fusion | flops 2101346304 | bytes 12915712 | tf_op jit(solution)/shard_map/logits/dot_general | solution.py:57
  114.6 30.3 %all-gather.3.cloned.1.call-done = bf16[256,8192]{1,0:T(8,128)(2,1)} async-done(((bf16[256,1024]{1,0:T(8,128)(2,1)}), bf16[256,8192]{1,0:T(8,128)(2,1)}) %all-gather.3.cloned.1.call-update) | async-done | bytes 4194320 | tf_op jit(solution)/shard_map/gather_targets/all_gather | solution.py:45
  144.9 6.3 %exponential_reduce_fusion.1 = (f32[256]{0:T(256)S(1)}, f32[256]{0:T(256)S(1)}, f32[256]{0:T(256)S(1)}, f32[256,501]{0,1:T(8,128)S(1)}) fusion(f32[256,501]{0,1:T(8,128)S(1)} %fusion.10, bf16[256,8192]{1,0:T(8,128)(2,1)} %all-gather.3.cloned.1.call-done, bf16[501,8192]{1,0:T(8,128)(2,1)} %param.11), kind=kOutput, calls=%fused_computation.13 | convolution fusion | flops 2101986816 | bytes 13431808 | tf_op jit(solution)/shard_map/logits/dot_general | solution.py:56
  151.3 7.7 %all_to_all.42 = f32[8,8,128]{2,1,0:T(8,128)S(1)} all-to-all(f32[8,8,128]{2,1,0:T(8,128)S(1)} %broadcast_in_dim.60), channel_id=1, replica_groups=mesh['rep'=32,'voc'=8] {'voc'}, dimensions={0} | all-to-all | bytes 65536 | tf_op jit(solution)/shard_map/totals/all_to_all | solution.py:11
  159.0 18.5 %all_to_all.43 = f32[32,8,128]{2,1,0:T(8,128)S(1)} all-to-all(f32[32,8,128]{2,1,0:T(8,128)S(1)} %broadcast_in_dim.61), channel_id=1, replica_groups=mesh['rep'=32,'voc'=8] {'rep'}, dimensions={0} | all-to-all | bytes 262144 | tf_op jit(solution)/shard_map/totals/all_to_all | solution.py:11
  178.2 7.8 %convolution_convert_fusion = bf16[256,8192]{1,0:T(8,128)(2,1)} fusion(bf16[501,8192]{1,0:T(8,128)(2,1)} %param.11, f32[256,501]{0,1:T(8,128)S(1)} %get-tuple-element.14, f32[256,501]{0,1:T(8,128)S(1)} %fusion.10, f32[256]{0:T(256)S(1)} %get-tuple-element.9, f32[256]{0:T(256)S(1)} %get-tuple-element.8), kind=kOutput, calls=%fused_computation.2 | convolution fusion | flops 2103956480 | bytes 13430784 | tf_op jit(solution)/shard_map/grad/dot_general | solution.py:75
  186.0 32.5 %reduce-scatter.2.cloned.1.call-done = bf16[32,8192]{1,0:T(8,128)(2,1)} async-done(((bf16[256,8192]{1,0:T(8,128)(2,1)}), bf16[32,8192]{1,0:T(8,128)(2,1)}) %reduce-scatter.2.cloned.1.call-update) | async-done | bytes 524304 | tf_op jit(solution)/shard_map/reduce_grad/reduce_scatter | solution.py:79
  218.6 1.1 copy.27
  219.7 21.0 %all_to_all.44 = bf16[32,32,256]{2,1,0:T(8,128)(2,1)S(1)} all-to-all(bf16[32,32,256]{2,1,0:T(8,128)(2,1)S(1)} %bitcast.43), channel_id=1, replica_groups=mesh['rep'=32,'voc'=8] {'rep'}, dimensions={0} | all-to-all | bytes 1048576 | tf_op jit(solution)/shard_map/reduce_grad/all_to_all | solution.py:11
  241.0 0.7 broadcast_in_dim.63
  241.7 10.3 %all-to-all-start.7 = ((bf16[8,48,256]{2,1,0:T(8,128)(2,1)}), bf16[8,48,256]{2,1,0:T(8,128)(2,1)S(1)}, u32[]{:S(2)}, u32[]{:S(2)}) async-start(bf16[8,48,256]{2,1,0:T(8,128)(2,1)} %broadcast_in_dim.63), calls=%async_computation.8 | async-start | bytes 393216 | tf_op jit(solution)/shard_map/finish/all_to_all | solution.py:11
  252.6 5.2 %all-to-all-done.7 = bf16[8,48,256]{2,1,0:T(8,128)(2,1)S(1)} async-done(((bf16[8,48,256]{2,1,0:T(8,128)(2,1)}), bf16[8,48,256]{2,1,0:T(8,128)(2,1)S(1)}, u32[]{:S(2)}, u32[]{:S(2)}) %all-to-all-start.7) | async-done | bytes 196640 | tf_op jit(solution)/shard_map/finish/all_to_all | solution.py:11
  258.5 1.3 fusion
  (45 shorter events, 3.9 us)
Async XLA Ops:
  7.2 1.2 copy-start
  7.2 31.5 %copy-start.1 = (bf16[1024,256]{1,0:T(8,128)(2,1)S(1)}, bf16[1024,256]{1,0:T(8,128)(2,1)}, u32[]{:S(2)}) copy-start(bf16[1024,256]{1,0:T(8,128)(2,1)} %param.9) | copy-start | bytes 1572868
  7.2 48.3 %copy-start.2 = (f32[256]{0:T(256)S(1)}, f32[256]{0:T(256)}, u32[]{:S(2)}) copy-start(f32[256]{0:T(256)} %param.10) | copy-start | bytes 3076
  10.0 64.8 %copy-start.3 = (s32[8]{0:T(128)S(1)}, s32[8]{0:T(128)}, u32[]{:S(2)}) copy-start(s32[8]{0:T(128)} %param.7) | copy-start | bytes 100
  10.0 64.9 %copy-start.4 = (s32[8]{0:T(128)S(1)}, s32[8]{0:T(128)}, u32[]{:S(2)}) copy-start(s32[8]{0:T(128)} %param.8) | copy-start | bytes 100
  10.0 28.6 %all-to-all-start.1 = ((bf16[32,8,1280]{2,1,0:T(8,128)(2,1)}), bf16[32,8,1280]{2,1,0:T(8,128)(2,1)S(1)}, u32[]{:S(2)}, u32[]{:S(2)}) async-start(bf16[32,8,1280]{2,1,0:T(8,128)(2,1)} %pad_maximum_fusion), calls=%async_computation.1 | async-start | bytes 1310720 | tf_op jit(solution)/shard_map/gather_inputs/all_to_all | solution.py:11
  39.6 15.8 %all-to-all-start.2 = ((f32[8,32,256]{2,1,0:T(8,128)}), f32[8,32,256]{2,1,0:T(8,128)S(1)}, u32[]{:S(2)}, u32[]{:S(2)}) async-start(f32[8,32,256]{2,1,0:T(8,128)} %fusion.2), calls=%async_computation.2 | async-start | bytes 524288 | tf_op jit(solution)/shard_map/head/all_to_all | solution.py:11
  49.0 59.4 %all-gather.5.cloned.1.call-start = ((), (), s32[]{:S(2)}) async-start(), calls=%async_computation.10 | async-start | bytes 4718592 | tf_op jit(solution)/shard_map/gather_heads/all_gather | solution.py:53
  74.8 70.1 %all-gather.3.cloned.1.call-start = ((), (), s32[]{:S(2)}) async-start(), calls=%async_computation.9 | async-start | bytes 4718592 | tf_op jit(solution)/shard_map/gather_targets/all_gather | solution.py:45
  97.3 121.3 %reduce-scatter.2.cloned.1.call-start = ((), (), s32[]{:S(2)}) async-start(), calls=%async_computation.11 | async-start | bytes 4718592 | tf_op jit(solution)/shard_map/reduce_grad/reduce_scatter | solution.py:79
  241.7 16.2 %all-to-all-start.7 = ((bf16[8,48,256]{2,1,0:T(8,128)(2,1)}), bf16[8,48,256]{2,1,0:T(8,128)(2,1)S(1)}, u32[]{:S(2)}, u32[]{:S(2)}) async-start(bf16[8,48,256]{2,1,0:T(8,128)(2,1)} %broadcast_in_dim.63), calls=%async_computation.8 | async-start | bytes 393216 | tf_op jit(solution)/shard_map/finish/all_to_all | solution.py:11
Sparse Core Ops, SparseCore 0:
  74.9 33.4 all-gather.4
  110.2 34.6 all-gather.2
  186.1 32.3 reduce-scatter.1

commit v2 on v1

v2 whole, which is shorter than its diff:
```python
import jax
import jax.numpy as jnp
from jax import lax
from jax.sharding import Mesh, PartitionSpec as P

BF16 = jnp.bfloat16
F32 = jnp.float32
REP = ("y", "z")
VOC = ("x", "c")
SIZES = {"y": 4, "z": 8, "x": 4, "c": 2}


def exchange(blocks, axis):
    return lax.all_to_all(blocks, axis, split_axis=0, concat_axis=0, tiled=True)


def gathered(block, axis, count):
    return exchange(jnp.broadcast_to(block[None], (count, *block.shape)), axis)


def swap(block, axis, step):
    return lax.ppermute(block, axis, [(i, i ^ step) for i in range(SIZES[axis])])


def thirds(value):
    high = lax.reduce_precision(value, 8, 7)
    middle = lax.reduce_precision(value - high, 8, 7)
    return jnp.stack([high, middle, value - high - middle])


def from_peers(block, axis):
    return [block] + [swap(block, axis, step) for step in range(1, SIZES[axis])]


def summed(blocks, axis):
    total = blocks[0].astype(F32)
    for step in range(1, SIZES[axis]):
        total = total + swap(blocks[step], axis, step).astype(F32)
    return total.astype(BF16)


def gather_heads(heads):
    rows, width = heads.shape
    half = rows // 2
    lines = gathered(heads, "z", 8).transpose(1, 0, 2).reshape(rows, -1)
    first, second = lines[:half], lines[half:]
    first = jnp.concatenate(from_peers(first, "y"), axis=1)
    second = jnp.concatenate(from_peers(second, "x"), axis=0)
    first_parts = from_peers(first, "x")
    second_parts = from_peers(second, "y")
    mine = jnp.concatenate([*first_parts, jnp.concatenate(second_parts, axis=1)], axis=0)
    return jnp.concatenate([mine, swap(mine, "c", 1)], axis=0)


def scatter_grad(part):
    rows, depth = part.shape
    own, other = part[: rows // 2], part[rows // 2 :]
    mine = (own.astype(F32) + swap(other, "c", 1).astype(F32)).astype(BF16)
    half = rows // 4
    block = half // 4
    width = depth // 4
    first = [mine[i * block : (i + 1) * block] for i in range(4)]
    second = [mine[half:, i * width : (i + 1) * width] for i in range(4)]
    first, second = summed(first, "x"), summed(second, "y")
    first = [first[:, i * width : (i + 1) * width] for i in range(4)]
    second = [second[i * block : (i + 1) * block] for i in range(4)]
    first, second = summed(first, "y"), summed(second, "x")
    lines = jnp.concatenate([first, second], axis=0)
    sent = lines.reshape(2 * block, 8, -1).transpose(1, 0, 2)
    return jnp.sum(exchange(sent, "z").astype(F32), axis=0)


def shards(log_hidden, positions, offsets, head_weight, head_bias, vocab_head):
    reps, vocs = 32, 8
    in_width, out_width = head_weight.shape
    own = positions.shape[0]
    count = own * reps
    rows = count // vocs
    at_x, at_y, at_c = lax.axis_index("x"), lax.axis_index("y"), lax.axis_index("c")
    voc_index = at_x * 2 + at_c
    inputs = jnp.take(log_hidden, positions, axis=0, mode="clip")
    targets = jnp.take(log_hidden, positions + offsets, axis=0, mode="clip")
    with jax.named_scope("gather_targets"):
        target_all = lax.all_gather(targets, REP, axis=0, tiled=True)
    with jax.named_scope("gather_inputs"):
        input_block = lax.dynamic_slice_in_dim(inputs, voc_index * in_width, in_width, 1)
        input_cols = inputs.reshape(own, reps, out_width).transpose(1, 0, 2)
        sent = jnp.concatenate(
            [jnp.broadcast_to(input_block[None], (reps, own, in_width)), input_cols], axis=2
        )
        got = exchange(sent, REP)
        input_rows = got[:, :, :in_width].reshape(count, in_width)
        residual = got[:, :, in_width:].reshape(count, out_width)
        residual = lax.dynamic_slice_in_dim(residual, voc_index * rows, rows, 0)
    with jax.named_scope("turn_columns"):
        quarter = vocab_head.shape[1] // 4
        turned = jnp.concatenate(
            [
                lax.dynamic_slice_in_dim(vocab_head, (at_y ^ step) * quarter, quarter, 1)
                for step in range(4)
            ],
            axis=1,
        )
    with jax.named_scope("head"):
        partial_pre = jnp.dot(input_rows, head_weight, preferred_element_type=F32)
        parts = exchange(partial_pre.reshape(vocs, rows, out_width), VOC)
        preact = jnp.sum(parts, axis=0) + head_bias
        heads = (residual.astype(F32) + jax.nn.silu(preact)).astype(BF16)
    with jax.named_scope("gather_heads"):
        head_all = gather_heads(heads)
    steps = jnp.arange(16)
    order = ((at_x ^ (steps % 4)) * 2 + (at_c ^ (steps // 8))) * 2 + (steps // 4) % 2
    with jax.named_scope("turn_targets"):
        target_all = target_all.reshape(16, count // 16, -1)[order].reshape(count, -1)
    contract = (((1,), (1,)), ((), ()))
    with jax.named_scope("logits"):
        teacher = lax.dot_general(vocab_head, target_all, contract, preferred_element_type=F32)
        student = lax.dot_general(turned, head_all, contract, preferred_element_type=F32)
        exp_teacher = jnp.exp(teacher)
        sums = jnp.stack(
            [
                jnp.sum(exp_teacher, axis=0),
                jnp.sum(jnp.exp(student), axis=0),
                jnp.sum(exp_teacher * (teacher - student), axis=0),
                jnp.zeros((count,), F32),
            ]
        )
        back = (steps // 2 % 2 ^ at_c) * 8 + steps % 2 * 4 + (steps // 4 ^ at_x)
        sums = sums.reshape(4, 16, -1)[:, back].reshape(8, -1)
    with jax.named_scope("totals"):
        sums = jnp.sum(gathered(sums, VOC, vocs), axis=0)
        sums = jnp.sum(gathered(sums, REP, reps), axis=0).reshape(4, count)
        log_teacher, log_student = jnp.log(sums[0]), jnp.log(sums[1])
        loss = jnp.sum(sums[2] / sums[0] - log_teacher + log_student) / count
        log_teacher = log_teacher.reshape(16, -1)[order].reshape(count)
        log_student = log_student.reshape(16, -1)[order].reshape(count)
    with jax.named_scope("grad"):
        grad_logits = (jnp.exp(student - log_student) - jnp.exp(teacher - log_teacher)).astype(BF16)
        outer = (((0,), (0,)), ((), ()))
        grad_part = lax.dot_general(
            grad_logits, turned, outer, preferred_element_type=F32
        ).astype(BF16)
    with jax.named_scope("reduce_grad"):
        grad_heads = scatter_grad(grad_part)
    with jax.named_scope("finish"):
        sigma = jax.nn.sigmoid(preact)
        grad_pre = grad_heads * (sigma * (1.0 + preact * (1.0 - sigma)))
        bias_part = thirds(jnp.sum(grad_pre, axis=0))
        sent = jnp.concatenate(
            [grad_pre, bias_part, jnp.zeros((13, out_width), F32)], axis=0
        ).astype(BF16)
        got = gathered(sent, VOC, vocs)
        grad_all = got[:, :rows].reshape(count, out_width)
        grad_bias = jnp.sum(got[:, rows : rows + 3].astype(F32), axis=(0, 1))
        grad_weight = lax.dot_general(
            input_rows, grad_all, (((0,), (0,)), ((), ())), preferred_element_type=F32
        )
    return (loss, grad_weight, grad_bias)


def solution(mesh):
    fine = Mesh(mesh.devices.reshape(tuple(SIZES.values())), tuple(SIZES))
    return jax.shard_map(
        shards,
        mesh=fine,
        in_specs=(
            P(REP, None),
            P(REP),
            P(REP),
            P(VOC, REP),
            P(REP),
            P((*REP, *VOC), None),
        ),
        out_specs=(P(), P(VOC, REP), P(REP)),
        check_vma=False,
    )
```

time: 268 us -> 262 us (0.978)
  blocking collectives: 87.3 us -> 36.9 us
  starting transfers between devices: 31.9 us -> 68.4 us
  local copies, waits for them, and re-layouts: 4.83 us -> 26.7 us
  waiting for transfers between devices: 102 us -> 89.2 us
  matrix products: 22.6 us -> 19 us
    all_to_all x5 -> x3, blocking collectives: 87.3 us -> 36.9 us  [exchange(): return lax.all_to_all(blocks, axis, split_axis=0, concat_axis=0, tiled=True)]
    ppermute x0 -> x26, starting transfers between devices: none -> 33.7 us  [swap(): lax.ppermute(block, axis, [(i, i ^ step) for i in range(SIZES[axis])])]
    reduce_scatter x1 -> x0, waiting for transfers between devices: 32.5 us -> none  [shards(): lax.psum_scatter(grad_part, 'voc', scatter_dimension=0, tiled=True)]
    ppermute x0 -> x26, waiting for transfers between devices: none -> 25.9 us  [swap(): lax.ppermute(block, axis, [(i, i ^ step) for i in range(SIZES[axis])])]
    all_gather x2 -> x1, waiting for transfers between devices: 41.3 us -> 28.7 us  [shards(): target_all = lax.all_gather(targets, REP, axis=0, tiled=True)]
    unnamed x10 -> x33, local copies, waits for them, and re-layouts: 0.45 us -> 7.59 us
    gather x0 -> x5, local copies, waits for them, and re-layouts: none -> 6.74 us  [the longest x1 5.02 us: shards(): target_all.reshape(16, count // 16, -1)[order].reshape(count, -1)]
    all_to_all x3 -> x4, waiting for transfers between devices: 28.1 us -> 34.6 us  [exchange(): return lax.all_to_all(blocks, axis, split_axis=0, concat_axis=0, tiled=True)]
  transfers between devices with their start and end apart: 6 -> 31, of which waited for: 6 -> 16; matrix products, arithmetic and copies ran while one was open for 3% -> 7% of each run, Pallas kernels for 0% -> 0%
where the time goes in v2:
time: 262 us
  waiting for transfers between devices  89.2 us (34%)
  starting transfers between devices  68.4 us (26%)
  blocking collectives  36.9 us (14%)
  local copies, waits for them, and re-layouts  26.7 us (10%)
  matrix products  19 us (7%)
  between operations  16.3 us (6%)
  other arithmetic  5.13 us (2%)
    all_to_all x3, blocking collectives, exchange(): return lax.all_to_all(blocks, axis, split_axis=0, concat_axis=0, tiled=True)  36.9 us
    all_to_all x4, starting transfers between devices, exchange(): return lax.all_to_all(blocks, axis, split_axis=0, concat_axis=0, tiled=True)  34.7 us
    all_to_all x4, waiting for transfers between devices, exchange(): return lax.all_to_all(blocks, axis, split_axis=0, concat_axis=0, tiled=True)  34.6 us
    ppermute x26, starting transfers between devices, swap(): lax.ppermute(block, axis, [(i, i ^ step) for i in range(SIZES[axis])])  33.7 us
    all_gather x1, waiting for transfers between devices, shards(): target_all = lax.all_gather(targets, REP, axis=0, tiled=True)  28.7 us
    ppermute x26, waiting for transfers between devices, swap(): lax.ppermute(block, axis, [(i, i ^ step) for i in range(SIZES[axis])])  25.9 us
    dot_general x1, matrix products, shards(): lax.dot_general(grad_logits, turned, outer, preferred_element_type=F32)  7.79 us
    unnamed x33, local copies, waits for them, and re-layouts  7.59 us
  transfers between devices with their start and end apart: 31, of which 16 were waited for; matrix products, arithmetic and copies ran while one was open for 7% of the time, Pallas kernels for 0%

profile of v2, /device:TPU:1, one launch (start us, length us, event | category | flops | bytes accessed | tf_op | source)
XLA Modules:
  0.0 261.6 jit_solution(15337318176101000016)
XLA Ops:
  10.2 12.0 %all-to-all-start = ((bf16[32,8,1280]{2,1,0:T(8,128)(2,1)}), bf16[32,8,1280]{2,1,0:T(8,128)(2,1)S(1)}, u32[]{:S(2)}, u32[]{:S(2)}) async-start(bf16[32,8,1280]{2,1,0:T(8,128)(2,1)} %pad_maximum_fusion.4), calls=%async_computation | async-start | bytes 1310720 | tf_op jit(solution)/shard_map/gather_inputs/all_to_all | solution.py:14
  22.2 16.4 %all-to-all-done = bf16[32,8,1280]{2,1,0:T(8,128)(2,1)S(1)} async-done(((bf16[32,8,1280]{2,1,0:T(8,128)(2,1)}), bf16[32,8,1280]{2,1,0:T(8,128)(2,1)S(1)}, u32[]{:S(2)}, u32[]{:S(2)}) %all-to-all-start) | async-done | bytes 655392 | tf_op jit(solution)/shard_map/gather_inputs/all_to_all | solution.py:14
  39.7 9.3 %all-to-all-start.1 = ((f32[8,32,256]{2,1,0:T(8,128)}), f32[8,32,256]{2,1,0:T(8,128)S(1)}, u32[]{:S(2)}, u32[]{:S(2)}) async-start(f32[8,32,256]{2,1,0:T(8,128)} %fusion.3), calls=%async_computation.1 | async-start | bytes 524288 | tf_op jit(solution)/shard_map/head/all_to_all | solution.py:14
  49.0 6.5 %all-to-all-done.1 = f32[8,32,256]{2,1,0:T(8,128)S(1)} async-done(((f32[8,32,256]{2,1,0:T(8,128)}), f32[8,32,256]{2,1,0:T(8,128)S(1)}, u32[]{:S(2)}, u32[]{:S(2)}) %all-to-all-start.1) | async-done | bytes 262176 | tf_op jit(solution)/shard_map/head/all_to_all | solution.py:14
  56.2 3.4 %all-to-all-start.2 = ((bf16[8,32,256]{2,1,0:T(8,128)(2,1)}), bf16[8,32,256]{2,1,0:T(8,128)(2,1)S(1)}, u32[]{:S(2)}, u32[]{:S(2)}) async-start(bf16[8,32,256]{2,1,0:T(8,128)(2,1)} %broadcast_in_dim.26), calls=%async_computation.2 | async-start | bytes 262144 | tf_op jit(solution)/shard_map/gather_heads/all_to_all | solution.py:14
  61.0 6.5 %all-to-all-done.2 = bf16[8,32,256]{2,1,0:T(8,128)(2,1)S(1)} async-done(((bf16[8,32,256]{2,1,0:T(8,128)(2,1)}), bf16[8,32,256]{2,1,0:T(8,128)(2,1)S(1)}, u32[]{:S(2)}, u32[]{:S(2)}) %all-to-all-start.2) | async-done | bytes 131104 | tf_op jit(solution)/shard_map/gather_heads/all_to_all | solution.py:14
  85.4 2.5 collective-permute-done.4
  88.7 4.3 %collective-permute-done.5 = bf16[16,8192]{1,0:T(8,128)(2,1)S(1)} collective-permute-done((bf16[16,8192]{1,0:T(8,128)(2,1)S(1)}, bf16[16,8192]{1,0:T(8,128)(2,1)S(1)}, u32[]{:S(2)}, u32[]{:S(2)}) %collective-permute-start.5) | collective-permute-done | bytes 262176 | tf_op jit(solution)/shard_map/gather_heads/ppermute | solution.py:22
  93.7 2.4 collective-permute-done.11
  101.6 4.4 %constant_dynamic-slice_fusion.4 = (bf16[501,2048]{1,0:T(8,128)(2,1)S(1)}, bf16[501,2048]{1,0:T(8,128)(2,1)S(1)}, bf16[501,2048]{1,0:T(8,128)(2,1)S(1)}, bf16[501,2048]{1,0:T(8,128)(2,1)S(1)}) fusion(bf16[501,8192]{1,0:T(8,128)(2,1)} %param.11, s32[]{:T(128)S(6)} %select_n.131, s32[]{:T(128)S(6)} %select_n.132, s32[]{:T(128)S(6)} %select_n.134, s32[]{:T(128)S(6)} %select_n.133), kind=kLoop, calls=%fused_computation.84 | loop fusion | bytes 16416784 | tf_op jit(solution)/shard_map/turn_columns/dynamic_slice | solution.py:99
  106.3 3.3 %constant_dynamic-update-slice_fusion.15 = bf16[256,8192]{1,0:T(8,128)(2,1)S(1)} fusion(bf16[256,8192]{1,0:T(8,128)(2,1)S(1)} %copy-done.8, bf16[128,8192]{1,0:T(8,128)(2,1)} %collective-permute-done.12), kind=kLoop, calls=%fused_computation.50 | loop fusion | bytes 4194304 | tf_op jit(solution)/shard_map/gather_heads/concatenate | solution.py:52
  109.6 2.6 fusion
  112.2 28.7 %all-gather.3.cloned.1.call-done = bf16[256,8192]{1,0:T(8,128)(2,1)} async-done(((bf16[8,8192]{1,0:T(8,128)(2,1)}), bf16[256,8192]{1,0:T(8,128)(2,1)}) %all-gather.3.cloned.1.call-update) | async-done | bytes 4194320 | tf_op jit(solution)/shard_map/gather_targets/all_gather | solution.py:84
  140.9 5.0 %gather_fusion.1 = bf16[16,16,8192]{2,1,0:T(8,128)(2,1)} fusion(bf16[16,16,8192]{2,1,0:T(8,128)(2,1)} %bitcast.43, s32[1024]{0:T(1024)S(1)} %get-tuple-element.56), kind=kCustom, calls=%fused_computation.1 | custom fusion | bytes 8388672 | tf_op jit(solution)/shard_map/turn_targets/gather | solution.py:114
  145.9 6.3 %exponential_reduce_fusion.1 = (f32[256]{0:T(256)S(1)}, f32[256]{0:T(256)S(1)}, f32[256]{0:T(256)S(1)}, f32[501,256]{1,0:T(8,128)S(1)}) fusion(f32[501,256]{1,0:T(8,128)S(1)} %fusion, bf16[256,8192]{1,0:T(8,128)(2,1)} %bitcast.44, bf16[501,8192]{1,0:T(8,128)(2,1)} %param.11), kind=kOutput, calls=%fused_computation.22 | convolution fusion | flops 2101986816 | bytes 13431808 | tf_op jit(solution)/shard_map/logits/dot_general | solution.py:117
  153.2 12.1 %all_to_all.35 = f32[8,8,128]{2,1,0:T(8,128)S(1)} all-to-all(f32[8,8,128]{2,1,0:T(8,128)S(1)} %broadcast_in_dim.55), channel_id=1, replica_groups=mesh['y'=4,'z'=8,'x'=4,'c'=2] {'x','c'}, dimensions={0} | all-to-all | bytes 65536 | tf_op jit(solution)/shard_map/totals/all_to_all | solution.py:14
  165.3 14.5 %all_to_all.36 = f32[32,8,128]{2,1,0:T(8,128)S(1)} all-to-all(f32[32,8,128]{2,1,0:T(8,128)S(1)} %broadcast_in_dim.56), channel_id=1, replica_groups=mesh['y'=4,'z'=8,'x'=4,'c'=2] {'y','z'}, dimensions={0} | all-to-all | bytes 262144 | tf_op jit(solution)/shard_map/totals/all_to_all | solution.py:14
  181.9 7.8 %convolution_convert_fusion = bf16[256,8192]{1,0:T(8,128)(2,1)S(1)} fusion(bf16[501,2048]{1,0:T(8,128)(2,1)} %copy-done.3, bf16[501,2048]{1,0:T(8,128)(2,1)} %copy-done.4, bf16[501,2048]{1,0:T(8,128)(2,1)} %copy-done.2, bf16[501,2048]{1,0:T(8,128)(2,1)} %copy-done.1, f32[501,256]{1,0:T(8,128)S(1)} %get-tuple-element.52, f32[501,256]{1,0:T(8,128)S(1)} %fusion, ...), kind=kOutput, calls=%fused_computation.6 | convolution fusion | flops 2136790016 | bytes 13430784 | tf_op jit(solution)/shard_map/grad/dot_general | solution.py:140
  192.1 3.8 %collective-permute-done.13 = bf16[128,8192]{1,0:T(8,128)(2,1)S(1)} collective-permute-done((bf16[128,8192]{1,0:T(8,128)(2,1)S(1)}, bf16[128,8192]{1,0:T(8,128)(2,1)S(1)}, u32[]{:S(2)}, u32[]{:S(2)}) %collective-permute-start.13) | collective-permute-done | bytes 2097184 | tf_op jit(solution)/shard_map/reduce_grad/ppermute | solution.py:22
  204.9 5.4 %collective-permute-done.15 = bf16[16,8192]{1,0:T(8,128)(2,1)S(1)} collective-permute-done((bf16[16,8192]{1,0:T(8,128)(2,1)S(1)}, bf16[16,8192]{1,0:T(8,128)(2,1)S(1)}, u32[]{:S(2)}, u32[]{:S(2)}) %collective-permute-start.15) | collective-permute-done | bytes 262176 | tf_op jit(solution)/shard_map/reduce_grad/ppermute | solution.py:22
  220.1 2.5 collective-permute-start.25
  224.6 10.3 %all_to_all.37 = bf16[8,32,256]{2,1,0:T(8,128)(2,1)S(1)} all-to-all(bf16[8,32,256]{2,1,0:T(8,128)(2,1)S(1)} %bitcast.49), channel_id=1, replica_groups=mesh['y'=4,'z'=8,'x'=4,'c'=2] {'z'}, dimensions={0} | all-to-all | bytes 262144 | tf_op jit(solution)/shard_map/reduce_grad/all_to_all | solution.py:14
  235.9 9.9 %all-to-all-start.6 = ((bf16[8,48,256]{2,1,0:T(8,128)(2,1)}), bf16[8,48,256]{2,1,0:T(8,128)(2,1)S(1)}, u32[]{:S(2)}, u32[]{:S(2)}) async-start(bf16[8,48,256]{2,1,0:T(8,128)(2,1)} %broadcast_in_dim.58), calls=%async_computation.6 | async-start | bytes 393216 | tf_op jit(solution)/shard_map/finish/all_to_all | solution.py:14
  246.4 5.2 %all-to-all-done.6 = bf16[8,48,256]{2,1,0:T(8,128)(2,1)S(1)} async-done(((bf16[8,48,256]{2,1,0:T(8,128)(2,1)}), bf16[8,48,256]{2,1,0:T(8,128)(2,1)S(1)}, u32[]{:S(2)}, u32[]{:S(2)}) %all-to-all-start.6) | async-done | bytes 196640 | tf_op jit(solution)/shard_map/finish/all_to_all | solution.py:14
  (142 shorter events, 60.2 us)
Async XLA Ops:
  10.2 28.4 %all-to-all-start = ((bf16[32,8,1280]{2,1,0:T(8,128)(2,1)}), bf16[32,8,1280]{2,1,0:T(8,128)(2,1)S(1)}, u32[]{:S(2)}, u32[]{:S(2)}) async-start(bf16[32,8,1280]{2,1,0:T(8,128)(2,1)} %pad_maximum_fusion.4), calls=%async_computation | async-start | bytes 1310720 | tf_op jit(solution)/shard_map/gather_inputs/all_to_all | solution.py:14
  39.7 15.8 %all-to-all-start.1 = ((f32[8,32,256]{2,1,0:T(8,128)}), f32[8,32,256]{2,1,0:T(8,128)S(1)}, u32[]{:S(2)}, u32[]{:S(2)}) async-start(f32[8,32,256]{2,1,0:T(8,128)} %fusion.3), calls=%async_computation.1 | async-start | bytes 524288 | tf_op jit(solution)/shard_map/head/all_to_all | solution.py:14
  56.2 11.3 %all-to-all-start.2 = ((bf16[8,32,256]{2,1,0:T(8,128)(2,1)}), bf16[8,32,256]{2,1,0:T(8,128)(2,1)S(1)}, u32[]{:S(2)}, u32[]{:S(2)}) async-start(bf16[8,32,256]{2,1,0:T(8,128)(2,1)} %broadcast_in_dim.26), calls=%async_computation.2 | async-start | bytes 262144 | tf_op jit(solution)/shard_map/gather_heads/all_to_all | solution.py:14
  59.6 81.3 %all-gather.3.cloned.1.call-start = ((), (), s32[]{:S(2)}) async-start(), calls=%async_computation.7 | async-start | bytes 4325376 | tf_op jit(solution)/shard_map/gather_targets/all_gather | solution.py:84
  68.6 8.1 %collective-permute-start.1 = (bf16[16,2048]{1,0:T(8,128)(2,1)S(1)}, bf16[16,2048]{1,0:T(8,128)(2,1)S(1)}, u32[]{:S(2)}, u32[]{:S(2)}) collective-permute-start(bf16[16,2048]{1,0:T(8,128)(2,1)S(1)} %bitcast.57), channel_id=1, source_target_pairs={{0,128},{64,192},{128,0},{192,64},{1,129},{65,193},{129,1},{193,65... | collective-permute-start | bytes 196616 | tf_op jit(solution)/shard_map/gather_heads/ppermute | solution.py:22
  70.3 7.1 %collective-permute-start.2 = (bf16[16,2048]{1,0:T(8,128)(2,1)S(1)}, bf16[16,2048]{1,0:T(8,128)(2,1)S(1)}, u32[]{:S(2)}, u32[]{:S(2)}) collective-permute-start(bf16[16,2048]{1,0:T(8,128)(2,1)S(1)} %bitcast.58), channel_id=1, source_target_pairs={{0,192},{64,128},{128,64},{192,0},{1,193},{65,129},{129,65},{193,1... | collective-permute-start | bytes 196616 | tf_op jit(solution)/shard_map/gather_heads/ppermute | solution.py:22
  72.1 8.0 %collective-permute-start.6 = (bf16[16,2048]{1,0:T(8,128)(2,1)S(1)}, bf16[16,2048]{1,0:T(8,128)(2,1)S(1)}, u32[]{:S(2)}, u32[]{:S(2)}) collective-permute-start(bf16[16,2048]{1,0:T(8,128)(2,1)S(1)} %bitcast.52), channel_id=1, source_target_pairs={{0,2},{2,0},{4,6},{6,4},{1,3},{3,1},{5,7},{7,5},{8,10},{10,8},{12,... | collective-permute-start | bytes 196616 | tf_op jit(solution)/shard_map/gather_heads/ppermute | solution.py:22
  72.5 9.4 %collective-permute-start.7 = (bf16[16,2048]{1,0:T(8,128)(2,1)S(1)}, bf16[16,2048]{1,0:T(8,128)(2,1)S(1)}, u32[]{:S(2)}, u32[]{:S(2)}) collective-permute-start(bf16[16,2048]{1,0:T(8,128)(2,1)S(1)} %bitcast.53), channel_id=1, source_target_pairs={{0,4},{2,6},{4,0},{6,2},{1,5},{3,7},{5,1},{7,3},{8,12},{10,14},{12... | collective-permute-start | bytes 196616 | tf_op jit(solution)/shard_map/gather_heads/ppermute | solution.py:22
  74.3 7.6 %collective-permute-start.8 = (bf16[16,2048]{1,0:T(8,128)(2,1)S(1)}, bf16[16,2048]{1,0:T(8,128)(2,1)S(1)}, u32[]{:S(2)}, u32[]{:S(2)}) collective-permute-start(bf16[16,2048]{1,0:T(8,128)(2,1)S(1)} %bitcast.54), channel_id=1, source_target_pairs={{0,6},{2,4},{4,2},{6,0},{1,7},{3,5},{5,3},{7,1},{8,14},{10,12},{12... | collective-permute-start | bytes 196616 | tf_op jit(solution)/shard_map/gather_heads/ppermute | solution.py:22
  78.0 9.9 %collective-permute-start.4 = (bf16[16,8192]{1,0:T(8,128)(2,1)S(1)}, bf16[16,8192]{1,0:T(8,128)(2,1)S(1)}, u32[]{:S(2)}, u32[]{:S(2)}) collective-permute-start(bf16[16,8192]{1,0:T(8,128)(2,1)S(1)} %get-tuple-element.36), channel_id=1, source_target_pairs={{0,4},{2,6},{4,0},{6,2},{1,5},{3,7},{5,1},{7,3},{8,12},{10,14},{12... | collective-permute-start | bytes 786440 | tf_op jit(solution)/shard_map/gather_heads/ppermute | solution.py:22
  80.1 12.8 %collective-permute-start.5 = (bf16[16,8192]{1,0:T(8,128)(2,1)S(1)}, bf16[16,8192]{1,0:T(8,128)(2,1)S(1)}, u32[]{:S(2)}, u32[]{:S(2)}) collective-permute-start(bf16[16,8192]{1,0:T(8,128)(2,1)S(1)} %get-tuple-element.36), channel_id=1, source_target_pairs={{0,6},{2,4},{4,2},{6,0},{1,7},{3,5},{5,3},{7,1},{8,14},{10,12},{12... | collective-permute-start | bytes 786440 | tf_op jit(solution)/shard_map/gather_heads/ppermute | solution.py:22
  81.9 11.7 %collective-permute-start.10 = (bf16[64,2048]{1,0:T(8,128)(2,1)S(1)}, bf16[64,2048]{1,0:T(8,128)(2,1)S(1)}, u32[]{:S(2)}, u32[]{:S(2)}) collective-permute-start(bf16[64,2048]{1,0:T(8,128)(2,1)S(1)} %constant_dynamic-update-slice_fusion.4), channel_id=1, source_target_pairs={{0,128},{64,192},{128,0},{192,64},{1,129},{65,193},{129,1},{193,65... | collective-permute-start | bytes 786440 | tf_op jit(solution)/shard_map/gather_heads/ppermute | solution.py:22
  82.0 14.0 %collective-permute-start.11 = (bf16[64,2048]{1,0:T(8,128)(2,1)S(1)}, bf16[64,2048]{1,0:T(8,128)(2,1)S(1)}, u32[]{:S(2)}, u32[]{:S(2)}) collective-permute-start(bf16[64,2048]{1,0:T(8,128)(2,1)S(1)} %constant_dynamic-update-slice_fusion.4), channel_id=1, source_target_pairs={{0,192},{64,128},{128,64},{192,0},{1,193},{65,129},{129,65},{193,1... | collective-permute-start | bytes 786440 | tf_op jit(solution)/shard_map/gather_heads/ppermute | solution.py:22
  83.7 12.4 %collective-permute-start.9 = (bf16[64,2048]{1,0:T(8,128)(2,1)S(1)}, bf16[64,2048]{1,0:T(8,128)(2,1)S(1)}, u32[]{:S(2)}, u32[]{:S(2)}) collective-permute-start(bf16[64,2048]{1,0:T(8,128)(2,1)S(1)} %constant_dynamic-update-slice_fusion.4), channel_id=1, source_target_pairs={{0,64},{64,0},{128,192},{192,128},{1,65},{65,1},{129,193},{193,129... | collective-permute-start | bytes 786440 | tf_op jit(solution)/shard_map/gather_heads/ppermute | solution.py:22
  196.4 7.6 %collective-permute-start.14 = (bf16[16,8192]{1,0:T(8,128)(2,1)S(1)}, bf16[16,8192]{1,0:T(8,128)(2,1)S(1)}, u32[]{:S(2)}, u32[]{:S(2)}) collective-permute-start(bf16[16,8192]{1,0:T(8,128)(2,1)S(1)} %get-tuple-element.12), channel_id=1, source_target_pairs={{0,2},{2,0},{4,6},{6,4},{1,3},{3,1},{5,7},{7,5},{8,10},{10,8},{12,... | collective-permute-start | bytes 786440 | tf_op jit(solution)/shard_map/reduce_grad/ppermute | solution.py:22
  196.8 13.5 %collective-permute-start.15 = (bf16[16,8192]{1,0:T(8,128)(2,1)S(1)}, bf16[16,8192]{1,0:T(8,128)(2,1)S(1)}, u32[]{:S(2)}, u32[]{:S(2)}) collective-permute-start(bf16[16,8192]{1,0:T(8,128)(2,1)S(1)} %get-tuple-element.14), channel_id=1, source_target_pairs={{0,4},{2,6},{4,0},{6,2},{1,5},{3,7},{5,1},{7,3},{8,12},{10,14},{12... | collective-permute-start | bytes 786440 | tf_op jit(solution)/shard_map/reduce_grad/ppermute | solution.py:22
  198.6 13.7 %collective-permute-start.16 = (bf16[16,8192]{1,0:T(8,128)(2,1)S(1)}, bf16[16,8192]{1,0:T(8,128)(2,1)S(1)}, u32[]{:S(2)}, u32[]{:S(2)}) collective-permute-start(bf16[16,8192]{1,0:T(8,128)(2,1)S(1)} %get-tuple-element.13), channel_id=1, source_target_pairs={{0,6},{2,4},{4,2},{6,0},{1,7},{3,5},{5,3},{7,1},{8,14},{10,12},{12... | collective-permute-start | bytes 786440 | tf_op jit(solution)/shard_map/reduce_grad/ppermute | solution.py:22
  200.4 14.1 %collective-permute-start.20 = (bf16[64,2048]{1,0:T(8,128)(2,1)S(1)}, bf16[64,2048]{1,0:T(8,128)(2,1)S(1)}, u32[]{:S(2)}, u32[]{:S(2)}) collective-permute-start(bf16[64,2048]{1,0:T(8,128)(2,1)S(1)} %get-tuple-element.15), channel_id=1, source_target_pairs={{0,64},{64,0},{128,192},{192,128},{1,65},{65,1},{129,193},{193,129... | collective-permute-start | bytes 786440 | tf_op jit(solution)/shard_map/reduce_grad/ppermute | solution.py:22
  200.8 15.5 %collective-permute-start.21 = (bf16[64,2048]{1,0:T(8,128)(2,1)S(1)}, bf16[64,2048]{1,0:T(8,128)(2,1)S(1)}, u32[]{:S(2)}, u32[]{:S(2)}) collective-permute-start(bf16[64,2048]{1,0:T(8,128)(2,1)S(1)} %get-tuple-element.17), channel_id=1, source_target_pairs={{0,128},{64,192},{128,0},{192,64},{1,129},{65,193},{129,1},{193,65... | collective-permute-start | bytes 786440 | tf_op jit(solution)/shard_map/reduce_grad/ppermute | solution.py:22
  204.0 14.4 %collective-permute-start.22 = (bf16[64,2048]{1,0:T(8,128)(2,1)S(1)}, bf16[64,2048]{1,0:T(8,128)(2,1)S(1)}, u32[]{:S(2)}, u32[]{:S(2)}) collective-permute-start(bf16[64,2048]{1,0:T(8,128)(2,1)S(1)} %get-tuple-element.16), channel_id=1, source_target_pairs={{0,192},{64,128},{128,64},{192,0},{1,193},{65,129},{129,65},{193,1... | collective-permute-start | bytes 786440 | tf_op jit(solution)/shard_map/reduce_grad/ppermute | solution.py:22
  212.4 7.6 %collective-permute-start.17 = (bf16[16,2048]{1,0:T(8,128)(2,1)S(1)}, bf16[16,2048]{1,0:T(8,128)(2,1)S(1)}, u32[]{:S(2)}, u32[]{:S(2)}) collective-permute-start(bf16[16,2048]{1,0:T(8,128)(2,1)S(1)} %get-tuple-element.20), channel_id=1, source_target_pairs={{0,64},{64,0},{128,192},{192,128},{1,65},{65,1},{129,193},{193,129... | collective-permute-start | bytes 196616 | tf_op jit(solution)/shard_map/reduce_grad/ppermute | solution.py:22
  212.9 9.7 %collective-permute-start.18 = (bf16[16,2048]{1,0:T(8,128)(2,1)S(1)}, bf16[16,2048]{1,0:T(8,128)(2,1)S(1)}, u32[]{:S(2)}, u32[]{:S(2)}) collective-permute-start(bf16[16,2048]{1,0:T(8,128)(2,1)S(1)} %get-tuple-element.22), channel_id=1, source_target_pairs={{0,128},{64,192},{128,0},{192,64},{1,129},{65,193},{129,1},{193,65... | collective-permute-start | bytes 196616 | tf_op jit(solution)/shard_map/reduce_grad/ppermute | solution.py:22
  214.6 8.0 %collective-permute-start.19 = (bf16[16,2048]{1,0:T(8,128)(2,1)S(1)}, bf16[16,2048]{1,0:T(8,128)(2,1)S(1)}, u32[]{:S(2)}, u32[]{:S(2)}) collective-permute-start(bf16[16,2048]{1,0:T(8,128)(2,1)S(1)} %get-tuple-element.21), channel_id=1, source_target_pairs={{0,192},{64,128},{128,64},{192,0},{1,193},{65,129},{129,65},{193,1... | collective-permute-start | bytes 196616 | tf_op jit(solution)/shard_map/reduce_grad/ppermute | solution.py:22
  235.9 15.8 %all-to-all-start.6 = ((bf16[8,48,256]{2,1,0:T(8,128)(2,1)}), bf16[8,48,256]{2,1,0:T(8,128)(2,1)S(1)}, u32[]{:S(2)}, u32[]{:S(2)}) async-start(bf16[8,48,256]{2,1,0:T(8,128)(2,1)} %broadcast_in_dim.58), calls=%async_computation.6 | async-start | bytes 393216 | tf_op jit(solution)/shard_map/finish/all_to_all | solution.py:14
  (18 other events, 244.5 us)
Sparse Core Ops, SparseCore 0:
  63.0 77.7 all-gather.2

commit v3 on v2

--- a/solution.py
+++ b/solution.py
@@ -1,12 +1,17 @@
 import jax
 import jax.numpy as jnp
 from jax import lax
+from jax.experimental import pallas as pl
+from jax.experimental.pallas import tpu as pltpu
 from jax.sharding import Mesh, PartitionSpec as P
 
 BF16 = jnp.bfloat16
 F32 = jnp.float32
 REP = ("y", "z")
 VOC = ("x", "c")
+CHUNKS = 4
+VMEM_LIMIT = 32 * 1024 * 1024
+HEAD_COST = 45_000_000_000
 SIZES = {"y": 4, "z": 8, "x": 4, "c": 2}
 
 
@@ -39,24 +44,230 @@
     return total.astype(BF16)
 
 
+def cost(flops, bytes_accessed, transcendentals=0):
+    return pl.CostEstimate(
+        flops=flops, bytes_accessed=bytes_accessed, transcendentals=transcendentals
+    )
+
+
+def whole(shape):
+    return pl.BlockSpec(shape, lambda *at: (0,) * len(shape))
+
+
+def scalar_call(kernel, steps, in_specs, out_specs, out_shape, estimate, scratch=()):
+    return pl.pallas_call(
+        kernel,
+        grid_spec=pltpu.PrefetchScalarGridSpec(
+            num_scalar_prefetch=1,
+            grid=(steps,),
+            in_specs=in_specs,
+            out_specs=out_specs,
+            scratch_shapes=scratch,
+        ),
+        out_shape=out_shape,
+        compiler_params=pltpu.CompilerParams(vmem_limit_bytes=VMEM_LIMIT),
+        cost_estimate=estimate,
+    )
+
+
+NT = (((1,), (1,)), ((), ()))
+
+
+def teacher_kernel(place, target_ref, vocab_ref, out_ref, total):
+    step = pl.program_id(0)
+    product = lax.dot_general(
+        target_ref[...], vocab_ref[...], NT, preferred_element_type=F32
+    )
+
+    @pl.when(step == 0)
+    def _():
+        total[...] = product
+
+    @pl.when(step > 0)
+    def _():
+        total[...] += product
+
+    @pl.when(step == CHUNKS - 1)
+    def _():
+        for at in range(16):
+            start = pl.multiple_of(place[at] * 16, 16)
+            out_ref[at * 16 : (at + 1) * 16] = total[pl.ds(start, 16)]
+
+
+def teacher_logits(place, target_all, vocab_head):
+    (count, depth), entries = target_all.shape, vocab_head.shape[0]
+    width = depth // CHUNKS
+    return scalar_call(
+        teacher_kernel,
+        CHUNKS,
+        [
+            pl.BlockSpec((count, width), lambda step, place: (0, step)),
+            pl.BlockSpec((entries, width), lambda step, place: (0, step)),
+        ],
+        whole((count, entries)),
+        jax.ShapeDtypeStruct((count, entries), F32),
+        cost(2 * count * entries * depth, 2 * (count + entries) * depth),
+        [pltpu.VMEM((count, entries), F32)],
+    )(place, target_all, vocab_head)
+
+
+def student_kernel(place, *refs):
+    firsts, seconds = refs[:8], refs[8:16]
+    vocab_ref, teacher_ref, out_ref, sums_ref, turned = refs[16:]
+    step = pl.program_id(0)
+
+    for at in range(CHUNKS):
+
+        @pl.when(step == at)
+        def _():
+            rows = []
+            for core in range(2):
+                rows += [ref[...] for ref in firsts[4 * core : 4 * core + 4]]
+                rows.append(seconds[4 * core + at][...])
+            product = lax.dot_general(
+                jnp.concatenate(rows, axis=0), vocab_ref[...], NT, preferred_element_type=F32
+            )
+            if at == 0:
+                out_ref[...] = product
+            else:
+                out_ref[...] += product
+
+    @pl.when(step == CHUNKS - 1)
+    def _():
+        student, teacher = out_ref[...], teacher_ref[...]
+        exp_teacher = jnp.exp(teacher)
+        columns = [
+            jnp.sum(exp_teacher, axis=1, keepdims=True),
+            jnp.sum(jnp.exp(student), axis=1, keepdims=True),
+            jnp.sum(exp_teacher * (teacher - student), axis=1, keepdims=True),
+        ]
+        lane = lax.broadcasted_iota(jnp.int32, turned.shape, 1)
+        table = jnp.zeros(turned.shape, F32)
+        for at, column in enumerate(columns):
+            table = jnp.where(lane == at, column, table)
+        for at in range(16):
+            start = pl.multiple_of(place[at] * 16, 16)
+            turned[pl.ds(start, 16)] = table[at * 16 : (at + 1) * 16]
+        sums_ref[...] = turned[...].T[:8]
+
+
+def student_logits(place, firsts, seconds, vocab_head, teacher):
+    count, entries = teacher.shape
+    depth = vocab_head.shape[1]
+    width = depth // CHUNKS
+    return scalar_call(
+        student_kernel,
+        CHUNKS,
+        [pl.BlockSpec((firsts[0].shape[0], width), lambda step, place: (0, step))] * 8
+        + [whole(seconds[0].shape)] * 8
+        + [
+            pl.BlockSpec((entries, width), lambda step, place: (0, step ^ place[16])),
+            whole((count, entries)),
+        ],
+        [whole((count, entries)), whole((8, count))],
+        [
+            jax.ShapeDtypeStruct((count, entries), F32),
+            jax.ShapeDtypeStruct((8, count), F32),
+        ],
+        cost(2 * count * entries * depth, 2 * (count + entries) * depth, 2 * count * entries),
+        [pltpu.VMEM((count, 128), F32)],
+    )(place, *firsts, *seconds, vocab_head, teacher)
+
+
+def grad_kernel(
+    place, teacher_ref, student_ref, logs_ref, vocab_ref, own_ref, other_ref, table, turned, grad
+):
+    count = grad.shape[0]
+
+    @pl.when(pl.program_id(0) == 0)
+    def _():
+        table[...] = jnp.concatenate([logs_ref[...], jnp.zeros((120, count), F32)], axis=0).T
+        for at in range(16):
+            start = pl.multiple_of(place[at] * 16, 16)
+            turned[at * 16 : (at + 1) * 16] = table[pl.ds(start, 16)]
+        student = jnp.exp(student_ref[...] - turned[:, 1:2])
+        teacher = jnp.exp(teacher_ref[...] - turned[:, 0:1])
+        grad[...] = (student - teacher).astype(BF16)
+
+    product = jnp.dot(grad[...], vocab_ref[...], preferred_element_type=F32).astype(BF16)
+    own_ref[...] = product[: count // 2]
+    other_ref[...] = product[count // 2 :]
+
+
+def grad_rows(place, teacher, student, logs, vocab_head):
+    count, entries = teacher.shape
+    depth = vocab_head.shape[1]
+    width = depth // CHUNKS
+    half = pl.BlockSpec((count // 2, width), lambda step, place: (0, step))
+    return scalar_call(
+        grad_kernel,
+        CHUNKS,
+        [
+            whole((count, entries)),
+            whole((count, entries)),
+            whole((8, count)),
+            pl.BlockSpec((entries, width), lambda step, place: (0, step ^ place[16])),
+        ],
+        [half, half],
+        [jax.ShapeDtypeStruct((count // 2, depth), BF16)] * 2,
+        cost(2 * count * entries * depth, 2 * (count + entries) * depth, 2 * count * entries),
+        [
+            pltpu.VMEM((count, 128), F32),
+            pltpu.VMEM((count, 128), F32),
+            pltpu.VMEM((count, entries), BF16),
+        ],
+    )(place, teacher, student, logs, vocab_head)
+
+
+def join_kernel(*refs):
+    firsts, seconds, (first_ref, second_ref) = refs[:4], refs[4:8], refs[8:]
+    (rows, width), (block, _) = firsts[0].shape, seconds[0].shape
+    for at in range(4):
+        first_ref[:, at * width : (at + 1) * width] = firsts[at][...]
+        second_ref[at * block : (at + 1) * block] = seconds[at][...]
+
+
+def join(firsts, seconds):
+    (rows, width), (block, across) = firsts[0].shape, seconds[0].shape
+    return pl.pallas_call(
+        join_kernel,
+        out_shape=[
+            jax.ShapeDtypeStruct((rows, 4 * width), BF16),
+            jax.ShapeDtypeStruct((4 * block, across), BF16),
+        ],
+        compiler_params=pltpu.CompilerParams(vmem_limit_bytes=VMEM_LIMIT),
+        cost_estimate=cost(0, 16 * rows * width),
+    )(*firsts, *seconds)
+
+
+def head_kernel(rows_ref, weight_ref, out_ref):
+    out_ref[...] = jnp.dot(rows_ref[...], weight_ref[...], preferred_element_type=F32)
+
+
+def head_partial(rows, weight):
+    return pl.pallas_call(
+        head_kernel,
+        out_shape=jax.ShapeDtypeStruct((rows.shape[0], weight.shape[1]), F32),
+        compiler_params=pltpu.CompilerParams(vmem_limit_bytes=VMEM_LIMIT),
+        cost_estimate=cost(HEAD_COST, 2 * (rows.size + weight.size)),
+    )(rows, weight)
+
+
 def gather_heads(heads):
     rows, width = heads.shape
     half = rows // 2
     lines = gathered(heads, "z", 8).transpose(1, 0, 2).reshape(rows, -1)
-    first, second = lines[:half], lines[half:]
-    first = jnp.concatenate(from_peers(first, "y"), axis=1)
-    second = jnp.concatenate(from_peers(second, "x"), axis=0)
-    first_parts = from_peers(first, "x")
-    second_parts = from_peers(second, "y")
-    mine = jnp.concatenate([*first_parts, jnp.concatenate(second_parts, axis=1)], axis=0)
-    return jnp.concatenate([mine, swap(mine, "c", 1)], axis=0)
-
-
-def scatter_grad(part):
-    rows, depth = part.shape
-    own, other = part[: rows // 2], part[rows // 2 :]
+    first, second = join(from_peers(lines[:half], "y"), from_peers(lines[half:], "x"))
+    firsts, seconds = from_peers(first, "x"), from_peers(second, "y")
+    firsts = firsts + [swap(block, "c", 1) for block in firsts]
+    seconds = seconds + [swap(block, "c", 1) for block in seconds]
+    return firsts, seconds
+
+
+def scatter_grad(own, other):
+    rows, depth = own.shape
     mine = (own.astype(F32) + swap(other, "c", 1).astype(F32)).astype(BF16)
-    half = rows // 4
+    half = rows // 2
     block = half // 4
     width = depth // 4
     first = [mine[i * block : (i + 1) * block] for i in range(4)]
@@ -92,56 +303,29 @@
         input_rows = got[:, :, :in_width].reshape(count, in_width)
         residual = got[:, :, in_width:].reshape(count, out_width)
         residual = lax.dynamic_slice_in_dim(residual, voc_index * rows, rows, 0)
-    with jax.named_scope("turn_columns"):
-        quarter = vocab_head.shape[1] // 4
-        turned = jnp.concatenate(
-            [
-                lax.dynamic_slice_in_dim(vocab_head, (at_y ^ step) * quarter, quarter, 1)
-                for step in range(4)
-            ],
-            axis=1,
-        )
     with jax.named_scope("head"):
-        partial_pre = jnp.dot(input_rows, head_weight, preferred_element_type=F32)
+        partial_pre = head_partial(input_rows, head_weight)
         parts = exchange(partial_pre.reshape(vocs, rows, out_width), VOC)
         preact = jnp.sum(parts, axis=0) + head_bias
         heads = (residual.astype(F32) + jax.nn.silu(preact)).astype(BF16)
-    with jax.named_scope("gather_heads"):
-        head_all = gather_heads(heads)
     steps = jnp.arange(16)
     order = ((at_x ^ (steps % 4)) * 2 + (at_c ^ (steps // 8))) * 2 + (steps // 4) % 2
-    with jax.named_scope("turn_targets"):
-        target_all = target_all.reshape(16, count // 16, -1)[order].reshape(count, -1)
-    contract = (((1,), (1,)), ((), ()))
-    with jax.named_scope("logits"):
-        teacher = lax.dot_general(vocab_head, target_all, contract, preferred_element_type=F32)
-        student = lax.dot_general(turned, head_all, contract, preferred_element_type=F32)
-        exp_teacher = jnp.exp(teacher)
-        sums = jnp.stack(
-            [
-                jnp.sum(exp_teacher, axis=0),
-                jnp.sum(jnp.exp(student), axis=0),
-                jnp.sum(exp_teacher * (teacher - student), axis=0),
-                jnp.zeros((count,), F32),
-            ]
-        )
-        back = (steps // 2 % 2 ^ at_c) * 8 + steps % 2 * 4 + (steps // 4 ^ at_x)
-        sums = sums.reshape(4, 16, -1)[:, back].reshape(8, -1)
+    place = jnp.concatenate([order, at_y[None]]).astype(jnp.int32)
+    with jax.named_scope("teacher"):
+        teacher = teacher_logits(place, target_all, vocab_head)
+    with jax.named_scope("gather_heads"):
+        firsts, seconds = gather_heads(heads)
+    with jax.named_scope("student"):
+        student, sums = student_logits(place, firsts, seconds, vocab_head, teacher)
     with jax.named_scope("totals"):
         sums = jnp.sum(gathered(sums, VOC, vocs), axis=0)
-        sums = jnp.sum(gathered(sums, REP, reps), axis=0).reshape(4, count)
-        log_teacher, log_student = jnp.log(sums[0]), jnp.log(sums[1])
-        loss = jnp.sum(sums[2] / sums[0] - log_teacher + log_student) / count
-        log_teacher = log_teacher.reshape(16, -1)[order].reshape(count)
-        log_student = log_student.reshape(16, -1)[order].reshape(count)
+        sums = jnp.sum(gathered(sums, REP, reps), axis=0)
+        logs = jnp.log(sums)
+        loss = jnp.sum(sums[2] / sums[0] - logs[0] + logs[1]) / count
     with jax.named_scope("grad"):
-        grad_logits = (jnp.exp(student - log_student) - jnp.exp(teacher - log_teacher)).astype(BF16)
-        outer = (((0,), (0,)), ((), ()))
-        grad_part = lax.dot_general(
-            grad_logits, turned, outer, preferred_element_type=F32
-        ).astype(BF16)
+        own_rows, other_rows = grad_rows(place, teacher, student, logs, vocab_head)
     with jax.named_scope("reduce_grad"):
-        grad_heads = scatter_grad(grad_part)
+        grad_heads = scatter_grad(own_rows, other_rows)
     with jax.named_scope("finish"):
         sigma = jax.nn.sigmoid(preact)
         grad_pre = grad_heads * (sigma * (1.0 + preact * (1.0 - sigma)))

time: 262 us -> 235 us (0.90)
  waiting for transfers between devices: 89.2 us -> 65.5 us
  matrix products: 19 us -> 1.32 us
  Pallas kernels: 0 us -> 16.2 us
  local copies, waits for them, and re-layouts: 26.7 us -> 18.4 us
  blocking collectives: 36.9 us -> 43.4 us
    all_gather x1, waiting for transfers between devices: 28.7 us -> 0.01 us  [shards(): target_all = lax.all_gather(targets, REP, axis=0, tiled=True)]
    dot_general x4 -> x0, matrix products: 17.7 us -> none  [the longest x1 7.79 us: shards(): lax.dot_general(grad_logits, turned, outer, preferred_element_type=F32)]
    pallas_call x0 -> x5, Pallas kernels: none -> 16.2 us  [the longest x1 5.92 us: student_logits(): scalar_call(student_kernel, CHUNKS, [pl.BlockSpec((firsts[0].shape[0], wi...]
    ppermute x26 -> x33, waiting for transfers between devices: 25.9 us -> 36.5 us  [swap(): lax.ppermute(block, axis, [(i, i ^ step) for i in range(SIZES[axis])])]
    unnamed x33 -> x31, local copies, waits for them, and re-layouts: 7.59 us -> 15.3 us
    gather x5 -> x0, local copies, waits for them, and re-layouts: 6.74 us -> none  [the longest x1 5.02 us: shards(): target_all.reshape(16, count // 16, -1)[order].reshape(count, -1)]
    all_to_all x3 -> x4, blocking collectives: 36.9 us -> 43.4 us  [exchange(): return lax.all_to_all(blocks, axis, split_axis=0, concat_axis=0, tiled=True)]
    all_to_all x4 -> x3, waiting for transfers between devices: 34.6 us -> 28.9 us  [exchange(): return lax.all_to_all(blocks, axis, split_axis=0, concat_axis=0, tiled=True)]
  transfers between devices with their start and end apart: 31 -> 37, of which waited for: 16 -> 15; matrix products, arithmetic and copies ran while one was open for 7% -> 1% of each run, Pallas kernels for 0% -> 2%
where the time goes in v3:
time: 235 us
  starting transfers between devices  69 us (29%)
  waiting for transfers between devices  65.5 us (28%)
  blocking collectives  43.4 us (18%)
  local copies, waits for them, and re-layouts  18.4 us (8%)
  Pallas kernels  16.2 us (7%)
  between operations  16.2 us (7%)
  other arithmetic  4.62 us (2%)
    all_to_all x4, blocking collectives, exchange(): return lax.all_to_all(blocks, axis, split_axis=0, concat_axis=0, tiled=True)  43.4 us
    ppermute x33, starting transfers between devices, swap(): lax.ppermute(block, axis, [(i, i ^ step) for i in range(SIZES[axis])])  38 us
    ppermute x33, waiting for transfers between devices, swap(): lax.ppermute(block, axis, [(i, i ^ step) for i in range(SIZES[axis])])  36.5 us
    all_to_all x3, starting transfers between devices, exchange(): return lax.all_to_all(blocks, axis, split_axis=0, concat_axis=0, tiled=True)  31 us
    all_to_all x3, waiting for transfers between devices, exchange(): return lax.all_to_all(blocks, axis, split_axis=0, concat_axis=0, tiled=True)  28.9 us
    unnamed x31, local copies, waits for them, and re-layouts  15.3 us
    pallas_call x1, Pallas kernels, student_logits(): scalar_call(student_kernel, CHUNKS, [pl.BlockSpec((firsts[0].shape[0], wi...  5.92 us
  transfers between devices with their start and end apart: 37, of which 15 were waited for; matrix products, arithmetic and copies ran while one was open for 1% of the time, Pallas kernels for 2%

profile of v3, /device:TPU:1, one launch (start us, length us, event | category | flops | bytes accessed | tf_op | source)
XLA Modules:
  0.0 234.7 jit_solution(2253116236244375995)
XLA Ops:
  12.0 12.0 %all-to-all-start = ((bf16[32,8,1280]{2,1,0:T(8,128)(2,1)}), bf16[32,8,1280]{2,1,0:T(8,128)(2,1)S(1)}, u32[]{:S(2)}, u32[]{:S(2)}) async-start(bf16[32,8,1280]{2,1,0:T(8,128)(2,1)} %pad_maximum_fusion), calls=%async_computation | async-start | bytes 1310720 | tf_op jit(solution)/shard_map/gather_inputs/all_to_all | solution.py:19
  24.0 17.8 %all-to-all-done = bf16[32,8,1280]{2,1,0:T(8,128)(2,1)S(1)} async-done(((bf16[32,8,1280]{2,1,0:T(8,128)(2,1)}), bf16[32,8,1280]{2,1,0:T(8,128)(2,1)S(1)}, u32[]{:S(2)}, u32[]{:S(2)}) %all-to-all-start) | async-done | bytes 655392 | tf_op jit(solution)/shard_map/gather_inputs/all_to_all | solution.py:19
  42.9 10.6 %all-to-all-start.1 = ((f32[8,32,256]{2,1,0:T(8,128)}), f32[8,32,256]{2,1,0:T(8,128)S(1)}, u32[]{:S(2)}, u32[]{:S(2)}) async-start(f32[8,32,256]{2,1,0:T(8,128)} %bitcast.5), calls=%async_computation.1 | async-start | bytes 524288 | tf_op jit(solution)/shard_map/head/all_to_all | solution.py:19
  53.6 6.5 %all-to-all-done.1 = f32[8,32,256]{2,1,0:T(8,128)S(1)} async-done(((f32[8,32,256]{2,1,0:T(8,128)}), f32[8,32,256]{2,1,0:T(8,128)S(1)}, u32[]{:S(2)}, u32[]{:S(2)}) %all-to-all-start.1) | async-done | bytes 262176 | tf_op jit(solution)/shard_map/head/all_to_all | solution.py:19
  60.1 11.2 %all_to_all.35 = bf16[8,32,256]{2,1,0:T(8,128)(2,1)S(1)} all-to-all(bf16[8,32,256]{2,1,0:T(8,128)(2,1)S(1)} %broadcast_in_dim.24), channel_id=1, replica_groups=mesh['y'=4,'z'=8,'x'=4,'c'=2] {'z'}, dimensions={0} | all-to-all | bytes 262144 | tf_op jit(solution)/shard_map/gather_heads/all_to_all | solution.py:19
  81.7 3.6 %collective-permute-start.9 = (bf16[16,8192]{1,0:T(8,128)(2,1)S(1)}, bf16[16,8192]{1,0:T(8,128)(2,1)S(1)}, u32[]{:S(2)}, u32[]{:S(2)}) collective-permute-start(bf16[16,8192]{1,0:T(8,128)(2,1)S(1)} %get-tuple-element.9.refs_0_), channel_id=1, source_target_pairs={{0,1},{1,0},{2,3},{3,2},{4,5},{5,4},{6,7},{7,6},{8,9},{9,8},{10,11... | collective-permute-start | bytes 786440 | tf_op jit(solution)/shard_map/gather_heads/ppermute | solution.py:27
  90.6 9.5 %collective-permute-done.8.refs_3_ = bf16[16,8192]{1,0:T(8,128)(2,1)S(1)} collective-permute-done((bf16[16,8192]{1,0:T(8,128)(2,1)S(1)}, bf16[16,8192]{1,0:T(8,128)(2,1)S(1)}, u32[]{:S(2)}, u32[]{:S(2)}) %collective-permute-start.8) | collective-permute-done | bytes 262176 | tf_op jit(solution)/shard_map/gather_heads/ppermute | solution.py:27
  103.7 5.1 %collective-permute-done.14.refs_10_ = bf16[64,2048]{1,0:T(8,128)(2,1)} collective-permute-done((bf16[64,2048]{1,0:T(8,128)(2,1)S(1)}, bf16[64,2048]{1,0:T(8,128)(2,1)}, u32[]{:S(2)}, u32[]{:S(2)}) %collective-permute-start.14) | collective-permute-done | bytes 262176 | tf_op jit(solution)/shard_map/gather_heads/ppermute | solution.py:27
  108.8 2.9 %collective-permute-start.19 = (bf16[64,2048]{1,0:T(8,128)(2,1)}, bf16[64,2048]{1,0:T(8,128)(2,1)}, u32[]{:S(2)}, u32[]{:S(2)}) collective-permute-start(bf16[64,2048]{1,0:T(8,128)(2,1)} %collective-permute-done.15.refs_11_), channel_id=1, source_target_pairs={{0,1},{1,0},{2,3},{3,2},{4,5},{5,4},{6,7},{7,6},{8,9},{9,8},{10,11... | collective-permute-start | bytes 786440 | tf_op jit(solution)/shard_map/gather_heads/ppermute | solution.py:27
  115.5 3.3 %copy-done.1 = bf16[501,8192]{1,0:T(8,128)(2,1)S(1)} copy-done((bf16[501,8192]{1,0:T(8,128)(2,1)S(1)}, bf16[501,8192]{1,0:T(8,128)(2,1)}, u32[]{:S(2)}) %copy-start.1) | copy-done | bytes 8208408
  121.1 4.6 %teacher.1.refs_17_.teacher_ref = f32[256,501]{1,0:T(8,128)S(1)} custom-call(s32[17]{0:T(128)S(1)} %pad_add_fusion.place, bf16[256,8192]{1,0:T(8,128)(2,1)S(1)} %copy-done.4, bf16[501,8192]{1,0:T(8,128)(2,1)S(1)} %copy-done.1), custom_call_target="tpu_custom_call" | custom-call | flops 2101346304 | bytes 12402688 | tf_op jit(solution)/shard_map/teacher/pallas_call | solution.py:100
  125.8 3.3 %copy-done.2 = bf16[501,8192]{1,0:T(8,128)(2,1)S(1)} copy-done((bf16[501,8192]{1,0:T(8,128)(2,1)S(1)}, bf16[501,8192]{1,0:T(8,128)(2,1)}, u32[]{:S(2)}) %copy-start.2) | copy-done | bytes 8208408
  131.0 5.9 %student.1 = (f32[256,501]{1,0:T(8,128)S(1)}, f32[8,256]{1,0:T(8,128)S(1)}) custom-call(s32[17]{0:T(128)S(1)} %pad_add_fusion.place, bf16[16,8192]{1,0:T(8,128)(2,1)S(1)} %get-tuple-element.9.refs_0_, bf16[16,8192]{1,0:T(8,128)(2,1)S(1)} %copy-done.6, bf16[16,8192]{1,0:T(8,128)(2,1)S(1)} %collective-permute-done.7.refs_2_, ...), custom_call_target="tpu_custom_call" | custom-call | flops 2101346304 | bytes 12402688 | tf_op jit(solution)/shard_map/student/pallas_call | solution.py:158
  136.9 7.8 %all_to_all.36 = f32[8,8,256]{2,1,0:T(8,128)S(1)} all-to-all(f32[8,8,256]{2,1,0:T(8,128)S(1)} %broadcast_in_dim.49), channel_id=1, replica_groups=mesh['y'=4,'z'=8,'x'=4,'c'=2] {'x','c'}, dimensions={0} | all-to-all | bytes 131072 | tf_op jit(solution)/shard_map/totals/all_to_all | solution.py:19
  144.8 13.6 %all_to_all.37 = f32[32,8,256]{2,1,0:T(8,128)S(1)} all-to-all(f32[32,8,256]{2,1,0:T(8,128)S(1)} %broadcast_in_dim.50), channel_id=1, replica_groups=mesh['y'=4,'z'=8,'x'=4,'c'=2] {'y','z'}, dimensions={0} | all-to-all | bytes 524288 | tf_op jit(solution)/shard_map/totals/all_to_all | solution.py:19
  158.5 3.3 %copy-done.3 = bf16[501,8192]{1,0:T(8,128)(2,1)S(1)} copy-done((bf16[501,8192]{1,0:T(8,128)(2,1)S(1)}, bf16[501,8192]{1,0:T(8,128)(2,1)}, u32[]{:S(2)}) %copy-start.3) | copy-done | bytes 8208408
  161.8 4.6 %grad.1 = (bf16[128,8192]{1,0:T(8,128)(2,1)S(1)}, bf16[128,8192]{1,0:T(8,128)(2,1)S(1)}) custom-call(s32[17]{0:T(128)S(1)} %pad_add_fusion.place, f32[256,501]{1,0:T(8,128)S(1)} %teacher.1.refs_17_.teacher_ref, f32[256,501]{1,0:T(8,128)S(1)} %get-tuple-element.12.student_ref, f32[8,256]{1,0:T(8,128)S(1)} %log.3.logs_ref, bf16[501,8192]{1,0:T(8,128)(2,1)S(1)} %copy-done.3), custom_call_target="tpu_custom_call" | custom-call | flops 2101346304 | bytes 12402688 | tf_op jit(solution)/shard_map/grad/pallas_call | solution.py:202
  166.5 3.7 %collective-permute-start.20 = (bf16[128,8192]{1,0:T(8,128)(2,1)S(1)}, bf16[128,8192]{1,0:T(8,128)(2,1)S(1)}, u32[]{:S(2)}, u32[]{:S(2)}) collective-permute-start(bf16[128,8192]{1,0:T(8,128)(2,1)S(1)} %get-tuple-element.14), channel_id=1, source_target_pairs={{0,1},{1,0},{2,3},{3,2},{4,5},{5,4},{6,7},{7,6},{8,9},{9,8},{10,11... | collective-permute-start | bytes 6291464 | tf_op jit(solution)/shard_map/reduce_grad/ppermute | solution.py:27
  170.2 3.8 %collective-permute-done.20 = bf16[128,8192]{1,0:T(8,128)(2,1)S(1)} collective-permute-done((bf16[128,8192]{1,0:T(8,128)(2,1)S(1)}, bf16[128,8192]{1,0:T(8,128)(2,1)S(1)}, u32[]{:S(2)}, u32[]{:S(2)}) %collective-permute-start.20) | collective-permute-done | bytes 2097184 | tf_op jit(solution)/shard_map/reduce_grad/ppermute | solution.py:27
  179.1 3.1 %collective-permute-done.27 = bf16[64,2048]{1,0:T(8,128)(2,1)S(1)} collective-permute-done((bf16[64,2048]{1,0:T(8,128)(2,1)S(1)}, bf16[64,2048]{1,0:T(8,128)(2,1)S(1)}, u32[]{:S(2)}, u32[]{:S(2)}) %collective-permute-start.27) | collective-permute-done | bytes 262176 | tf_op jit(solution)/shard_map/reduce_grad/ppermute | solution.py:27
  184.1 4.4 %collective-permute-done.28 = bf16[64,2048]{1,0:T(8,128)(2,1)S(1)} collective-permute-done((bf16[64,2048]{1,0:T(8,128)(2,1)S(1)}, bf16[64,2048]{1,0:T(8,128)(2,1)S(1)}, u32[]{:S(2)}, u32[]{:S(2)}) %collective-permute-start.28) | collective-permute-done | bytes 262176 | tf_op jit(solution)/shard_map/reduce_grad/ppermute | solution.py:27
  198.8 10.8 %all_to_all.38 = bf16[8,32,256]{2,1,0:T(8,128)(2,1)S(1)} all-to-all(bf16[8,32,256]{2,1,0:T(8,128)(2,1)S(1)} %bitcast.38), channel_id=1, replica_groups=mesh['y'=4,'z'=8,'x'=4,'c'=2] {'z'}, dimensions={0} | all-to-all | bytes 262144 | tf_op jit(solution)/shard_map/reduce_grad/all_to_all | solution.py:19
  210.5 8.3 %all-to-all-start.6 = ((bf16[8,48,256]{2,1,0:T(8,128)(2,1)}), bf16[8,48,256]{2,1,0:T(8,128)(2,1)S(1)}, u32[]{:S(2)}, u32[]{:S(2)}) async-start(bf16[8,48,256]{2,1,0:T(8,128)(2,1)} %broadcast_in_dim.52), calls=%async_computation.6 | async-start | bytes 393216 | tf_op jit(solution)/shard_map/finish/all_to_all | solution.py:19
  220.1 4.6 %all-to-all-done.6 = bf16[8,48,256]{2,1,0:T(8,128)(2,1)S(1)} async-done(((bf16[8,48,256]{2,1,0:T(8,128)(2,1)}), bf16[8,48,256]{2,1,0:T(8,128)(2,1)S(1)}, u32[]{:S(2)}, u32[]{:S(2)}) %all-to-all-start.6) | async-done | bytes 196640 | tf_op jit(solution)/shard_map/finish/all_to_all | solution.py:19
  (135 shorter events, 53.8 us)
Async XLA Ops:
  7.2 108.4 %all-gather.3.cloned.1.call-start = ((), (), s32[]{:S(2)}) async-start(), calls=%async_computation.7 | async-start | bytes 4325376 | tf_op jit(solution)/shard_map/gather_targets/all_gather | solution.py:295
  12.0 29.8 %all-to-all-start = ((bf16[32,8,1280]{2,1,0:T(8,128)(2,1)}), bf16[32,8,1280]{2,1,0:T(8,128)(2,1)S(1)}, u32[]{:S(2)}, u32[]{:S(2)}) async-start(bf16[32,8,1280]{2,1,0:T(8,128)(2,1)} %pad_maximum_fusion), calls=%async_computation | async-start | bytes 1310720 | tf_op jit(solution)/shard_map/gather_inputs/all_to_all | solution.py:19
  42.9 17.1 %all-to-all-start.1 = ((f32[8,32,256]{2,1,0:T(8,128)}), f32[8,32,256]{2,1,0:T(8,128)S(1)}, u32[]{:S(2)}, u32[]{:S(2)}) async-start(f32[8,32,256]{2,1,0:T(8,128)} %bitcast.5), calls=%async_computation.1 | async-start | bytes 524288 | tf_op jit(solution)/shard_map/head/all_to_all | solution.py:19
  81.7 7.8 %collective-permute-start.9 = (bf16[16,8192]{1,0:T(8,128)(2,1)S(1)}, bf16[16,8192]{1,0:T(8,128)(2,1)S(1)}, u32[]{:S(2)}, u32[]{:S(2)}) collective-permute-start(bf16[16,8192]{1,0:T(8,128)(2,1)S(1)} %get-tuple-element.9.refs_0_), channel_id=1, source_target_pairs={{0,1},{1,0},{2,3},{3,2},{4,5},{5,4},{6,7},{7,6},{8,9},{9,8},{10,11... | collective-permute-start | bytes 786440 | tf_op jit(solution)/shard_map/gather_heads/ppermute | solution.py:27
  85.3 14.8 %collective-permute-start.8 = (bf16[16,8192]{1,0:T(8,128)(2,1)S(1)}, bf16[16,8192]{1,0:T(8,128)(2,1)S(1)}, u32[]{:S(2)}, u32[]{:S(2)}) collective-permute-start(bf16[16,8192]{1,0:T(8,128)(2,1)S(1)} %get-tuple-element.9.refs_0_), channel_id=1, source_target_pairs={{0,6},{2,4},{4,2},{6,0},{1,7},{3,5},{5,3},{7,1},{8,14},{10,12},{12... | collective-permute-start | bytes 786440 | tf_op jit(solution)/shard_map/gather_heads/ppermute | solution.py:27
  86.7 14.4 %collective-permute-start.7 = (bf16[16,8192]{1,0:T(8,128)(2,1)S(1)}, bf16[16,8192]{1,0:T(8,128)(2,1)S(1)}, u32[]{:S(2)}, u32[]{:S(2)}) collective-permute-start(bf16[16,8192]{1,0:T(8,128)(2,1)S(1)} %get-tuple-element.9.refs_0_), channel_id=1, source_target_pairs={{0,4},{2,6},{4,0},{6,2},{1,5},{3,7},{5,1},{7,3},{8,12},{10,14},{12... | collective-permute-start | bytes 786440 | tf_op jit(solution)/shard_map/gather_heads/ppermute | solution.py:27
  87.9 13.9 %collective-permute-start.6 = (bf16[16,8192]{1,0:T(8,128)(2,1)S(1)}, bf16[16,8192]{1,0:T(8,128)(2,1)S(1)}, u32[]{:S(2)}, u32[]{:S(2)}) collective-permute-start(bf16[16,8192]{1,0:T(8,128)(2,1)S(1)} %get-tuple-element.9.refs_0_), channel_id=1, source_target_pairs={{0,2},{2,0},{4,6},{6,4},{1,3},{3,1},{5,7},{7,5},{8,10},{10,8},{12,... | collective-permute-start | bytes 786440 | tf_op jit(solution)/shard_map/gather_heads/ppermute | solution.py:27
  88.6 14.5 %collective-permute-start.16 = (bf16[64,2048]{1,0:T(8,128)(2,1)S(1)}, bf16[64,2048]{1,0:T(8,128)(2,1)S(1)}, u32[]{:S(2)}, u32[]{:S(2)}) collective-permute-start(bf16[64,2048]{1,0:T(8,128)(2,1)S(1)} %get-tuple-element.10.refs_8_), channel_id=1, source_target_pairs={{0,1},{1,0},{2,3},{3,2},{4,5},{5,4},{6,7},{7,6},{8,9},{9,8},{10,11... | collective-permute-start | bytes 786440 | tf_op jit(solution)/shard_map/gather_heads/ppermute | solution.py:27
  89.5 13.7 %collective-permute-start.15 = (bf16[64,2048]{1,0:T(8,128)(2,1)S(1)}, bf16[64,2048]{1,0:T(8,128)(2,1)}, u32[]{:S(2)}, u32[]{:S(2)}) collective-permute-start(bf16[64,2048]{1,0:T(8,128)(2,1)S(1)} %get-tuple-element.10.refs_8_), channel_id=1, source_target_pairs={{0,192},{64,128},{128,64},{192,0},{1,193},{65,129},{129,65},{193,1... | collective-permute-start | bytes 786440 | tf_op jit(solution)/shard_map/gather_heads/ppermute | solution.py:27
  100.1 8.7 %collective-permute-start.14 = (bf16[64,2048]{1,0:T(8,128)(2,1)S(1)}, bf16[64,2048]{1,0:T(8,128)(2,1)}, u32[]{:S(2)}, u32[]{:S(2)}) collective-permute-start(bf16[64,2048]{1,0:T(8,128)(2,1)S(1)} %get-tuple-element.10.refs_8_), channel_id=1, source_target_pairs={{0,128},{64,192},{128,0},{192,64},{1,129},{65,193},{129,1},{193,65... | collective-permute-start | bytes 786440 | tf_op jit(solution)/shard_map/gather_heads/ppermute | solution.py:27
  101.1 12.0 %collective-permute-start.13 = (bf16[64,2048]{1,0:T(8,128)(2,1)S(1)}, bf16[64,2048]{1,0:T(8,128)(2,1)}, u32[]{:S(2)}, u32[]{:S(2)}) collective-permute-start(bf16[64,2048]{1,0:T(8,128)(2,1)S(1)} %get-tuple-element.10.refs_8_), channel_id=1, source_target_pairs={{0,64},{64,0},{128,192},{192,128},{1,65},{65,1},{129,193},{193,129... | collective-permute-start | bytes 786440 | tf_op jit(solution)/shard_map/gather_heads/ppermute | solution.py:27
  101.8 13.0 %collective-permute-start.12 = (bf16[16,8192]{1,0:T(8,128)(2,1)S(1)}, bf16[16,8192]{1,0:T(8,128)(2,1)S(1)}, u32[]{:S(2)}, u32[]{:S(2)}) collective-permute-start(bf16[16,8192]{1,0:T(8,128)(2,1)S(1)} %collective-permute-done.8.refs_3_), channel_id=1, source_target_pairs={{0,1},{1,0},{2,3},{3,2},{4,5},{5,4},{6,7},{7,6},{8,9},{9,8},{10,11... | collective-permute-start | bytes 786440 | tf_op jit(solution)/shard_map/gather_heads/ppermute | solution.py:27
  103.1 22.6 %collective-permute-start.11 = (bf16[16,8192]{1,0:T(8,128)(2,1)S(1)}, bf16[16,8192]{1,0:T(8,128)(2,1)}, u32[]{:S(2)}, u32[]{:S(2)}) collective-permute-start(bf16[16,8192]{1,0:T(8,128)(2,1)S(1)} %collective-permute-done.7.refs_2_), channel_id=1, source_target_pairs={{0,1},{1,0},{2,3},{3,2},{4,5},{5,4},{6,7},{7,6},{8,9},{9,8},{10,11... | collective-permute-start | bytes 786440 | tf_op jit(solution)/shard_map/gather_heads/ppermute | solution.py:27
  103.2 22.5 %collective-permute-start.10 = (bf16[16,8192]{1,0:T(8,128)(2,1)S(1)}, bf16[16,8192]{1,0:T(8,128)(2,1)}, u32[]{:S(2)}, u32[]{:S(2)}) collective-permute-start(bf16[16,8192]{1,0:T(8,128)(2,1)S(1)} %collective-permute-done.6.refs_1_), channel_id=1, source_target_pairs={{0,1},{1,0},{2,3},{3,2},{4,5},{5,4},{6,7},{7,6},{8,9},{9,8},{10,11... | collective-permute-start | bytes 786440 | tf_op jit(solution)/shard_map/gather_heads/ppermute | solution.py:27
  108.8 16.9 %collective-permute-start.19 = (bf16[64,2048]{1,0:T(8,128)(2,1)}, bf16[64,2048]{1,0:T(8,128)(2,1)}, u32[]{:S(2)}, u32[]{:S(2)}) collective-permute-start(bf16[64,2048]{1,0:T(8,128)(2,1)} %collective-permute-done.15.refs_11_), channel_id=1, source_target_pairs={{0,1},{1,0},{2,3},{3,2},{4,5},{5,4},{6,7},{7,6},{8,9},{9,8},{10,11... | collective-permute-start | bytes 786440 | tf_op jit(solution)/shard_map/gather_heads/ppermute | solution.py:27
  113.1 12.6 %collective-permute-start.18 = (bf16[64,2048]{1,0:T(8,128)(2,1)}, bf16[64,2048]{1,0:T(8,128)(2,1)}, u32[]{:S(2)}, u32[]{:S(2)}) collective-permute-start(bf16[64,2048]{1,0:T(8,128)(2,1)} %collective-permute-done.14.refs_10_), channel_id=1, source_target_pairs={{0,1},{1,0},{2,3},{3,2},{4,5},{5,4},{6,7},{7,6},{8,9},{9,8},{10,11... | collective-permute-start | bytes 786440 | tf_op jit(solution)/shard_map/gather_heads/ppermute | solution.py:27
  115.4 10.3 %collective-permute-start.17 = (bf16[64,2048]{1,0:T(8,128)(2,1)}, bf16[64,2048]{1,0:T(8,128)(2,1)}, u32[]{:S(2)}, u32[]{:S(2)}) collective-permute-start(bf16[64,2048]{1,0:T(8,128)(2,1)} %collective-permute-done.13.refs_9_), channel_id=1, source_target_pairs={{0,1},{1,0},{2,3},{3,2},{4,5},{5,4},{6,7},{7,6},{8,9},{9,8},{10,11... | collective-permute-start | bytes 786440 | tf_op jit(solution)/shard_map/gather_heads/ppermute | solution.py:27
  174.6 7.6 %collective-permute-start.27 = (bf16[64,2048]{1,0:T(8,128)(2,1)S(1)}, bf16[64,2048]{1,0:T(8,128)(2,1)S(1)}, u32[]{:S(2)}, u32[]{:S(2)}) collective-permute-start(bf16[64,2048]{1,0:T(8,128)(2,1)S(1)} %get-tuple-element.20), channel_id=1, source_target_pairs={{0,64},{64,0},{128,192},{192,128},{1,65},{65,1},{129,193},{193,129... | collective-permute-start | bytes 786440 | tf_op jit(solution)/shard_map/reduce_grad/ppermute | solution.py:27
  175.0 9.0 %collective-permute-start.29 = (bf16[64,2048]{1,0:T(8,128)(2,1)S(1)}, bf16[64,2048]{1,0:T(8,128)(2,1)S(1)}, u32[]{:S(2)}, u32[]{:S(2)}) collective-permute-start(bf16[64,2048]{1,0:T(8,128)(2,1)S(1)} %get-tuple-element.21), channel_id=1, source_target_pairs={{0,192},{64,128},{128,64},{192,0},{1,193},{65,129},{129,65},{193,1... | collective-permute-start | bytes 786440 | tf_op jit(solution)/shard_map/reduce_grad/ppermute | solution.py:27
  176.2 12.3 %collective-permute-start.28 = (bf16[64,2048]{1,0:T(8,128)(2,1)S(1)}, bf16[64,2048]{1,0:T(8,128)(2,1)S(1)}, u32[]{:S(2)}, u32[]{:S(2)}) collective-permute-start(bf16[64,2048]{1,0:T(8,128)(2,1)S(1)} %get-tuple-element.22), channel_id=1, source_target_pairs={{0,128},{64,192},{128,0},{192,64},{1,129},{65,193},{129,1},{193,65... | collective-permute-start | bytes 786440 | tf_op jit(solution)/shard_map/reduce_grad/ppermute | solution.py:27
  178.0 11.7 %collective-permute-start.21 = (bf16[16,8192]{1,0:T(8,128)(2,1)S(1)}, bf16[16,8192]{1,0:T(8,128)(2,1)S(1)}, u32[]{:S(2)}, u32[]{:S(2)}) collective-permute-start(bf16[16,8192]{1,0:T(8,128)(2,1)S(1)} %get-tuple-element.17), channel_id=1, source_target_pairs={{0,2},{2,0},{4,6},{6,4},{1,3},{3,1},{5,7},{7,5},{8,10},{10,8},{12,... | collective-permute-start | bytes 786440 | tf_op jit(solution)/shard_map/reduce_grad/ppermute | solution.py:27
  178.4 13.6 %collective-permute-start.23 = (bf16[16,8192]{1,0:T(8,128)(2,1)S(1)}, bf16[16,8192]{1,0:T(8,128)(2,1)S(1)}, u32[]{:S(2)}, u32[]{:S(2)}) collective-permute-start(bf16[16,8192]{1,0:T(8,128)(2,1)S(1)} %get-tuple-element.18), channel_id=1, source_target_pairs={{0,6},{2,4},{4,2},{6,0},{1,7},{3,5},{5,3},{7,1},{8,14},{10,12},{12... | collective-permute-start | bytes 786440 | tf_op jit(solution)/shard_map/reduce_grad/ppermute | solution.py:27
  182.2 9.8 %collective-permute-start.22 = (bf16[16,8192]{1,0:T(8,128)(2,1)S(1)}, bf16[16,8192]{1,0:T(8,128)(2,1)S(1)}, u32[]{:S(2)}, u32[]{:S(2)}) collective-permute-start(bf16[16,8192]{1,0:T(8,128)(2,1)S(1)} %get-tuple-element.19), channel_id=1, source_target_pairs={{0,4},{2,6},{4,0},{6,2},{1,5},{3,7},{5,1},{7,3},{8,12},{10,14},{12... | collective-permute-start | bytes 786440 | tf_op jit(solution)/shard_map/reduce_grad/ppermute | solution.py:27
  210.5 14.2 %all-to-all-start.6 = ((bf16[8,48,256]{2,1,0:T(8,128)(2,1)}), bf16[8,48,256]{2,1,0:T(8,128)(2,1)S(1)}, u32[]{:S(2)}, u32[]{:S(2)}) async-start(bf16[8,48,256]{2,1,0:T(8,128)(2,1)} %broadcast_in_dim.52), calls=%async_computation.6 | async-start | bytes 393216 | tf_op jit(solution)/shard_map/finish/all_to_all | solution.py:19
  (28 other events, 235.5 us)
Sparse Core Ops, SparseCore 0:
  10.6 88.3 all-gather.2

commit v4 on v2

--- a/solution.py
+++ b/solution.py
@@ -1,12 +1,20 @@
+import functools
+
 import jax
 import jax.numpy as jnp
 from jax import lax
+from jax.experimental import pallas as pl
+from jax.experimental.pallas import tpu as pltpu
 from jax.sharding import Mesh, PartitionSpec as P
 
 BF16 = jnp.bfloat16
 F32 = jnp.float32
 REP = ("y", "z")
 VOC = ("x", "c")
+CHUNKS = 4
+PADDED = 512
+LIMIT = 24 * 1024 * 1024
+HEAD_COST = 45_000_000_000
 SIZES = {"y": 4, "z": 8, "x": 4, "c": 2}
 
 
@@ -39,24 +47,236 @@
     return total.astype(BF16)
 
 
+def cost(flops, bytes_accessed, transcendentals=0):
+    return pl.CostEstimate(
+        flops=flops, bytes_accessed=bytes_accessed, transcendentals=transcendentals
+    )
+
+
+def local_call(kernel, out_shape, estimate, scratch=(), limit=LIMIT, scalars=True):
+    def call(*operands):
+        specs = [pl.BlockSpec(memory_space=pltpu.VMEM)] * len(operands)
+        if scalars:
+            specs[0] = pl.BlockSpec(memory_space=pltpu.SMEM)
+        return pl.pallas_call(
+            kernel,
+            in_specs=specs,
+            out_specs=jax.tree.map(lambda _: pl.BlockSpec(memory_space=pltpu.VMEM), out_shape),
+            out_shape=out_shape,
+            scratch_shapes=scratch,
+            compiler_params=pltpu.CompilerParams(vmem_limit_bytes=limit),
+            cost_estimate=estimate,
+        )(*operands)
+
+    return call
+
+
+def shape(*sizes, dtype=F32):
+    return jax.ShapeDtypeStruct(sizes, dtype)
+
+
+def prepare_kernel(place, vocab_ref, across_ref, down_ref, wide):
+    entries, depth = vocab_ref.shape
+    width = depth // CHUNKS
+    wide[...] = jnp.zeros(wide.shape, F32)
+    for at in range(CHUNKS):
+        start = pl.multiple_of((place[16] ^ at) * width, width)
+        wide[:entries] = vocab_ref[:, pl.ds(start, width)].astype(F32)
+        block = wide[...]
+        across_ref[:, at * width : (at + 1) * width] = block.astype(BF16)
+        down_ref[at * width : (at + 1) * width] = block.T.astype(BF16)
+
+
+def prepare(place, vocab_head):
+    depth = vocab_head.shape[1]
+    return local_call(
+        prepare_kernel,
+        [shape(PADDED, depth, dtype=BF16), shape(depth, PADDED, dtype=BF16)],
+        cost(0, 6 * PADDED * depth),
+        [pltpu.VMEM((PADDED, depth // CHUNKS), F32)],
+    )(place, vocab_head)
+
+
+def teacher_kernel(place, target_ref, down_ref, out_ref, total):
+    width = down_ref.shape[0] // CHUNKS
+    for at in range(CHUNKS):
+        start = pl.multiple_of((place[16] ^ at) * width, width)
+        product = jnp.dot(
+            target_ref[:, pl.ds(start, width)],
+            down_ref[at * width : (at + 1) * width],
+            preferred_element_type=F32,
+        )
+        total[...] = product if at == 0 else total[...] + product
+    for at in range(16):
+        start = pl.multiple_of(place[at] * 16, 16)
+        out_ref[at * 16 : (at + 1) * 16] = total[pl.ds(start, 16)]
+
+
+def teacher_logits(place, target_all, down):
+    count, depth = target_all.shape
+    return local_call(
+        teacher_kernel,
+        shape(count, PADDED),
+        cost(2 * count * PADDED * depth, 2 * (count + PADDED) * depth),
+        [pltpu.VMEM((count, PADDED), F32)],
+    )(place, target_all, down)
+
+
+def student_part(entries, core, firsts, seconds, teacher_ref, down_ref, out_ref):
+    width = down_ref.shape[0] // CHUNKS
+    rows = out_ref.shape[0]
+    for at in range(CHUNKS):
+        blocks = [ref[:, at * width : (at + 1) * width] for ref in firsts] + [seconds[at][...]]
+        product = jnp.dot(
+            jnp.concatenate(blocks, axis=0),
+            down_ref[at * width : (at + 1) * width],
+            preferred_element_type=F32,
+        )
+        out_ref[...] = product if at == 0 else out_ref[...] + product
+    student, teacher = out_ref[...], teacher_ref[core * rows : (core + 1) * rows]
+    real = lax.broadcasted_iota(jnp.int32, student.shape, 1) < entries
+    exp_teacher = jnp.where(real, jnp.exp(teacher), 0.0)
+    columns = [
+        jnp.sum(exp_teacher, axis=1, keepdims=True),
+        jnp.sum(jnp.where(real, jnp.exp(student), 0.0), axis=1, keepdims=True),
+        jnp.sum(exp_teacher * (teacher - student), axis=1, keepdims=True),
+    ]
+    lane = lax.broadcasted_iota(jnp.int32, (rows, 128), 1)
+    table = jnp.zeros((rows, 128), F32)
+    for at, column in enumerate(columns):
+        table = jnp.where(lane == at, column, table)
+    return table
+
+
+def own_student_kernel(entries, *refs):
+    teacher_ref, down_ref, out_ref, table_ref = refs[8:]
+    table_ref[...] = student_part(
+        entries, 0, refs[:4], refs[4:8], teacher_ref, down_ref, out_ref
+    )
+
+
+def other_student_kernel(entries, place, *refs):
+    teacher_ref, down_ref, own_ref, out_ref, sums_ref, turned = refs[8:]
+    other = student_part(entries, 1, refs[:4], refs[4:8], teacher_ref, down_ref, out_ref)
+    for core, table in enumerate((own_ref[...], other)):
+        for at in range(8):
+            start = pl.multiple_of(place[core * 8 + at] * 16, 16)
+            turned[pl.ds(start, 16)] = table[at * 16 : (at + 1) * 16]
+    sums_ref[...] = turned[...].T[:8]
+
+
+def own_student(entries, blocks, teacher, down):
+    rows = teacher.shape[0] // 2
+    return local_call(
+        functools.partial(own_student_kernel, entries),
+        [shape(rows, PADDED), shape(rows, 128)],
+        cost(2 * rows * down.size, 2 * down.size, 2 * rows * PADDED),
+        scalars=False,
+    )(*blocks, teacher, down)
+
+
+def other_student(entries, place, blocks, teacher, down, table):
+    rows = teacher.shape[0] // 2
+    return local_call(
+        functools.partial(other_student_kernel, entries),
+        [shape(rows, PADDED), shape(8, 2 * rows)],
+        cost(2 * rows * down.size, 2 * down.size, 2 * rows * PADDED),
+        [pltpu.VMEM((2 * rows, 128), F32)],
+    )(place, *blocks, teacher, down, table)
+
+
+def grad_kernel(core, place, teacher_ref, student_ref, logs_ref, across_ref, out_ref, table, turned):
+    rows, depth = out_ref.shape
+    width = depth // CHUNKS
+    table[...] = jnp.concatenate(
+        [logs_ref[...], jnp.zeros((120, 2 * rows), F32)], axis=0
+    ).T
+    for at in range(8):
+        start = pl.multiple_of(place[core * 8 + at] * 16, 16)
+        turned[at * 16 : (at + 1) * 16] = table[pl.ds(start, 16)]
+    student = jnp.exp(student_ref[...] - turned[:, 1:2])
+    teacher = jnp.exp(teacher_ref[core * rows : (core + 1) * rows] - turned[:, 0:1])
+    grad = (student - teacher).astype(BF16)
+    for at in range(CHUNKS):
+        columns = slice(at * width, (at + 1) * width)
+        out_ref[:, columns] = jnp.dot(
+            grad, across_ref[:, columns], preferred_element_type=F32
+        ).astype(BF16)
+
+
+def grad_rows(core, place, teacher, student, logs, across):
+    rows, depth = student.shape[0], across.shape[1]
+    return local_call(
+        functools.partial(grad_kernel, core),
+        shape(rows, depth, dtype=BF16),
+        cost(2 * rows * across.size, 2 * across.size, 2 * rows * PADDED),
+        [pltpu.VMEM((2 * rows, 128), F32), pltpu.VMEM((rows, 128), F32)],
+    )(place, teacher, student, logs, across)
+
+
+def pass_kernel(*refs):
+    pass
+
+
+def settled(blocks):
+    return pl.pallas_call(
+        pass_kernel,
+        in_specs=[pl.BlockSpec(memory_space=pl.ANY)] * len(blocks),
+        out_specs=[pl.BlockSpec(memory_space=pl.ANY)] * len(blocks),
+        out_shape=[jax.ShapeDtypeStruct(block.shape, block.dtype) for block in blocks],
+        input_output_aliases={at: at for at in range(len(blocks))},
+        cost_estimate=cost(0, 0),
+    )(*blocks)
+
+
+def join_kernel(*refs):
+    firsts, seconds, (first_ref, second_ref) = refs[:4], refs[4:8], refs[8:]
+    (rows, width), (block, _) = firsts[0].shape, seconds[0].shape
+    for at in range(4):
+        first_ref[:, at * width : (at + 1) * width] = firsts[at][...]
+        second_ref[at * block : (at + 1) * block] = seconds[at][...]
+
+
+def join(firsts, seconds):
+    (rows, width), (block, across) = firsts[0].shape, seconds[0].shape
+    return pl.pallas_call(
+        join_kernel,
+        out_shape=[
+            jax.ShapeDtypeStruct((rows, 4 * width), BF16),
+            jax.ShapeDtypeStruct((4 * block, across), BF16),
+        ],
+        compiler_params=pltpu.CompilerParams(vmem_limit_bytes=LIMIT),
+        cost_estimate=cost(0, 16 * rows * width),
+    )(*firsts, *seconds)
+
+
+def head_kernel(rows_ref, weight_ref, down_ref, out_ref):
+    out_ref[...] = jnp.dot(rows_ref[...], weight_ref[...], preferred_element_type=F32)
+
+
+def head_partial(rows, weight, down):
+    return pl.pallas_call(
+        head_kernel,
+        in_specs=[pl.BlockSpec(memory_space=pltpu.VMEM)] * 2 + [pl.BlockSpec(memory_space=pl.ANY)],
+        out_shape=jax.ShapeDtypeStruct((rows.shape[0], weight.shape[1]), F32),
+        compiler_params=pltpu.CompilerParams(vmem_limit_bytes=LIMIT),
+        cost_estimate=cost(HEAD_COST, 2 * (rows.size + weight.size)),
+    )(rows, weight, down)
+
+
 def gather_heads(heads):
     rows, width = heads.shape
     half = rows // 2
     lines = gathered(heads, "z", 8).transpose(1, 0, 2).reshape(rows, -1)
-    first, second = lines[:half], lines[half:]
-    first = jnp.concatenate(from_peers(first, "y"), axis=1)
-    second = jnp.concatenate(from_peers(second, "x"), axis=0)
-    first_parts = from_peers(first, "x")
-    second_parts = from_peers(second, "y")
-    mine = jnp.concatenate([*first_parts, jnp.concatenate(second_parts, axis=1)], axis=0)
-    return jnp.concatenate([mine, swap(mine, "c", 1)], axis=0)
-
-
-def scatter_grad(part):
-    rows, depth = part.shape
-    own, other = part[: rows // 2], part[rows // 2 :]
+    first, second = join(from_peers(lines[:half], "y"), from_peers(lines[half:], "x"))
+    blocks = settled(from_peers(first, "x") + from_peers(second, "y"))
+    return blocks, [swap(block, "c", 1) for block in blocks]
+
+
+def scatter_grad(own, other):
+    rows, depth = own.shape
     mine = (own.astype(F32) + swap(other, "c", 1).astype(F32)).astype(BF16)
-    half = rows // 4
+    half = rows // 2
     block = half // 4
     width = depth // 4
     first = [mine[i * block : (i + 1) * block] for i in range(4)]
@@ -92,56 +312,34 @@
         input_rows = got[:, :, :in_width].reshape(count, in_width)
         residual = got[:, :, in_width:].reshape(count, out_width)
         residual = lax.dynamic_slice_in_dim(residual, voc_index * rows, rows, 0)
-    with jax.named_scope("turn_columns"):
-        quarter = vocab_head.shape[1] // 4
-        turned = jnp.concatenate(
-            [
-                lax.dynamic_slice_in_dim(vocab_head, (at_y ^ step) * quarter, quarter, 1)
-                for step in range(4)
-            ],
-            axis=1,
-        )
+    steps = jnp.arange(16)
+    order = ((at_x ^ (steps % 4)) * 2 + (at_c ^ (steps // 8))) * 2 + (steps // 4) % 2
+    place = jnp.concatenate([order, at_y[None]]).astype(jnp.int32)
+    with jax.named_scope("prepare"):
+        across, down = prepare(place, vocab_head)
     with jax.named_scope("head"):
-        partial_pre = jnp.dot(input_rows, head_weight, preferred_element_type=F32)
+        partial_pre = head_partial(input_rows, head_weight, down)
         parts = exchange(partial_pre.reshape(vocs, rows, out_width), VOC)
         preact = jnp.sum(parts, axis=0) + head_bias
         heads = (residual.astype(F32) + jax.nn.silu(preact)).astype(BF16)
+    with jax.named_scope("teacher"):
+        teacher = teacher_logits(place, target_all, down)
     with jax.named_scope("gather_heads"):
-        head_all = gather_heads(heads)
-    steps = jnp.arange(16)
-    order = ((at_x ^ (steps % 4)) * 2 + (at_c ^ (steps // 8))) * 2 + (steps // 4) % 2
-    with jax.named_scope("turn_targets"):
-        target_all = target_all.reshape(16, count // 16, -1)[order].reshape(count, -1)
-    contract = (((1,), (1,)), ((), ()))
-    with jax.named_scope("logits"):
-        teacher = lax.dot_general(vocab_head, target_all, contract, preferred_element_type=F32)
-        student = lax.dot_general(turned, head_all, contract, preferred_element_type=F32)
-        exp_teacher = jnp.exp(teacher)
-        sums = jnp.stack(
-            [
-                jnp.sum(exp_teacher, axis=0),
-                jnp.sum(jnp.exp(student), axis=0),
-                jnp.sum(exp_teacher * (teacher - student), axis=0),
-                jnp.zeros((count,), F32),
-            ]
-        )
-        back = (steps // 2 % 2 ^ at_c) * 8 + steps % 2 * 4 + (steps // 4 ^ at_x)
-        sums = sums.reshape(4, 16, -1)[:, back].reshape(8, -1)
+        own_blocks, other_blocks = gather_heads(heads)
+    with jax.named_scope("student"):
+        entries = vocab_head.shape[0]
+        own_logits, table = own_student(entries, own_blocks, teacher, down)
+        other_logits, sums = other_student(entries, place, other_blocks, teacher, down, table)
     with jax.named_scope("totals"):
         sums = jnp.sum(gathered(sums, VOC, vocs), axis=0)
-        sums = jnp.sum(gathered(sums, REP, reps), axis=0).reshape(4, count)
-        log_teacher, log_student = jnp.log(sums[0]), jnp.log(sums[1])
-        loss = jnp.sum(sums[2] / sums[0] - log_teacher + log_student) / count
-        log_teacher = log_teacher.reshape(16, -1)[order].reshape(count)
-        log_student = log_student.reshape(16, -1)[order].reshape(count)
+        sums = jnp.sum(gathered(sums, REP, reps), axis=0)
+        logs = jnp.log(sums)
+        loss = jnp.sum(sums[2] / sums[0] - logs[0] + logs[1]) / count
     with jax.named_scope("grad"):
-        grad_logits = (jnp.exp(student - log_student) - jnp.exp(teacher - log_teacher)).astype(BF16)
-        outer = (((0,), (0,)), ((), ()))
-        grad_part = lax.dot_general(
-            grad_logits, turned, outer, preferred_element_type=F32
-        ).astype(BF16)
+        other_rows = grad_rows(1, place, teacher, other_logits, logs, across)
+        own_rows = grad_rows(0, place, teacher, own_logits, logs, across)
     with jax.named_scope("reduce_grad"):
-        grad_heads = scatter_grad(grad_part)
+        grad_heads = scatter_grad(own_rows, other_rows)
     with jax.named_scope("finish"):
         sigma = jax.nn.sigmoid(preact)
         grad_pre = grad_heads * (sigma * (1.0 + preact * (1.0 - sigma)))

time: 262 us -> 223 us (0.85)
  waiting for transfers between devices: 89.2 us -> 48.1 us
  matrix products: 19 us -> 1.32 us
  Pallas kernels: 0 us -> 15.3 us
  blocking collectives: 36.9 us -> 43.7 us
  starting transfers between devices: 68.4 us -> 62.9 us
  local copies, waits for them, and re-layouts: 26.7 us -> 29.4 us
    all_gather x1, waiting for transfers between devices: 28.7 us -> 0.01 us  [shards(): target_all = lax.all_gather(targets, REP, axis=0, tiled=True)]
    all_to_all x4 -> x3, waiting for transfers between devices: 34.6 us -> 15.5 us  [exchange(): return lax.all_to_all(blocks, axis, split_axis=0, concat_axis=0, tiled=True)]
    unnamed x33 -> x63, local copies, waits for them, and re-layouts: 7.59 us -> 26.3 us
    dot_general x4 -> x0, matrix products: 17.7 us -> none  [the longest x1 7.79 us: shards(): lax.dot_general(grad_logits, turned, outer, preferred_element_type=F32)]
    pallas_call x0 -> x9, Pallas kernels: none -> 15.3 us  [the longest x6 14.2 us: call(): pl.pallas_call(kernel, in_specs=specs, out_specs=jax.tree.map(lambda _: p...]
    all_to_all x3 -> x4, blocking collectives: 36.9 us -> 43.7 us  [exchange(): return lax.all_to_all(blocks, axis, split_axis=0, concat_axis=0, tiled=True)]
    gather x5 -> x0, local copies, waits for them, and re-layouts: 6.74 us -> none  [the longest x1 5.02 us: shards(): target_all.reshape(16, count // 16, -1)[order].reshape(count, -1)]
    ppermute x26 -> x33, waiting for transfers between devices: 25.9 us -> 32.6 us  [swap(): lax.ppermute(block, axis, [(i, i ^ step) for i in range(SIZES[axis])])]
  transfers between devices with their start and end apart: 31 -> 37, of which waited for: 16 -> 16; matrix products, arithmetic and copies ran while one was open for 7% -> 2% of each run, Pallas kernels for 0% -> 5%
where the time goes in v4:
time: 223 us; the launch traced here: 222 us
  starting transfers between devices  62.9 us (28%)
  waiting for transfers between devices  48.1 us (22%)
  blocking collectives  43.7 us (20%)
  local copies, waits for them, and re-layouts  29.4 us (13%)
  between operations  16.4 us (7%)
  Pallas kernels  15.3 us (7%)
  other arithmetic  4.72 us (2%)
    all_to_all x4, blocking collectives, exchange(): return lax.all_to_all(blocks, axis, split_axis=0, concat_axis=0, tiled=True)  43.7 us
    ppermute x33, waiting for transfers between devices, swap(): lax.ppermute(block, axis, [(i, i ^ step) for i in range(SIZES[axis])])  32.6 us
    ppermute x33, starting transfers between devices, swap(): lax.ppermute(block, axis, [(i, i ^ step) for i in range(SIZES[axis])])  31.9 us
    all_to_all x3, starting transfers between devices, exchange(): return lax.all_to_all(blocks, axis, split_axis=0, concat_axis=0, tiled=True)  31 us
    unnamed x63, local copies, waits for them, and re-layouts  26.3 us
    all_to_all x3, waiting for transfers between devices, exchange(): return lax.all_to_all(blocks, axis, split_axis=0, concat_axis=0, tiled=True)  15.5 us
    pallas_call x6, Pallas kernels, call(): pl.pallas_call(kernel, in_specs=specs, out_specs=jax.tree.map(lambda _: p...  14.2 us
  transfers between devices with their start and end apart: 37, of which 16 were waited for; matrix products, arithmetic and copies ran while one was open for 2% of the time, Pallas kernels for 5%

profile of v4, /device:TPU:1, one launch (start us, length us, event | category | flops | bytes accessed | tf_op | source)
XLA Modules:
  0.0 221.8 jit_solution(3346337085427993731)
XLA Ops:
  12.0 12.0 %all-to-all-start = ((bf16[32,8,1280]{2,1,0:T(8,128)(2,1)}), bf16[32,8,1280]{2,1,0:T(8,128)(2,1)S(1)}, u32[]{:S(2)}, u32[]{:S(2)}) async-start(bf16[32,8,1280]{2,1,0:T(8,128)(2,1)} %pad_maximum_fusion), calls=%async_computation | async-start | bytes 1310720 | tf_op jit(solution)/shard_map/gather_inputs/all_to_all | solution.py:22
  24.1 3.4 %copy-done.7 = bf16[501,8192]{1,0:T(8,128)(2,1)S(1)} copy-done((bf16[501,8192]{1,0:T(8,128)(2,1)S(1)}, bf16[501,8192]{1,0:T(8,128)(2,1)}, u32[]{:S(2)}) %copy-start.7) | copy-done | bytes 8208408
  27.6 3.3 %prepare.1 = (bf16[512,8192]{1,0:T(8,128)(2,1)S(1)}, bf16[8192,512]{1,0:T(8,128)(2,1)S(1)}) custom-call(s32[17]{0:T(128)S(1)} %pad_add_fusion.place, bf16[501,8192]{1,0:T(8,128)(2,1)S(1)} %copy-done.7), custom_call_target="tpu_custom_call" | custom-call | bytes 25165824 | tf_op jit(solution)/shard_map/prepare/pallas_call | solution.py:61
  30.9 3.3 %copy-done.1 = bf16[8192,512]{1,0:T(8,128)(2,1)} copy-done((bf16[8192,512]{1,0:T(8,128)(2,1)}, bf16[8192,512]{1,0:T(8,128)(2,1)S(1)}, u32[]{:S(2)}) %copy-start.1) | copy-done | bytes 8388632
  34.2 3.3 %copy-done.5 = bf16[512,8192]{1,0:T(8,128)(2,1)} copy-done((bf16[512,8192]{1,0:T(8,128)(2,1)}, bf16[512,8192]{1,0:T(8,128)(2,1)S(1)}, u32[]{:S(2)}) %copy-start.5) | copy-done | bytes 8388632
  37.5 4.3 %all-to-all-done = bf16[32,8,1280]{2,1,0:T(8,128)(2,1)S(1)} async-done(((bf16[32,8,1280]{2,1,0:T(8,128)(2,1)}), bf16[32,8,1280]{2,1,0:T(8,128)(2,1)S(1)}, u32[]{:S(2)}, u32[]{:S(2)}) %all-to-all-start) | async-done | bytes 655392 | tf_op jit(solution)/shard_map/gather_inputs/all_to_all | solution.py:22
  41.9 3.6 %copy-done.2 = bf16[8192,512]{1,0:T(8,128)(2,1)S(1)} copy-done((bf16[8192,512]{1,0:T(8,128)(2,1)S(1)}, bf16[8192,512]{1,0:T(8,128)(2,1)}, u32[]{:S(2)}) %copy-start.2) | copy-done | bytes 8388632
  46.5 10.6 %all-to-all-start.1 = ((f32[8,32,256]{2,1,0:T(8,128)}), f32[8,32,256]{2,1,0:T(8,128)S(1)}, u32[]{:S(2)}, u32[]{:S(2)}) async-start(f32[8,32,256]{2,1,0:T(8,128)} %bitcast.5), calls=%async_computation.1 | async-start | bytes 524288 | tf_op jit(solution)/shard_map/head/all_to_all | solution.py:22
  57.1 6.5 %all-to-all-done.1 = f32[8,32,256]{2,1,0:T(8,128)S(1)} async-done(((f32[8,32,256]{2,1,0:T(8,128)}), f32[8,32,256]{2,1,0:T(8,128)S(1)}, u32[]{:S(2)}, u32[]{:S(2)}) %all-to-all-start.1) | async-done | bytes 262176 | tf_op jit(solution)/shard_map/head/all_to_all | solution.py:22
  63.7 12.5 %all_to_all.35 = bf16[8,32,256]{2,1,0:T(8,128)(2,1)S(1)} all-to-all(bf16[8,32,256]{2,1,0:T(8,128)(2,1)S(1)} %broadcast_in_dim.24), channel_id=1, replica_groups=mesh['y'=4,'z'=8,'x'=4,'c'=2] {'z'}, dimensions={0} | all-to-all | bytes 262144 | tf_op jit(solution)/shard_map/gather_heads/all_to_all | solution.py:22
  91.4 9.0 %collective-permute-done.8.refs_3_ = bf16[16,8192]{1,0:T(8,128)(2,1)S(1)} collective-permute-done((bf16[16,8192]{1,0:T(8,128)(2,1)S(1)}, bf16[16,8192]{1,0:T(8,128)(2,1)S(1)}, u32[]{:S(2)}, u32[]{:S(2)}) %collective-permute-start.8) | collective-permute-done | bytes 262176 | tf_op jit(solution)/shard_map/gather_heads/ppermute | solution.py:30
  100.5 6.0 %collective-permute-done.9.refs_5_ = bf16[64,2048]{1,0:T(8,128)(2,1)S(1)} collective-permute-done((bf16[64,2048]{1,0:T(8,128)(2,1)S(1)}, bf16[64,2048]{1,0:T(8,128)(2,1)S(1)}, u32[]{:S(2)}, u32[]{:S(2)}) %collective-permute-start.9) | collective-permute-done | bytes 262176 | tf_op jit(solution)/shard_map/gather_heads/ppermute | solution.py:30
  107.3 2.7 %collective-permute-start.12 = (bf16[16,8192]{1,0:T(8,128)(2,1)}, bf16[16,8192]{1,0:T(8,128)(2,1)S(1)}, u32[]{:S(2)}, u32[]{:S(2)}) collective-permute-start(bf16[16,8192]{1,0:T(8,128)(2,1)} %get-tuple-element.22.refs_0_), channel_id=1, source_target_pairs={{0,1},{1,0},{2,3},{3,2},{4,5},{5,4},{6,7},{7,6},{8,9},{9,8},{10,11... | collective-permute-start | bytes 786440 | tf_op jit(solution)/shard_map/gather_heads/ppermute | solution.py:30
  112.4 3.4 %copy-done.3 = bf16[8192,512]{1,0:T(8,128)(2,1)S(1)} copy-done((bf16[8192,512]{1,0:T(8,128)(2,1)S(1)}, bf16[8192,512]{1,0:T(8,128)(2,1)}, u32[]{:S(2)}) %copy-start.3) | copy-done | bytes 8388632
  118.1 2.9 %teacher.1.refs_8_.teacher_ref = f32[256,512]{1,0:T(8,128)S(1)} custom-call(s32[17]{0:T(128)S(1)} %pad_add_fusion.place, bf16[256,8192]{1,0:T(8,128)(2,1)S(1)} %copy-done.8, bf16[8192,512]{1,0:T(8,128)(2,1)S(1)} %copy-done.3), custom_call_target="tpu_custom_call" | custom-call | flops 2147483648 | bytes 12582912 | tf_op jit(solution)/shard_map/teacher/pallas_call | solution.py:61
  126.6 7.3 %all_to_all.36 = f32[8,8,256]{2,1,0:T(8,128)S(1)} all-to-all(f32[8,8,256]{2,1,0:T(8,128)S(1)} %broadcast_in_dim.49), channel_id=1, replica_groups=mesh['y'=4,'z'=8,'x'=4,'c'=2] {'x','c'}, dimensions={0} | all-to-all | bytes 131072 | tf_op jit(solution)/shard_map/totals/all_to_all | solution.py:22
  134.0 13.1 %all_to_all.37 = f32[32,8,256]{2,1,0:T(8,128)S(1)} all-to-all(f32[32,8,256]{2,1,0:T(8,128)S(1)} %broadcast_in_dim.50), channel_id=1, replica_groups=mesh['y'=4,'z'=8,'x'=4,'c'=2] {'y','z'}, dimensions={0} | all-to-all | bytes 524288 | tf_op jit(solution)/shard_map/totals/all_to_all | solution.py:22
  147.2 3.4 %copy-done.6 = bf16[512,8192]{1,0:T(8,128)(2,1)S(1)} copy-done((bf16[512,8192]{1,0:T(8,128)(2,1)S(1)}, bf16[512,8192]{1,0:T(8,128)(2,1)}, u32[]{:S(2)}) %copy-start.6) | copy-done | bytes 8388632
  153.5 3.7 %collective-permute-start.20 = (bf16[128,8192]{1,0:T(8,128)(2,1)S(1)}, bf16[128,8192]{1,0:T(8,128)(2,1)S(1)}, u32[]{:S(2)}, u32[]{:S(2)}) collective-permute-start(bf16[128,8192]{1,0:T(8,128)(2,1)S(1)} %grad.3), channel_id=1, source_target_pairs={{0,1},{1,0},{2,3},{3,2},{4,5},{5,4},{6,7},{7,6},{8,9},{9,8},{10,11... | collective-permute-start | bytes 6291464 | tf_op jit(solution)/shard_map/reduce_grad/ppermute | solution.py:30
  166.2 3.1 %collective-permute-done.27 = bf16[64,2048]{1,0:T(8,128)(2,1)S(1)} collective-permute-done((bf16[64,2048]{1,0:T(8,128)(2,1)S(1)}, bf16[64,2048]{1,0:T(8,128)(2,1)S(1)}, u32[]{:S(2)}, u32[]{:S(2)}) %collective-permute-start.27) | collective-permute-done | bytes 262176 | tf_op jit(solution)/shard_map/reduce_grad/ppermute | solution.py:30
  171.2 4.4 %collective-permute-done.28 = bf16[64,2048]{1,0:T(8,128)(2,1)S(1)} collective-permute-done((bf16[64,2048]{1,0:T(8,128)(2,1)S(1)}, bf16[64,2048]{1,0:T(8,128)(2,1)S(1)}, u32[]{:S(2)}, u32[]{:S(2)}) %collective-permute-start.28) | collective-permute-done | bytes 262176 | tf_op jit(solution)/shard_map/reduce_grad/ppermute | solution.py:30
  186.0 10.8 %all_to_all.38 = bf16[8,32,256]{2,1,0:T(8,128)(2,1)S(1)} all-to-all(bf16[8,32,256]{2,1,0:T(8,128)(2,1)S(1)} %bitcast.38), channel_id=1, replica_groups=mesh['y'=4,'z'=8,'x'=4,'c'=2] {'z'}, dimensions={0} | all-to-all | bytes 262144 | tf_op jit(solution)/shard_map/reduce_grad/all_to_all | solution.py:22
  197.7 8.3 %all-to-all-start.6 = ((bf16[8,48,256]{2,1,0:T(8,128)(2,1)}), bf16[8,48,256]{2,1,0:T(8,128)(2,1)S(1)}, u32[]{:S(2)}, u32[]{:S(2)}) async-start(bf16[8,48,256]{2,1,0:T(8,128)(2,1)} %broadcast_in_dim.52), calls=%async_computation.6 | async-start | bytes 393216 | tf_op jit(solution)/shard_map/finish/all_to_all | solution.py:22
  207.3 4.6 %all-to-all-done.6 = bf16[8,48,256]{2,1,0:T(8,128)(2,1)S(1)} async-done(((bf16[8,48,256]{2,1,0:T(8,128)(2,1)}), bf16[8,48,256]{2,1,0:T(8,128)(2,1)S(1)}, u32[]{:S(2)}, u32[]{:S(2)}) %all-to-all-start.6) | async-done | bytes 196640 | tf_op jit(solution)/shard_map/finish/all_to_all | solution.py:22
  (171 shorter events, 59.9 us)
Async XLA Ops:
  7.2 105.2 %all-gather.3.cloned.1.call-start = ((), (), s32[]{:S(2)}) async-start(), calls=%async_computation.7 | async-start | bytes 4325376 | tf_op jit(solution)/shard_map/gather_targets/all_gather | solution.py:304
  12.0 29.8 %all-to-all-start = ((bf16[32,8,1280]{2,1,0:T(8,128)(2,1)}), bf16[32,8,1280]{2,1,0:T(8,128)(2,1)S(1)}, u32[]{:S(2)}, u32[]{:S(2)}) async-start(bf16[32,8,1280]{2,1,0:T(8,128)(2,1)} %pad_maximum_fusion), calls=%async_computation | async-start | bytes 1310720 | tf_op jit(solution)/shard_map/gather_inputs/all_to_all | solution.py:22
  46.5 17.1 %all-to-all-start.1 = ((f32[8,32,256]{2,1,0:T(8,128)}), f32[8,32,256]{2,1,0:T(8,128)S(1)}, u32[]{:S(2)}, u32[]{:S(2)}) async-start(f32[8,32,256]{2,1,0:T(8,128)} %bitcast.5), calls=%async_computation.1 | async-start | bytes 524288 | tf_op jit(solution)/shard_map/head/all_to_all | solution.py:22
  76.2 6.8 %collective-permute-start.2 = (bf16[16,2048]{1,0:T(8,128)(2,1)S(1)}, bf16[16,2048]{1,0:T(8,128)(2,1)S(1)}, u32[]{:S(2)}, u32[]{:S(2)}) collective-permute-start(bf16[16,2048]{1,0:T(8,128)(2,1)S(1)} %bitcast.27), channel_id=1, source_target_pairs={{0,192},{64,128},{128,64},{192,0},{1,193},{65,129},{129,65},{193,1... | collective-permute-start | bytes 196616 | tf_op jit(solution)/shard_map/gather_heads/ppermute | solution.py:30
  76.3 7.5 %collective-permute-start.1 = (bf16[16,2048]{1,0:T(8,128)(2,1)S(1)}, bf16[16,2048]{1,0:T(8,128)(2,1)S(1)}, u32[]{:S(2)}, u32[]{:S(2)}) collective-permute-start(bf16[16,2048]{1,0:T(8,128)(2,1)S(1)} %bitcast.28), channel_id=1, source_target_pairs={{0,128},{64,192},{128,0},{192,64},{1,129},{65,193},{129,1},{193,65... | collective-permute-start | bytes 196616 | tf_op jit(solution)/shard_map/gather_heads/ppermute | solution.py:30
  86.6 13.9 %collective-permute-start.8 = (bf16[16,8192]{1,0:T(8,128)(2,1)S(1)}, bf16[16,8192]{1,0:T(8,128)(2,1)S(1)}, u32[]{:S(2)}, u32[]{:S(2)}) collective-permute-start(bf16[16,8192]{1,0:T(8,128)(2,1)S(1)} %get-tuple-element.20.refs_0_), channel_id=1, source_target_pairs={{0,6},{2,4},{4,2},{6,0},{1,7},{3,5},{5,3},{7,1},{8,14},{10,12},{12... | collective-permute-start | bytes 786440 | tf_op jit(solution)/shard_map/gather_heads/ppermute | solution.py:30
  87.2 13.3 %collective-permute-start.7 = (bf16[16,8192]{1,0:T(8,128)(2,1)S(1)}, bf16[16,8192]{1,0:T(8,128)(2,1)S(1)}, u32[]{:S(2)}, u32[]{:S(2)}) collective-permute-start(bf16[16,8192]{1,0:T(8,128)(2,1)S(1)} %get-tuple-element.20.refs_0_), channel_id=1, source_target_pairs={{0,4},{2,6},{4,0},{6,2},{1,5},{3,7},{5,1},{7,3},{8,12},{10,14},{12... | collective-permute-start | bytes 786440 | tf_op jit(solution)/shard_map/gather_heads/ppermute | solution.py:30
  89.3 11.2 %collective-permute-start.6 = (bf16[16,8192]{1,0:T(8,128)(2,1)S(1)}, bf16[16,8192]{1,0:T(8,128)(2,1)S(1)}, u32[]{:S(2)}, u32[]{:S(2)}) collective-permute-start(bf16[16,8192]{1,0:T(8,128)(2,1)S(1)} %get-tuple-element.20.refs_0_), channel_id=1, source_target_pairs={{0,2},{2,0},{4,6},{6,4},{1,3},{3,1},{5,7},{7,5},{8,10},{10,8},{12,... | collective-permute-start | bytes 786440 | tf_op jit(solution)/shard_map/gather_heads/ppermute | solution.py:30
  89.9 10.6 %collective-permute-start.11 = (bf16[64,2048]{1,0:T(8,128)(2,1)S(1)}, bf16[64,2048]{1,0:T(8,128)(2,1)S(1)}, u32[]{:S(2)}, u32[]{:S(2)}) collective-permute-start(bf16[64,2048]{1,0:T(8,128)(2,1)S(1)} %get-tuple-element.21.refs_4_), channel_id=1, source_target_pairs={{0,192},{64,128},{128,64},{192,0},{1,193},{65,129},{129,65},{193,1... | collective-permute-start | bytes 786440 | tf_op jit(solution)/shard_map/gather_heads/ppermute | solution.py:30
  89.9 10.6 %collective-permute-start.10 = (bf16[64,2048]{1,0:T(8,128)(2,1)S(1)}, bf16[64,2048]{1,0:T(8,128)(2,1)S(1)}, u32[]{:S(2)}, u32[]{:S(2)}) collective-permute-start(bf16[64,2048]{1,0:T(8,128)(2,1)S(1)} %get-tuple-element.21.refs_4_), channel_id=1, source_target_pairs={{0,128},{64,192},{128,0},{192,64},{1,129},{65,193},{129,1},{193,65... | collective-permute-start | bytes 786440 | tf_op jit(solution)/shard_map/gather_heads/ppermute | solution.py:30
  110.4 12.8 %collective-permute-start.15 = (bf16[16,8192]{1,0:T(8,128)(2,1)}, bf16[16,8192]{1,0:T(8,128)(2,1)S(1)}, u32[]{:S(2)}, u32[]{:S(2)}) collective-permute-start(bf16[16,8192]{1,0:T(8,128)(2,1)} %get-tuple-element.25.refs_3_), channel_id=1, source_target_pairs={{0,1},{1,0},{2,3},{3,2},{4,5},{5,4},{6,7},{7,6},{8,9},{9,8},{10,11... | collective-permute-start | bytes 786440 | tf_op jit(solution)/shard_map/gather_heads/ppermute | solution.py:30
  110.4 12.8 %collective-permute-start.16 = (bf16[64,2048]{1,0:T(8,128)(2,1)}, bf16[64,2048]{1,0:T(8,128)(2,1)S(1)}, u32[]{:S(2)}, u32[]{:S(2)}) collective-permute-start(bf16[64,2048]{1,0:T(8,128)(2,1)} %get-tuple-element.26.refs_4_), channel_id=1, source_target_pairs={{0,1},{1,0},{2,3},{3,2},{4,5},{5,4},{6,7},{7,6},{8,9},{9,8},{10,11... | collective-permute-start | bytes 786440 | tf_op jit(solution)/shard_map/gather_heads/ppermute | solution.py:30
  111.3 12.0 %collective-permute-start.17 = (bf16[64,2048]{1,0:T(8,128)(2,1)}, bf16[64,2048]{1,0:T(8,128)(2,1)S(1)}, u32[]{:S(2)}, u32[]{:S(2)}) collective-permute-start(bf16[64,2048]{1,0:T(8,128)(2,1)} %get-tuple-element.27.refs_5_), channel_id=1, source_target_pairs={{0,1},{1,0},{2,3},{3,2},{4,5},{5,4},{6,7},{7,6},{8,9},{9,8},{10,11... | collective-permute-start | bytes 786440 | tf_op jit(solution)/shard_map/gather_heads/ppermute | solution.py:30
  111.7 11.6 %collective-permute-start.18 = (bf16[64,2048]{1,0:T(8,128)(2,1)}, bf16[64,2048]{1,0:T(8,128)(2,1)}, u32[]{:S(2)}, u32[]{:S(2)}) collective-permute-start(bf16[64,2048]{1,0:T(8,128)(2,1)} %get-tuple-element.28.refs_6_), channel_id=1, source_target_pairs={{0,1},{1,0},{2,3},{3,2},{4,5},{5,4},{6,7},{7,6},{8,9},{9,8},{10,11... | collective-permute-start | bytes 786440 | tf_op jit(solution)/shard_map/gather_heads/ppermute | solution.py:30
  112.0 11.2 %collective-permute-start.19 = (bf16[64,2048]{1,0:T(8,128)(2,1)}, bf16[64,2048]{1,0:T(8,128)(2,1)}, u32[]{:S(2)}, u32[]{:S(2)}) collective-permute-start(bf16[64,2048]{1,0:T(8,128)(2,1)} %get-tuple-element.29.refs_7_), channel_id=1, source_target_pairs={{0,1},{1,0},{2,3},{3,2},{4,5},{5,4},{6,7},{7,6},{8,9},{9,8},{10,11... | collective-permute-start | bytes 786440 | tf_op jit(solution)/shard_map/gather_heads/ppermute | solution.py:30
  153.5 7.5 %collective-permute-start.20 = (bf16[128,8192]{1,0:T(8,128)(2,1)S(1)}, bf16[128,8192]{1,0:T(8,128)(2,1)S(1)}, u32[]{:S(2)}, u32[]{:S(2)}) collective-permute-start(bf16[128,8192]{1,0:T(8,128)(2,1)S(1)} %grad.3), channel_id=1, source_target_pairs={{0,1},{1,0},{2,3},{3,2},{4,5},{5,4},{6,7},{7,6},{8,9},{9,8},{10,11... | collective-permute-start | bytes 6291464 | tf_op jit(solution)/shard_map/reduce_grad/ppermute | solution.py:30
  161.7 7.6 %collective-permute-start.27 = (bf16[64,2048]{1,0:T(8,128)(2,1)S(1)}, bf16[64,2048]{1,0:T(8,128)(2,1)S(1)}, u32[]{:S(2)}, u32[]{:S(2)}) collective-permute-start(bf16[64,2048]{1,0:T(8,128)(2,1)S(1)} %get-tuple-element.40), channel_id=1, source_target_pairs={{0,64},{64,0},{128,192},{192,128},{1,65},{65,1},{129,193},{193,129... | collective-permute-start | bytes 786440 | tf_op jit(solution)/shard_map/reduce_grad/ppermute | solution.py:30
  162.2 9.0 %collective-permute-start.29 = (bf16[64,2048]{1,0:T(8,128)(2,1)S(1)}, bf16[64,2048]{1,0:T(8,128)(2,1)S(1)}, u32[]{:S(2)}, u32[]{:S(2)}) collective-permute-start(bf16[64,2048]{1,0:T(8,128)(2,1)S(1)} %get-tuple-element.41), channel_id=1, source_target_pairs={{0,192},{64,128},{128,64},{192,0},{1,193},{65,129},{129,65},{193,1... | collective-permute-start | bytes 786440 | tf_op jit(solution)/shard_map/reduce_grad/ppermute | solution.py:30
  163.4 12.3 %collective-permute-start.28 = (bf16[64,2048]{1,0:T(8,128)(2,1)S(1)}, bf16[64,2048]{1,0:T(8,128)(2,1)S(1)}, u32[]{:S(2)}, u32[]{:S(2)}) collective-permute-start(bf16[64,2048]{1,0:T(8,128)(2,1)S(1)} %get-tuple-element.42), channel_id=1, source_target_pairs={{0,128},{64,192},{128,0},{192,64},{1,129},{65,193},{129,1},{193,65... | collective-permute-start | bytes 786440 | tf_op jit(solution)/shard_map/reduce_grad/ppermute | solution.py:30
  165.1 11.7 %collective-permute-start.21 = (bf16[16,8192]{1,0:T(8,128)(2,1)S(1)}, bf16[16,8192]{1,0:T(8,128)(2,1)S(1)}, u32[]{:S(2)}, u32[]{:S(2)}) collective-permute-start(bf16[16,8192]{1,0:T(8,128)(2,1)S(1)} %get-tuple-element.37), channel_id=1, source_target_pairs={{0,2},{2,0},{4,6},{6,4},{1,3},{3,1},{5,7},{7,5},{8,10},{10,8},{12,... | collective-permute-start | bytes 786440 | tf_op jit(solution)/shard_map/reduce_grad/ppermute | solution.py:30
  165.5 13.6 %collective-permute-start.23 = (bf16[16,8192]{1,0:T(8,128)(2,1)S(1)}, bf16[16,8192]{1,0:T(8,128)(2,1)S(1)}, u32[]{:S(2)}, u32[]{:S(2)}) collective-permute-start(bf16[16,8192]{1,0:T(8,128)(2,1)S(1)} %get-tuple-element.38), channel_id=1, source_target_pairs={{0,6},{2,4},{4,2},{6,0},{1,7},{3,5},{5,3},{7,1},{8,14},{10,12},{12... | collective-permute-start | bytes 786440 | tf_op jit(solution)/shard_map/reduce_grad/ppermute | solution.py:30
  169.4 9.8 %collective-permute-start.22 = (bf16[16,8192]{1,0:T(8,128)(2,1)S(1)}, bf16[16,8192]{1,0:T(8,128)(2,1)S(1)}, u32[]{:S(2)}, u32[]{:S(2)}) collective-permute-start(bf16[16,8192]{1,0:T(8,128)(2,1)S(1)} %get-tuple-element.39), channel_id=1, source_target_pairs={{0,4},{2,6},{4,0},{6,2},{1,5},{3,7},{5,1},{7,3},{8,12},{10,14},{12... | collective-permute-start | bytes 786440 | tf_op jit(solution)/shard_map/reduce_grad/ppermute | solution.py:30
  176.2 6.5 %collective-permute-start.32 = (bf16[16,2048]{1,0:T(8,128)(2,1)S(1)}, bf16[16,2048]{1,0:T(8,128)(2,1)S(1)}, u32[]{:S(2)}, u32[]{:S(2)}) collective-permute-start(bf16[16,2048]{1,0:T(8,128)(2,1)S(1)} %get-tuple-element.47), channel_id=1, source_target_pairs={{0,6},{2,4},{4,2},{6,0},{1,7},{3,5},{5,3},{7,1},{8,14},{10,12},{12... | collective-permute-start | bytes 196616 | tf_op jit(solution)/shard_map/reduce_grad/ppermute | solution.py:30
  197.7 14.2 %all-to-all-start.6 = ((bf16[8,48,256]{2,1,0:T(8,128)(2,1)}), bf16[8,48,256]{2,1,0:T(8,128)(2,1)S(1)}, u32[]{:S(2)}, u32[]{:S(2)}) async-start(bf16[8,48,256]{2,1,0:T(8,128)(2,1)} %broadcast_in_dim.52), calls=%async_computation.6 | async-start | bytes 393216 | tf_op jit(solution)/shard_map/finish/all_to_all | solution.py:22
  (44 other events, 267.7 us)
Sparse Core Ops, SparseCore 0:
  10.6 87.0 all-gather.2

commit v5 on v4

--- a/solution.py
+++ b/solution.py
@@ -75,7 +75,8 @@
     return jax.ShapeDtypeStruct(sizes, dtype)
 
 
-def prepare_kernel(place, vocab_ref, across_ref, down_ref, wide):
+def prepare_kernel(place, vocab_ref, across_ref, down_ref, done_ref, wide):
+    done_ref[...] = jnp.zeros(done_ref.shape, F32)
     entries, depth = vocab_ref.shape
     width = depth // CHUNKS
     wide[...] = jnp.zeros(wide.shape, F32)
@@ -91,7 +92,7 @@
     depth = vocab_head.shape[1]
     return local_call(
         prepare_kernel,
-        [shape(PADDED, depth, dtype=BF16), shape(depth, PADDED, dtype=BF16)],
+        [shape(PADDED, depth, dtype=BF16), shape(depth, PADDED, dtype=BF16), shape(8, 128)],
         cost(0, 6 * PADDED * depth),
         [pltpu.VMEM((PADDED, depth // CHUNKS), F32)],
     )(place, vocab_head)
@@ -162,7 +163,9 @@
         for at in range(8):
             start = pl.multiple_of(place[core * 8 + at] * 16, 16)
             turned[pl.ds(start, 16)] = table[at * 16 : (at + 1) * 16]
-    sums_ref[...] = turned[...].T[:8]
+    sums = turned[...].T[:8]
+    for at in range(16):
+        sums_ref[at] = sums
 
 
 def own_student(entries, blocks, teacher, down):
@@ -179,7 +182,7 @@
     rows = teacher.shape[0] // 2
     return local_call(
         functools.partial(other_student_kernel, entries),
-        [shape(rows, PADDED), shape(8, 2 * rows)],
+        [shape(rows, PADDED), shape(16, 8, 2 * rows)],
         cost(2 * rows * down.size, 2 * down.size, 2 * rows * PADDED),
         [pltpu.VMEM((2 * rows, 128), F32)],
     )(place, *blocks, teacher, down, table)
@@ -218,15 +221,42 @@
     pass
 
 
-def settled(blocks):
+def settled(blocks, teacher):
     return pl.pallas_call(
         pass_kernel,
-        in_specs=[pl.BlockSpec(memory_space=pl.ANY)] * len(blocks),
+        in_specs=[pl.BlockSpec(memory_space=pl.ANY)] * (len(blocks) + 1),
         out_specs=[pl.BlockSpec(memory_space=pl.ANY)] * len(blocks),
-        out_shape=[jax.ShapeDtypeStruct(block.shape, block.dtype) for block in blocks],
+        out_shape=[shape(*block.shape, dtype=block.dtype) for block in blocks],
         input_output_aliases={at: at for at in range(len(blocks))},
+        compiler_params=pltpu.CompilerParams(vmem_limit_bytes=1024 * 1024),
         cost_estimate=cost(0, 0),
-    )(*blocks)
+    )(*blocks, teacher)
+
+
+def total_kernel(last, parts_ref, out_ref):
+    sums = parts_ref[0]
+    for at in range(1, 16):
+        sums = sums + parts_ref[at]
+    if last:
+        logs = jnp.log(sums[:2])
+        terms = sums[2:3] / sums[:1] - logs[:1] + logs[1:]
+        out_ref[...] = jnp.zeros(out_ref.shape, F32)
+        out_ref[:2] = logs
+        out_ref[2:3] = terms
+    else:
+        for at in range(16):
+            out_ref[at] = sums
+
+
+def totalled(parts, last):
+    _, rows, count = parts.shape
+    return local_call(
+        functools.partial(total_kernel, last),
+        shape(rows, count) if last else shape(*parts.shape),
+        cost(parts.size, 4 * parts.size),
+        limit=2 * 1024 * 1024,
+        scalars=False,
+    )(parts)
 
 
 def join_kernel(*refs):
@@ -250,26 +280,26 @@
     )(*firsts, *seconds)
 
 
-def head_kernel(rows_ref, weight_ref, down_ref, out_ref):
+def head_kernel(rows_ref, weight_ref, done_ref, out_ref):
     out_ref[...] = jnp.dot(rows_ref[...], weight_ref[...], preferred_element_type=F32)
 
 
-def head_partial(rows, weight, down):
+def head_partial(rows, weight, done):
     return pl.pallas_call(
         head_kernel,
-        in_specs=[pl.BlockSpec(memory_space=pltpu.VMEM)] * 2 + [pl.BlockSpec(memory_space=pl.ANY)],
+        in_specs=[pl.BlockSpec(memory_space=pltpu.VMEM)] * 3,
         out_shape=jax.ShapeDtypeStruct((rows.shape[0], weight.shape[1]), F32),
         compiler_params=pltpu.CompilerParams(vmem_limit_bytes=LIMIT),
         cost_estimate=cost(HEAD_COST, 2 * (rows.size + weight.size)),
-    )(rows, weight, down)
-
-
-def gather_heads(heads):
+    )(rows, weight, done)
+
+
+def gather_heads(heads, teacher):
     rows, width = heads.shape
     half = rows // 2
     lines = gathered(heads, "z", 8).transpose(1, 0, 2).reshape(rows, -1)
     first, second = join(from_peers(lines[:half], "y"), from_peers(lines[half:], "x"))
-    blocks = settled(from_peers(first, "x") + from_peers(second, "y"))
+    blocks = settled(from_peers(first, "x") + from_peers(second, "y"), teacher)
     return blocks, [swap(block, "c", 1) for block in blocks]
 
 
@@ -316,25 +346,24 @@
     order = ((at_x ^ (steps % 4)) * 2 + (at_c ^ (steps // 8))) * 2 + (steps // 4) % 2
     place = jnp.concatenate([order, at_y[None]]).astype(jnp.int32)
     with jax.named_scope("prepare"):
-        across, down = prepare(place, vocab_head)
+        across, down, done = prepare(place, vocab_head)
     with jax.named_scope("head"):
-        partial_pre = head_partial(input_rows, head_weight, down)
+        partial_pre = head_partial(input_rows, head_weight, done)
         parts = exchange(partial_pre.reshape(vocs, rows, out_width), VOC)
         preact = jnp.sum(parts, axis=0) + head_bias
         heads = (residual.astype(F32) + jax.nn.silu(preact)).astype(BF16)
     with jax.named_scope("teacher"):
         teacher = teacher_logits(place, target_all, down)
     with jax.named_scope("gather_heads"):
-        own_blocks, other_blocks = gather_heads(heads)
+        own_blocks, other_blocks = gather_heads(heads, teacher)
     with jax.named_scope("student"):
         entries = vocab_head.shape[0]
         own_logits, table = own_student(entries, own_blocks, teacher, down)
         other_logits, sums = other_student(entries, place, other_blocks, teacher, down, table)
     with jax.named_scope("totals"):
-        sums = jnp.sum(gathered(sums, VOC, vocs), axis=0)
-        sums = jnp.sum(gathered(sums, REP, reps), axis=0)
-        logs = jnp.log(sums)
-        loss = jnp.sum(sums[2] / sums[0] - logs[0] + logs[1]) / count
+        sums = totalled(exchange(sums, ("z", "c")), False)
+        logs = totalled(exchange(sums, ("y", "x")), True)
+        loss = jnp.sum(logs[2]) / count
     with jax.named_scope("grad"):
         other_rows = grad_rows(1, place, teacher, other_logits, logs, across)
         own_rows = grad_rows(0, place, teacher, own_logits, logs, across)

time: 223 us -> 216 us (0.969)
  local copies, waits for them, and re-layouts: 29.4 us -> 19.1 us
  blocking collectives: 43.7 us -> 47.8 us
  waiting for transfers between devices: 48.1 us -> 51 us
  starting transfers between devices: 62.9 us -> 60.3 us
    unnamed x63 -> x27, local copies, waits for them, and re-layouts: 26.3 us -> 16 us
    all_gather x1, waiting for transfers between devices: 0.01 us -> 7.58 us  [shards(): target_all = lax.all_gather(targets, REP, axis=0, tiled=True)]
    ppermute x33, waiting for transfers between devices: 32.6 us -> 27.9 us  [swap(): lax.ppermute(block, axis, [(i, i ^ step) for i in range(SIZES[axis])])]
    all_to_all x4, blocking collectives: 43.7 us -> 47.8 us  [exchange(): return lax.all_to_all(blocks, axis, split_axis=0, concat_axis=0, tiled=True)]
    pallas_call x6 -> x8, Pallas kernels: 14.2 us -> 13.8 us  [call(): pl.pallas_call(kernel, in_specs=specs, out_specs=jax.tree.map(lambda _: p...]
  transfers between devices with their start and end apart: 37 -> 37, of which waited for: 16 -> 14; matrix products, arithmetic and copies ran while one was open for 2% -> 2% of each run, Pallas kernels for 5% -> 5%
where the time goes in v5:
time: 216 us; the launch traced here: 215 us
  starting transfers between devices  60.3 us (28%)
  waiting for transfers between devices  51 us (24%)
  blocking collectives  47.8 us (22%)
  local copies, waits for them, and re-layouts  19.1 us (9%)
  between operations  16.3 us (8%)
  Pallas kernels  14.8 us (7%)
  other arithmetic  4.57 us (2%)
    all_to_all x4, blocking collectives, exchange(): return lax.all_to_all(blocks, axis, split_axis=0, concat_axis=0, tiled=True)  47.8 us
    all_to_all x3, starting transfers between devices, exchange(): return lax.all_to_all(blocks, axis, split_axis=0, concat_axis=0, tiled=True)  30.4 us
    ppermute x33, starting transfers between devices, swap(): lax.ppermute(block, axis, [(i, i ^ step) for i in range(SIZES[axis])])  29.9 us
    ppermute x33, waiting for transfers between devices, swap(): lax.ppermute(block, axis, [(i, i ^ step) for i in range(SIZES[axis])])  27.9 us
    unnamed x27, local copies, waits for them, and re-layouts  16 us
    all_to_all x3, waiting for transfers between devices, exchange(): return lax.all_to_all(blocks, axis, split_axis=0, concat_axis=0, tiled=True)  15.5 us
    pallas_call x8, Pallas kernels, call(): pl.pallas_call(kernel, in_specs=specs, out_specs=jax.tree.map(lambda _: p...  13.8 us
    all_gather x1, waiting for transfers between devices, shards(): target_all = lax.all_gather(targets, REP, axis=0, tiled=True)  7.58 us
  transfers between devices with their start and end apart: 37, of which 14 were waited for; matrix products, arithmetic and copies ran while one was open for 2% of the time, Pallas kernels for 5%

profile of v5, /device:TPU:1, one launch (start us, length us, event | category | flops | bytes accessed | tf_op | source)
XLA Modules:
  0.0 215.3 jit_solution(5035992510882529336)
XLA Ops:
  12.0 12.0 %all-to-all-start = ((bf16[32,8,1280]{2,1,0:T(8,128)(2,1)}), bf16[32,8,1280]{2,1,0:T(8,128)(2,1)S(1)}, u32[]{:S(2)}, u32[]{:S(2)}) async-start(bf16[32,8,1280]{2,1,0:T(8,128)(2,1)} %pad_maximum_fusion), calls=%async_computation | async-start | bytes 1310720 | tf_op jit(solution)/shard_map/gather_inputs/all_to_all | solution.py:22
  24.1 3.4 %copy-done.5 = bf16[501,8192]{1,0:T(8,128)(2,1)S(1)} copy-done((bf16[501,8192]{1,0:T(8,128)(2,1)S(1)}, bf16[501,8192]{1,0:T(8,128)(2,1)}, u32[]{:S(2)}) %copy-start.5) | copy-done | bytes 8208408
  27.6 3.3 %prepare.1 = (bf16[512,8192]{1,0:T(8,128)(2,1)S(1)}, bf16[8192,512]{1,0:T(8,128)(2,1)S(1)}, f32[8,128]{1,0:T(8,128)S(1)}) custom-call(s32[17]{0:T(128)S(1)} %pad_add_fusion.place, bf16[501,8192]{1,0:T(8,128)(2,1)S(1)} %copy-done.5), custom_call_target="tpu_custom_call" | custom-call | bytes 25165824 | tf_op jit(solution)/shard_map/prepare/pallas_call | solution.py:61
  30.9 3.3 %copy-done.1 = bf16[8192,512]{1,0:T(8,128)(2,1)} copy-done((bf16[8192,512]{1,0:T(8,128)(2,1)}, bf16[8192,512]{1,0:T(8,128)(2,1)S(1)}, u32[]{:S(2)}) %copy-start.1) | copy-done | bytes 8388632
  34.2 3.3 %copy-done.4 = bf16[512,8192]{1,0:T(8,128)(2,1)} copy-done((bf16[512,8192]{1,0:T(8,128)(2,1)}, bf16[512,8192]{1,0:T(8,128)(2,1)S(1)}, u32[]{:S(2)}) %copy-start.4) | copy-done | bytes 8388632
  37.4 4.4 %all-to-all-done = bf16[32,8,1280]{2,1,0:T(8,128)(2,1)S(1)} async-done(((bf16[32,8,1280]{2,1,0:T(8,128)(2,1)}), bf16[32,8,1280]{2,1,0:T(8,128)(2,1)S(1)}, u32[]{:S(2)}, u32[]{:S(2)}) %all-to-all-start) | async-done | bytes 655392 | tf_op jit(solution)/shard_map/gather_inputs/all_to_all | solution.py:22
  42.9 10.6 %all-to-all-start.1 = ((f32[8,32,256]{2,1,0:T(8,128)}), f32[8,32,256]{2,1,0:T(8,128)S(1)}, u32[]{:S(2)}, u32[]{:S(2)}) async-start(f32[8,32,256]{2,1,0:T(8,128)} %bitcast.5), calls=%async_computation.1 | async-start | bytes 524288 | tf_op jit(solution)/shard_map/head/all_to_all | solution.py:22
  53.6 6.5 %all-to-all-done.1 = f32[8,32,256]{2,1,0:T(8,128)S(1)} async-done(((f32[8,32,256]{2,1,0:T(8,128)}), f32[8,32,256]{2,1,0:T(8,128)S(1)}, u32[]{:S(2)}, u32[]{:S(2)}) %all-to-all-start.1) | async-done | bytes 262176 | tf_op jit(solution)/shard_map/head/all_to_all | solution.py:22
  60.1 11.2 %all_to_all.35 = bf16[8,32,256]{2,1,0:T(8,128)(2,1)S(1)} all-to-all(bf16[8,32,256]{2,1,0:T(8,128)(2,1)S(1)} %broadcast_in_dim.35), channel_id=1, replica_groups=mesh['y'=4,'z'=8,'x'=4,'c'=2] {'z'}, dimensions={0} | all-to-all | bytes 262144 | tf_op jit(solution)/shard_map/gather_heads/all_to_all | solution.py:22
  78.3 2.2 %collective-permute-done.refs_1_ = bf16[16,2048]{1,0:T(8,128)(2,1)S(1)} collective-permute-done((bf16[16,2048]{1,0:T(8,128)(2,1)S(1)}, bf16[16,2048]{1,0:T(8,128)(2,1)S(1)}, u32[]{:S(2)}, u32[]{:S(2)}) %collective-permute-start) | collective-permute-done | bytes 65568 | tf_op jit(solution)/shard_map/gather_heads/ppermute | solution.py:30
  86.1 9.6 %collective-permute-done.8.refs_3_ = bf16[16,8192]{1,0:T(8,128)(2,1)S(1)} collective-permute-done((bf16[16,8192]{1,0:T(8,128)(2,1)S(1)}, bf16[16,8192]{1,0:T(8,128)(2,1)S(1)}, u32[]{:S(2)}, u32[]{:S(2)}) %collective-permute-start.8) | collective-permute-done | bytes 262176 | tf_op jit(solution)/shard_map/gather_heads/ppermute | solution.py:30
  95.7 7.6 %all-gather.3.cloned.1.call-done.target_ref = bf16[256,8192]{1,0:T(8,128)(2,1)} async-done(((bf16[8,8192]{1,0:T(8,128)(2,1)}), bf16[256,8192]{1,0:T(8,128)(2,1)}) %all-gather.3.cloned.1.call-update) | async-done | bytes 4194320 | tf_op jit(solution)/shard_map/gather_targets/all_gather | solution.py:334
  103.3 3.4 %copy-done.2 = bf16[8192,512]{1,0:T(8,128)(2,1)S(1)} copy-done((bf16[8192,512]{1,0:T(8,128)(2,1)S(1)}, bf16[8192,512]{1,0:T(8,128)(2,1)}, u32[]{:S(2)}) %copy-start.2) | copy-done | bytes 8388632
  108.9 2.9 %teacher.1.refs_8_.teacher_ref = f32[256,512]{1,0:T(8,128)S(1)} custom-call(s32[17]{0:T(128)S(1)} %pad_add_fusion.place, bf16[256,8192]{1,0:T(8,128)(2,1)S(1)} %copy-done.6, bf16[8192,512]{1,0:T(8,128)(2,1)S(1)} %copy-done.2), custom_call_target="tpu_custom_call" | custom-call | flops 2147483648 | bytes 12582912 | tf_op jit(solution)/shard_map/teacher/pallas_call | solution.py:61
  111.8 4.5 %collective-permute-start.12 = (bf16[16,8192]{1,0:T(8,128)(2,1)S(1)}, bf16[16,8192]{1,0:T(8,128)(2,1)S(1)}, u32[]{:S(2)}, u32[]{:S(2)}) collective-permute-start(bf16[16,8192]{1,0:T(8,128)(2,1)S(1)} %get-tuple-element.24.refs_0_), channel_id=1, source_target_pairs={{0,1},{1,0},{2,3},{3,2},{4,5},{5,4},{6,7},{7,6},{8,9},{9,8},{10,11... | collective-permute-start | bytes 786440 | tf_op jit(solution)/shard_map/gather_heads/ppermute | solution.py:30
  122.1 14.2 %all_to_all.36.parts_ref = f32[16,8,256]{2,1,0:T(8,128)S(1)} all-to-all(f32[16,8,256]{2,1,0:T(8,128)S(1)} %get-tuple-element.33), channel_id=1, replica_groups=mesh['y'=4,'z'=8,'x'=4,'c'=2] {'z','c'}, dimensions={0} | all-to-all | bytes 262144 | tf_op jit(solution)/shard_map/totals/all_to_all | solution.py:22
  136.4 12.0 %all_to_all.37.parts_ref = f32[16,8,256]{2,1,0:T(8,128)S(1)} all-to-all(f32[16,8,256]{2,1,0:T(8,128)S(1)} %totals.2), channel_id=1, replica_groups=mesh['y'=4,'z'=8,'x'=4,'c'=2] {'y','x'}, dimensions={0} | all-to-all | bytes 262144 | tf_op jit(solution)/shard_map/totals/all_to_all | solution.py:22
  157.0 2.4 %collective-permute-start.28 = (bf16[64,2048]{1,0:T(8,128)(2,1)S(1)}, bf16[64,2048]{1,0:T(8,128)(2,1)S(1)}, u32[]{:S(2)}, u32[]{:S(2)}) collective-permute-start(bf16[64,2048]{1,0:T(8,128)(2,1)S(1)} %get-tuple-element.44), channel_id=1, source_target_pairs={{0,128},{64,192},{128,0},{192,64},{1,129},{65,193},{129,1},{193,65... | collective-permute-start | bytes 786440 | tf_op jit(solution)/shard_map/reduce_grad/ppermute | solution.py:30
  160.7 2.9 %collective-permute-done.27 = bf16[64,2048]{1,0:T(8,128)(2,1)S(1)} collective-permute-done((bf16[64,2048]{1,0:T(8,128)(2,1)S(1)}, bf16[64,2048]{1,0:T(8,128)(2,1)S(1)}, u32[]{:S(2)}, u32[]{:S(2)}) %collective-permute-start.27) | collective-permute-done | bytes 262176 | tf_op jit(solution)/shard_map/reduce_grad/ppermute | solution.py:30
  164.5 6.0 %collective-permute-done.29 = bf16[64,2048]{1,0:T(8,128)(2,1)S(1)} collective-permute-done((bf16[64,2048]{1,0:T(8,128)(2,1)S(1)}, bf16[64,2048]{1,0:T(8,128)(2,1)S(1)}, u32[]{:S(2)}, u32[]{:S(2)}) %collective-permute-start.29) | collective-permute-done | bytes 262176 | tf_op jit(solution)/shard_map/reduce_grad/ppermute | solution.py:30
  171.4 2.7 %collective-permute-start.31 = (bf16[16,2048]{1,0:T(8,128)(2,1)S(1)}, bf16[16,2048]{1,0:T(8,128)(2,1)S(1)}, u32[]{:S(2)}, u32[]{:S(2)}) collective-permute-start(bf16[16,2048]{1,0:T(8,128)(2,1)S(1)} %get-tuple-element.50), channel_id=1, source_target_pairs={{0,4},{2,6},{4,0},{6,2},{1,5},{3,7},{5,1},{7,3},{8,12},{10,14},{12... | collective-permute-start | bytes 196616 | tf_op jit(solution)/shard_map/reduce_grad/ppermute | solution.py:30
  180.3 10.4 %all_to_all.38 = bf16[8,32,256]{2,1,0:T(8,128)(2,1)S(1)} all-to-all(bf16[8,32,256]{2,1,0:T(8,128)(2,1)S(1)} %bitcast.40), channel_id=1, replica_groups=mesh['y'=4,'z'=8,'x'=4,'c'=2] {'z'}, dimensions={0} | all-to-all | bytes 262144 | tf_op jit(solution)/shard_map/reduce_grad/all_to_all | solution.py:22
  191.7 7.7 %all-to-all-start.6 = ((bf16[8,48,256]{2,1,0:T(8,128)(2,1)}), bf16[8,48,256]{2,1,0:T(8,128)(2,1)S(1)}, u32[]{:S(2)}, u32[]{:S(2)}) async-start(bf16[8,48,256]{2,1,0:T(8,128)(2,1)} %broadcast_in_dim.38), calls=%async_computation.6 | async-start | bytes 393216 | tf_op jit(solution)/shard_map/finish/all_to_all | solution.py:22
  200.7 4.7 %all-to-all-done.6 = bf16[8,48,256]{2,1,0:T(8,128)(2,1)S(1)} async-done(((bf16[8,48,256]{2,1,0:T(8,128)(2,1)}), bf16[8,48,256]{2,1,0:T(8,128)(2,1)S(1)}, u32[]{:S(2)}, u32[]{:S(2)}) %all-to-all-start.6) | async-done | bytes 196640 | tf_op jit(solution)/shard_map/finish/all_to_all | solution.py:22
  (133 shorter events, 47.8 us)
Async XLA Ops:
  7.2 96.1 %all-gather.3.cloned.1.call-start = ((), (), s32[]{:S(2)}) async-start(), calls=%async_computation.7 | async-start | bytes 4325376 | tf_op jit(solution)/shard_map/gather_targets/all_gather | solution.py:334
  12.0 29.8 %all-to-all-start = ((bf16[32,8,1280]{2,1,0:T(8,128)(2,1)}), bf16[32,8,1280]{2,1,0:T(8,128)(2,1)S(1)}, u32[]{:S(2)}, u32[]{:S(2)}) async-start(bf16[32,8,1280]{2,1,0:T(8,128)(2,1)} %pad_maximum_fusion), calls=%async_computation | async-start | bytes 1310720 | tf_op jit(solution)/shard_map/gather_inputs/all_to_all | solution.py:22
  42.9 17.1 %all-to-all-start.1 = ((f32[8,32,256]{2,1,0:T(8,128)}), f32[8,32,256]{2,1,0:T(8,128)S(1)}, u32[]{:S(2)}, u32[]{:S(2)}) async-start(f32[8,32,256]{2,1,0:T(8,128)} %bitcast.5), calls=%async_computation.1 | async-start | bytes 524288 | tf_op jit(solution)/shard_map/head/all_to_all | solution.py:22
  71.4 6.8 %collective-permute-start.2 = (bf16[16,2048]{1,0:T(8,128)(2,1)S(1)}, bf16[16,2048]{1,0:T(8,128)(2,1)S(1)}, u32[]{:S(2)}, u32[]{:S(2)}) collective-permute-start(bf16[16,2048]{1,0:T(8,128)(2,1)S(1)} %bitcast.29), channel_id=1, source_target_pairs={{0,192},{64,128},{128,64},{192,0},{1,193},{65,129},{129,65},{193,1... | collective-permute-start | bytes 196616 | tf_op jit(solution)/shard_map/gather_heads/ppermute | solution.py:30
  72.1 6.2 %collective-permute-start.1 = (bf16[16,2048]{1,0:T(8,128)(2,1)S(1)}, bf16[16,2048]{1,0:T(8,128)(2,1)S(1)}, u32[]{:S(2)}, u32[]{:S(2)}) collective-permute-start(bf16[16,2048]{1,0:T(8,128)(2,1)S(1)} %bitcast.30), channel_id=1, source_target_pairs={{0,128},{64,192},{128,0},{192,64},{1,129},{65,193},{129,1},{193,65... | collective-permute-start | bytes 196616 | tf_op jit(solution)/shard_map/gather_heads/ppermute | solution.py:30
  73.4 7.0 %collective-permute-start = (bf16[16,2048]{1,0:T(8,128)(2,1)S(1)}, bf16[16,2048]{1,0:T(8,128)(2,1)S(1)}, u32[]{:S(2)}, u32[]{:S(2)}) collective-permute-start(bf16[16,2048]{1,0:T(8,128)(2,1)S(1)} %bitcast.31), channel_id=1, source_target_pairs={{0,64},{64,0},{128,192},{192,128},{1,65},{65,1},{129,193},{193,129... | collective-permute-start | bytes 196616 | tf_op jit(solution)/shard_map/gather_heads/ppermute | solution.py:30
  74.7 5.7 %collective-permute-start.5 = (bf16[16,2048]{1,0:T(8,128)(2,1)S(1)}, bf16[16,2048]{1,0:T(8,128)(2,1)S(1)}, u32[]{:S(2)}, u32[]{:S(2)}) collective-permute-start(bf16[16,2048]{1,0:T(8,128)(2,1)S(1)} %bitcast.33), channel_id=1, source_target_pairs={{0,6},{2,4},{4,2},{6,0},{1,7},{3,5},{5,3},{7,1},{8,14},{10,12},{12... | collective-permute-start | bytes 196616 | tf_op jit(solution)/shard_map/gather_heads/ppermute | solution.py:30
  75.5 5.0 %collective-permute-start.4 = (bf16[16,2048]{1,0:T(8,128)(2,1)S(1)}, bf16[16,2048]{1,0:T(8,128)(2,1)S(1)}, u32[]{:S(2)}, u32[]{:S(2)}) collective-permute-start(bf16[16,2048]{1,0:T(8,128)(2,1)S(1)} %bitcast.34), channel_id=1, source_target_pairs={{0,4},{2,6},{4,0},{6,2},{1,5},{3,7},{5,1},{7,3},{8,12},{10,14},{12... | collective-permute-start | bytes 196616 | tf_op jit(solution)/shard_map/gather_heads/ppermute | solution.py:30
  81.7 14.1 %collective-permute-start.8 = (bf16[16,8192]{1,0:T(8,128)(2,1)S(1)}, bf16[16,8192]{1,0:T(8,128)(2,1)S(1)}, u32[]{:S(2)}, u32[]{:S(2)}) collective-permute-start(bf16[16,8192]{1,0:T(8,128)(2,1)S(1)} %get-tuple-element.21.refs_0_), channel_id=1, source_target_pairs={{0,6},{2,4},{4,2},{6,0},{1,7},{3,5},{5,3},{7,1},{8,14},{10,12},{12... | collective-permute-start | bytes 786440 | tf_op jit(solution)/shard_map/gather_heads/ppermute | solution.py:30
  82.5 29.3 %collective-permute-start.7 = (bf16[16,8192]{1,0:T(8,128)(2,1)S(1)}, bf16[16,8192]{1,0:T(8,128)(2,1)S(1)}, u32[]{:S(2)}, u32[]{:S(2)}) collective-permute-start(bf16[16,8192]{1,0:T(8,128)(2,1)S(1)} %get-tuple-element.21.refs_0_), channel_id=1, source_target_pairs={{0,4},{2,6},{4,0},{6,2},{1,5},{3,7},{5,1},{7,3},{8,12},{10,14},{12... | collective-permute-start | bytes 786440 | tf_op jit(solution)/shard_map/gather_heads/ppermute | solution.py:30
  83.7 28.1 %collective-permute-start.6 = (bf16[16,8192]{1,0:T(8,128)(2,1)S(1)}, bf16[16,8192]{1,0:T(8,128)(2,1)S(1)}, u32[]{:S(2)}, u32[]{:S(2)}) collective-permute-start(bf16[16,8192]{1,0:T(8,128)(2,1)S(1)} %get-tuple-element.21.refs_0_), channel_id=1, source_target_pairs={{0,2},{2,0},{4,6},{6,4},{1,3},{3,1},{5,7},{7,5},{8,10},{10,8},{12,... | collective-permute-start | bytes 786440 | tf_op jit(solution)/shard_map/gather_heads/ppermute | solution.py:30
  85.0 26.8 %collective-permute-start.11 = (bf16[64,2048]{1,0:T(8,128)(2,1)S(1)}, bf16[64,2048]{1,0:T(8,128)(2,1)S(1)}, u32[]{:S(2)}, u32[]{:S(2)}) collective-permute-start(bf16[64,2048]{1,0:T(8,128)(2,1)S(1)} %get-tuple-element.22.refs_4_), channel_id=1, source_target_pairs={{0,192},{64,128},{128,64},{192,0},{1,193},{65,129},{129,65},{193,1... | collective-permute-start | bytes 786440 | tf_op jit(solution)/shard_map/gather_heads/ppermute | solution.py:30
  85.0 26.8 %collective-permute-start.10 = (bf16[64,2048]{1,0:T(8,128)(2,1)S(1)}, bf16[64,2048]{1,0:T(8,128)(2,1)S(1)}, u32[]{:S(2)}, u32[]{:S(2)}) collective-permute-start(bf16[64,2048]{1,0:T(8,128)(2,1)S(1)} %get-tuple-element.22.refs_4_), channel_id=1, source_target_pairs={{0,128},{64,192},{128,0},{192,64},{1,129},{65,193},{129,1},{193,65... | collective-permute-start | bytes 786440 | tf_op jit(solution)/shard_map/gather_heads/ppermute | solution.py:30
  95.7 16.1 %collective-permute-start.9 = (bf16[64,2048]{1,0:T(8,128)(2,1)S(1)}, bf16[64,2048]{1,0:T(8,128)(2,1)S(1)}, u32[]{:S(2)}, u32[]{:S(2)}) collective-permute-start(bf16[64,2048]{1,0:T(8,128)(2,1)S(1)} %get-tuple-element.22.refs_4_), channel_id=1, source_target_pairs={{0,64},{64,0},{128,192},{192,128},{1,65},{65,1},{129,193},{193,129... | collective-permute-start | bytes 786440 | tf_op jit(solution)/shard_map/gather_heads/ppermute | solution.py:30
  111.8 5.6 %collective-permute-start.12 = (bf16[16,8192]{1,0:T(8,128)(2,1)S(1)}, bf16[16,8192]{1,0:T(8,128)(2,1)S(1)}, u32[]{:S(2)}, u32[]{:S(2)}) collective-permute-start(bf16[16,8192]{1,0:T(8,128)(2,1)S(1)} %get-tuple-element.24.refs_0_), channel_id=1, source_target_pairs={{0,1},{1,0},{2,3},{3,2},{4,5},{5,4},{6,7},{7,6},{8,9},{9,8},{10,11... | collective-permute-start | bytes 786440 | tf_op jit(solution)/shard_map/gather_heads/ppermute | solution.py:30
  156.0 7.6 %collective-permute-start.27 = (bf16[64,2048]{1,0:T(8,128)(2,1)S(1)}, bf16[64,2048]{1,0:T(8,128)(2,1)S(1)}, u32[]{:S(2)}, u32[]{:S(2)}) collective-permute-start(bf16[64,2048]{1,0:T(8,128)(2,1)S(1)} %get-tuple-element.42), channel_id=1, source_target_pairs={{0,64},{64,0},{128,192},{192,128},{1,65},{65,1},{129,193},{193,129... | collective-permute-start | bytes 786440 | tf_op jit(solution)/shard_map/reduce_grad/ppermute | solution.py:30
  156.1 14.4 %collective-permute-start.29 = (bf16[64,2048]{1,0:T(8,128)(2,1)S(1)}, bf16[64,2048]{1,0:T(8,128)(2,1)S(1)}, u32[]{:S(2)}, u32[]{:S(2)}) collective-permute-start(bf16[64,2048]{1,0:T(8,128)(2,1)S(1)} %get-tuple-element.43), channel_id=1, source_target_pairs={{0,192},{64,128},{128,64},{192,0},{1,193},{65,129},{129,65},{193,1... | collective-permute-start | bytes 786440 | tf_op jit(solution)/shard_map/reduce_grad/ppermute | solution.py:30
  157.0 13.5 %collective-permute-start.28 = (bf16[64,2048]{1,0:T(8,128)(2,1)S(1)}, bf16[64,2048]{1,0:T(8,128)(2,1)S(1)}, u32[]{:S(2)}, u32[]{:S(2)}) collective-permute-start(bf16[64,2048]{1,0:T(8,128)(2,1)S(1)} %get-tuple-element.44), channel_id=1, source_target_pairs={{0,128},{64,192},{128,0},{192,64},{1,129},{65,193},{129,1},{193,65... | collective-permute-start | bytes 786440 | tf_op jit(solution)/shard_map/reduce_grad/ppermute | solution.py:30
  159.4 11.9 %collective-permute-start.21 = (bf16[16,8192]{1,0:T(8,128)(2,1)S(1)}, bf16[16,8192]{1,0:T(8,128)(2,1)S(1)}, u32[]{:S(2)}, u32[]{:S(2)}) collective-permute-start(bf16[16,8192]{1,0:T(8,128)(2,1)S(1)} %get-tuple-element.39), channel_id=1, source_target_pairs={{0,2},{2,0},{4,6},{6,4},{1,3},{3,1},{5,7},{7,5},{8,10},{10,8},{12,... | collective-permute-start | bytes 786440 | tf_op jit(solution)/shard_map/reduce_grad/ppermute | solution.py:30
  159.8 14.3 %collective-permute-start.23 = (bf16[16,8192]{1,0:T(8,128)(2,1)S(1)}, bf16[16,8192]{1,0:T(8,128)(2,1)S(1)}, u32[]{:S(2)}, u32[]{:S(2)}) collective-permute-start(bf16[16,8192]{1,0:T(8,128)(2,1)S(1)} %get-tuple-element.40), channel_id=1, source_target_pairs={{0,6},{2,4},{4,2},{6,0},{1,7},{3,5},{5,3},{7,1},{8,14},{10,12},{12... | collective-permute-start | bytes 786440 | tf_op jit(solution)/shard_map/reduce_grad/ppermute | solution.py:30
  163.6 10.4 %collective-permute-start.22 = (bf16[16,8192]{1,0:T(8,128)(2,1)S(1)}, bf16[16,8192]{1,0:T(8,128)(2,1)S(1)}, u32[]{:S(2)}, u32[]{:S(2)}) collective-permute-start(bf16[16,8192]{1,0:T(8,128)(2,1)S(1)} %get-tuple-element.41), channel_id=1, source_target_pairs={{0,4},{2,6},{4,0},{6,2},{1,5},{3,7},{5,1},{7,3},{8,12},{10,14},{12... | collective-permute-start | bytes 786440 | tf_op jit(solution)/shard_map/reduce_grad/ppermute | solution.py:30
  171.1 6.5 %collective-permute-start.32 = (bf16[16,2048]{1,0:T(8,128)(2,1)S(1)}, bf16[16,2048]{1,0:T(8,128)(2,1)S(1)}, u32[]{:S(2)}, u32[]{:S(2)}) collective-permute-start(bf16[16,2048]{1,0:T(8,128)(2,1)S(1)} %get-tuple-element.49), channel_id=1, source_target_pairs={{0,6},{2,4},{4,2},{6,0},{1,7},{3,5},{5,3},{7,1},{8,14},{10,12},{12... | collective-permute-start | bytes 196616 | tf_op jit(solution)/shard_map/reduce_grad/ppermute | solution.py:30
  171.4 6.2 %collective-permute-start.31 = (bf16[16,2048]{1,0:T(8,128)(2,1)S(1)}, bf16[16,2048]{1,0:T(8,128)(2,1)S(1)}, u32[]{:S(2)}, u32[]{:S(2)}) collective-permute-start(bf16[16,2048]{1,0:T(8,128)(2,1)S(1)} %get-tuple-element.50), channel_id=1, source_target_pairs={{0,4},{2,6},{4,0},{6,2},{1,5},{3,7},{5,1},{7,3},{8,12},{10,14},{12... | collective-permute-start | bytes 196616 | tf_op jit(solution)/shard_map/reduce_grad/ppermute | solution.py:30
  191.7 13.7 %all-to-all-start.6 = ((bf16[8,48,256]{2,1,0:T(8,128)(2,1)}), bf16[8,48,256]{2,1,0:T(8,128)(2,1)S(1)}, u32[]{:S(2)}, u32[]{:S(2)}) async-start(bf16[8,48,256]{2,1,0:T(8,128)(2,1)} %broadcast_in_dim.38), calls=%async_computation.6 | async-start | bytes 393216 | tf_op jit(solution)/shard_map/finish/all_to_all | solution.py:22
  (26 other events, 206.2 us)
Sparse Core Ops, SparseCore 0:
  10.6 92.6 all-gather.2

commit v6 on v5

--- a/solution.py
+++ b/solution.py
@@ -14,7 +14,7 @@
 CHUNKS = 4
 PADDED = 512
 LIMIT = 24 * 1024 * 1024
-HEAD_COST = 45_000_000_000
+HEAD_COST = 60_000_000_000
 SIZES = {"y": 4, "z": 8, "x": 4, "c": 2}
 
 
@@ -98,29 +98,31 @@
     )(place, vocab_head)
 
 
-def teacher_kernel(place, target_ref, down_ref, out_ref, total):
+def teacher_kernel(place, own_ref, other_ref, down_ref, out_ref, total):
     width = down_ref.shape[0] // CHUNKS
-    for at in range(CHUNKS):
-        start = pl.multiple_of((place[16] ^ at) * width, width)
-        product = jnp.dot(
-            target_ref[:, pl.ds(start, width)],
-            down_ref[at * width : (at + 1) * width],
-            preferred_element_type=F32,
-        )
-        total[...] = product if at == 0 else total[...] + product
+    for half, target_ref in enumerate((own_ref, other_ref)):
+        for at in range(2):
+            group = (place[17] ^ half) * 2 + at
+            start = pl.multiple_of((group ^ place[16]) * width, width)
+            product = jnp.dot(
+                target_ref[:, at * width : (at + 1) * width],
+                down_ref[pl.ds(start, width)],
+                preferred_element_type=F32,
+            )
+            total[...] = product if half + at == 0 else total[...] + product
     for at in range(16):
         start = pl.multiple_of(place[at] * 16, 16)
         out_ref[at * 16 : (at + 1) * 16] = total[pl.ds(start, 16)]
 
 
-def teacher_logits(place, target_all, down):
-    count, depth = target_all.shape
+def teacher_logits(place, own_half, other_half, down):
+    count, depth = own_half.shape[0], down.shape[0]
     return local_call(
         teacher_kernel,
         shape(count, PADDED),
         cost(2 * count * PADDED * depth, 2 * (count + PADDED) * depth),
         [pltpu.VMEM((count, PADDED), F32)],
-    )(place, target_all, down)
+    )(place, own_half, other_half, down)
 
 
 def student_part(entries, core, firsts, seconds, teacher_ref, down_ref, out_ref):
@@ -149,6 +151,11 @@
     return table
 
 
+def packed(table):
+    lanes = table.shape[1] // 2
+    return jnp.concatenate([table[:, :lanes], table[:, lanes:]], axis=0)
+
+
 def own_student_kernel(entries, *refs):
     teacher_ref, down_ref, out_ref, table_ref = refs[8:]
     table_ref[...] = student_part(
@@ -163,8 +170,8 @@
         for at in range(8):
             start = pl.multiple_of(place[core * 8 + at] * 16, 16)
             turned[pl.ds(start, 16)] = table[at * 16 : (at + 1) * 16]
-    sums = turned[...].T[:8]
-    for at in range(16):
+    sums = packed(turned[...].T[:4])
+    for at in range(sums_ref.shape[0]):
         sums_ref[at] = sums
 
 
@@ -182,7 +189,7 @@
     rows = teacher.shape[0] // 2
     return local_call(
         functools.partial(other_student_kernel, entries),
-        [shape(rows, PADDED), shape(16, 8, 2 * rows)],
+        [shape(rows, PADDED), shape(8, 8, rows)],
         cost(2 * rows * down.size, 2 * down.size, 2 * rows * PADDED),
         [pltpu.VMEM((2 * rows, 128), F32)],
     )(place, *blocks, teacher, down, table)
@@ -221,7 +228,7 @@
     pass
 
 
-def settled(blocks, teacher):
+def settled(blocks, awaited):
     return pl.pallas_call(
         pass_kernel,
         in_specs=[pl.BlockSpec(memory_space=pl.ANY)] * (len(blocks) + 1),
@@ -230,29 +237,35 @@
         input_output_aliases={at: at for at in range(len(blocks))},
         compiler_params=pltpu.CompilerParams(vmem_limit_bytes=1024 * 1024),
         cost_estimate=cost(0, 0),
-    )(*blocks, teacher)
-
-
-def total_kernel(last, parts_ref, out_ref):
-    sums = parts_ref[0]
-    for at in range(1, 16):
-        sums = sums + parts_ref[at]
-    if last:
-        logs = jnp.log(sums[:2])
-        terms = sums[2:3] / sums[:1] - logs[:1] + logs[1:]
-        out_ref[...] = jnp.zeros(out_ref.shape, F32)
-        out_ref[:2] = logs
-        out_ref[2:3] = terms
-    else:
-        for at in range(16):
-            out_ref[at] = sums
-
-
-def totalled(parts, last):
-    _, rows, count = parts.shape
-    return local_call(
-        functools.partial(total_kernel, last),
-        shape(rows, count) if last else shape(*parts.shape),
+    )(*blocks, awaited)
+
+
+def summed_parts(parts_ref):
+    parts = [parts_ref[at] for at in range(parts_ref.shape[0])]
+    while len(parts) > 1:
+        parts = [parts[at] + parts[at + 1] for at in range(0, len(parts), 2)]
+    return parts[0]
+
+
+def total_kernel(parts_ref, out_ref):
+    sums = summed_parts(parts_ref)
+    for at in range(out_ref.shape[0]):
+        out_ref[at] = sums
+
+
+def log_kernel(parts_ref, out_ref):
+    sums = summed_parts(parts_ref)
+    sums = jnp.concatenate([sums[:4], sums[4:]], axis=1)
+    logs = jnp.log(sums[:2])
+    out_ref[...] = jnp.zeros(out_ref.shape, F32)
+    out_ref[:2] = logs
+    out_ref[2:3] = sums[2:3] / sums[:1] - logs[:1] + logs[1:]
+
+
+def totalled(kernel, parts, *sizes):
+    return local_call(
+        kernel,
+        shape(*sizes),
         cost(parts.size, 4 * parts.size),
         limit=2 * 1024 * 1024,
         scalars=False,
@@ -294,10 +307,12 @@
     )(rows, weight, done)
 
 
-def gather_heads(heads, teacher):
-    rows, width = heads.shape
-    half = rows // 2
-    lines = gathered(heads, "z", 8).transpose(1, 0, 2).reshape(rows, -1)
+def gather_lines(heads):
+    return gathered(heads, "z", 8).transpose(1, 0, 2).reshape(heads.shape[0], -1)
+
+
+def gather_heads(lines, teacher):
+    half = lines.shape[0] // 2
     first, second = join(from_peers(lines[:half], "y"), from_peers(lines[half:], "x"))
     blocks = settled(from_peers(first, "x") + from_peers(second, "y"), teacher)
     return blocks, [swap(block, "c", 1) for block in blocks]
@@ -328,10 +343,13 @@
     rows = count // vocs
     at_x, at_y, at_c = lax.axis_index("x"), lax.axis_index("y"), lax.axis_index("c")
     voc_index = at_x * 2 + at_c
-    inputs = jnp.take(log_hidden, positions, axis=0, mode="clip")
-    targets = jnp.take(log_hidden, positions + offsets, axis=0, mode="clip")
+    taken = jnp.concatenate([positions, positions + offsets])
+    taken = jnp.take(log_hidden, taken, axis=0, mode="clip")
+    inputs, targets = taken[:own], taken[own:]
     with jax.named_scope("gather_targets"):
-        target_all = lax.all_gather(targets, REP, axis=0, tiled=True)
+        half = targets.shape[1] // 2
+        target_half = lax.dynamic_slice_in_dim(targets, at_c * half, half, 1)
+        target_half = lax.all_gather(target_half, REP, axis=0, tiled=True)
     with jax.named_scope("gather_inputs"):
         input_block = lax.dynamic_slice_in_dim(inputs, voc_index * in_width, in_width, 1)
         input_cols = inputs.reshape(own, reps, out_width).transpose(1, 0, 2)
@@ -344,7 +362,7 @@
         residual = lax.dynamic_slice_in_dim(residual, voc_index * rows, rows, 0)
     steps = jnp.arange(16)
     order = ((at_x ^ (steps % 4)) * 2 + (at_c ^ (steps // 8))) * 2 + (steps // 4) % 2
-    place = jnp.concatenate([order, at_y[None]]).astype(jnp.int32)
+    place = jnp.concatenate([order, at_y[None], at_c[None]]).astype(jnp.int32)
     with jax.named_scope("prepare"):
         across, down, done = prepare(place, vocab_head)
     with jax.named_scope("head"):
@@ -352,17 +370,22 @@
         parts = exchange(partial_pre.reshape(vocs, rows, out_width), VOC)
         preact = jnp.sum(parts, axis=0) + head_bias
         heads = (residual.astype(F32) + jax.nn.silu(preact)).astype(BF16)
+    with jax.named_scope("gather_heads"):
+        lines = gather_lines(heads)
     with jax.named_scope("teacher"):
-        teacher = teacher_logits(place, target_all, down)
+        target_half = pltpu.with_memory_space_constraint(target_half, pltpu.HBM)
+        (target_half,) = settled([target_half], lines)
+        other_half = swap(target_half, "c", 1)
+        teacher = teacher_logits(place, target_half, other_half, down)
     with jax.named_scope("gather_heads"):
-        own_blocks, other_blocks = gather_heads(heads, teacher)
+        own_blocks, other_blocks = gather_heads(lines, teacher)
     with jax.named_scope("student"):
         entries = vocab_head.shape[0]
         own_logits, table = own_student(entries, own_blocks, teacher, down)
         other_logits, sums = other_student(entries, place, other_blocks, teacher, down, table)
     with jax.named_scope("totals"):
-        sums = totalled(exchange(sums, ("z", "c")), False)
-        logs = totalled(exchange(sums, ("y", "x")), True)
+        sums = totalled(total_kernel, exchange(sums, VOC), reps, 8, count // 2)
+        logs = totalled(log_kernel, exchange(sums, REP), 8, count)
         loss = jnp.sum(logs[2]) / count
     with jax.named_scope("grad"):
         other_rows = grad_rows(1, place, teacher, other_logits, logs, across)

time: 216 us -> 244 us (1.13)
  waiting for transfers between devices: 51 us -> 70.2 us
  starting transfers between devices: 60.3 us -> 73.8 us
  blocking collectives: 47.8 us -> 44.5 us
    all_gather x1, waiting for transfers between devices: 7.58 us -> 35.1 us  [shards(): target_half = lax.all_gather(target_half, REP, axis=0, tiled=True)]
    ppermute x33 -> x34, starting transfers between devices: 29.9 us -> 42.5 us  [swap(): lax.ppermute(block, axis, [(i, i ^ step) for i in range(SIZES[axis])])]
    ppermute x33 -> x34, waiting for transfers between devices: 27.9 us -> 21.5 us  [swap(): lax.ppermute(block, axis, [(i, i ^ step) for i in range(SIZES[axis])])]
    all_to_all x4, blocking collectives: 47.8 us -> 44.5 us  [exchange(): return lax.all_to_all(blocks, axis, split_axis=0, concat_axis=0, tiled=True)]
    unnamed x27 -> x23, local copies, waits for them, and re-layouts: 16 us -> 14.9 us
  transfers between devices with their start and end apart: 37 -> 38, of which waited for: 14 -> 17; matrix products, arithmetic and copies ran while one was open for 2% -> 1% of each run, Pallas kernels for 5% -> 4%
where the time goes in v6:
time: 244 us; the launch traced here: 243 us
  starting transfers between devices  73.8 us (30%)
  waiting for transfers between devices  70.2 us (29%)
  blocking collectives  44.5 us (18%)
  local copies, waits for them, and re-layouts  17.5 us (7%)
  between operations  16.2 us (7%)
  Pallas kernels  14.7 us (6%)
  other arithmetic  4.61 us (2%)
    all_to_all x4, blocking collectives, exchange(): return lax.all_to_all(blocks, axis, split_axis=0, concat_axis=0, tiled=True)  44.5 us
    ppermute x34, starting transfers between devices, swap(): lax.ppermute(block, axis, [(i, i ^ step) for i in range(SIZES[axis])])  42.5 us
    all_gather x1, waiting for transfers between devices, shards(): target_half = lax.all_gather(target_half, REP, axis=0, tiled=True)  35.1 us
    all_to_all x3, starting transfers between devices, exchange(): return lax.all_to_all(blocks, axis, split_axis=0, concat_axis=0, tiled=True)  31.3 us
    ppermute x34, waiting for transfers between devices, swap(): lax.ppermute(block, axis, [(i, i ^ step) for i in range(SIZES[axis])])  21.5 us
    unnamed x23, local copies, waits for them, and re-layouts  14.9 us
    pallas_call x8, Pallas kernels, call(): pl.pallas_call(kernel, in_specs=specs, out_specs=jax.tree.map(lambda _: p...  13.7 us
    all_to_all x3, waiting for transfers between devices, exchange(): return lax.all_to_all(blocks, axis, split_axis=0, concat_axis=0, tiled=True)  13.6 us
  transfers between devices with their start and end apart: 38, of which 17 were waited for; matrix products, arithmetic and copies ran while one was open for 1% of the time, Pallas kernels for 4%

profile of v6, /device:TPU:1, one launch (start us, length us, event | category | flops | bytes accessed | tf_op | source)
XLA Modules:
  0.0 242.9 jit_solution(13093538964677424557)
XLA Ops:
  10.4 12.0 %all-to-all-start = ((bf16[32,8,1280]{2,1,0:T(8,128)(2,1)}), bf16[32,8,1280]{2,1,0:T(8,128)(2,1)S(1)}, u32[]{:S(2)}, u32[]{:S(2)}) async-start(bf16[32,8,1280]{2,1,0:T(8,128)(2,1)} %pad_maximum_fusion), calls=%async_computation | async-start | bytes 1310720 | tf_op jit(solution)/shard_map/gather_inputs/all_to_all | solution.py:22
  23.3 3.3 %copy-done.6 = bf16[501,8192]{1,0:T(8,128)(2,1)S(1)} copy-done((bf16[501,8192]{1,0:T(8,128)(2,1)S(1)}, bf16[501,8192]{1,0:T(8,128)(2,1)}, u32[]{:S(2)}) %copy-start.6) | copy-done | bytes 8208408
  26.6 3.2 %prepare.1 = (bf16[512,8192]{1,0:T(8,128)(2,1)S(1)}, bf16[8192,512]{1,0:T(8,128)(2,1)S(1)}, f32[8,128]{1,0:T(8,128)S(1)}) custom-call(s32[18]{0:T(128)S(1)} %pad_add_fusion.place, bf16[501,8192]{1,0:T(8,128)(2,1)S(1)} %copy-done.6), custom_call_target="tpu_custom_call" | custom-call | bytes 25165824 | tf_op jit(solution)/shard_map/prepare/pallas_call | solution.py:61
  29.8 3.3 %copy-done.1 = bf16[8192,512]{1,0:T(8,128)(2,1)} copy-done((bf16[8192,512]{1,0:T(8,128)(2,1)}, bf16[8192,512]{1,0:T(8,128)(2,1)S(1)}, u32[]{:S(2)}) %copy-start.1) | copy-done | bytes 8388632
  33.1 3.3 %copy-done.4 = bf16[512,8192]{1,0:T(8,128)(2,1)} copy-done((bf16[512,8192]{1,0:T(8,128)(2,1)}, bf16[512,8192]{1,0:T(8,128)(2,1)S(1)}, u32[]{:S(2)}) %copy-start.4) | copy-done | bytes 8388632
  36.4 2.4 all-to-all-done
  39.9 9.3 %all-to-all-start.1 = ((f32[8,32,256]{2,1,0:T(8,128)}), f32[8,32,256]{2,1,0:T(8,128)S(1)}, u32[]{:S(2)}, u32[]{:S(2)}) async-start(f32[8,32,256]{2,1,0:T(8,128)} %bitcast.6), calls=%async_computation.1 | async-start | bytes 524288 | tf_op jit(solution)/shard_map/head/all_to_all | solution.py:22
  49.2 6.5 %all-to-all-done.1 = f32[8,32,256]{2,1,0:T(8,128)S(1)} async-done(((f32[8,32,256]{2,1,0:T(8,128)}), f32[8,32,256]{2,1,0:T(8,128)S(1)}, u32[]{:S(2)}, u32[]{:S(2)}) %all-to-all-start.1) | async-done | bytes 262176 | tf_op jit(solution)/shard_map/head/all_to_all | solution.py:22
  55.8 11.2 %all_to_all.35 = bf16[8,32,256]{2,1,0:T(8,128)(2,1)S(1)} all-to-all(bf16[8,32,256]{2,1,0:T(8,128)(2,1)S(1)} %broadcast_in_dim.36), channel_id=1, replica_groups=mesh['y'=4,'z'=8,'x'=4,'c'=2] {'z'}, dimensions={0} | all-to-all | bytes 262144 | tf_op jit(solution)/shard_map/gather_heads/all_to_all | solution.py:22
  67.0 35.1 %all-gather.2.cloned.1.call-done.refs_0_ = bf16[256,4096]{1,0:T(8,128)(2,1)} async-done(((bf16[8,4096]{1,0:T(8,128)(2,1)}), bf16[256,4096]{1,0:T(8,128)(2,1)}) %all-gather.2.cloned.1.call-update) | async-done | bytes 2097168 | tf_op jit(solution)/shard_map/gather_targets/all_gather | solution.py:352
  102.1 4.6 %collective-permute-start.12 = (bf16[256,4096]{1,0:T(8,128)(2,1)}, bf16[256,4096]{1,0:T(8,128)(2,1)S(1)}, u32[]{:S(2)}, u32[]{:S(2)}) collective-permute-start(bf16[256,4096]{1,0:T(8,128)(2,1)} %teacher.2.own_ref), channel_id=1, source_target_pairs={{0,1},{1,0},{2,3},{3,2},{4,5},{5,4},{6,7},{7,6},{8,9},{9,8},{10,11... | collective-permute-start | bytes 6291464 | tf_op jit(solution)/shard_map/teacher/ppermute | solution.py:30
  120.6 2.7 %collective-permute-start.7 = (bf16[16,8192]{1,0:T(8,128)(2,1)S(1)}, bf16[16,8192]{1,0:T(8,128)(2,1)S(1)}, u32[]{:S(2)}, u32[]{:S(2)}) collective-permute-start(bf16[16,8192]{1,0:T(8,128)(2,1)S(1)} %get-tuple-element.21.refs_0_), channel_id=1, source_target_pairs={{0,4},{2,6},{4,0},{6,2},{1,5},{3,7},{5,1},{7,3},{8,12},{10,14},{12... | collective-permute-start | bytes 786440 | tf_op jit(solution)/shard_map/gather_heads/ppermute | solution.py:30
  125.7 3.1 %collective-permute-start.8 = (bf16[16,8192]{1,0:T(8,128)(2,1)S(1)}, bf16[16,8192]{1,0:T(8,128)(2,1)S(1)}, u32[]{:S(2)}, u32[]{:S(2)}) collective-permute-start(bf16[16,8192]{1,0:T(8,128)(2,1)S(1)} %get-tuple-element.21.refs_0_), channel_id=1, source_target_pairs={{0,6},{2,4},{4,2},{6,0},{1,7},{3,5},{5,3},{7,1},{8,14},{10,12},{12... | collective-permute-start | bytes 786440 | tf_op jit(solution)/shard_map/gather_heads/ppermute | solution.py:30
  128.8 3.4 %copy-done.2 = bf16[8192,512]{1,0:T(8,128)(2,1)S(1)} copy-done((bf16[8192,512]{1,0:T(8,128)(2,1)S(1)}, bf16[8192,512]{1,0:T(8,128)(2,1)}, u32[]{:S(2)}) %copy-start.2) | copy-done | bytes 8388632
  133.7 2.9 %teacher.3.refs_8_.teacher_ref = f32[256,512]{1,0:T(8,128)S(1)} custom-call(s32[18]{0:T(128)S(1)} %pad_add_fusion.place, bf16[256,4096]{1,0:T(8,128)(2,1)S(1)} %copy-done.5, bf16[256,4096]{1,0:T(8,128)(2,1)S(1)} %collective-permute-done.12.other_ref, bf16[8192,512]{1,0:T(8,128)(2,1)S(1)} %copy-done.2), custom_call_target="tpu_custom_call" | custom-call | flops 2147483648 | bytes 12582912 | tf_op jit(solution)/shard_map/teacher/pallas_call | solution.py:61
  137.4 2.5 %collective-permute-start.13 = (bf16[16,8192]{1,0:T(8,128)(2,1)S(1)}, bf16[16,8192]{1,0:T(8,128)(2,1)S(1)}, u32[]{:S(2)}, u32[]{:S(2)}) collective-permute-start(bf16[16,8192]{1,0:T(8,128)(2,1)S(1)} %get-tuple-element.24.refs_0_), channel_id=1, source_target_pairs={{0,1},{1,0},{2,3},{3,2},{4,5},{5,4},{6,7},{7,6},{8,9},{9,8},{10,11... | collective-permute-start | bytes 786440 | tf_op jit(solution)/shard_map/gather_heads/ppermute | solution.py:30
  145.7 8.2 %all_to_all.36.parts_ref = f32[8,8,128]{2,1,0:T(8,128)S(1)} all-to-all(f32[8,8,128]{2,1,0:T(8,128)S(1)} %get-tuple-element.33), channel_id=1, replica_groups=mesh['y'=4,'z'=8,'x'=4,'c'=2] {'x','c'}, dimensions={0} | all-to-all | bytes 65536 | tf_op jit(solution)/shard_map/totals/all_to_all | solution.py:22
  154.0 14.8 %all_to_all.37.parts_ref = f32[32,8,128]{2,1,0:T(8,128)S(1)} all-to-all(f32[32,8,128]{2,1,0:T(8,128)S(1)} %totals.2), channel_id=1, replica_groups=mesh['y'=4,'z'=8,'x'=4,'c'=2] {'y','z'}, dimensions={0} | all-to-all | bytes 262144 | tf_op jit(solution)/shard_map/totals/all_to_all | solution.py:22
  170.9 2.4 %collective-permute-start.21 = (bf16[128,8192]{1,0:T(8,128)(2,1)S(1)}, bf16[128,8192]{1,0:T(8,128)(2,1)S(1)}, u32[]{:S(2)}, u32[]{:S(2)}) collective-permute-start(bf16[128,8192]{1,0:T(8,128)(2,1)S(1)} %grad.3), channel_id=1, source_target_pairs={{0,1},{1,0},{2,3},{3,2},{4,5},{5,4},{6,7},{7,6},{8,9},{9,8},{10,11... | collective-permute-start | bytes 6291464 | tf_op jit(solution)/shard_map/reduce_grad/ppermute | solution.py:30
  186.2 5.4 %collective-permute-done.23 = bf16[16,8192]{1,0:T(8,128)(2,1)S(1)} collective-permute-done((bf16[16,8192]{1,0:T(8,128)(2,1)S(1)}, bf16[16,8192]{1,0:T(8,128)(2,1)S(1)}, u32[]{:S(2)}, u32[]{:S(2)}) %collective-permute-start.23) | collective-permute-done | bytes 262176 | tf_op jit(solution)/shard_map/reduce_grad/ppermute | solution.py:30
  201.3 2.5 %collective-permute-start.33 = (bf16[16,2048]{1,0:T(8,128)(2,1)S(1)}, bf16[16,2048]{1,0:T(8,128)(2,1)S(1)}, u32[]{:S(2)}, u32[]{:S(2)}) collective-permute-start(bf16[16,2048]{1,0:T(8,128)(2,1)S(1)} %get-tuple-element.49), channel_id=1, source_target_pairs={{0,6},{2,4},{4,2},{6,0},{1,7},{3,5},{5,3},{7,1},{8,14},{10,12},{12... | collective-permute-start | bytes 196616 | tf_op jit(solution)/shard_map/reduce_grad/ppermute | solution.py:30
  205.9 10.3 %all_to_all.38 = bf16[8,32,256]{2,1,0:T(8,128)(2,1)S(1)} all-to-all(bf16[8,32,256]{2,1,0:T(8,128)(2,1)S(1)} %bitcast.45), channel_id=1, replica_groups=mesh['y'=4,'z'=8,'x'=4,'c'=2] {'z'}, dimensions={0} | all-to-all | bytes 262144 | tf_op jit(solution)/shard_map/reduce_grad/all_to_all | solution.py:22
  217.1 9.9 %all-to-all-start.6 = ((bf16[8,48,256]{2,1,0:T(8,128)(2,1)}), bf16[8,48,256]{2,1,0:T(8,128)(2,1)S(1)}, u32[]{:S(2)}, u32[]{:S(2)}) async-start(bf16[8,48,256]{2,1,0:T(8,128)(2,1)} %broadcast_in_dim.38), calls=%async_computation.6 | async-start | bytes 393216 | tf_op jit(solution)/shard_map/finish/all_to_all | solution.py:22
  228.3 4.6 %all-to-all-done.6 = bf16[8,48,256]{2,1,0:T(8,128)(2,1)S(1)} async-done(((bf16[8,48,256]{2,1,0:T(8,128)(2,1)}), bf16[8,48,256]{2,1,0:T(8,128)(2,1)S(1)}, u32[]{:S(2)}, u32[]{:S(2)}) %all-to-all-start.6) | async-done | bytes 196640 | tf_op jit(solution)/shard_map/finish/all_to_all | solution.py:22
  (134 shorter events, 59.6 us)
Async XLA Ops:
  10.4 28.4 %all-to-all-start = ((bf16[32,8,1280]{2,1,0:T(8,128)(2,1)}), bf16[32,8,1280]{2,1,0:T(8,128)(2,1)S(1)}, u32[]{:S(2)}, u32[]{:S(2)}) async-start(bf16[32,8,1280]{2,1,0:T(8,128)(2,1)} %pad_maximum_fusion), calls=%async_computation | async-start | bytes 1310720 | tf_op jit(solution)/shard_map/gather_inputs/all_to_all | solution.py:22
  22.4 79.7 %all-gather.2.cloned.1.call-start = ((), (), s32[]{:S(2)}) async-start(), calls=%async_computation.7 | async-start | bytes 2162688 | tf_op jit(solution)/shard_map/gather_targets/all_gather | solution.py:352
  39.9 15.8 %all-to-all-start.1 = ((f32[8,32,256]{2,1,0:T(8,128)}), f32[8,32,256]{2,1,0:T(8,128)S(1)}, u32[]{:S(2)}, u32[]{:S(2)}) async-start(f32[8,32,256]{2,1,0:T(8,128)} %bitcast.6), calls=%async_computation.1 | async-start | bytes 524288 | tf_op jit(solution)/shard_map/head/all_to_all | solution.py:22
  102.1 26.6 %collective-permute-start.12 = (bf16[256,4096]{1,0:T(8,128)(2,1)}, bf16[256,4096]{1,0:T(8,128)(2,1)S(1)}, u32[]{:S(2)}, u32[]{:S(2)}) collective-permute-start(bf16[256,4096]{1,0:T(8,128)(2,1)} %teacher.2.own_ref), channel_id=1, source_target_pairs={{0,1},{1,0},{2,3},{3,2},{4,5},{5,4},{6,7},{7,6},{8,9},{9,8},{10,11... | collective-permute-start | bytes 6291464 | tf_op jit(solution)/shard_map/teacher/ppermute | solution.py:30
  106.7 5.1 %collective-permute-start = (bf16[16,2048]{1,0:T(8,128)(2,1)S(1)}, bf16[16,2048]{1,0:T(8,128)(2,1)S(1)}, u32[]{:S(2)}, u32[]{:S(2)}) collective-permute-start(bf16[16,2048]{1,0:T(8,128)(2,1)S(1)} %bitcast.33), channel_id=1, source_target_pairs={{0,64},{64,0},{128,192},{192,128},{1,65},{65,1},{129,193},{193,129... | collective-permute-start | bytes 196616 | tf_op jit(solution)/shard_map/gather_heads/ppermute | solution.py:30
  106.8 7.4 %collective-permute-start.1 = (bf16[16,2048]{1,0:T(8,128)(2,1)S(1)}, bf16[16,2048]{1,0:T(8,128)(2,1)S(1)}, u32[]{:S(2)}, u32[]{:S(2)}) collective-permute-start(bf16[16,2048]{1,0:T(8,128)(2,1)S(1)} %bitcast.34), channel_id=1, source_target_pairs={{0,128},{64,192},{128,0},{192,64},{1,129},{65,193},{129,1},{193,65... | collective-permute-start | bytes 196616 | tf_op jit(solution)/shard_map/gather_heads/ppermute | solution.py:30
  108.9 6.1 %collective-permute-start.2 = (bf16[16,2048]{1,0:T(8,128)(2,1)S(1)}, bf16[16,2048]{1,0:T(8,128)(2,1)S(1)}, u32[]{:S(2)}, u32[]{:S(2)}) collective-permute-start(bf16[16,2048]{1,0:T(8,128)(2,1)S(1)} %bitcast.35), channel_id=1, source_target_pairs={{0,192},{64,128},{128,64},{192,0},{1,193},{65,129},{129,65},{193,1... | collective-permute-start | bytes 196616 | tf_op jit(solution)/shard_map/gather_heads/ppermute | solution.py:30
  118.8 6.9 %collective-permute-start.10 = (bf16[64,2048]{1,0:T(8,128)(2,1)S(1)}, bf16[64,2048]{1,0:T(8,128)(2,1)S(1)}, u32[]{:S(2)}, u32[]{:S(2)}) collective-permute-start(bf16[64,2048]{1,0:T(8,128)(2,1)S(1)} %get-tuple-element.22.refs_4_), channel_id=1, source_target_pairs={{0,128},{64,192},{128,0},{192,64},{1,129},{65,193},{129,1},{193,65... | collective-permute-start | bytes 786440 | tf_op jit(solution)/shard_map/gather_heads/ppermute | solution.py:30
  119.0 17.6 %collective-permute-start.11 = (bf16[64,2048]{1,0:T(8,128)(2,1)S(1)}, bf16[64,2048]{1,0:T(8,128)(2,1)S(1)}, u32[]{:S(2)}, u32[]{:S(2)}) collective-permute-start(bf16[64,2048]{1,0:T(8,128)(2,1)S(1)} %get-tuple-element.22.refs_4_), channel_id=1, source_target_pairs={{0,192},{64,128},{128,64},{192,0},{1,193},{65,129},{129,65},{193,1... | collective-permute-start | bytes 786440 | tf_op jit(solution)/shard_map/gather_heads/ppermute | solution.py:30
  120.1 16.6 %collective-permute-start.6 = (bf16[16,8192]{1,0:T(8,128)(2,1)S(1)}, bf16[16,8192]{1,0:T(8,128)(2,1)S(1)}, u32[]{:S(2)}, u32[]{:S(2)}) collective-permute-start(bf16[16,8192]{1,0:T(8,128)(2,1)S(1)} %get-tuple-element.21.refs_0_), channel_id=1, source_target_pairs={{0,2},{2,0},{4,6},{6,4},{1,3},{3,1},{5,7},{7,5},{8,10},{10,8},{12,... | collective-permute-start | bytes 786440 | tf_op jit(solution)/shard_map/gather_heads/ppermute | solution.py:30
  120.6 16.1 %collective-permute-start.7 = (bf16[16,8192]{1,0:T(8,128)(2,1)S(1)}, bf16[16,8192]{1,0:T(8,128)(2,1)S(1)}, u32[]{:S(2)}, u32[]{:S(2)}) collective-permute-start(bf16[16,8192]{1,0:T(8,128)(2,1)S(1)} %get-tuple-element.21.refs_0_), channel_id=1, source_target_pairs={{0,4},{2,6},{4,0},{6,2},{1,5},{3,7},{5,1},{7,3},{8,12},{10,14},{12... | collective-permute-start | bytes 786440 | tf_op jit(solution)/shard_map/gather_heads/ppermute | solution.py:30
  125.7 11.7 %collective-permute-start.8 = (bf16[16,8192]{1,0:T(8,128)(2,1)S(1)}, bf16[16,8192]{1,0:T(8,128)(2,1)S(1)}, u32[]{:S(2)}, u32[]{:S(2)}) collective-permute-start(bf16[16,8192]{1,0:T(8,128)(2,1)S(1)} %get-tuple-element.21.refs_0_), channel_id=1, source_target_pairs={{0,6},{2,4},{4,2},{6,0},{1,7},{3,5},{5,3},{7,1},{8,14},{10,12},{12... | collective-permute-start | bytes 786440 | tf_op jit(solution)/shard_map/gather_heads/ppermute | solution.py:30
  128.7 8.6 %collective-permute-start.9 = (bf16[64,2048]{1,0:T(8,128)(2,1)S(1)}, bf16[64,2048]{1,0:T(8,128)(2,1)S(1)}, u32[]{:S(2)}, u32[]{:S(2)}) collective-permute-start(bf16[64,2048]{1,0:T(8,128)(2,1)S(1)} %get-tuple-element.22.refs_4_), channel_id=1, source_target_pairs={{0,64},{64,0},{128,192},{192,128},{1,65},{65,1},{129,193},{193,129... | collective-permute-start | bytes 786440 | tf_op jit(solution)/shard_map/gather_heads/ppermute | solution.py:30
  170.9 6.2 %collective-permute-start.21 = (bf16[128,8192]{1,0:T(8,128)(2,1)S(1)}, bf16[128,8192]{1,0:T(8,128)(2,1)S(1)}, u32[]{:S(2)}, u32[]{:S(2)}) collective-permute-start(bf16[128,8192]{1,0:T(8,128)(2,1)S(1)} %grad.3), channel_id=1, source_target_pairs={{0,1},{1,0},{2,3},{3,2},{4,5},{5,4},{6,7},{7,6},{8,9},{9,8},{10,11... | collective-permute-start | bytes 6291464 | tf_op jit(solution)/shard_map/reduce_grad/ppermute | solution.py:30
  177.7 7.6 %collective-permute-start.22 = (bf16[16,8192]{1,0:T(8,128)(2,1)S(1)}, bf16[16,8192]{1,0:T(8,128)(2,1)S(1)}, u32[]{:S(2)}, u32[]{:S(2)}) collective-permute-start(bf16[16,8192]{1,0:T(8,128)(2,1)S(1)} %get-tuple-element.39), channel_id=1, source_target_pairs={{0,2},{2,0},{4,6},{6,4},{1,3},{3,1},{5,7},{7,5},{8,10},{10,8},{12,... | collective-permute-start | bytes 786440 | tf_op jit(solution)/shard_map/reduce_grad/ppermute | solution.py:30
  178.1 13.5 %collective-permute-start.23 = (bf16[16,8192]{1,0:T(8,128)(2,1)S(1)}, bf16[16,8192]{1,0:T(8,128)(2,1)S(1)}, u32[]{:S(2)}, u32[]{:S(2)}) collective-permute-start(bf16[16,8192]{1,0:T(8,128)(2,1)S(1)} %get-tuple-element.41), channel_id=1, source_target_pairs={{0,4},{2,6},{4,0},{6,2},{1,5},{3,7},{5,1},{7,3},{8,12},{10,14},{12... | collective-permute-start | bytes 786440 | tf_op jit(solution)/shard_map/reduce_grad/ppermute | solution.py:30
  179.8 13.7 %collective-permute-start.24 = (bf16[16,8192]{1,0:T(8,128)(2,1)S(1)}, bf16[16,8192]{1,0:T(8,128)(2,1)S(1)}, u32[]{:S(2)}, u32[]{:S(2)}) collective-permute-start(bf16[16,8192]{1,0:T(8,128)(2,1)S(1)} %get-tuple-element.40), channel_id=1, source_target_pairs={{0,6},{2,4},{4,2},{6,0},{1,7},{3,5},{5,3},{7,1},{8,14},{10,12},{12... | collective-permute-start | bytes 786440 | tf_op jit(solution)/shard_map/reduce_grad/ppermute | solution.py:30
  181.7 14.2 %collective-permute-start.28 = (bf16[64,2048]{1,0:T(8,128)(2,1)S(1)}, bf16[64,2048]{1,0:T(8,128)(2,1)S(1)}, u32[]{:S(2)}, u32[]{:S(2)}) collective-permute-start(bf16[64,2048]{1,0:T(8,128)(2,1)S(1)} %get-tuple-element.42), channel_id=1, source_target_pairs={{0,64},{64,0},{128,192},{192,128},{1,65},{65,1},{129,193},{193,129... | collective-permute-start | bytes 786440 | tf_op jit(solution)/shard_map/reduce_grad/ppermute | solution.py:30
  182.1 15.5 %collective-permute-start.29 = (bf16[64,2048]{1,0:T(8,128)(2,1)S(1)}, bf16[64,2048]{1,0:T(8,128)(2,1)S(1)}, u32[]{:S(2)}, u32[]{:S(2)}) collective-permute-start(bf16[64,2048]{1,0:T(8,128)(2,1)S(1)} %get-tuple-element.44), channel_id=1, source_target_pairs={{0,128},{64,192},{128,0},{192,64},{1,129},{65,193},{129,1},{193,65... | collective-permute-start | bytes 786440 | tf_op jit(solution)/shard_map/reduce_grad/ppermute | solution.py:30
  185.3 14.4 %collective-permute-start.30 = (bf16[64,2048]{1,0:T(8,128)(2,1)S(1)}, bf16[64,2048]{1,0:T(8,128)(2,1)S(1)}, u32[]{:S(2)}, u32[]{:S(2)}) collective-permute-start(bf16[64,2048]{1,0:T(8,128)(2,1)S(1)} %get-tuple-element.43), channel_id=1, source_target_pairs={{0,192},{64,128},{128,64},{192,0},{1,193},{65,129},{129,65},{193,1... | collective-permute-start | bytes 786440 | tf_op jit(solution)/shard_map/reduce_grad/ppermute | solution.py:30
  193.7 7.6 %collective-permute-start.25 = (bf16[16,2048]{1,0:T(8,128)(2,1)S(1)}, bf16[16,2048]{1,0:T(8,128)(2,1)S(1)}, u32[]{:S(2)}, u32[]{:S(2)}) collective-permute-start(bf16[16,2048]{1,0:T(8,128)(2,1)S(1)} %get-tuple-element.45), channel_id=1, source_target_pairs={{0,64},{64,0},{128,192},{192,128},{1,65},{65,1},{129,193},{193,129... | collective-permute-start | bytes 196616 | tf_op jit(solution)/shard_map/reduce_grad/ppermute | solution.py:30
  194.1 9.7 %collective-permute-start.26 = (bf16[16,2048]{1,0:T(8,128)(2,1)S(1)}, bf16[16,2048]{1,0:T(8,128)(2,1)S(1)}, u32[]{:S(2)}, u32[]{:S(2)}) collective-permute-start(bf16[16,2048]{1,0:T(8,128)(2,1)S(1)} %get-tuple-element.47), channel_id=1, source_target_pairs={{0,128},{64,192},{128,0},{192,64},{1,129},{65,193},{129,1},{193,65... | collective-permute-start | bytes 196616 | tf_op jit(solution)/shard_map/reduce_grad/ppermute | solution.py:30
  195.9 8.0 %collective-permute-start.27 = (bf16[16,2048]{1,0:T(8,128)(2,1)S(1)}, bf16[16,2048]{1,0:T(8,128)(2,1)S(1)}, u32[]{:S(2)}, u32[]{:S(2)}) collective-permute-start(bf16[16,2048]{1,0:T(8,128)(2,1)S(1)} %get-tuple-element.46), channel_id=1, source_target_pairs={{0,192},{64,128},{128,64},{192,0},{1,193},{65,129},{129,65},{193,1... | collective-permute-start | bytes 196616 | tf_op jit(solution)/shard_map/reduce_grad/ppermute | solution.py:30
  217.1 15.8 %all-to-all-start.6 = ((bf16[8,48,256]{2,1,0:T(8,128)(2,1)}), bf16[8,48,256]{2,1,0:T(8,128)(2,1)S(1)}, u32[]{:S(2)}, u32[]{:S(2)}) async-start(bf16[8,48,256]{2,1,0:T(8,128)(2,1)} %broadcast_in_dim.38), calls=%async_computation.6 | async-start | bytes 393216 | tf_op jit(solution)/shard_map/finish/all_to_all | solution.py:22
  (25 other events, 152.4 us)
Sparse Core Ops, SparseCore 0:
  25.9 76.1 all-gather.1

commit v7 on v6

--- a/solution.py
+++ b/solution.py
@@ -14,7 +14,7 @@
 CHUNKS = 4
 PADDED = 512
 LIMIT = 24 * 1024 * 1024
-HEAD_COST = 60_000_000_000
+HEAD_COST = 90_000_000_000
 SIZES = {"y": 4, "z": 8, "x": 4, "c": 2}
 
 
@@ -75,8 +75,7 @@
     return jax.ShapeDtypeStruct(sizes, dtype)
 
 
-def prepare_kernel(place, vocab_ref, across_ref, down_ref, done_ref, wide):
-    done_ref[...] = jnp.zeros(done_ref.shape, F32)
+def prepare_kernel(place, vocab_ref, awaited_ref, across_ref, down_ref, wide):
     entries, depth = vocab_ref.shape
     width = depth // CHUNKS
     wide[...] = jnp.zeros(wide.shape, F32)
@@ -88,41 +87,47 @@
         down_ref[at * width : (at + 1) * width] = block.T.astype(BF16)
 
 
-def prepare(place, vocab_head):
+def prepare(place, vocab_head, awaited):
     depth = vocab_head.shape[1]
-    return local_call(
+    vmem = pl.BlockSpec(memory_space=pltpu.VMEM)
+    return pl.pallas_call(
         prepare_kernel,
-        [shape(PADDED, depth, dtype=BF16), shape(depth, PADDED, dtype=BF16), shape(8, 128)],
-        cost(0, 6 * PADDED * depth),
-        [pltpu.VMEM((PADDED, depth // CHUNKS), F32)],
-    )(place, vocab_head)
-
-
-def teacher_kernel(place, own_ref, other_ref, down_ref, out_ref, total):
+        in_specs=[
+            pl.BlockSpec(memory_space=pltpu.SMEM),
+            vmem,
+            pl.BlockSpec(memory_space=pl.ANY),
+        ],
+        out_specs=[vmem, vmem],
+        out_shape=[shape(PADDED, depth, dtype=BF16), shape(depth, PADDED, dtype=BF16)],
+        scratch_shapes=[pltpu.VMEM((PADDED, depth // CHUNKS), F32)],
+        compiler_params=pltpu.CompilerParams(vmem_limit_bytes=LIMIT),
+        cost_estimate=cost(0, 6 * PADDED * depth),
+    )(place, vocab_head, awaited)
+
+
+def teacher_kernel(place, target_ref, down_ref, out_ref, total):
     width = down_ref.shape[0] // CHUNKS
-    for half, target_ref in enumerate((own_ref, other_ref)):
-        for at in range(2):
-            group = (place[17] ^ half) * 2 + at
-            start = pl.multiple_of((group ^ place[16]) * width, width)
-            product = jnp.dot(
-                target_ref[:, at * width : (at + 1) * width],
-                down_ref[pl.ds(start, width)],
-                preferred_element_type=F32,
-            )
-            total[...] = product if half + at == 0 else total[...] + product
+    for at in range(CHUNKS):
+        start = pl.multiple_of((place[16] ^ at) * width, width)
+        product = jnp.dot(
+            target_ref[:, pl.ds(start, width)],
+            down_ref[at * width : (at + 1) * width],
+            preferred_element_type=F32,
+        )
+        total[...] = product if at == 0 else total[...] + product
     for at in range(16):
-        start = pl.multiple_of(place[at] * 16, 16)
+        start = pl.multiple_of(place[17 + at] * 16, 16)
         out_ref[at * 16 : (at + 1) * 16] = total[pl.ds(start, 16)]
 
 
-def teacher_logits(place, own_half, other_half, down):
-    count, depth = own_half.shape[0], down.shape[0]
+def teacher_logits(place, target_all, down):
+    count, depth = target_all.shape
     return local_call(
         teacher_kernel,
         shape(count, PADDED),
         cost(2 * count * PADDED * depth, 2 * (count + PADDED) * depth),
         [pltpu.VMEM((count, PADDED), F32)],
-    )(place, own_half, other_half, down)
+    )(place, target_all, down)
 
 
 def student_part(entries, core, firsts, seconds, teacher_ref, down_ref, out_ref):
@@ -189,7 +194,7 @@
     rows = teacher.shape[0] // 2
     return local_call(
         functools.partial(other_student_kernel, entries),
-        [shape(rows, PADDED), shape(8, 8, rows)],
+        [shape(rows, PADDED), shape(32, 8, rows)],
         cost(2 * rows * down.size, 2 * down.size, 2 * rows * PADDED),
         [pltpu.VMEM((2 * rows, 128), F32)],
     )(place, *blocks, teacher, down, table)
@@ -293,18 +298,37 @@
     )(*firsts, *seconds)
 
 
-def head_kernel(rows_ref, weight_ref, done_ref, out_ref):
+def stack_kernel(*refs):
+    blocks, (out_ref, ready_ref) = refs[:4], refs[4:]
+    rows = blocks[0].shape[0]
+    for at, block in enumerate(blocks):
+        out_ref[at * rows : (at + 1) * rows] = block[...]
+    ready_ref[...] = jnp.zeros(ready_ref.shape, F32)
+
+
+def stacked(blocks):
+    rows, across = blocks[0].shape
+    return local_call(
+        stack_kernel,
+        [shape(4 * rows, across, dtype=BF16), shape(8, 128)],
+        cost(0, 16 * rows * across),
+        limit=4 * 1024 * 1024,
+        scalars=False,
+    )(*blocks)
+
+
+def head_kernel(rows_ref, weight_ref, ready_ref, out_ref):
     out_ref[...] = jnp.dot(rows_ref[...], weight_ref[...], preferred_element_type=F32)
 
 
-def head_partial(rows, weight, done):
+def head_partial(rows, weight, ready):
     return pl.pallas_call(
         head_kernel,
         in_specs=[pl.BlockSpec(memory_space=pltpu.VMEM)] * 3,
         out_shape=jax.ShapeDtypeStruct((rows.shape[0], weight.shape[1]), F32),
         compiler_params=pltpu.CompilerParams(vmem_limit_bytes=LIMIT),
         cost_estimate=cost(HEAD_COST, 2 * (rows.size + weight.size)),
-    )(rows, weight, done)
+    )(rows, weight, ready)
 
 
 def gather_lines(heads):
@@ -345,38 +369,48 @@
     voc_index = at_x * 2 + at_c
     taken = jnp.concatenate([positions, positions + offsets])
     taken = jnp.take(log_hidden, taken, axis=0, mode="clip")
-    inputs, targets = taken[:own], taken[own:]
-    with jax.named_scope("gather_targets"):
-        half = targets.shape[1] // 2
-        target_half = lax.dynamic_slice_in_dim(targets, at_c * half, half, 1)
-        target_half = lax.all_gather(target_half, REP, axis=0, tiled=True)
+    inputs = taken[:own]
+    with jax.named_scope("gather_z"):
+        blocks = lax.dynamic_slice_in_dim(
+            taken.reshape(2, own, -1), voc_index * in_width, in_width, 2
+        )
+        input_cols = inputs.reshape(own, 4, 8, out_width).transpose(2, 0, 1, 3)
+        sent = jnp.concatenate(
+            [
+                jnp.broadcast_to(blocks[0], (8, own, in_width)),
+                jnp.broadcast_to(blocks[1], (8, own, in_width)),
+                input_cols.reshape(8, own, -1),
+            ],
+            axis=2,
+        )
+        lines = exchange(sent, "z").reshape(8 * own, -1)
+        input_lines, target_lines = lines[:, :in_width], lines[:, in_width : 2 * in_width]
+        input_cols = lines[:, 2 * in_width :].reshape(-1, 4, out_width).transpose(1, 0, 2)
     with jax.named_scope("gather_inputs"):
-        input_block = lax.dynamic_slice_in_dim(inputs, voc_index * in_width, in_width, 1)
-        input_cols = inputs.reshape(own, reps, out_width).transpose(1, 0, 2)
         sent = jnp.concatenate(
-            [jnp.broadcast_to(input_block[None], (reps, own, in_width)), input_cols], axis=2
-        )
-        got = exchange(sent, REP)
+            [jnp.broadcast_to(input_lines, (4, *input_lines.shape)), input_cols], axis=2
+        )
+        got = exchange(sent, "y")
         input_rows = got[:, :, :in_width].reshape(count, in_width)
         residual = got[:, :, in_width:].reshape(count, out_width)
         residual = lax.dynamic_slice_in_dim(residual, voc_index * rows, rows, 0)
+    with jax.named_scope("gather_targets"):
+        target_rows, ready = stacked(from_peers(target_lines, "y"))
+        target_all = lax.all_gather(target_rows, VOC, axis=1, tiled=True)
     steps = jnp.arange(16)
     order = ((at_x ^ (steps % 4)) * 2 + (at_c ^ (steps // 8))) * 2 + (steps // 4) % 2
-    place = jnp.concatenate([order, at_y[None], at_c[None]]).astype(jnp.int32)
-    with jax.named_scope("prepare"):
-        across, down, done = prepare(place, vocab_head)
+    target_order = (order // 4 ^ at_y) * 4 + order % 4
+    place = jnp.concatenate([order, at_y[None], target_order]).astype(jnp.int32)
     with jax.named_scope("head"):
-        partial_pre = head_partial(input_rows, head_weight, done)
+        partial_pre = head_partial(input_rows, head_weight, ready)
         parts = exchange(partial_pre.reshape(vocs, rows, out_width), VOC)
         preact = jnp.sum(parts, axis=0) + head_bias
         heads = (residual.astype(F32) + jax.nn.silu(preact)).astype(BF16)
     with jax.named_scope("gather_heads"):
         lines = gather_lines(heads)
     with jax.named_scope("teacher"):
-        target_half = pltpu.with_memory_space_constraint(target_half, pltpu.HBM)
-        (target_half,) = settled([target_half], lines)
-        other_half = swap(target_half, "c", 1)
-        teacher = teacher_logits(place, target_half, other_half, down)
+        across, down = prepare(place, vocab_head, target_all)
+        teacher = teacher_logits(place, target_all, down)
     with jax.named_scope("gather_heads"):
         own_blocks, other_blocks = gather_heads(lines, teacher)
     with jax.named_scope("student"):
@@ -384,8 +418,8 @@
         own_logits, table = own_student(entries, own_blocks, teacher, down)
         other_logits, sums = other_student(entries, place, other_blocks, teacher, down, table)
     with jax.named_scope("totals"):
-        sums = totalled(total_kernel, exchange(sums, VOC), reps, 8, count // 2)
-        logs = totalled(log_kernel, exchange(sums, REP), 8, count)
+        sums = totalled(total_kernel, exchange(sums, ("y", "x", "c")), 8, 8, count // 2)
+        logs = totalled(log_kernel, exchange(sums, "z"), 8, count)
         loss = jnp.sum(logs[2]) / count
     with jax.named_scope("grad"):
         other_rows = grad_rows(1, place, teacher, other_logits, logs, across)

time: 244 us -> 220 us (0.902)
  waiting for transfers between devices: 70.2 us -> 39.8 us
  blocking collectives: 44.5 us -> 64.7 us
  local copies, waits for them, and re-layouts: 17.5 us -> 7.51 us
  starting transfers between devices: 73.8 us -> 68.9 us
    all_gather x1, waiting for transfers between devices: 35.1 us -> 0.01 us  [shards(): target_all = lax.all_gather(target_rows, VOC, axis=1, tiled=True)]
    all_to_all x4 -> x5, blocking collectives: 44.5 us -> 64.7 us  [exchange(): return lax.all_to_all(blocks, axis, split_axis=0, concat_axis=0, tiled=True)]
    all_to_all x3, starting transfers between devices: 31.3 us -> 21.6 us  [exchange(): return lax.all_to_all(blocks, axis, split_axis=0, concat_axis=0, tiled=True)]
    unnamed x23 -> x11, local copies, waits for them, and re-layouts: 14.9 us -> 5.56 us
    ppermute x34 -> x36, waiting for transfers between devices: 21.5 us -> 27.9 us  [swap(): lax.ppermute(block, axis, [(i, i ^ step) for i in range(SIZES[axis])])]
    ppermute x34 -> x36, starting transfers between devices: 42.5 us -> 47.3 us  [swap(): lax.ppermute(block, axis, [(i, i ^ step) for i in range(SIZES[axis])])]
    pallas_call x0 -> x1, Pallas kernels: none -> 3.29 us  [prepare(): pl.pallas_call(prepare_kernel, in_specs=[pl.BlockSpec(memory_space=pltpu....]
  transfers between devices with their start and end apart: 38 -> 40, of which waited for: 17 -> 16; matrix products, arithmetic and copies ran while one was open for 1% -> 1% of each run, Pallas kernels for 4% -> 6%
where the time goes in v7:
time: 220 us
  starting transfers between devices  68.9 us (31%)
  blocking collectives  64.7 us (29%)
  waiting for transfers between devices  39.8 us (18%)
  Pallas kernels  16.7 us (8%)
  between operations  16.3 us (7%)
  local copies, waits for them, and re-layouts  7.51 us (3%)
  other arithmetic  4.63 us (2%)
    all_to_all x5, blocking collectives, exchange(): return lax.all_to_all(blocks, axis, split_axis=0, concat_axis=0, tiled=True)  64.7 us
    ppermute x36, starting transfers between devices, swap(): lax.ppermute(block, axis, [(i, i ^ step) for i in range(SIZES[axis])])  47.3 us
    ppermute x36, waiting for transfers between devices, swap(): lax.ppermute(block, axis, [(i, i ^ step) for i in range(SIZES[axis])])  27.9 us
    all_to_all x3, starting transfers between devices, exchange(): return lax.all_to_all(blocks, axis, split_axis=0, concat_axis=0, tiled=True)  21.6 us
    pallas_call x8, Pallas kernels, call(): pl.pallas_call(kernel, in_specs=specs, out_specs=jax.tree.map(lambda _: p...  12.3 us
    all_to_all x3, waiting for transfers between devices, exchange(): return lax.all_to_all(blocks, axis, split_axis=0, concat_axis=0, tiled=True)  11.8 us
    unnamed x11, local copies, waits for them, and re-layouts  5.56 us
  transfers between devices with their start and end apart: 40, of which 16 were waited for; matrix products, arithmetic and copies ran while one was open for 1% of the time, Pallas kernels for 6%

profile of v7, /device:TPU:1, one launch (start us, length us, event | category | flops | bytes accessed | tf_op | source)
XLA Modules:
  0.0 219.8 jit_solution(3835838530412723074)
XLA Ops:
  9.5 22.3 %all_to_all.40 = bf16[8,8,3072]{2,1,0:T(8,128)(2,1)S(1)} all-to-all(bf16[8,8,3072]{2,1,0:T(8,128)(2,1)S(1)} %pad_maximum_fusion.1), channel_id=1, replica_groups=mesh['y'=4,'z'=8,'x'=4,'c'=2] {'z'}, dimensions={0} | all-to-all | bytes 786432 | tf_op jit(solution)/shard_map/gather_z/all_to_all | solution.py:22
  32.9 4.2 %all-to-all-start.1 = ((bf16[4,64,1280]{2,1,0:T(8,128)(2,1)}), bf16[4,64,1280]{2,1,0:T(8,128)(2,1)S(1)}, u32[]{:S(2)}, u32[]{:S(2)}) async-start(bf16[4,64,1280]{2,1,0:T(8,128)(2,1)} %pad_maximum_fusion), calls=%async_computation.1 | async-start | bytes 1310720 | tf_op jit(solution)/shard_map/gather_inputs/all_to_all | solution.py:22
  38.5 2.4 %collective-permute-start.1 = (bf16[64,1024]{1,0:T(8,128)(2,1)S(1)}, bf16[64,1024]{1,0:T(8,128)(2,1)S(1)}, u32[]{:S(2)}, u32[]{:S(2)}) collective-permute-start(bf16[64,1024]{1,0:T(8,128)(2,1)S(1)} %get-tuple-element.49.refs_0_), channel_id=1, source_target_pairs={{0,128},{64,192},{128,0},{192,64},{1,129},{65,193},{129,1},{193,65... | collective-permute-start | bytes 393224 | tf_op jit(solution)/shard_map/gather_targets/ppermute | solution.py:30
  40.9 6.0 %collective-permute-done.refs_1_ = bf16[64,1024]{1,0:T(8,128)(2,1)S(1)} collective-permute-done((bf16[64,1024]{1,0:T(8,128)(2,1)S(1)}, bf16[64,1024]{1,0:T(8,128)(2,1)S(1)}, u32[]{:S(2)}, u32[]{:S(2)}) %collective-permute-start) | collective-permute-done | bytes 131104 | tf_op jit(solution)/shard_map/gather_targets/ppermute | solution.py:30
  47.0 4.3 %collective-permute-done.1.refs_2_ = bf16[64,1024]{1,0:T(8,128)(2,1)S(1)} collective-permute-done((bf16[64,1024]{1,0:T(8,128)(2,1)S(1)}, bf16[64,1024]{1,0:T(8,128)(2,1)S(1)}, u32[]{:S(2)}, u32[]{:S(2)}) %collective-permute-start.1) | collective-permute-done | bytes 131104 | tf_op jit(solution)/shard_map/gather_targets/ppermute | solution.py:30
  53.2 7.6 %all-to-all-start.2 = ((f32[8,32,256]{2,1,0:T(8,128)}), f32[8,32,256]{2,1,0:T(8,128)S(1)}, u32[]{:S(2)}, u32[]{:S(2)}) async-start(f32[8,32,256]{2,1,0:T(8,128)} %bitcast.11), calls=%async_computation.2 | async-start | bytes 524288 | tf_op jit(solution)/shard_map/head/all_to_all | solution.py:22
  60.8 7.2 %all-to-all-done.2 = f32[8,32,256]{2,1,0:T(8,128)S(1)} async-done(((f32[8,32,256]{2,1,0:T(8,128)}), f32[8,32,256]{2,1,0:T(8,128)S(1)}, u32[]{:S(2)}, u32[]{:S(2)}) %all-to-all-start.2) | async-done | bytes 262176 | tf_op jit(solution)/shard_map/head/all_to_all | solution.py:22
  68.1 10.3 %all_to_all.41 = bf16[8,32,256]{2,1,0:T(8,128)(2,1)S(1)} all-to-all(bf16[8,32,256]{2,1,0:T(8,128)(2,1)S(1)} %broadcast_in_dim.37), channel_id=1, replica_groups=mesh['y'=4,'z'=8,'x'=4,'c'=2] {'z'}, dimensions={0} | all-to-all | bytes 262144 | tf_op jit(solution)/shard_map/gather_heads/all_to_all | solution.py:22
  80.0 2.4 %collective-permute-start.5 = (bf16[16,2048]{1,0:T(8,128)(2,1)S(1)}, bf16[16,2048]{1,0:T(8,128)(2,1)S(1)}, u32[]{:S(2)}, u32[]{:S(2)}) collective-permute-start(bf16[16,2048]{1,0:T(8,128)(2,1)S(1)} %bitcast.43), channel_id=1, source_target_pairs={{0,192},{64,128},{128,64},{192,0},{1,193},{65,129},{129,65},{193,1... | collective-permute-start | bytes 196616 | tf_op jit(solution)/shard_map/gather_heads/ppermute | solution.py:30
  84.2 2.1 collective-permute-start.8
  92.9 2.2 collective-permute-start.14
  96.0 2.2 copy-done.1
  98.2 3.3 %copy-done.2 = bf16[501,8192]{1,0:T(8,128)(2,1)S(1)} copy-done((bf16[501,8192]{1,0:T(8,128)(2,1)S(1)}, bf16[501,8192]{1,0:T(8,128)(2,1)}, u32[]{:S(2)}) %copy-start.2) | copy-done | bytes 8208408
  101.5 3.3 %teacher.2 = (bf16[512,8192]{1,0:T(8,128)(2,1)S(1)}, bf16[8192,512]{1,0:T(8,128)(2,1)S(1)}) custom-call(s32[33]{0:T(128)S(1)} %pad_add_fusion.place, bf16[501,8192]{1,0:T(8,128)(2,1)S(1)} %copy-done.2, bf16[256,8192]{1,0:T(8,128)(2,1)S(1)} %copy-done.1), custom_call_target="tpu_custom_call" | custom-call | bytes 25165824 | tf_op jit(solution)/shard_map/teacher/pallas_call | solution.py:93
  104.8 2.9 %teacher.3.refs_8_.teacher_ref = f32[256,512]{1,0:T(8,128)S(1)} custom-call(s32[33]{0:T(128)S(1)} %pad_add_fusion.place, bf16[256,8192]{1,0:T(8,128)(2,1)S(1)} %copy-done.1, bf16[8192,512]{1,0:T(8,128)(2,1)S(1)} %get-tuple-element.25.down_ref.refs_9_), custom_call_target="tpu_custom_call" | custom-call | flops 2147483648 | bytes 12582912 | tf_op jit(solution)/shard_map/teacher/pallas_call | solution.py:61
  107.8 10.3 %collective-permute-start.15 = (bf16[16,8192]{1,0:T(8,128)(2,1)S(1)}, bf16[16,8192]{1,0:T(8,128)(2,1)S(1)}, u32[]{:S(2)}, u32[]{:S(2)}) collective-permute-start(bf16[16,8192]{1,0:T(8,128)(2,1)S(1)} %get-tuple-element.26.refs_0_), channel_id=1, source_target_pairs={{0,1},{1,0},{2,3},{3,2},{4,5},{5,4},{6,7},{7,6},{8,9},{9,8},{10,11... | collective-permute-start | bytes 786440 | tf_op jit(solution)/shard_map/gather_heads/ppermute | solution.py:30
  120.4 2.4 %student.2 = (f32[128,512]{1,0:T(8,128)S(1)}, f32[128,128]{1,0:T(8,128)S(1)}) custom-call(bf16[16,8192]{1,0:T(8,128)(2,1)S(1)} %get-tuple-element.26.refs_0_, bf16[16,8192]{1,0:T(8,128)(2,1)} %get-tuple-element.27.refs_1_, bf16[16,8192]{1,0:T(8,128)(2,1)S(1)} %get-tuple-element.28.refs_2_, bf16[16,8192]{1,0:T(8,128)(2,1)S(1)} %get-tuple-element.29.refs_3_, ...), custom_call_target="tpu_custom_call" | custom-call | flops 1073741824 | bytes 8388608 | tf_op jit(solution)/shard_map/student/pallas_call | solution.py:61
  124.9 12.5 %all_to_all.42.parts_ref = f32[32,8,128]{2,1,0:T(8,128)S(1)} all-to-all(f32[32,8,128]{2,1,0:T(8,128)S(1)} %get-tuple-element.35), channel_id=1, replica_groups=mesh['y'=4,'z'=8,'x'=4,'c'=2] {'y','x','c'}, dimensions={0} | all-to-all | bytes 262144 | tf_op jit(solution)/shard_map/totals/all_to_all | solution.py:22
  137.4 9.2 %all_to_all.43.parts_ref = f32[8,8,128]{2,1,0:T(8,128)S(1)} all-to-all(f32[8,8,128]{2,1,0:T(8,128)S(1)} %totals.2), channel_id=1, replica_groups=mesh['y'=4,'z'=8,'x'=4,'c'=2] {'z'}, dimensions={0} | all-to-all | bytes 65536 | tf_op jit(solution)/shard_map/totals/all_to_all | solution.py:22
  163.2 5.5 %collective-permute-done.25 = bf16[16,8192]{1,0:T(8,128)(2,1)S(1)} collective-permute-done((bf16[16,8192]{1,0:T(8,128)(2,1)S(1)}, bf16[16,8192]{1,0:T(8,128)(2,1)S(1)}, u32[]{:S(2)}, u32[]{:S(2)}) %collective-permute-start.25) | collective-permute-done | bytes 262176 | tf_op jit(solution)/shard_map/reduce_grad/ppermute | solution.py:30
  178.5 2.4 %collective-permute-start.35 = (bf16[16,2048]{1,0:T(8,128)(2,1)S(1)}, bf16[16,2048]{1,0:T(8,128)(2,1)S(1)}, u32[]{:S(2)}, u32[]{:S(2)}) collective-permute-start(bf16[16,2048]{1,0:T(8,128)(2,1)S(1)} %get-tuple-element.56), channel_id=1, source_target_pairs={{0,6},{2,4},{4,2},{6,0},{1,7},{3,5},{5,3},{7,1},{8,14},{10,12},{12... | collective-permute-start | bytes 196616 | tf_op jit(solution)/shard_map/reduce_grad/ppermute | solution.py:30
  182.9 10.3 %all_to_all.44 = bf16[8,32,256]{2,1,0:T(8,128)(2,1)S(1)} all-to-all(bf16[8,32,256]{2,1,0:T(8,128)(2,1)S(1)} %bitcast.54), channel_id=1, replica_groups=mesh['y'=4,'z'=8,'x'=4,'c'=2] {'z'}, dimensions={0} | all-to-all | bytes 262144 | tf_op jit(solution)/shard_map/reduce_grad/all_to_all | solution.py:22
  194.2 9.8 %all-to-all-start.7 = ((bf16[8,48,256]{2,1,0:T(8,128)(2,1)}), bf16[8,48,256]{2,1,0:T(8,128)(2,1)S(1)}, u32[]{:S(2)}, u32[]{:S(2)}) async-start(bf16[8,48,256]{2,1,0:T(8,128)(2,1)} %broadcast_in_dim.39), calls=%async_computation.7 | async-start | bytes 393216 | tf_op jit(solution)/shard_map/finish/all_to_all | solution.py:22
  205.3 4.6 %all-to-all-done.7 = bf16[8,48,256]{2,1,0:T(8,128)(2,1)S(1)} async-done(((bf16[8,48,256]{2,1,0:T(8,128)(2,1)}), bf16[8,48,256]{2,1,0:T(8,128)(2,1)S(1)}, u32[]{:S(2)}, u32[]{:S(2)}) %all-to-all-start.7) | async-done | bytes 196640 | tf_op jit(solution)/shard_map/finish/all_to_all | solution.py:22
  (129 shorter events, 53.7 us)
Async XLA Ops:
  32.9 19.2 %all-to-all-start.1 = ((bf16[4,64,1280]{2,1,0:T(8,128)(2,1)}), bf16[4,64,1280]{2,1,0:T(8,128)(2,1)S(1)}, u32[]{:S(2)}, u32[]{:S(2)}) async-start(bf16[4,64,1280]{2,1,0:T(8,128)(2,1)} %pad_maximum_fusion), calls=%async_computation.1 | async-start | bytes 1310720 | tf_op jit(solution)/shard_map/gather_inputs/all_to_all | solution.py:22
  37.1 58.9 %all-gather.2.cloned.1.call-start = ((), (), s32[]{:S(2)}) async-start(), calls=%async_computation.8 | async-start | bytes 4718592 | tf_op jit(solution)/shard_map/gather_targets/all_gather | solution.py:399
  37.1 9.9 %collective-permute-start = (bf16[64,1024]{1,0:T(8,128)(2,1)S(1)}, bf16[64,1024]{1,0:T(8,128)(2,1)S(1)}, u32[]{:S(2)}, u32[]{:S(2)}) collective-permute-start(bf16[64,1024]{1,0:T(8,128)(2,1)S(1)} %get-tuple-element.49.refs_0_), channel_id=1, source_target_pairs={{0,64},{64,0},{128,192},{192,128},{1,65},{65,1},{129,193},{193,129... | collective-permute-start | bytes 393224 | tf_op jit(solution)/shard_map/gather_targets/ppermute | solution.py:30
  38.5 12.7 %collective-permute-start.1 = (bf16[64,1024]{1,0:T(8,128)(2,1)S(1)}, bf16[64,1024]{1,0:T(8,128)(2,1)S(1)}, u32[]{:S(2)}, u32[]{:S(2)}) collective-permute-start(bf16[64,1024]{1,0:T(8,128)(2,1)S(1)} %get-tuple-element.49.refs_0_), channel_id=1, source_target_pairs={{0,128},{64,192},{128,0},{192,64},{1,129},{65,193},{129,1},{193,65... | collective-permute-start | bytes 393224 | tf_op jit(solution)/shard_map/gather_targets/ppermute | solution.py:30
  40.9 10.3 %collective-permute-start.2 = (bf16[64,1024]{1,0:T(8,128)(2,1)S(1)}, bf16[64,1024]{1,0:T(8,128)(2,1)S(1)}, u32[]{:S(2)}, u32[]{:S(2)}) collective-permute-start(bf16[64,1024]{1,0:T(8,128)(2,1)S(1)} %get-tuple-element.49.refs_0_), channel_id=1, source_target_pairs={{0,192},{64,128},{128,64},{192,0},{1,193},{65,129},{129,65},{193,1... | collective-permute-start | bytes 393224 | tf_op jit(solution)/shard_map/gather_targets/ppermute | solution.py:30
  53.2 14.8 %all-to-all-start.2 = ((f32[8,32,256]{2,1,0:T(8,128)}), f32[8,32,256]{2,1,0:T(8,128)S(1)}, u32[]{:S(2)}, u32[]{:S(2)}) async-start(f32[8,32,256]{2,1,0:T(8,128)} %bitcast.11), calls=%async_computation.2 | async-start | bytes 524288 | tf_op jit(solution)/shard_map/head/all_to_all | solution.py:22
  78.6 7.7 %collective-permute-start.4 = (bf16[16,2048]{1,0:T(8,128)(2,1)S(1)}, bf16[16,2048]{1,0:T(8,128)(2,1)S(1)}, u32[]{:S(2)}, u32[]{:S(2)}) collective-permute-start(bf16[16,2048]{1,0:T(8,128)(2,1)S(1)} %bitcast.42), channel_id=1, source_target_pairs={{0,128},{64,192},{128,0},{192,64},{1,129},{65,193},{129,1},{193,65... | collective-permute-start | bytes 196616 | tf_op jit(solution)/shard_map/gather_heads/ppermute | solution.py:30
  88.5 6.9 %collective-permute-start.10 = (bf16[16,8192]{1,0:T(8,128)(2,1)S(1)}, bf16[16,8192]{1,0:T(8,128)(2,1)S(1)}, u32[]{:S(2)}, u32[]{:S(2)}) collective-permute-start(bf16[16,8192]{1,0:T(8,128)(2,1)S(1)} %get-tuple-element.22.refs_0_), channel_id=1, source_target_pairs={{0,4},{2,6},{4,0},{6,2},{1,5},{3,7},{5,1},{7,3},{8,12},{10,14},{12... | collective-permute-start | bytes 786440 | tf_op jit(solution)/shard_map/gather_heads/ppermute | solution.py:30
  89.7 18.0 %collective-permute-start.11 = (bf16[16,8192]{1,0:T(8,128)(2,1)S(1)}, bf16[16,8192]{1,0:T(8,128)(2,1)S(1)}, u32[]{:S(2)}, u32[]{:S(2)}) collective-permute-start(bf16[16,8192]{1,0:T(8,128)(2,1)S(1)} %get-tuple-element.22.refs_0_), channel_id=1, source_target_pairs={{0,6},{2,4},{4,2},{6,0},{1,7},{3,5},{5,3},{7,1},{8,14},{10,12},{12... | collective-permute-start | bytes 786440 | tf_op jit(solution)/shard_map/gather_heads/ppermute | solution.py:30
  91.2 16.5 %collective-permute-start.12 = (bf16[64,2048]{1,0:T(8,128)(2,1)S(1)}, bf16[64,2048]{1,0:T(8,128)(2,1)S(1)}, u32[]{:S(2)}, u32[]{:S(2)}) collective-permute-start(bf16[64,2048]{1,0:T(8,128)(2,1)S(1)} %get-tuple-element.23.refs_4_), channel_id=1, source_target_pairs={{0,64},{64,0},{128,192},{192,128},{1,65},{65,1},{129,193},{193,129... | collective-permute-start | bytes 786440 | tf_op jit(solution)/shard_map/gather_heads/ppermute | solution.py:30
  91.2 16.5 %collective-permute-start.13 = (bf16[64,2048]{1,0:T(8,128)(2,1)S(1)}, bf16[64,2048]{1,0:T(8,128)(2,1)S(1)}, u32[]{:S(2)}, u32[]{:S(2)}) collective-permute-start(bf16[64,2048]{1,0:T(8,128)(2,1)S(1)} %get-tuple-element.23.refs_4_), channel_id=1, source_target_pairs={{0,128},{64,192},{128,0},{192,64},{1,129},{65,193},{129,1},{193,65... | collective-permute-start | bytes 786440 | tf_op jit(solution)/shard_map/gather_heads/ppermute | solution.py:30
  92.9 14.8 %collective-permute-start.14 = (bf16[64,2048]{1,0:T(8,128)(2,1)S(1)}, bf16[64,2048]{1,0:T(8,128)(2,1)S(1)}, u32[]{:S(2)}, u32[]{:S(2)}) collective-permute-start(bf16[64,2048]{1,0:T(8,128)(2,1)S(1)} %get-tuple-element.23.refs_4_), channel_id=1, source_target_pairs={{0,192},{64,128},{128,64},{192,0},{1,193},{65,129},{129,65},{193,1... | collective-permute-start | bytes 786440 | tf_op jit(solution)/shard_map/gather_heads/ppermute | solution.py:30
  95.5 12.3 %collective-permute-start.9 = (bf16[16,8192]{1,0:T(8,128)(2,1)S(1)}, bf16[16,8192]{1,0:T(8,128)(2,1)}, u32[]{:S(2)}, u32[]{:S(2)}) collective-permute-start(bf16[16,8192]{1,0:T(8,128)(2,1)S(1)} %get-tuple-element.22.refs_0_), channel_id=1, source_target_pairs={{0,2},{2,0},{4,6},{6,4},{1,3},{3,1},{5,7},{7,5},{8,10},{10,8},{12,... | collective-permute-start | bytes 786440 | tf_op jit(solution)/shard_map/gather_heads/ppermute | solution.py:30
  107.8 11.5 %collective-permute-start.15 = (bf16[16,8192]{1,0:T(8,128)(2,1)S(1)}, bf16[16,8192]{1,0:T(8,128)(2,1)S(1)}, u32[]{:S(2)}, u32[]{:S(2)}) collective-permute-start(bf16[16,8192]{1,0:T(8,128)(2,1)S(1)} %get-tuple-element.26.refs_0_), channel_id=1, source_target_pairs={{0,1},{1,0},{2,3},{3,2},{4,5},{5,4},{6,7},{7,6},{8,9},{9,8},{10,11... | collective-permute-start | bytes 786440 | tf_op jit(solution)/shard_map/gather_heads/ppermute | solution.py:30
  154.7 7.6 %collective-permute-start.24 = (bf16[16,8192]{1,0:T(8,128)(2,1)S(1)}, bf16[16,8192]{1,0:T(8,128)(2,1)S(1)}, u32[]{:S(2)}, u32[]{:S(2)}) collective-permute-start(bf16[16,8192]{1,0:T(8,128)(2,1)S(1)} %get-tuple-element.43), channel_id=1, source_target_pairs={{0,2},{2,0},{4,6},{6,4},{1,3},{3,1},{5,7},{7,5},{8,10},{10,8},{12,... | collective-permute-start | bytes 786440 | tf_op jit(solution)/shard_map/reduce_grad/ppermute | solution.py:30
  155.1 13.6 %collective-permute-start.25 = (bf16[16,8192]{1,0:T(8,128)(2,1)S(1)}, bf16[16,8192]{1,0:T(8,128)(2,1)S(1)}, u32[]{:S(2)}, u32[]{:S(2)}) collective-permute-start(bf16[16,8192]{1,0:T(8,128)(2,1)S(1)} %get-tuple-element.45), channel_id=1, source_target_pairs={{0,4},{2,6},{4,0},{6,2},{1,5},{3,7},{5,1},{7,3},{8,12},{10,14},{12... | collective-permute-start | bytes 786440 | tf_op jit(solution)/shard_map/reduce_grad/ppermute | solution.py:30
  157.0 13.7 %collective-permute-start.26 = (bf16[16,8192]{1,0:T(8,128)(2,1)S(1)}, bf16[16,8192]{1,0:T(8,128)(2,1)S(1)}, u32[]{:S(2)}, u32[]{:S(2)}) collective-permute-start(bf16[16,8192]{1,0:T(8,128)(2,1)S(1)} %get-tuple-element.44), channel_id=1, source_target_pairs={{0,6},{2,4},{4,2},{6,0},{1,7},{3,5},{5,3},{7,1},{8,14},{10,12},{12... | collective-permute-start | bytes 786440 | tf_op jit(solution)/shard_map/reduce_grad/ppermute | solution.py:30
  158.7 14.3 %collective-permute-start.30 = (bf16[64,2048]{1,0:T(8,128)(2,1)S(1)}, bf16[64,2048]{1,0:T(8,128)(2,1)S(1)}, u32[]{:S(2)}, u32[]{:S(2)}) collective-permute-start(bf16[64,2048]{1,0:T(8,128)(2,1)S(1)} %get-tuple-element.46), channel_id=1, source_target_pairs={{0,64},{64,0},{128,192},{192,128},{1,65},{65,1},{129,193},{193,129... | collective-permute-start | bytes 786440 | tf_op jit(solution)/shard_map/reduce_grad/ppermute | solution.py:30
  159.1 15.7 %collective-permute-start.31 = (bf16[64,2048]{1,0:T(8,128)(2,1)S(1)}, bf16[64,2048]{1,0:T(8,128)(2,1)S(1)}, u32[]{:S(2)}, u32[]{:S(2)}) collective-permute-start(bf16[64,2048]{1,0:T(8,128)(2,1)S(1)} %get-tuple-element.48), channel_id=1, source_target_pairs={{0,128},{64,192},{128,0},{192,64},{1,129},{65,193},{129,1},{193,65... | collective-permute-start | bytes 786440 | tf_op jit(solution)/shard_map/reduce_grad/ppermute | solution.py:30
  162.3 14.4 %collective-permute-start.32 = (bf16[64,2048]{1,0:T(8,128)(2,1)S(1)}, bf16[64,2048]{1,0:T(8,128)(2,1)S(1)}, u32[]{:S(2)}, u32[]{:S(2)}) collective-permute-start(bf16[64,2048]{1,0:T(8,128)(2,1)S(1)} %get-tuple-element.47), channel_id=1, source_target_pairs={{0,192},{64,128},{128,64},{192,0},{1,193},{65,129},{129,65},{193,1... | collective-permute-start | bytes 786440 | tf_op jit(solution)/shard_map/reduce_grad/ppermute | solution.py:30
  170.8 7.6 %collective-permute-start.27 = (bf16[16,2048]{1,0:T(8,128)(2,1)S(1)}, bf16[16,2048]{1,0:T(8,128)(2,1)S(1)}, u32[]{:S(2)}, u32[]{:S(2)}) collective-permute-start(bf16[16,2048]{1,0:T(8,128)(2,1)S(1)} %get-tuple-element.52), channel_id=1, source_target_pairs={{0,64},{64,0},{128,192},{192,128},{1,65},{65,1},{129,193},{193,129... | collective-permute-start | bytes 196616 | tf_op jit(solution)/shard_map/reduce_grad/ppermute | solution.py:30
  171.2 9.6 %collective-permute-start.28 = (bf16[16,2048]{1,0:T(8,128)(2,1)S(1)}, bf16[16,2048]{1,0:T(8,128)(2,1)S(1)}, u32[]{:S(2)}, u32[]{:S(2)}) collective-permute-start(bf16[16,2048]{1,0:T(8,128)(2,1)S(1)} %get-tuple-element.54), channel_id=1, source_target_pairs={{0,128},{64,192},{128,0},{192,64},{1,129},{65,193},{129,1},{193,65... | collective-permute-start | bytes 196616 | tf_op jit(solution)/shard_map/reduce_grad/ppermute | solution.py:30
  173.0 7.9 %collective-permute-start.29 = (bf16[16,2048]{1,0:T(8,128)(2,1)S(1)}, bf16[16,2048]{1,0:T(8,128)(2,1)S(1)}, u32[]{:S(2)}, u32[]{:S(2)}) collective-permute-start(bf16[16,2048]{1,0:T(8,128)(2,1)S(1)} %get-tuple-element.53), channel_id=1, source_target_pairs={{0,192},{64,128},{128,64},{192,0},{1,193},{65,129},{129,65},{193,1... | collective-permute-start | bytes 196616 | tf_op jit(solution)/shard_map/reduce_grad/ppermute | solution.py:30
  194.2 15.7 %all-to-all-start.7 = ((bf16[8,48,256]{2,1,0:T(8,128)(2,1)}), bf16[8,48,256]{2,1,0:T(8,128)(2,1)S(1)}, u32[]{:S(2)}, u32[]{:S(2)}) async-start(bf16[8,48,256]{2,1,0:T(8,128)(2,1)} %broadcast_in_dim.39), calls=%async_computation.7 | async-start | bytes 393216 | tf_op jit(solution)/shard_map/finish/all_to_all | solution.py:22
  (21 other events, 107.8 us)
Sparse Core Ops, SparseCore 0:
  52.2 34.1 all-gather.1

commit v8 on v7

--- a/solution.py
+++ b/solution.py
@@ -13,8 +13,8 @@
 VOC = ("x", "c")
 CHUNKS = 4
 PADDED = 512
-LIMIT = 24 * 1024 * 1024
-HEAD_COST = 90_000_000_000
+LIMIT = 14 * 1024 * 1024
+HEADS_COST = 60_000_000_000
 SIZES = {"y": 4, "z": 8, "x": 4, "c": 2}
 
 
@@ -278,66 +278,76 @@
 
 
 def join_kernel(*refs):
-    firsts, seconds, (first_ref, second_ref) = refs[:4], refs[4:8], refs[8:]
+    firsts, seconds, (first_ref, second_ref) = refs[:4], refs[4:8], refs[-2:]
     (rows, width), (block, _) = firsts[0].shape, seconds[0].shape
     for at in range(4):
         first_ref[:, at * width : (at + 1) * width] = firsts[at][...]
         second_ref[at * block : (at + 1) * block] = seconds[at][...]
 
 
-def join(firsts, seconds):
+def join(firsts, seconds, awaited):
     (rows, width), (block, across) = firsts[0].shape, seconds[0].shape
+    vmem = pl.BlockSpec(memory_space=pltpu.VMEM)
     return pl.pallas_call(
         join_kernel,
+        in_specs=[vmem] * 8 + [pl.BlockSpec(memory_space=pl.ANY)],
+        out_specs=[vmem] * 2,
         out_shape=[
-            jax.ShapeDtypeStruct((rows, 4 * width), BF16),
-            jax.ShapeDtypeStruct((4 * block, across), BF16),
+            shape(rows, 4 * width, dtype=BF16),
+            shape(4 * block, across, dtype=BF16),
         ],
-        compiler_params=pltpu.CompilerParams(vmem_limit_bytes=LIMIT),
+        compiler_params=pltpu.CompilerParams(vmem_limit_bytes=4 * 1024 * 1024),
         cost_estimate=cost(0, 16 * rows * width),
-    )(*firsts, *seconds)
+    )(*firsts, *seconds, pltpu.with_memory_space_constraint(awaited, pltpu.HBM))
 
 
 def stack_kernel(*refs):
-    blocks, (out_ref, ready_ref) = refs[:4], refs[4:]
+    blocks, out_ref = refs[:4], refs[-1]
     rows = blocks[0].shape[0]
     for at, block in enumerate(blocks):
         out_ref[at * rows : (at + 1) * rows] = block[...]
-    ready_ref[...] = jnp.zeros(ready_ref.shape, F32)
-
-
-def stacked(blocks):
+
+
+def stacked(blocks, awaited):
     rows, across = blocks[0].shape
-    return local_call(
+    return pl.pallas_call(
         stack_kernel,
-        [shape(4 * rows, across, dtype=BF16), shape(8, 128)],
-        cost(0, 16 * rows * across),
+        in_specs=[pl.BlockSpec(memory_space=pltpu.VMEM)] * 4 + [pl.BlockSpec(memory_space=pl.ANY)],
+        out_specs=pl.BlockSpec(memory_space=pltpu.VMEM),
+        out_shape=shape(4 * rows, across, dtype=BF16),
+        compiler_params=pltpu.CompilerParams(vmem_limit_bytes=4 * 1024 * 1024),
+        cost_estimate=cost(0, 16 * rows * across),
+    )(*blocks, awaited)
+
+
+def heads_kernel(parts_ref, residual_ref, bias_ref, heads_ref, preact_ref):
+    preact = summed_parts(parts_ref) + bias_ref[...]
+    preact_ref[...] = preact
+    heads = residual_ref[...].astype(F32) + preact * jax.nn.sigmoid(preact)
+    for at in range(heads_ref.shape[0]):
+        heads_ref[at] = heads.astype(BF16)
+
+
+def heads_of(parts, residual, bias):
+    rows, across = residual.shape
+    return local_call(
+        heads_kernel,
+        [shape(8, rows, across, dtype=BF16), shape(rows, across)],
+        cost(HEADS_COST, 4 * parts.size),
         limit=4 * 1024 * 1024,
         scalars=False,
-    )(*blocks)
-
-
-def head_kernel(rows_ref, weight_ref, ready_ref, out_ref):
-    out_ref[...] = jnp.dot(rows_ref[...], weight_ref[...], preferred_element_type=F32)
-
-
-def head_partial(rows, weight, ready):
-    return pl.pallas_call(
-        head_kernel,
-        in_specs=[pl.BlockSpec(memory_space=pltpu.VMEM)] * 3,
-        out_shape=jax.ShapeDtypeStruct((rows.shape[0], weight.shape[1]), F32),
-        compiler_params=pltpu.CompilerParams(vmem_limit_bytes=LIMIT),
-        cost_estimate=cost(HEAD_COST, 2 * (rows.size + weight.size)),
-    )(rows, weight, ready)
+    )(parts, residual, bias[None])
 
 
 def gather_lines(heads):
-    return gathered(heads, "z", 8).transpose(1, 0, 2).reshape(heads.shape[0], -1)
-
-
-def gather_heads(lines, teacher):
+    return exchange(heads, "z").transpose(1, 0, 2).reshape(heads.shape[1], -1)
+
+
+def gather_heads(lines, target_all, teacher):
     half = lines.shape[0] // 2
-    first, second = join(from_peers(lines[:half], "y"), from_peers(lines[half:], "x"))
+    first, second = join(
+        from_peers(lines[:half], "y"), from_peers(lines[half:], "x"), target_all
+    )
     blocks = settled(from_peers(first, "x") + from_peers(second, "y"), teacher)
     return blocks, [swap(block, "c", 1) for block in blocks]
 
@@ -394,25 +404,24 @@
         input_rows = got[:, :, :in_width].reshape(count, in_width)
         residual = got[:, :, in_width:].reshape(count, out_width)
         residual = lax.dynamic_slice_in_dim(residual, voc_index * rows, rows, 0)
+    with jax.named_scope("head"):
+        partial_pre = jnp.dot(input_rows, head_weight, preferred_element_type=F32)
+        parts = exchange(partial_pre.reshape(vocs, rows, out_width), VOC)
+        heads, preact = heads_of(parts, residual, head_bias)
     with jax.named_scope("gather_targets"):
-        target_rows, ready = stacked(from_peers(target_lines, "y"))
+        target_rows = stacked(from_peers(target_lines, "y"), partial_pre)
         target_all = lax.all_gather(target_rows, VOC, axis=1, tiled=True)
     steps = jnp.arange(16)
     order = ((at_x ^ (steps % 4)) * 2 + (at_c ^ (steps // 8))) * 2 + (steps // 4) % 2
     target_order = (order // 4 ^ at_y) * 4 + order % 4
     place = jnp.concatenate([order, at_y[None], target_order]).astype(jnp.int32)
-    with jax.named_scope("head"):
-        partial_pre = head_partial(input_rows, head_weight, ready)
-        parts = exchange(partial_pre.reshape(vocs, rows, out_width), VOC)
-        preact = jnp.sum(parts, axis=0) + head_bias
-        heads = (residual.astype(F32) + jax.nn.silu(preact)).astype(BF16)
     with jax.named_scope("gather_heads"):
         lines = gather_lines(heads)
     with jax.named_scope("teacher"):
         across, down = prepare(place, vocab_head, target_all)
         teacher = teacher_logits(place, target_all, down)
     with jax.named_scope("gather_heads"):
-        own_blocks, other_blocks = gather_heads(lines, teacher)
+        own_blocks, other_blocks = gather_heads(lines, target_all, teacher)
     with jax.named_scope("student"):
         entries = vocab_head.shape[0]
         own_logits, table = own_student(entries, own_blocks, teacher, down)

time: 220 us -> 216 us (0.982)
    ppermute x36, waiting for transfers between devices: 27.9 us -> 22.7 us  [swap(): lax.ppermute(block, axis, [(i, i ^ step) for i in range(SIZES[axis])])]
    all_to_all x3, waiting for transfers between devices: 11.8 us -> 15.4 us  [exchange(): return lax.all_to_all(blocks, axis, split_axis=0, concat_axis=0, tiled=True)]
  transfers between devices with their start and end apart: 40 -> 40, of which waited for: 16 -> 16; matrix products, arithmetic and copies ran while one was open for 1% -> 1% of each run, Pallas kernels for 6% -> 5%
where the time goes in v8:
time: 216 us; the launch traced here: 215 us
  starting transfers between devices  68.8 us (32%)
  blocking collectives  65.1 us (30%)
  waiting for transfers between devices  38.2 us (18%)
  between operations  16.2 us (8%)
  Pallas kernels  14.7 us (7%)
  local copies, waits for them, and re-layouts  5.42 us (3%)
  other arithmetic  4.58 us (2%)
  matrix products  2.35 us (1%)
    all_to_all x5, blocking collectives, exchange(): return lax.all_to_all(blocks, axis, split_axis=0, concat_axis=0, tiled=True)  65.1 us
    ppermute x36, starting transfers between devices, swap(): lax.ppermute(block, axis, [(i, i ^ step) for i in range(SIZES[axis])])  47.1 us
    ppermute x36, waiting for transfers between devices, swap(): lax.ppermute(block, axis, [(i, i ^ step) for i in range(SIZES[axis])])  22.7 us
    all_to_all x3, starting transfers between devices, exchange(): return lax.all_to_all(blocks, axis, split_axis=0, concat_axis=0, tiled=True)  21.6 us
    all_to_all x3, waiting for transfers between devices, exchange(): return lax.all_to_all(blocks, axis, split_axis=0, concat_axis=0, tiled=True)  15.4 us
    pallas_call x8, Pallas kernels, call(): pl.pallas_call(kernel, in_specs=specs, out_specs=jax.tree.map(lambda _: p...  10.5 us
  transfers between devices with their start and end apart: 40, of which 16 were waited for; matrix products, arithmetic and copies ran while one was open for 1% of the time, Pallas kernels for 5%

profile of v8, /device:TPU:1, one launch (start us, length us, event | category | flops | bytes accessed | tf_op | source)
XLA Modules:
  0.0 215.3 jit_solution(11025408762750456173)
XLA Ops:
  9.5 22.3 %all_to_all.40 = bf16[8,8,3072]{2,1,0:T(8,128)(2,1)S(1)} all-to-all(bf16[8,8,3072]{2,1,0:T(8,128)(2,1)S(1)} %pad_maximum_fusion.1), channel_id=1, replica_groups=mesh['y'=4,'z'=8,'x'=4,'c'=2] {'z'}, dimensions={0} | all-to-all | bytes 786432 | tf_op jit(solution)/shard_map/gather_z/all_to_all | solution.py:22
  33.0 4.2 %all-to-all-start.1 = ((bf16[4,64,1280]{2,1,0:T(8,128)(2,1)}), bf16[4,64,1280]{2,1,0:T(8,128)(2,1)S(1)}, u32[]{:S(2)}, u32[]{:S(2)}) async-start(bf16[4,64,1280]{2,1,0:T(8,128)(2,1)} %pad_maximum_fusion), calls=%async_computation.1 | async-start | bytes 1310720 | tf_op jit(solution)/shard_map/gather_inputs/all_to_all | solution.py:22
  38.6 2.4 %collective-permute-start.7 = (bf16[64,1024]{1,0:T(8,128)(2,1)S(1)}, bf16[64,1024]{1,0:T(8,128)(2,1)S(1)}, u32[]{:S(2)}, u32[]{:S(2)}) collective-permute-start(bf16[64,1024]{1,0:T(8,128)(2,1)S(1)} %get-tuple-element.49.refs_0_), channel_id=1, source_target_pairs={{0,128},{64,192},{128,0},{192,64},{1,129},{65,193},{129,1},{193,65... | collective-permute-start | bytes 393224 | tf_op jit(solution)/shard_map/gather_targets/ppermute | solution.py:30
  41.0 4.3 %all-to-all-done.1 = bf16[4,64,1280]{2,1,0:T(8,128)(2,1)S(1)} async-done(((bf16[4,64,1280]{2,1,0:T(8,128)(2,1)}), bf16[4,64,1280]{2,1,0:T(8,128)(2,1)S(1)}, u32[]{:S(2)}, u32[]{:S(2)}) %all-to-all-start.1) | async-done | bytes 655392 | tf_op jit(solution)/shard_map/gather_inputs/all_to_all | solution.py:22
  47.1 4.3 %collective-permute-done.7.refs_2_ = bf16[64,1024]{1,0:T(8,128)(2,1)S(1)} collective-permute-done((bf16[64,1024]{1,0:T(8,128)(2,1)S(1)}, bf16[64,1024]{1,0:T(8,128)(2,1)S(1)}, u32[]{:S(2)}, u32[]{:S(2)}) %collective-permute-start.7) | collective-permute-done | bytes 131104 | tf_op jit(solution)/shard_map/gather_targets/ppermute | solution.py:30
  52.2 7.6 %all-to-all-start.2 = ((f32[8,32,256]{2,1,0:T(8,128)}), f32[8,32,256]{2,1,0:T(8,128)S(1)}, u32[]{:S(2)}, u32[]{:S(2)}) async-start(f32[8,32,256]{2,1,0:T(8,128)} %bitcast.10), calls=%async_computation.2 | async-start | bytes 524288 | tf_op jit(solution)/shard_map/head/all_to_all | solution.py:22
  59.8 6.5 %all-to-all-done.2.parts_ref = f32[8,32,256]{2,1,0:T(8,128)S(1)} async-done(((f32[8,32,256]{2,1,0:T(8,128)}), f32[8,32,256]{2,1,0:T(8,128)S(1)}, u32[]{:S(2)}, u32[]{:S(2)}) %all-to-all-start.2) | async-done | bytes 262176 | tf_op jit(solution)/shard_map/head/all_to_all | solution.py:22
  66.3 10.4 %all_to_all.41 = bf16[8,32,256]{2,1,0:T(8,128)(2,1)S(1)} all-to-all(bf16[8,32,256]{2,1,0:T(8,128)(2,1)S(1)} %get-tuple-element.21), channel_id=1, replica_groups=mesh['y'=4,'z'=8,'x'=4,'c'=2] {'z'}, dimensions={0} | all-to-all | bytes 262144 | tf_op jit(solution)/shard_map/gather_heads/all_to_all | solution.py:22
  90.0 2.6 %collective-permute-start.13 = (bf16[64,2048]{1,0:T(8,128)(2,1)S(1)}, bf16[64,2048]{1,0:T(8,128)(2,1)S(1)}, u32[]{:S(2)}, u32[]{:S(2)}) collective-permute-start(bf16[64,2048]{1,0:T(8,128)(2,1)S(1)} %get-tuple-element.23.refs_4_), channel_id=1, source_target_pairs={{0,128},{64,192},{128,0},{192,64},{1,129},{65,193},{129,1},{193,65... | collective-permute-start | bytes 786440 | tf_op jit(solution)/shard_map/gather_heads/ppermute | solution.py:30
  94.3 3.3 %copy-done.2 = bf16[501,8192]{1,0:T(8,128)(2,1)S(1)} copy-done((bf16[501,8192]{1,0:T(8,128)(2,1)S(1)}, bf16[501,8192]{1,0:T(8,128)(2,1)}, u32[]{:S(2)}) %copy-start.2) | copy-done | bytes 8208408
  97.7 3.3 %teacher.2 = (bf16[512,8192]{1,0:T(8,128)(2,1)S(1)}, bf16[8192,512]{1,0:T(8,128)(2,1)S(1)}) custom-call(s32[33]{0:T(128)S(1)} %pad_add_fusion.place, bf16[501,8192]{1,0:T(8,128)(2,1)S(1)} %copy-done.2, bf16[256,8192]{1,0:T(8,128)(2,1)S(1)} %copy-done.1), custom_call_target="tpu_custom_call" | custom-call | bytes 25165824 | tf_op jit(solution)/shard_map/teacher/pallas_call | solution.py:93
  101.0 2.9 %teacher.3.refs_8_.teacher_ref = f32[256,512]{1,0:T(8,128)S(1)} custom-call(s32[33]{0:T(128)S(1)} %pad_add_fusion.place, bf16[256,8192]{1,0:T(8,128)(2,1)S(1)} %copy-done.1, bf16[8192,512]{1,0:T(8,128)(2,1)S(1)} %get-tuple-element.24.down_ref.refs_9_), custom_call_target="tpu_custom_call" | custom-call | flops 2147483648 | bytes 12582912 | tf_op jit(solution)/shard_map/teacher/pallas_call | solution.py:61
  103.9 10.3 %collective-permute-start.15 = (bf16[16,8192]{1,0:T(8,128)(2,1)S(1)}, bf16[16,8192]{1,0:T(8,128)(2,1)S(1)}, u32[]{:S(2)}, u32[]{:S(2)}) collective-permute-start(bf16[16,8192]{1,0:T(8,128)(2,1)S(1)} %get-tuple-element.25.refs_0_), channel_id=1, source_target_pairs={{0,1},{1,0},{2,3},{3,2},{4,5},{5,4},{6,7},{7,6},{8,9},{9,8},{10,11... | collective-permute-start | bytes 786440 | tf_op jit(solution)/shard_map/gather_heads/ppermute | solution.py:30
  118.1 2.0 student.3
  120.1 12.8 %all_to_all.42.parts_ref = f32[32,8,128]{2,1,0:T(8,128)S(1)} all-to-all(f32[32,8,128]{2,1,0:T(8,128)S(1)} %get-tuple-element.34), channel_id=1, replica_groups=mesh['y'=4,'z'=8,'x'=4,'c'=2] {'y','x','c'}, dimensions={0} | all-to-all | bytes 262144 | tf_op jit(solution)/shard_map/totals/all_to_all | solution.py:22
  132.9 9.2 %all_to_all.43.parts_ref = f32[8,8,128]{2,1,0:T(8,128)S(1)} all-to-all(f32[8,8,128]{2,1,0:T(8,128)S(1)} %totals.2), channel_id=1, replica_groups=mesh['y'=4,'z'=8,'x'=4,'c'=2] {'z'}, dimensions={0} | all-to-all | bytes 65536 | tf_op jit(solution)/shard_map/totals/all_to_all | solution.py:22
  142.2 2.0 grad.3
  145.9 2.0 grad.2
  158.7 5.5 %collective-permute-done.25 = bf16[16,8192]{1,0:T(8,128)(2,1)S(1)} collective-permute-done((bf16[16,8192]{1,0:T(8,128)(2,1)S(1)}, bf16[16,8192]{1,0:T(8,128)(2,1)S(1)}, u32[]{:S(2)}, u32[]{:S(2)}) %collective-permute-start.25) | collective-permute-done | bytes 262176 | tf_op jit(solution)/shard_map/reduce_grad/ppermute | solution.py:30
  164.2 2.0 collective-permute-done.26
  174.0 2.4 %collective-permute-start.35 = (bf16[16,2048]{1,0:T(8,128)(2,1)S(1)}, bf16[16,2048]{1,0:T(8,128)(2,1)S(1)}, u32[]{:S(2)}, u32[]{:S(2)}) collective-permute-start(bf16[16,2048]{1,0:T(8,128)(2,1)S(1)} %get-tuple-element.56), channel_id=1, source_target_pairs={{0,6},{2,4},{4,2},{6,0},{1,7},{3,5},{5,3},{7,1},{8,14},{10,12},{12... | collective-permute-start | bytes 196616 | tf_op jit(solution)/shard_map/reduce_grad/ppermute | solution.py:30
  178.5 10.3 %all_to_all.44 = bf16[8,32,256]{2,1,0:T(8,128)(2,1)S(1)} all-to-all(bf16[8,32,256]{2,1,0:T(8,128)(2,1)S(1)} %bitcast.52), channel_id=1, replica_groups=mesh['y'=4,'z'=8,'x'=4,'c'=2] {'z'}, dimensions={0} | all-to-all | bytes 262144 | tf_op jit(solution)/shard_map/reduce_grad/all_to_all | solution.py:22
  189.7 9.8 %all-to-all-start.7 = ((bf16[8,48,256]{2,1,0:T(8,128)(2,1)}), bf16[8,48,256]{2,1,0:T(8,128)(2,1)S(1)}, u32[]{:S(2)}, u32[]{:S(2)}) async-start(bf16[8,48,256]{2,1,0:T(8,128)(2,1)} %broadcast_in_dim.35), calls=%async_computation.7 | async-start | bytes 393216 | tf_op jit(solution)/shard_map/finish/all_to_all | solution.py:22
  200.8 4.6 %all-to-all-done.7 = bf16[8,48,256]{2,1,0:T(8,128)(2,1)S(1)} async-done(((bf16[8,48,256]{2,1,0:T(8,128)(2,1)}), bf16[8,48,256]{2,1,0:T(8,128)(2,1)S(1)}, u32[]{:S(2)}, u32[]{:S(2)}) %all-to-all-start.7) | async-done | bytes 196640 | tf_op jit(solution)/shard_map/finish/all_to_all | solution.py:22
  (129 shorter events, 51.8 us)
Async XLA Ops:
  33.0 12.4 %all-to-all-start.1 = ((bf16[4,64,1280]{2,1,0:T(8,128)(2,1)}), bf16[4,64,1280]{2,1,0:T(8,128)(2,1)S(1)}, u32[]{:S(2)}, u32[]{:S(2)}) async-start(bf16[4,64,1280]{2,1,0:T(8,128)(2,1)} %pad_maximum_fusion), calls=%async_computation.1 | async-start | bytes 1310720 | tf_op jit(solution)/shard_map/gather_inputs/all_to_all | solution.py:22
  37.1 50.0 %all-gather.2.cloned.1.call-start = ((), (), s32[]{:S(2)}) async-start(), calls=%async_computation.8 | async-start | bytes 4718592 | tf_op jit(solution)/shard_map/gather_targets/all_gather | solution.py:413
  37.1 9.9 %collective-permute-start.6 = (bf16[64,1024]{1,0:T(8,128)(2,1)S(1)}, bf16[64,1024]{1,0:T(8,128)(2,1)S(1)}, u32[]{:S(2)}, u32[]{:S(2)}) collective-permute-start(bf16[64,1024]{1,0:T(8,128)(2,1)S(1)} %get-tuple-element.49.refs_0_), channel_id=1, source_target_pairs={{0,64},{64,0},{128,192},{192,128},{1,65},{65,1},{129,193},{193,129... | collective-permute-start | bytes 393224 | tf_op jit(solution)/shard_map/gather_targets/ppermute | solution.py:30
  38.6 12.7 %collective-permute-start.7 = (bf16[64,1024]{1,0:T(8,128)(2,1)S(1)}, bf16[64,1024]{1,0:T(8,128)(2,1)S(1)}, u32[]{:S(2)}, u32[]{:S(2)}) collective-permute-start(bf16[64,1024]{1,0:T(8,128)(2,1)S(1)} %get-tuple-element.49.refs_0_), channel_id=1, source_target_pairs={{0,128},{64,192},{128,0},{192,64},{1,129},{65,193},{129,1},{193,65... | collective-permute-start | bytes 393224 | tf_op jit(solution)/shard_map/gather_targets/ppermute | solution.py:30
  41.0 10.3 %collective-permute-start.8 = (bf16[64,1024]{1,0:T(8,128)(2,1)S(1)}, bf16[64,1024]{1,0:T(8,128)(2,1)S(1)}, u32[]{:S(2)}, u32[]{:S(2)}) collective-permute-start(bf16[64,1024]{1,0:T(8,128)(2,1)S(1)} %get-tuple-element.49.refs_0_), channel_id=1, source_target_pairs={{0,192},{64,128},{128,64},{192,0},{1,193},{65,129},{129,65},{193,1... | collective-permute-start | bytes 393224 | tf_op jit(solution)/shard_map/gather_targets/ppermute | solution.py:30
  52.2 14.1 %all-to-all-start.2 = ((f32[8,32,256]{2,1,0:T(8,128)}), f32[8,32,256]{2,1,0:T(8,128)S(1)}, u32[]{:S(2)}, u32[]{:S(2)}) async-start(f32[8,32,256]{2,1,0:T(8,128)} %bitcast.10), calls=%async_computation.2 | async-start | bytes 524288 | tf_op jit(solution)/shard_map/head/all_to_all | solution.py:22
  77.2 7.4 %collective-permute-start.1 = (bf16[16,2048]{1,0:T(8,128)(2,1)S(1)}, bf16[16,2048]{1,0:T(8,128)(2,1)S(1)}, u32[]{:S(2)}, u32[]{:S(2)}) collective-permute-start(bf16[16,2048]{1,0:T(8,128)(2,1)S(1)} %bitcast.37), channel_id=1, source_target_pairs={{0,128},{64,192},{128,0},{192,64},{1,129},{65,193},{129,1},{193,65... | collective-permute-start | bytes 196616 | tf_op jit(solution)/shard_map/gather_heads/ppermute | solution.py:30
  87.2 6.9 %collective-permute-start.10 = (bf16[16,8192]{1,0:T(8,128)(2,1)S(1)}, bf16[16,8192]{1,0:T(8,128)(2,1)S(1)}, u32[]{:S(2)}, u32[]{:S(2)}) collective-permute-start(bf16[16,8192]{1,0:T(8,128)(2,1)S(1)} %get-tuple-element.22.refs_0_), channel_id=1, source_target_pairs={{0,4},{2,6},{4,0},{6,2},{1,5},{3,7},{5,1},{7,3},{8,12},{10,14},{12... | collective-permute-start | bytes 786440 | tf_op jit(solution)/shard_map/gather_heads/ppermute | solution.py:30
  88.3 15.6 %collective-permute-start.11 = (bf16[16,8192]{1,0:T(8,128)(2,1)S(1)}, bf16[16,8192]{1,0:T(8,128)(2,1)S(1)}, u32[]{:S(2)}, u32[]{:S(2)}) collective-permute-start(bf16[16,8192]{1,0:T(8,128)(2,1)S(1)} %get-tuple-element.22.refs_0_), channel_id=1, source_target_pairs={{0,6},{2,4},{4,2},{6,0},{1,7},{3,5},{5,3},{7,1},{8,14},{10,12},{12... | collective-permute-start | bytes 786440 | tf_op jit(solution)/shard_map/gather_heads/ppermute | solution.py:30
  89.8 14.1 %collective-permute-start.12 = (bf16[64,2048]{1,0:T(8,128)(2,1)S(1)}, bf16[64,2048]{1,0:T(8,128)(2,1)S(1)}, u32[]{:S(2)}, u32[]{:S(2)}) collective-permute-start(bf16[64,2048]{1,0:T(8,128)(2,1)S(1)} %get-tuple-element.23.refs_4_), channel_id=1, source_target_pairs={{0,64},{64,0},{128,192},{192,128},{1,65},{65,1},{129,193},{193,129... | collective-permute-start | bytes 786440 | tf_op jit(solution)/shard_map/gather_heads/ppermute | solution.py:30
  90.0 13.9 %collective-permute-start.13 = (bf16[64,2048]{1,0:T(8,128)(2,1)S(1)}, bf16[64,2048]{1,0:T(8,128)(2,1)S(1)}, u32[]{:S(2)}, u32[]{:S(2)}) collective-permute-start(bf16[64,2048]{1,0:T(8,128)(2,1)S(1)} %get-tuple-element.23.refs_4_), channel_id=1, source_target_pairs={{0,128},{64,192},{128,0},{192,64},{1,129},{65,193},{129,1},{193,65... | collective-permute-start | bytes 786440 | tf_op jit(solution)/shard_map/gather_heads/ppermute | solution.py:30
  92.6 11.3 %collective-permute-start.14 = (bf16[64,2048]{1,0:T(8,128)(2,1)S(1)}, bf16[64,2048]{1,0:T(8,128)(2,1)S(1)}, u32[]{:S(2)}, u32[]{:S(2)}) collective-permute-start(bf16[64,2048]{1,0:T(8,128)(2,1)S(1)} %get-tuple-element.23.refs_4_), channel_id=1, source_target_pairs={{0,192},{64,128},{128,64},{192,0},{1,193},{65,129},{129,65},{193,1... | collective-permute-start | bytes 786440 | tf_op jit(solution)/shard_map/gather_heads/ppermute | solution.py:30
  94.1 9.8 %collective-permute-start.9 = (bf16[16,8192]{1,0:T(8,128)(2,1)S(1)}, bf16[16,8192]{1,0:T(8,128)(2,1)S(1)}, u32[]{:S(2)}, u32[]{:S(2)}) collective-permute-start(bf16[16,8192]{1,0:T(8,128)(2,1)S(1)} %get-tuple-element.22.refs_0_), channel_id=1, source_target_pairs={{0,2},{2,0},{4,6},{6,4},{1,3},{3,1},{5,7},{7,5},{8,10},{10,8},{12,... | collective-permute-start | bytes 786440 | tf_op jit(solution)/shard_map/gather_heads/ppermute | solution.py:30
  103.9 11.5 %collective-permute-start.15 = (bf16[16,8192]{1,0:T(8,128)(2,1)S(1)}, bf16[16,8192]{1,0:T(8,128)(2,1)S(1)}, u32[]{:S(2)}, u32[]{:S(2)}) collective-permute-start(bf16[16,8192]{1,0:T(8,128)(2,1)S(1)} %get-tuple-element.25.refs_0_), channel_id=1, source_target_pairs={{0,1},{1,0},{2,3},{3,2},{4,5},{5,4},{6,7},{7,6},{8,9},{9,8},{10,11... | collective-permute-start | bytes 786440 | tf_op jit(solution)/shard_map/gather_heads/ppermute | solution.py:30
  150.2 7.6 %collective-permute-start.24 = (bf16[16,8192]{1,0:T(8,128)(2,1)S(1)}, bf16[16,8192]{1,0:T(8,128)(2,1)S(1)}, u32[]{:S(2)}, u32[]{:S(2)}) collective-permute-start(bf16[16,8192]{1,0:T(8,128)(2,1)S(1)} %get-tuple-element.43), channel_id=1, source_target_pairs={{0,2},{2,0},{4,6},{6,4},{1,3},{3,1},{5,7},{7,5},{8,10},{10,8},{12,... | collective-permute-start | bytes 786440 | tf_op jit(solution)/shard_map/reduce_grad/ppermute | solution.py:30
  150.6 13.6 %collective-permute-start.25 = (bf16[16,8192]{1,0:T(8,128)(2,1)S(1)}, bf16[16,8192]{1,0:T(8,128)(2,1)S(1)}, u32[]{:S(2)}, u32[]{:S(2)}) collective-permute-start(bf16[16,8192]{1,0:T(8,128)(2,1)S(1)} %get-tuple-element.45), channel_id=1, source_target_pairs={{0,4},{2,6},{4,0},{6,2},{1,5},{3,7},{5,1},{7,3},{8,12},{10,14},{12... | collective-permute-start | bytes 786440 | tf_op jit(solution)/shard_map/reduce_grad/ppermute | solution.py:30
  152.5 13.7 %collective-permute-start.26 = (bf16[16,8192]{1,0:T(8,128)(2,1)S(1)}, bf16[16,8192]{1,0:T(8,128)(2,1)S(1)}, u32[]{:S(2)}, u32[]{:S(2)}) collective-permute-start(bf16[16,8192]{1,0:T(8,128)(2,1)S(1)} %get-tuple-element.44), channel_id=1, source_target_pairs={{0,6},{2,4},{4,2},{6,0},{1,7},{3,5},{5,3},{7,1},{8,14},{10,12},{12... | collective-permute-start | bytes 786440 | tf_op jit(solution)/shard_map/reduce_grad/ppermute | solution.py:30
  154.2 14.3 %collective-permute-start.30 = (bf16[64,2048]{1,0:T(8,128)(2,1)S(1)}, bf16[64,2048]{1,0:T(8,128)(2,1)S(1)}, u32[]{:S(2)}, u32[]{:S(2)}) collective-permute-start(bf16[64,2048]{1,0:T(8,128)(2,1)S(1)} %get-tuple-element.46), channel_id=1, source_target_pairs={{0,64},{64,0},{128,192},{192,128},{1,65},{65,1},{129,193},{193,129... | collective-permute-start | bytes 786440 | tf_op jit(solution)/shard_map/reduce_grad/ppermute | solution.py:30
  154.6 15.7 %collective-permute-start.31 = (bf16[64,2048]{1,0:T(8,128)(2,1)S(1)}, bf16[64,2048]{1,0:T(8,128)(2,1)S(1)}, u32[]{:S(2)}, u32[]{:S(2)}) collective-permute-start(bf16[64,2048]{1,0:T(8,128)(2,1)S(1)} %get-tuple-element.48), channel_id=1, source_target_pairs={{0,128},{64,192},{128,0},{192,64},{1,129},{65,193},{129,1},{193,65... | collective-permute-start | bytes 786440 | tf_op jit(solution)/shard_map/reduce_grad/ppermute | solution.py:30
  157.8 14.4 %collective-permute-start.32 = (bf16[64,2048]{1,0:T(8,128)(2,1)S(1)}, bf16[64,2048]{1,0:T(8,128)(2,1)S(1)}, u32[]{:S(2)}, u32[]{:S(2)}) collective-permute-start(bf16[64,2048]{1,0:T(8,128)(2,1)S(1)} %get-tuple-element.47), channel_id=1, source_target_pairs={{0,192},{64,128},{128,64},{192,0},{1,193},{65,129},{129,65},{193,1... | collective-permute-start | bytes 786440 | tf_op jit(solution)/shard_map/reduce_grad/ppermute | solution.py:30
  166.4 7.6 %collective-permute-start.27 = (bf16[16,2048]{1,0:T(8,128)(2,1)S(1)}, bf16[16,2048]{1,0:T(8,128)(2,1)S(1)}, u32[]{:S(2)}, u32[]{:S(2)}) collective-permute-start(bf16[16,2048]{1,0:T(8,128)(2,1)S(1)} %get-tuple-element.52), channel_id=1, source_target_pairs={{0,64},{64,0},{128,192},{192,128},{1,65},{65,1},{129,193},{193,129... | collective-permute-start | bytes 196616 | tf_op jit(solution)/shard_map/reduce_grad/ppermute | solution.py:30
  166.8 9.6 %collective-permute-start.28 = (bf16[16,2048]{1,0:T(8,128)(2,1)S(1)}, bf16[16,2048]{1,0:T(8,128)(2,1)S(1)}, u32[]{:S(2)}, u32[]{:S(2)}) collective-permute-start(bf16[16,2048]{1,0:T(8,128)(2,1)S(1)} %get-tuple-element.54), channel_id=1, source_target_pairs={{0,128},{64,192},{128,0},{192,64},{1,129},{65,193},{129,1},{193,65... | collective-permute-start | bytes 196616 | tf_op jit(solution)/shard_map/reduce_grad/ppermute | solution.py:30
  168.5 7.9 %collective-permute-start.29 = (bf16[16,2048]{1,0:T(8,128)(2,1)S(1)}, bf16[16,2048]{1,0:T(8,128)(2,1)S(1)}, u32[]{:S(2)}, u32[]{:S(2)}) collective-permute-start(bf16[16,2048]{1,0:T(8,128)(2,1)S(1)} %get-tuple-element.53), channel_id=1, source_target_pairs={{0,192},{64,128},{128,64},{192,0},{1,193},{65,129},{129,65},{193,1... | collective-permute-start | bytes 196616 | tf_op jit(solution)/shard_map/reduce_grad/ppermute | solution.py:30
  189.7 15.7 %all-to-all-start.7 = ((bf16[8,48,256]{2,1,0:T(8,128)(2,1)}), bf16[8,48,256]{2,1,0:T(8,128)(2,1)S(1)}, u32[]{:S(2)}, u32[]{:S(2)}) async-start(bf16[8,48,256]{2,1,0:T(8,128)(2,1)} %broadcast_in_dim.35), calls=%async_computation.7 | async-start | bytes 393216 | tf_op jit(solution)/shard_map/finish/all_to_all | solution.py:22
  (21 other events, 105.9 us)
Sparse Core Ops, SparseCore 0:
  52.3 33.2 all-gather.1

commit v9 on v8

--- a/solution.py
+++ b/solution.py
@@ -28,12 +28,6 @@
 
 def swap(block, axis, step):
     return lax.ppermute(block, axis, [(i, i ^ step) for i in range(SIZES[axis])])
-
-
-def thirds(value):
-    high = lax.reduce_precision(value, 8, 7)
-    middle = lax.reduce_precision(value - high, 8, 7)
-    return jnp.stack([high, middle, value - high - middle])
 
 
 def from_peers(block, axis):
@@ -75,59 +69,66 @@
     return jax.ShapeDtypeStruct(sizes, dtype)
 
 
-def prepare_kernel(place, vocab_ref, awaited_ref, across_ref, down_ref, wide):
+def prepare_kernel(place, vocab_ref, down_ref, done_ref, wide):
     entries, depth = vocab_ref.shape
     width = depth // CHUNKS
+    done_ref[...] = jnp.zeros(done_ref.shape, F32)
     wide[...] = jnp.zeros(wide.shape, F32)
     for at in range(CHUNKS):
         start = pl.multiple_of((place[16] ^ at) * width, width)
         wide[:entries] = vocab_ref[:, pl.ds(start, width)].astype(F32)
-        block = wide[...]
-        across_ref[:, at * width : (at + 1) * width] = block.astype(BF16)
-        down_ref[at * width : (at + 1) * width] = block.T.astype(BF16)
-
-
-def prepare(place, vocab_head, awaited):
+        down_ref[at * width : (at + 1) * width] = wide[...].T.astype(BF16)
+
+
+def prepare(place, vocab_head):
     depth = vocab_head.shape[1]
+    return local_call(
+        prepare_kernel,
+        [shape(depth, PADDED, dtype=BF16), shape(8, 128)],
+        cost(0, 4 * PADDED * depth),
+        [pltpu.VMEM((PADDED, depth // CHUNKS), F32)],
+    )(place, vocab_head)
+
+
+def teacher_kernel(place, target_ref, stored_ref, out_ref, down_ref, total, arrived):
+    width = down_ref.shape[0] // CHUNKS
+    copies = []
+    for at in range(CHUNKS):
+        rows = pl.ds(at * width, width)
+        copies.append(
+            pltpu.make_async_copy(stored_ref.at[rows], down_ref.at[rows], arrived.at[at])
+        )
+        copies[at].start()
+    for at in range(CHUNKS):
+        start = pl.multiple_of((place[16] ^ at) * width, width)
+        copies[at].wait()
+        product = jnp.dot(
+            target_ref[:, pl.ds(start, width)],
+            down_ref[at * width : (at + 1) * width],
+            preferred_element_type=F32,
+        )
+        total[...] = product if at == 0 else total[...] + product
+    for at in range(16):
+        start = pl.multiple_of(place[17 + at] * 16, 16)
+        out_ref[at * 16 : (at + 1) * 16] = total[pl.ds(start, 16)]
+
+
+def teacher_logits(place, target_all, stored):
+    count, depth = target_all.shape
     vmem = pl.BlockSpec(memory_space=pltpu.VMEM)
     return pl.pallas_call(
-        prepare_kernel,
+        teacher_kernel,
         in_specs=[
             pl.BlockSpec(memory_space=pltpu.SMEM),
             vmem,
             pl.BlockSpec(memory_space=pl.ANY),
         ],
         out_specs=[vmem, vmem],
-        out_shape=[shape(PADDED, depth, dtype=BF16), shape(depth, PADDED, dtype=BF16)],
-        scratch_shapes=[pltpu.VMEM((PADDED, depth // CHUNKS), F32)],
+        out_shape=[shape(count, PADDED), shape(*stored.shape, dtype=BF16)],
+        scratch_shapes=[pltpu.VMEM((count, PADDED), F32), pltpu.SemaphoreType.DMA((CHUNKS,))],
         compiler_params=pltpu.CompilerParams(vmem_limit_bytes=LIMIT),
-        cost_estimate=cost(0, 6 * PADDED * depth),
-    )(place, vocab_head, awaited)
-
-
-def teacher_kernel(place, target_ref, down_ref, out_ref, total):
-    width = down_ref.shape[0] // CHUNKS
-    for at in range(CHUNKS):
-        start = pl.multiple_of((place[16] ^ at) * width, width)
-        product = jnp.dot(
-            target_ref[:, pl.ds(start, width)],
-            down_ref[at * width : (at + 1) * width],
-            preferred_element_type=F32,
-        )
-        total[...] = product if at == 0 else total[...] + product
-    for at in range(16):
-        start = pl.multiple_of(place[17 + at] * 16, 16)
-        out_ref[at * 16 : (at + 1) * 16] = total[pl.ds(start, 16)]
-
-
-def teacher_logits(place, target_all, down):
-    count, depth = target_all.shape
-    return local_call(
-        teacher_kernel,
-        shape(count, PADDED),
-        cost(2 * count * PADDED * depth, 2 * (count + PADDED) * depth),
-        [pltpu.VMEM((count, PADDED), F32)],
-    )(place, target_all, down)
+        cost_estimate=cost(2 * count * PADDED * depth, 2 * (count + PADDED) * depth),
+    )(place, target_all, pltpu.with_memory_space_constraint(stored, pltpu.HBM))
 
 
 def student_part(entries, core, firsts, seconds, teacher_ref, down_ref, out_ref):
@@ -200,9 +201,9 @@
     )(place, *blocks, teacher, down, table)
 
 
-def grad_kernel(core, place, teacher_ref, student_ref, logs_ref, across_ref, out_ref, table, turned):
+def grad_kernel(core, place, teacher_ref, student_ref, logs_ref, vocab_ref, out_ref, table, turned):
     rows, depth = out_ref.shape
-    width = depth // CHUNKS
+    entries, width = vocab_ref.shape[0], depth // CHUNKS
     table[...] = jnp.concatenate(
         [logs_ref[...], jnp.zeros((120, 2 * rows), F32)], axis=0
     ).T
@@ -211,22 +212,51 @@
         turned[at * 16 : (at + 1) * 16] = table[pl.ds(start, 16)]
     student = jnp.exp(student_ref[...] - turned[:, 1:2])
     teacher = jnp.exp(teacher_ref[core * rows : (core + 1) * rows] - turned[:, 0:1])
-    grad = (student - teacher).astype(BF16)
+    grad = (student - teacher)[:, :entries].astype(BF16)
     for at in range(CHUNKS):
-        columns = slice(at * width, (at + 1) * width)
-        out_ref[:, columns] = jnp.dot(
-            grad, across_ref[:, columns], preferred_element_type=F32
+        start = pl.multiple_of((place[16] ^ at) * width, width)
+        out_ref[:, at * width : (at + 1) * width] = jnp.dot(
+            grad, vocab_ref[:, pl.ds(start, width)], preferred_element_type=F32
         ).astype(BF16)
 
 
-def grad_rows(core, place, teacher, student, logs, across):
-    rows, depth = student.shape[0], across.shape[1]
+def grad_rows(core, place, teacher, student, logs, vocab_head):
+    rows, depth = student.shape[0], vocab_head.shape[1]
     return local_call(
         functools.partial(grad_kernel, core),
         shape(rows, depth, dtype=BF16),
-        cost(2 * rows * across.size, 2 * across.size, 2 * rows * PADDED),
+        cost(2 * rows * vocab_head.size, 2 * vocab_head.size, 2 * rows * PADDED),
         [pltpu.VMEM((2 * rows, 128), F32), pltpu.VMEM((rows, 128), F32)],
-    )(place, teacher, student, logs, across)
+    )(place, teacher, student, logs, vocab_head)
+
+
+def finish_kernel(parts_ref, preact_ref, out_ref):
+    grad_heads = parts_ref[0].astype(F32)
+    for at in range(1, parts_ref.shape[0]):
+        grad_heads = grad_heads + parts_ref[at].astype(F32)
+    preact = preact_ref[...]
+    sigma = jax.nn.sigmoid(preact)
+    grad_pre = grad_heads * (sigma * (1.0 + preact * (1.0 - sigma)))
+    total = jnp.sum(grad_pre, axis=0, keepdims=True)
+    high = total.astype(BF16).astype(F32)
+    middle = (total - high).astype(BF16).astype(F32)
+    row = lax.broadcasted_iota(jnp.int32, (16, grad_pre.shape[1]), 0)
+    extra = jnp.where(row == 0, high, jnp.where(row == 1, middle, total - high - middle))
+    extra = jnp.where(row < 3, extra, 0.0).astype(BF16)
+    for at in range(out_ref.shape[0]):
+        out_ref[at, : grad_pre.shape[0]] = grad_pre.astype(BF16)
+        out_ref[at, grad_pre.shape[0] :] = extra
+
+
+def finished(parts, preact):
+    rows, across = preact.shape
+    return local_call(
+        finish_kernel,
+        shape(8, rows + 16, across, dtype=BF16),
+        cost(0, 4 * parts.size),
+        limit=4 * 1024 * 1024,
+        scalars=False,
+    )(parts, preact)
 
 
 def pass_kernel(*refs):
@@ -366,7 +396,7 @@
     first, second = summed(first, "y"), summed(second, "x")
     lines = jnp.concatenate([first, second], axis=0)
     sent = lines.reshape(2 * block, 8, -1).transpose(1, 0, 2)
-    return jnp.sum(exchange(sent, "z").astype(F32), axis=0)
+    return exchange(sent, "z")
 
 
 def shards(log_hidden, positions, offsets, head_weight, head_bias, vocab_head):
@@ -380,6 +410,12 @@
     taken = jnp.concatenate([positions, positions + offsets])
     taken = jnp.take(log_hidden, taken, axis=0, mode="clip")
     inputs = taken[:own]
+    steps = jnp.arange(16)
+    order = ((at_x ^ (steps % 4)) * 2 + (at_c ^ (steps // 8))) * 2 + (steps // 4) % 2
+    target_order = (order // 4 ^ at_y) * 4 + order % 4
+    place = jnp.concatenate([order, at_y[None], target_order]).astype(jnp.int32)
+    with jax.named_scope("prepare"):
+        stored, done = prepare(place, vocab_head)
     with jax.named_scope("gather_z"):
         blocks = lax.dynamic_slice_in_dim(
             taken.reshape(2, own, -1), voc_index * in_width, in_width, 2
@@ -393,7 +429,8 @@
             ],
             axis=2,
         )
-        lines = exchange(sent, "z").reshape(8 * own, -1)
+        (lines,) = settled([exchange(sent, "z")], done)
+        lines = lines.reshape(8 * own, -1)
         input_lines, target_lines = lines[:, :in_width], lines[:, in_width : 2 * in_width]
         input_cols = lines[:, 2 * in_width :].reshape(-1, 4, out_width).transpose(1, 0, 2)
     with jax.named_scope("gather_inputs"):
@@ -411,15 +448,10 @@
     with jax.named_scope("gather_targets"):
         target_rows = stacked(from_peers(target_lines, "y"), partial_pre)
         target_all = lax.all_gather(target_rows, VOC, axis=1, tiled=True)
-    steps = jnp.arange(16)
-    order = ((at_x ^ (steps % 4)) * 2 + (at_c ^ (steps // 8))) * 2 + (steps // 4) % 2
-    target_order = (order // 4 ^ at_y) * 4 + order % 4
-    place = jnp.concatenate([order, at_y[None], target_order]).astype(jnp.int32)
     with jax.named_scope("gather_heads"):
         lines = gather_lines(heads)
     with jax.named_scope("teacher"):
-        across, down = prepare(place, vocab_head, target_all)
-        teacher = teacher_logits(place, target_all, down)
+        teacher, down = teacher_logits(place, target_all, stored)
     with jax.named_scope("gather_heads"):
         own_blocks, other_blocks = gather_heads(lines, target_all, teacher)
     with jax.named_scope("student"):
@@ -431,18 +463,12 @@
         logs = totalled(log_kernel, exchange(sums, "z"), 8, count)
         loss = jnp.sum(logs[2]) / count
     with jax.named_scope("grad"):
-        other_rows = grad_rows(1, place, teacher, other_logits, logs, across)
-        own_rows = grad_rows(0, place, teacher, own_logits, logs, across)
+        other_rows = grad_rows(1, place, teacher, other_logits, logs, vocab_head)
+        own_rows = grad_rows(0, place, teacher, own_logits, logs, vocab_head)
     with jax.named_scope("reduce_grad"):
-        grad_heads = scatter_grad(own_rows, other_rows)
+        grad_parts = scatter_grad(own_rows, other_rows)
     with jax.named_scope("finish"):
-        sigma = jax.nn.sigmoid(preact)
-        grad_pre = grad_heads * (sigma * (1.0 + preact * (1.0 - sigma)))
-        bias_part = thirds(jnp.sum(grad_pre, axis=0))
-        sent = jnp.concatenate(
-            [grad_pre, bias_part, jnp.zeros((13, out_width), F32)], axis=0
-        ).astype(BF16)
-        got = gathered(sent, VOC, vocs)
+        got = exchange(finished(grad_parts, preact), VOC)
         grad_all = got[:, :rows].reshape(count, out_width)
         grad_bias = jnp.sum(got[:, rows : rows + 3].astype(F32), axis=(0, 1))
         grad_weight = lax.dot_general(

time: 216 us -> 213 us (0.986)
  blocking collectives: 65.1 us -> 48.1 us
  waiting for transfers between devices: 38.2 us -> 44.3 us
  local copies, waits for them, and re-layouts: 5.42 us -> 7.87 us
  Pallas kernels: 14.7 us -> 17.1 us
  starting transfers between devices: 68.8 us -> 71.1 us
    all_to_all x5 -> x4, blocking collectives: 65.1 us -> 48.1 us  [exchange(): return lax.all_to_all(blocks, axis, split_axis=0, concat_axis=0, tiled=True)]
    all_to_all x3 -> x4, starting transfers between devices: 21.6 us -> 29.3 us  [exchange(): return lax.all_to_all(blocks, axis, split_axis=0, concat_axis=0, tiled=True)]
    all_to_all x3 -> x4, waiting for transfers between devices: 15.4 us -> 21 us  [exchange(): return lax.all_to_all(blocks, axis, split_axis=0, concat_axis=0, tiled=True)]
    ppermute x36, starting transfers between devices: 47.1 us -> 41.8 us  [swap(): lax.ppermute(block, axis, [(i, i ^ step) for i in range(SIZES[axis])])]
    unnamed x11 -> x17, local copies, waits for them, and re-layouts: 3.38 us -> 6.69 us
    pallas_call x8 -> x9, Pallas kernels: 10.5 us -> 11.5 us  [call(): pl.pallas_call(kernel, in_specs=specs, out_specs=jax.tree.map(lambda _: p...]
  transfers between devices with their start and end apart: 40 -> 41, of which waited for: 16 -> 18; matrix products, arithmetic and copies ran while one was open for 1% -> 1% of each run, Pallas kernels for 5% -> 5%
where the time goes in v9:
time: 213 us; the launch traced here: 212 us
  starting transfers between devices  71.1 us (33%)
  blocking collectives  48.1 us (23%)
  waiting for transfers between devices  44.3 us (21%)
  Pallas kernels  17.1 us (8%)
  between operations  16.2 us (8%)
  local copies, waits for them, and re-layouts  7.87 us (4%)
  other arithmetic  5.26 us (2%)
  matrix products  2.33 us (1%)
    all_to_all x4, blocking collectives, exchange(): return lax.all_to_all(blocks, axis, split_axis=0, concat_axis=0, tiled=True)  48.1 us
    ppermute x36, starting transfers between devices, swap(): lax.ppermute(block, axis, [(i, i ^ step) for i in range(SIZES[axis])])  41.8 us
    all_to_all x4, starting transfers between devices, exchange(): return lax.all_to_all(blocks, axis, split_axis=0, concat_axis=0, tiled=True)  29.3 us
    ppermute x36, waiting for transfers between devices, swap(): lax.ppermute(block, axis, [(i, i ^ step) for i in range(SIZES[axis])])  23.2 us
    all_to_all x4, waiting for transfers between devices, exchange(): return lax.all_to_all(blocks, axis, split_axis=0, concat_axis=0, tiled=True)  21 us
    pallas_call x9, Pallas kernels, call(): pl.pallas_call(kernel, in_specs=specs, out_specs=jax.tree.map(lambda _: p...  11.5 us
    unnamed x17, local copies, waits for them, and re-layouts  6.69 us
    pallas_call x1, Pallas kernels, teacher_logits(): pl.pallas_call(teacher_kernel, in_specs=[pl.BlockSpec(memory_space=pltpu....  4.78 us
  transfers between devices with their start and end apart: 41, of which 18 were waited for; matrix products, arithmetic and copies ran while one was open for 1% of the time, Pallas kernels for 5%

profile of v9, /device:TPU:1, one launch (start us, length us, event | category | flops | bytes accessed | tf_op | source)
XLA Modules:
  0.0 212.3 jit_solution(8206928020246725853)
XLA Ops:
  10.3 9.0 %all-to-all-start = ((bf16[8,8,3072]{2,1,0:T(8,128)(2,1)}), bf16[8,8,3072]{2,1,0:T(8,128)(2,1)S(1)}, u32[]{:S(2)}, u32[]{:S(2)}) async-start(bf16[8,8,3072]{2,1,0:T(8,128)(2,1)} %pad_maximum_fusion.1), calls=%async_computation | async-start | bytes 786432 | tf_op jit(solution)/shard_map/gather_z/all_to_all | solution.py:22
  19.4 3.3 %copy-done.1 = bf16[501,8192]{1,0:T(8,128)(2,1)S(1)} copy-done((bf16[501,8192]{1,0:T(8,128)(2,1)S(1)}, bf16[501,8192]{1,0:T(8,128)(2,1)}, u32[]{:S(2)}) %copy-start.1) | copy-done | bytes 8208408
  22.7 3.2 %prepare.1 = (bf16[8192,512]{1,0:T(8,128)(2,1)S(1)}, f32[8,128]{1,0:T(8,128)S(1)}) custom-call(s32[33]{0:T(128)S(1)} %pad_add_fusion.place, bf16[501,8192]{1,0:T(8,128)(2,1)S(1)} %copy-done.1), custom_call_target="tpu_custom_call" | custom-call | bytes 16777216 | tf_op jit(solution)/shard_map/prepare/pallas_call | solution.py:55
  25.9 3.3 %copy-done.3 = bf16[8192,512]{1,0:T(8,128)(2,1)} copy-done((bf16[8192,512]{1,0:T(8,128)(2,1)}, bf16[8192,512]{1,0:T(8,128)(2,1)S(1)}, u32[]{:S(2)}) %copy-start.3) | copy-done | bytes 8388632
  29.2 4.3 %all-to-all-done.refs_0_ = bf16[8,8,3072]{2,1,0:T(8,128)(2,1)S(1)} async-done(((bf16[8,8,3072]{2,1,0:T(8,128)(2,1)}), bf16[8,8,3072]{2,1,0:T(8,128)(2,1)S(1)}, u32[]{:S(2)}, u32[]{:S(2)}) %all-to-all-start) | async-done | bytes 393248 | tf_op jit(solution)/shard_map/gather_z/all_to_all | solution.py:22
  34.6 4.2 %all-to-all-start.1 = ((bf16[4,64,1280]{2,1,0:T(8,128)(2,1)}), bf16[4,64,1280]{2,1,0:T(8,128)(2,1)S(1)}, u32[]{:S(2)}, u32[]{:S(2)}) async-start(bf16[4,64,1280]{2,1,0:T(8,128)(2,1)} %pad_maximum_fusion), calls=%async_computation.1 | async-start | bytes 1310720 | tf_op jit(solution)/shard_map/gather_inputs/all_to_all | solution.py:22
  38.8 2.7 %collective-permute-start.8 = (bf16[64,1024]{1,0:T(8,128)(2,1)S(1)}, bf16[64,1024]{1,0:T(8,128)(2,1)S(1)}, u32[]{:S(2)}, u32[]{:S(2)}) collective-permute-start(bf16[64,1024]{1,0:T(8,128)(2,1)S(1)} %get-tuple-element.51.refs_0_), channel_id=1, source_target_pairs={{0,192},{64,128},{128,64},{192,0},{1,193},{65,129},{129,65},{193,1... | collective-permute-start | bytes 393224 | tf_op jit(solution)/shard_map/gather_targets/ppermute | solution.py:30
  42.1 5.6 %all-to-all-done.1 = bf16[4,64,1280]{2,1,0:T(8,128)(2,1)S(1)} async-done(((bf16[4,64,1280]{2,1,0:T(8,128)(2,1)}), bf16[4,64,1280]{2,1,0:T(8,128)(2,1)S(1)}, u32[]{:S(2)}, u32[]{:S(2)}) %all-to-all-start.1) | async-done | bytes 655392 | tf_op jit(solution)/shard_map/gather_inputs/all_to_all | solution.py:22
  48.8 2.6 %collective-permute-done.8.refs_3_ = bf16[64,1024]{1,0:T(8,128)(2,1)S(1)} collective-permute-done((bf16[64,1024]{1,0:T(8,128)(2,1)S(1)}, bf16[64,1024]{1,0:T(8,128)(2,1)S(1)}, u32[]{:S(2)}, u32[]{:S(2)}) %collective-permute-start.8) | collective-permute-done | bytes 131104 | tf_op jit(solution)/shard_map/gather_targets/ppermute | solution.py:30
  52.9 8.2 %all-to-all-start.2 = ((f32[8,32,256]{2,1,0:T(8,128)}), f32[8,32,256]{2,1,0:T(8,128)S(1)}, u32[]{:S(2)}, u32[]{:S(2)}) async-start(f32[8,32,256]{2,1,0:T(8,128)} %bitcast.10), calls=%async_computation.2 | async-start | bytes 524288 | tf_op jit(solution)/shard_map/head/all_to_all | solution.py:22
  61.1 6.5 %all-to-all-done.2.parts_ref = f32[8,32,256]{2,1,0:T(8,128)S(1)} async-done(((f32[8,32,256]{2,1,0:T(8,128)}), f32[8,32,256]{2,1,0:T(8,128)S(1)}, u32[]{:S(2)}, u32[]{:S(2)}) %all-to-all-start.2) | async-done | bytes 262176 | tf_op jit(solution)/shard_map/head/all_to_all | solution.py:22
  67.6 10.1 %all_to_all.40 = bf16[8,32,256]{2,1,0:T(8,128)(2,1)S(1)} all-to-all(bf16[8,32,256]{2,1,0:T(8,128)(2,1)S(1)} %get-tuple-element.24), channel_id=1, replica_groups=mesh['y'=4,'z'=8,'x'=4,'c'=2] {'z'}, dimensions={0} | all-to-all | bytes 262144 | tf_op jit(solution)/shard_map/gather_heads/all_to_all | solution.py:22
  90.4 3.6 %collective-permute-start.14 = (bf16[64,2048]{1,0:T(8,128)(2,1)S(1)}, bf16[64,2048]{1,0:T(8,128)(2,1)S(1)}, u32[]{:S(2)}, u32[]{:S(2)}) collective-permute-start(bf16[64,2048]{1,0:T(8,128)(2,1)S(1)} %get-tuple-element.26.refs_4_), channel_id=1, source_target_pairs={{0,192},{64,128},{128,64},{192,0},{1,193},{65,129},{129,65},{193,1... | collective-permute-start | bytes 786440 | tf_op jit(solution)/shard_map/gather_heads/ppermute | solution.py:30
  94.4 2.8 %collective-permute-done.11.refs_3_ = bf16[16,8192]{1,0:T(8,128)(2,1)S(1)} collective-permute-done((bf16[16,8192]{1,0:T(8,128)(2,1)S(1)}, bf16[16,8192]{1,0:T(8,128)(2,1)S(1)}, u32[]{:S(2)}, u32[]{:S(2)}) %collective-permute-start.11) | collective-permute-done | bytes 262176 | tf_op jit(solution)/shard_map/gather_heads/ppermute | solution.py:30
  97.2 6.8 %collective-permute-start.12 = (bf16[64,2048]{1,0:T(8,128)(2,1)S(1)}, bf16[64,2048]{1,0:T(8,128)(2,1)S(1)}, u32[]{:S(2)}, u32[]{:S(2)}) collective-permute-start(bf16[64,2048]{1,0:T(8,128)(2,1)S(1)} %get-tuple-element.26.refs_4_), channel_id=1, source_target_pairs={{0,64},{64,0},{128,192},{192,128},{1,65},{65,1},{129,193},{193,129... | collective-permute-start | bytes 786440 | tf_op jit(solution)/shard_map/gather_heads/ppermute | solution.py:30
  104.0 4.8 %teacher.1 = (f32[256,512]{1,0:T(8,128)S(1)}, bf16[8192,512]{1,0:T(8,128)(2,1)S(1)}) custom-call(s32[33]{0:T(128)S(1)} %pad_add_fusion.place, bf16[256,8192]{1,0:T(8,128)(2,1)S(1)} %copy-done.2, bf16[8192,512]{1,0:T(8,128)(2,1)} %copy-done.3), custom_call_target="tpu_custom_call" | custom-call | flops 2147483648 | bytes 12582912 | tf_op jit(solution)/shard_map/teacher/pallas_call | solution.py:119
  117.0 12.6 %all_to_all.41.parts_ref = f32[32,8,128]{2,1,0:T(8,128)S(1)} all-to-all(f32[32,8,128]{2,1,0:T(8,128)S(1)} %get-tuple-element.39), channel_id=1, replica_groups=mesh['y'=4,'z'=8,'x'=4,'c'=2] {'y','x','c'}, dimensions={0} | all-to-all | bytes 262144 | tf_op jit(solution)/shard_map/totals/all_to_all | solution.py:22
  129.6 15.1 %all_to_all.42.parts_ref = f32[8,8,128]{2,1,0:T(8,128)S(1)} all-to-all(f32[8,8,128]{2,1,0:T(8,128)S(1)} %totals.2), channel_id=1, replica_groups=mesh['y'=4,'z'=8,'x'=4,'c'=2] {'z'}, dimensions={0} | all-to-all | bytes 65536 | tf_op jit(solution)/shard_map/totals/all_to_all | solution.py:22
  157.8 3.0 %collective-permute-done.30 = bf16[64,2048]{1,0:T(8,128)(2,1)S(1)} collective-permute-done((bf16[64,2048]{1,0:T(8,128)(2,1)S(1)}, bf16[64,2048]{1,0:T(8,128)(2,1)S(1)}, u32[]{:S(2)}, u32[]{:S(2)}) %collective-permute-start.30) | collective-permute-done | bytes 262176 | tf_op jit(solution)/shard_map/reduce_grad/ppermute | solution.py:30
  162.6 4.4 %collective-permute-done.31 = bf16[64,2048]{1,0:T(8,128)(2,1)S(1)} collective-permute-done((bf16[64,2048]{1,0:T(8,128)(2,1)S(1)}, bf16[64,2048]{1,0:T(8,128)(2,1)S(1)}, u32[]{:S(2)}, u32[]{:S(2)}) %collective-permute-start.31) | collective-permute-done | bytes 262176 | tf_op jit(solution)/shard_map/reduce_grad/ppermute | solution.py:30
  175.2 2.2 %collective-permute-done.28 = bf16[16,2048]{1,0:T(8,128)(2,1)S(1)} collective-permute-done((bf16[16,2048]{1,0:T(8,128)(2,1)S(1)}, bf16[16,2048]{1,0:T(8,128)(2,1)S(1)}, u32[]{:S(2)}, u32[]{:S(2)}) %collective-permute-start.28) | collective-permute-done | bytes 65568 | tf_op jit(solution)/shard_map/reduce_grad/ppermute | solution.py:30
  177.5 10.3 %all_to_all.43.parts_ref = bf16[8,32,256]{2,1,0:T(8,128)(2,1)S(1)} all-to-all(bf16[8,32,256]{2,1,0:T(8,128)(2,1)S(1)} %bitcast.53), channel_id=1, replica_groups=mesh['y'=4,'z'=8,'x'=4,'c'=2] {'z'}, dimensions={0} | all-to-all | bytes 262144 | tf_op jit(solution)/shard_map/reduce_grad/all_to_all | solution.py:22
  188.5 7.9 %all-to-all-start.7 = ((bf16[8,48,256]{2,1,0:T(8,128)(2,1)}), bf16[8,48,256]{2,1,0:T(8,128)(2,1)S(1)}, u32[]{:S(2)}, u32[]{:S(2)}) async-start(bf16[8,48,256]{2,1,0:T(8,128)(2,1)} %finish.1), calls=%async_computation.7 | async-start | bytes 393216 | tf_op jit(solution)/shard_map/finish/all_to_all | solution.py:22
  197.7 4.7 %all-to-all-done.7 = bf16[8,48,256]{2,1,0:T(8,128)(2,1)S(1)} async-done(((bf16[8,48,256]{2,1,0:T(8,128)(2,1)}), bf16[8,48,256]{2,1,0:T(8,128)(2,1)S(1)}, u32[]{:S(2)}, u32[]{:S(2)}) %all-to-all-start.7) | async-done | bytes 196640 | tf_op jit(solution)/shard_map/finish/all_to_all | solution.py:22
  (132 shorter events, 55.0 us)
Async XLA Ops:
  10.3 23.2 %all-to-all-start = ((bf16[8,8,3072]{2,1,0:T(8,128)(2,1)}), bf16[8,8,3072]{2,1,0:T(8,128)(2,1)S(1)}, u32[]{:S(2)}, u32[]{:S(2)}) async-start(bf16[8,8,3072]{2,1,0:T(8,128)(2,1)} %pad_maximum_fusion.1), calls=%async_computation | async-start | bytes 786432 | tf_op jit(solution)/shard_map/gather_z/all_to_all | solution.py:22
  34.6 13.1 %all-to-all-start.1 = ((bf16[4,64,1280]{2,1,0:T(8,128)(2,1)}), bf16[4,64,1280]{2,1,0:T(8,128)(2,1)S(1)}, u32[]{:S(2)}, u32[]{:S(2)}) async-start(bf16[4,64,1280]{2,1,0:T(8,128)(2,1)} %pad_maximum_fusion), calls=%async_computation.1 | async-start | bytes 1310720 | tf_op jit(solution)/shard_map/gather_inputs/all_to_all | solution.py:22
  38.8 48.2 %all-gather.2.cloned.1.call-start = ((), (), s32[]{:S(2)}) async-start(), calls=%async_computation.8 | async-start | bytes 4718592 | tf_op jit(solution)/shard_map/gather_targets/all_gather | solution.py:450
  38.8 12.6 %collective-permute-start.8 = (bf16[64,1024]{1,0:T(8,128)(2,1)S(1)}, bf16[64,1024]{1,0:T(8,128)(2,1)S(1)}, u32[]{:S(2)}, u32[]{:S(2)}) collective-permute-start(bf16[64,1024]{1,0:T(8,128)(2,1)S(1)} %get-tuple-element.51.refs_0_), channel_id=1, source_target_pairs={{0,192},{64,128},{128,64},{192,0},{1,193},{65,129},{129,65},{193,1... | collective-permute-start | bytes 393224 | tf_op jit(solution)/shard_map/gather_targets/ppermute | solution.py:30
  41.4 9.9 %collective-permute-start.7 = (bf16[64,1024]{1,0:T(8,128)(2,1)S(1)}, bf16[64,1024]{1,0:T(8,128)(2,1)S(1)}, u32[]{:S(2)}, u32[]{:S(2)}) collective-permute-start(bf16[64,1024]{1,0:T(8,128)(2,1)S(1)} %get-tuple-element.51.refs_0_), channel_id=1, source_target_pairs={{0,128},{64,192},{128,0},{192,64},{1,129},{65,193},{129,1},{193,65... | collective-permute-start | bytes 393224 | tf_op jit(solution)/shard_map/gather_targets/ppermute | solution.py:30
  42.0 10.1 %collective-permute-start.6 = (bf16[64,1024]{1,0:T(8,128)(2,1)S(1)}, bf16[64,1024]{1,0:T(8,128)(2,1)S(1)}, u32[]{:S(2)}, u32[]{:S(2)}) collective-permute-start(bf16[64,1024]{1,0:T(8,128)(2,1)S(1)} %get-tuple-element.51.refs_0_), channel_id=1, source_target_pairs={{0,64},{64,0},{128,192},{192,128},{1,65},{65,1},{129,193},{193,129... | collective-permute-start | bytes 393224 | tf_op jit(solution)/shard_map/gather_targets/ppermute | solution.py:30
  52.9 14.7 %all-to-all-start.2 = ((f32[8,32,256]{2,1,0:T(8,128)}), f32[8,32,256]{2,1,0:T(8,128)S(1)}, u32[]{:S(2)}, u32[]{:S(2)}) async-start(f32[8,32,256]{2,1,0:T(8,128)} %bitcast.10), calls=%async_computation.2 | async-start | bytes 524288 | tf_op jit(solution)/shard_map/head/all_to_all | solution.py:22
  78.5 6.0 %collective-permute-start.1 = (bf16[16,2048]{1,0:T(8,128)(2,1)S(1)}, bf16[16,2048]{1,0:T(8,128)(2,1)S(1)}, u32[]{:S(2)}, u32[]{:S(2)}) collective-permute-start(bf16[16,2048]{1,0:T(8,128)(2,1)S(1)} %bitcast.39), channel_id=1, source_target_pairs={{0,128},{64,192},{128,0},{192,64},{1,129},{65,193},{129,1},{193,65... | collective-permute-start | bytes 196616 | tf_op jit(solution)/shard_map/gather_heads/ppermute | solution.py:30
  87.0 10.2 %collective-permute-start.11 = (bf16[16,8192]{1,0:T(8,128)(2,1)S(1)}, bf16[16,8192]{1,0:T(8,128)(2,1)S(1)}, u32[]{:S(2)}, u32[]{:S(2)}) collective-permute-start(bf16[16,8192]{1,0:T(8,128)(2,1)S(1)} %get-tuple-element.25.refs_0_), channel_id=1, source_target_pairs={{0,6},{2,4},{4,2},{6,0},{1,7},{3,5},{5,3},{7,1},{8,14},{10,12},{12... | collective-permute-start | bytes 786440 | tf_op jit(solution)/shard_map/gather_heads/ppermute | solution.py:30
  88.6 20.2 %collective-permute-start.10 = (bf16[16,8192]{1,0:T(8,128)(2,1)S(1)}, bf16[16,8192]{1,0:T(8,128)(2,1)S(1)}, u32[]{:S(2)}, u32[]{:S(2)}) collective-permute-start(bf16[16,8192]{1,0:T(8,128)(2,1)S(1)} %get-tuple-element.25.refs_0_), channel_id=1, source_target_pairs={{0,4},{2,6},{4,0},{6,2},{1,5},{3,7},{5,1},{7,3},{8,12},{10,14},{12... | collective-permute-start | bytes 786440 | tf_op jit(solution)/shard_map/gather_heads/ppermute | solution.py:30
  90.4 18.4 %collective-permute-start.9 = (bf16[16,8192]{1,0:T(8,128)(2,1)S(1)}, bf16[16,8192]{1,0:T(8,128)(2,1)S(1)}, u32[]{:S(2)}, u32[]{:S(2)}) collective-permute-start(bf16[16,8192]{1,0:T(8,128)(2,1)S(1)} %get-tuple-element.25.refs_0_), channel_id=1, source_target_pairs={{0,2},{2,0},{4,6},{6,4},{1,3},{3,1},{5,7},{7,5},{8,10},{10,8},{12,... | collective-permute-start | bytes 786440 | tf_op jit(solution)/shard_map/gather_heads/ppermute | solution.py:30
  90.4 18.4 %collective-permute-start.14 = (bf16[64,2048]{1,0:T(8,128)(2,1)S(1)}, bf16[64,2048]{1,0:T(8,128)(2,1)S(1)}, u32[]{:S(2)}, u32[]{:S(2)}) collective-permute-start(bf16[64,2048]{1,0:T(8,128)(2,1)S(1)} %get-tuple-element.26.refs_4_), channel_id=1, source_target_pairs={{0,192},{64,128},{128,64},{192,0},{1,193},{65,129},{129,65},{193,1... | collective-permute-start | bytes 786440 | tf_op jit(solution)/shard_map/gather_heads/ppermute | solution.py:30
  94.0 14.8 %collective-permute-start.13 = (bf16[64,2048]{1,0:T(8,128)(2,1)S(1)}, bf16[64,2048]{1,0:T(8,128)(2,1)S(1)}, u32[]{:S(2)}, u32[]{:S(2)}) collective-permute-start(bf16[64,2048]{1,0:T(8,128)(2,1)S(1)} %get-tuple-element.26.refs_4_), channel_id=1, source_target_pairs={{0,128},{64,192},{128,0},{192,64},{1,129},{65,193},{129,1},{193,65... | collective-permute-start | bytes 786440 | tf_op jit(solution)/shard_map/gather_heads/ppermute | solution.py:30
  97.2 12.5 %collective-permute-start.12 = (bf16[64,2048]{1,0:T(8,128)(2,1)S(1)}, bf16[64,2048]{1,0:T(8,128)(2,1)S(1)}, u32[]{:S(2)}, u32[]{:S(2)}) collective-permute-start(bf16[64,2048]{1,0:T(8,128)(2,1)S(1)} %get-tuple-element.26.refs_4_), channel_id=1, source_target_pairs={{0,64},{64,0},{128,192},{192,128},{1,65},{65,1},{129,193},{193,129... | collective-permute-start | bytes 786440 | tf_op jit(solution)/shard_map/gather_heads/ppermute | solution.py:30
  146.8 5.8 %collective-permute-start.23 = (bf16[128,8192]{1,0:T(8,128)(2,1)S(1)}, bf16[128,8192]{1,0:T(8,128)(2,1)S(1)}, u32[]{:S(2)}, u32[]{:S(2)}) collective-permute-start(bf16[128,8192]{1,0:T(8,128)(2,1)S(1)} %grad.3), channel_id=1, source_target_pairs={{0,1},{1,0},{2,3},{3,2},{4,5},{5,4},{6,7},{7,6},{8,9},{9,8},{10,11... | collective-permute-start | bytes 6291464 | tf_op jit(solution)/shard_map/reduce_grad/ppermute | solution.py:30
  153.2 7.6 %collective-permute-start.30 = (bf16[64,2048]{1,0:T(8,128)(2,1)S(1)}, bf16[64,2048]{1,0:T(8,128)(2,1)S(1)}, u32[]{:S(2)}, u32[]{:S(2)}) collective-permute-start(bf16[64,2048]{1,0:T(8,128)(2,1)S(1)} %get-tuple-element.48), channel_id=1, source_target_pairs={{0,64},{64,0},{128,192},{192,128},{1,65},{65,1},{129,193},{193,129... | collective-permute-start | bytes 786440 | tf_op jit(solution)/shard_map/reduce_grad/ppermute | solution.py:30
  153.6 9.0 %collective-permute-start.32 = (bf16[64,2048]{1,0:T(8,128)(2,1)S(1)}, bf16[64,2048]{1,0:T(8,128)(2,1)S(1)}, u32[]{:S(2)}, u32[]{:S(2)}) collective-permute-start(bf16[64,2048]{1,0:T(8,128)(2,1)S(1)} %get-tuple-element.49), channel_id=1, source_target_pairs={{0,192},{64,128},{128,64},{192,0},{1,193},{65,129},{129,65},{193,1... | collective-permute-start | bytes 786440 | tf_op jit(solution)/shard_map/reduce_grad/ppermute | solution.py:30
  154.5 12.5 %collective-permute-start.31 = (bf16[64,2048]{1,0:T(8,128)(2,1)S(1)}, bf16[64,2048]{1,0:T(8,128)(2,1)S(1)}, u32[]{:S(2)}, u32[]{:S(2)}) collective-permute-start(bf16[64,2048]{1,0:T(8,128)(2,1)S(1)} %get-tuple-element.50), channel_id=1, source_target_pairs={{0,128},{64,192},{128,0},{192,64},{1,129},{65,193},{129,1},{193,65... | collective-permute-start | bytes 786440 | tf_op jit(solution)/shard_map/reduce_grad/ppermute | solution.py:30
  156.6 11.8 %collective-permute-start.24 = (bf16[16,8192]{1,0:T(8,128)(2,1)S(1)}, bf16[16,8192]{1,0:T(8,128)(2,1)S(1)}, u32[]{:S(2)}, u32[]{:S(2)}) collective-permute-start(bf16[16,8192]{1,0:T(8,128)(2,1)S(1)} %get-tuple-element.45), channel_id=1, source_target_pairs={{0,2},{2,0},{4,6},{6,4},{1,3},{3,1},{5,7},{7,5},{8,10},{10,8},{12,... | collective-permute-start | bytes 786440 | tf_op jit(solution)/shard_map/reduce_grad/ppermute | solution.py:30
  157.0 13.5 %collective-permute-start.26 = (bf16[16,8192]{1,0:T(8,128)(2,1)S(1)}, bf16[16,8192]{1,0:T(8,128)(2,1)S(1)}, u32[]{:S(2)}, u32[]{:S(2)}) collective-permute-start(bf16[16,8192]{1,0:T(8,128)(2,1)S(1)} %get-tuple-element.46), channel_id=1, source_target_pairs={{0,6},{2,4},{4,2},{6,0},{1,7},{3,5},{5,3},{7,1},{8,14},{10,12},{12... | collective-permute-start | bytes 786440 | tf_op jit(solution)/shard_map/reduce_grad/ppermute | solution.py:30
  160.8 9.7 %collective-permute-start.25 = (bf16[16,8192]{1,0:T(8,128)(2,1)S(1)}, bf16[16,8192]{1,0:T(8,128)(2,1)S(1)}, u32[]{:S(2)}, u32[]{:S(2)}) collective-permute-start(bf16[16,8192]{1,0:T(8,128)(2,1)S(1)} %get-tuple-element.47), channel_id=1, source_target_pairs={{0,4},{2,6},{4,0},{6,2},{1,5},{3,7},{5,1},{7,3},{8,12},{10,14},{12... | collective-permute-start | bytes 786440 | tf_op jit(solution)/shard_map/reduce_grad/ppermute | solution.py:30
  167.6 6.4 %collective-permute-start.35 = (bf16[16,2048]{1,0:T(8,128)(2,1)S(1)}, bf16[16,2048]{1,0:T(8,128)(2,1)S(1)}, u32[]{:S(2)}, u32[]{:S(2)}) collective-permute-start(bf16[16,2048]{1,0:T(8,128)(2,1)S(1)} %get-tuple-element.58), channel_id=1, source_target_pairs={{0,6},{2,4},{4,2},{6,0},{1,7},{3,5},{5,3},{7,1},{8,14},{10,12},{12... | collective-permute-start | bytes 196616 | tf_op jit(solution)/shard_map/reduce_grad/ppermute | solution.py:30
  168.4 5.7 %collective-permute-start.34 = (bf16[16,2048]{1,0:T(8,128)(2,1)S(1)}, bf16[16,2048]{1,0:T(8,128)(2,1)S(1)}, u32[]{:S(2)}, u32[]{:S(2)}) collective-permute-start(bf16[16,2048]{1,0:T(8,128)(2,1)S(1)} %get-tuple-element.59), channel_id=1, source_target_pairs={{0,4},{2,6},{4,0},{6,2},{1,5},{3,7},{5,1},{7,3},{8,12},{10,14},{12... | collective-permute-start | bytes 196616 | tf_op jit(solution)/shard_map/reduce_grad/ppermute | solution.py:30
  188.5 13.8 %all-to-all-start.7 = ((bf16[8,48,256]{2,1,0:T(8,128)(2,1)}), bf16[8,48,256]{2,1,0:T(8,128)(2,1)S(1)}, u32[]{:S(2)}, u32[]{:S(2)}) async-start(bf16[8,48,256]{2,1,0:T(8,128)(2,1)} %finish.1), calls=%async_computation.7 | async-start | bytes 393216 | tf_op jit(solution)/shard_map/finish/all_to_all | solution.py:22
  (25 other events, 180.3 us)
Sparse Core Ops, SparseCore 0:
  53.0 33.8 all-gather.1

commit v10 on v9

--- a/solution.py
+++ b/solution.py
@@ -24,6 +24,10 @@
 
 def gathered(block, axis, count):
     return exchange(jnp.broadcast_to(block[None], (count, *block.shape)), axis)
+
+
+PEERS = (0, 2, 3, 1)
+SETTLED = (*PEERS, *(4 + at for at in PEERS))
 
 
 def swap(block, axis, step):
@@ -310,13 +314,14 @@
 def join_kernel(*refs):
     firsts, seconds, (first_ref, second_ref) = refs[:4], refs[4:8], refs[-2:]
     (rows, width), (block, _) = firsts[0].shape, seconds[0].shape
-    for at in range(4):
-        first_ref[:, at * width : (at + 1) * width] = firsts[at][...]
-        second_ref[at * block : (at + 1) * block] = seconds[at][...]
+    for at, peer in enumerate(PEERS):
+        first_ref[:, peer * width : (peer + 1) * width] = firsts[at][...]
+        second_ref[peer * block : (peer + 1) * block] = seconds[at][...]
 
 
 def join(firsts, seconds, awaited):
     (rows, width), (block, across) = firsts[0].shape, seconds[0].shape
+    firsts, seconds = [firsts[peer] for peer in PEERS], [seconds[peer] for peer in PEERS]
     vmem = pl.BlockSpec(memory_space=pltpu.VMEM)
     return pl.pallas_call(
         join_kernel,
@@ -378,7 +383,9 @@
     first, second = join(
         from_peers(lines[:half], "y"), from_peers(lines[half:], "x"), target_all
     )
-    blocks = settled(from_peers(first, "x") + from_peers(second, "y"), teacher)
+    blocks = from_peers(first, "x") + from_peers(second, "y")
+    blocks = settled([blocks[at] for at in SETTLED], teacher)
+    blocks = [blocks[SETTLED.index(at)] for at in range(8)]
     return blocks, [swap(block, "c", 1) for block in blocks]
 
 

time: 213 us -> 210 us (0.986)
  starting transfers between devices: 71.1 us -> 68.9 us
    ppermute x36, starting transfers between devices: 41.8 us -> 39.6 us  [swap(): lax.ppermute(block, axis, [(i, i ^ step) for i in range(SIZES[axis])])]
where the time goes in v10:
time: 210 us; the launch traced here: 209 us
  starting transfers between devices  68.9 us (33%)
  blocking collectives  47.5 us (23%)
  waiting for transfers between devices  43.7 us (21%)
  Pallas kernels  17.1 us (8%)
  between operations  16.2 us (8%)
  local copies, waits for them, and re-layouts  7.87 us (4%)
  other arithmetic  5.26 us (3%)
  matrix products  2.33 us (1%)
    all_to_all x4, blocking collectives, exchange(): return lax.all_to_all(blocks, axis, split_axis=0, concat_axis=0, tiled=True)  47.5 us
    ppermute x36, starting transfers between devices, swap(): lax.ppermute(block, axis, [(i, i ^ step) for i in range(SIZES[axis])])  39.6 us
    all_to_all x4, starting transfers between devices, exchange(): return lax.all_to_all(blocks, axis, split_axis=0, concat_axis=0, tiled=True)  29.3 us
    ppermute x36, waiting for transfers between devices, swap(): lax.ppermute(block, axis, [(i, i ^ step) for i in range(SIZES[axis])])  22.6 us
    all_to_all x4, waiting for transfers between devices, exchange(): return lax.all_to_all(blocks, axis, split_axis=0, concat_axis=0, tiled=True)  21 us
    pallas_call x9, Pallas kernels, call(): pl.pallas_call(kernel, in_specs=specs, out_specs=jax.tree.map(lambda _: p...  11.5 us
    unnamed x17, local copies, waits for them, and re-layouts  6.69 us
    pallas_call x1, Pallas kernels, teacher_logits(): pl.pallas_call(teacher_kernel, in_specs=[pl.BlockSpec(memory_space=pltpu....  4.78 us
  transfers between devices with their start and end apart: 41, of which 18 were waited for; matrix products, arithmetic and copies ran while one was open for 1% of the time, Pallas kernels for 5%

profile of v10, /device:TPU:1, one launch (start us, length us, event | category | flops | bytes accessed | tf_op | source)
XLA Modules:
  0.0 209.0 jit_solution(15422562895422279767)
XLA Ops:
  10.3 9.0 %all-to-all-start = ((bf16[8,8,3072]{2,1,0:T(8,128)(2,1)}), bf16[8,8,3072]{2,1,0:T(8,128)(2,1)S(1)}, u32[]{:S(2)}, u32[]{:S(2)}) async-start(bf16[8,8,3072]{2,1,0:T(8,128)(2,1)} %pad_maximum_fusion.1), calls=%async_computation | async-start | bytes 786432 | tf_op jit(solution)/shard_map/gather_z/all_to_all | solution.py:22
  19.4 3.3 %copy-done.1 = bf16[501,8192]{1,0:T(8,128)(2,1)S(1)} copy-done((bf16[501,8192]{1,0:T(8,128)(2,1)S(1)}, bf16[501,8192]{1,0:T(8,128)(2,1)}, u32[]{:S(2)}) %copy-start.1) | copy-done | bytes 8208408
  22.7 3.2 %prepare.1 = (bf16[8192,512]{1,0:T(8,128)(2,1)S(1)}, f32[8,128]{1,0:T(8,128)S(1)}) custom-call(s32[33]{0:T(128)S(1)} %pad_add_fusion.place, bf16[501,8192]{1,0:T(8,128)(2,1)S(1)} %copy-done.1), custom_call_target="tpu_custom_call" | custom-call | bytes 16777216 | tf_op jit(solution)/shard_map/prepare/pallas_call | solution.py:59
  25.9 3.3 %copy-done.3 = bf16[8192,512]{1,0:T(8,128)(2,1)} copy-done((bf16[8192,512]{1,0:T(8,128)(2,1)}, bf16[8192,512]{1,0:T(8,128)(2,1)S(1)}, u32[]{:S(2)}) %copy-start.3) | copy-done | bytes 8388632
  29.2 4.3 %all-to-all-done.refs_0_ = bf16[8,8,3072]{2,1,0:T(8,128)(2,1)S(1)} async-done(((bf16[8,8,3072]{2,1,0:T(8,128)(2,1)}), bf16[8,8,3072]{2,1,0:T(8,128)(2,1)S(1)}, u32[]{:S(2)}, u32[]{:S(2)}) %all-to-all-start) | async-done | bytes 393248 | tf_op jit(solution)/shard_map/gather_z/all_to_all | solution.py:22
  34.6 4.2 %all-to-all-start.1 = ((bf16[4,64,1280]{2,1,0:T(8,128)(2,1)}), bf16[4,64,1280]{2,1,0:T(8,128)(2,1)S(1)}, u32[]{:S(2)}, u32[]{:S(2)}) async-start(bf16[4,64,1280]{2,1,0:T(8,128)(2,1)} %pad_maximum_fusion), calls=%async_computation.1 | async-start | bytes 1310720 | tf_op jit(solution)/shard_map/gather_inputs/all_to_all | solution.py:22
  38.8 2.7 %collective-permute-start.8 = (bf16[64,1024]{1,0:T(8,128)(2,1)S(1)}, bf16[64,1024]{1,0:T(8,128)(2,1)S(1)}, u32[]{:S(2)}, u32[]{:S(2)}) collective-permute-start(bf16[64,1024]{1,0:T(8,128)(2,1)S(1)} %get-tuple-element.51.refs_0_), channel_id=1, source_target_pairs={{0,192},{64,128},{128,64},{192,0},{1,193},{65,129},{129,65},{193,1... | collective-permute-start | bytes 393224 | tf_op jit(solution)/shard_map/gather_targets/ppermute | solution.py:34
  42.1 5.6 %all-to-all-done.1 = bf16[4,64,1280]{2,1,0:T(8,128)(2,1)S(1)} async-done(((bf16[4,64,1280]{2,1,0:T(8,128)(2,1)}), bf16[4,64,1280]{2,1,0:T(8,128)(2,1)S(1)}, u32[]{:S(2)}, u32[]{:S(2)}) %all-to-all-start.1) | async-done | bytes 655392 | tf_op jit(solution)/shard_map/gather_inputs/all_to_all | solution.py:22
  48.8 2.6 %collective-permute-done.8.refs_3_ = bf16[64,1024]{1,0:T(8,128)(2,1)S(1)} collective-permute-done((bf16[64,1024]{1,0:T(8,128)(2,1)S(1)}, bf16[64,1024]{1,0:T(8,128)(2,1)S(1)}, u32[]{:S(2)}, u32[]{:S(2)}) %collective-permute-start.8) | collective-permute-done | bytes 131104 | tf_op jit(solution)/shard_map/gather_targets/ppermute | solution.py:34
  52.9 8.2 %all-to-all-start.2 = ((f32[8,32,256]{2,1,0:T(8,128)}), f32[8,32,256]{2,1,0:T(8,128)S(1)}, u32[]{:S(2)}, u32[]{:S(2)}) async-start(f32[8,32,256]{2,1,0:T(8,128)} %bitcast.10), calls=%async_computation.2 | async-start | bytes 524288 | tf_op jit(solution)/shard_map/head/all_to_all | solution.py:22
  61.1 6.5 %all-to-all-done.2.parts_ref = f32[8,32,256]{2,1,0:T(8,128)S(1)} async-done(((f32[8,32,256]{2,1,0:T(8,128)}), f32[8,32,256]{2,1,0:T(8,128)S(1)}, u32[]{:S(2)}, u32[]{:S(2)}) %all-to-all-start.2) | async-done | bytes 262176 | tf_op jit(solution)/shard_map/head/all_to_all | solution.py:22
  67.6 10.1 %all_to_all.40 = bf16[8,32,256]{2,1,0:T(8,128)(2,1)S(1)} all-to-all(bf16[8,32,256]{2,1,0:T(8,128)(2,1)S(1)} %get-tuple-element.24), channel_id=1, replica_groups=mesh['y'=4,'z'=8,'x'=4,'c'=2] {'z'}, dimensions={0} | all-to-all | bytes 262144 | tf_op jit(solution)/shard_map/gather_heads/all_to_all | solution.py:22
  82.2 2.2 %collective-permute-start.3 = (bf16[16,2048]{1,0:T(8,128)(2,1)S(1)}, bf16[16,2048]{1,0:T(8,128)(2,1)S(1)}, u32[]{:S(2)}, u32[]{:S(2)}) collective-permute-start(bf16[16,2048]{1,0:T(8,128)(2,1)S(1)} %bitcast.44), channel_id=1, source_target_pairs={{0,4},{2,6},{4,0},{6,2},{1,5},{3,7},{5,1},{7,3},{8,12},{10,14},{12... | collective-permute-start | bytes 196616 | tf_op jit(solution)/shard_map/gather_heads/ppermute | solution.py:34
  91.8 2.4 %collective-permute-start.13 = (bf16[64,2048]{1,0:T(8,128)(2,1)S(1)}, bf16[64,2048]{1,0:T(8,128)(2,1)S(1)}, u32[]{:S(2)}, u32[]{:S(2)}) collective-permute-start(bf16[64,2048]{1,0:T(8,128)(2,1)S(1)} %get-tuple-element.26.refs_4_), channel_id=1, source_target_pairs={{0,192},{64,128},{128,64},{192,0},{1,193},{65,129},{129,65},{193,1... | collective-permute-start | bytes 786440 | tf_op jit(solution)/shard_map/gather_heads/ppermute | solution.py:34
  96.3 4.8 %teacher.1 = (f32[256,512]{1,0:T(8,128)S(1)}, bf16[8192,512]{1,0:T(8,128)(2,1)S(1)}) custom-call(s32[33]{0:T(128)S(1)} %pad_add_fusion.place, bf16[256,8192]{1,0:T(8,128)(2,1)S(1)} %copy-done.2, bf16[8192,512]{1,0:T(8,128)(2,1)} %copy-done.3), custom_call_target="tpu_custom_call" | custom-call | flops 2147483648 | bytes 12582912 | tf_op jit(solution)/shard_map/teacher/pallas_call | solution.py:123
  101.1 3.0 %collective-permute-done.12.refs_5_ = bf16[64,2048]{1,0:T(8,128)(2,1)S(1)} collective-permute-done((bf16[64,2048]{1,0:T(8,128)(2,1)S(1)}, bf16[64,2048]{1,0:T(8,128)(2,1)S(1)}, u32[]{:S(2)}, u32[]{:S(2)}) %collective-permute-start.12) | collective-permute-done | bytes 262176 | tf_op jit(solution)/shard_map/gather_heads/ppermute | solution.py:34
  104.1 4.5 %collective-permute-start.15 = (bf16[16,8192]{1,0:T(8,128)(2,1)S(1)}, bf16[16,8192]{1,0:T(8,128)(2,1)S(1)}, u32[]{:S(2)}, u32[]{:S(2)}) collective-permute-start(bf16[16,8192]{1,0:T(8,128)(2,1)S(1)} %get-tuple-element.29.refs_0_), channel_id=1, source_target_pairs={{0,1},{1,0},{2,3},{3,2},{4,5},{5,4},{6,7},{7,6},{8,9},{9,8},{10,11... | collective-permute-start | bytes 786440 | tf_op jit(solution)/shard_map/gather_heads/ppermute | solution.py:34
  114.3 12.9 %all_to_all.41.parts_ref = f32[32,8,128]{2,1,0:T(8,128)S(1)} all-to-all(f32[32,8,128]{2,1,0:T(8,128)S(1)} %get-tuple-element.39), channel_id=1, replica_groups=mesh['y'=4,'z'=8,'x'=4,'c'=2] {'y','x','c'}, dimensions={0} | all-to-all | bytes 262144 | tf_op jit(solution)/shard_map/totals/all_to_all | solution.py:22
  127.3 14.2 %all_to_all.42.parts_ref = f32[8,8,128]{2,1,0:T(8,128)S(1)} all-to-all(f32[8,8,128]{2,1,0:T(8,128)S(1)} %totals.2), channel_id=1, replica_groups=mesh['y'=4,'z'=8,'x'=4,'c'=2] {'z'}, dimensions={0} | all-to-all | bytes 65536 | tf_op jit(solution)/shard_map/totals/all_to_all | solution.py:22
  154.5 3.0 %collective-permute-done.30 = bf16[64,2048]{1,0:T(8,128)(2,1)S(1)} collective-permute-done((bf16[64,2048]{1,0:T(8,128)(2,1)S(1)}, bf16[64,2048]{1,0:T(8,128)(2,1)S(1)}, u32[]{:S(2)}, u32[]{:S(2)}) %collective-permute-start.30) | collective-permute-done | bytes 262176 | tf_op jit(solution)/shard_map/reduce_grad/ppermute | solution.py:34
  159.4 4.4 %collective-permute-done.31 = bf16[64,2048]{1,0:T(8,128)(2,1)S(1)} collective-permute-done((bf16[64,2048]{1,0:T(8,128)(2,1)S(1)}, bf16[64,2048]{1,0:T(8,128)(2,1)S(1)}, u32[]{:S(2)}, u32[]{:S(2)}) %collective-permute-start.31) | collective-permute-done | bytes 262176 | tf_op jit(solution)/shard_map/reduce_grad/ppermute | solution.py:34
  174.2 10.3 %all_to_all.43.parts_ref = bf16[8,32,256]{2,1,0:T(8,128)(2,1)S(1)} all-to-all(bf16[8,32,256]{2,1,0:T(8,128)(2,1)S(1)} %bitcast.53), channel_id=1, replica_groups=mesh['y'=4,'z'=8,'x'=4,'c'=2] {'z'}, dimensions={0} | all-to-all | bytes 262144 | tf_op jit(solution)/shard_map/reduce_grad/all_to_all | solution.py:22
  185.2 7.9 %all-to-all-start.7 = ((bf16[8,48,256]{2,1,0:T(8,128)(2,1)}), bf16[8,48,256]{2,1,0:T(8,128)(2,1)S(1)}, u32[]{:S(2)}, u32[]{:S(2)}) async-start(bf16[8,48,256]{2,1,0:T(8,128)(2,1)} %finish.1), calls=%async_computation.7 | async-start | bytes 393216 | tf_op jit(solution)/shard_map/finish/all_to_all | solution.py:22
  194.4 4.7 %all-to-all-done.7 = bf16[8,48,256]{2,1,0:T(8,128)(2,1)S(1)} async-done(((bf16[8,48,256]{2,1,0:T(8,128)(2,1)}), bf16[8,48,256]{2,1,0:T(8,128)(2,1)S(1)}, u32[]{:S(2)}, u32[]{:S(2)}) %all-to-all-start.7) | async-done | bytes 196640 | tf_op jit(solution)/shard_map/finish/all_to_all | solution.py:22
  (132 shorter events, 55.5 us)
Async XLA Ops:
  10.3 23.2 %all-to-all-start = ((bf16[8,8,3072]{2,1,0:T(8,128)(2,1)}), bf16[8,8,3072]{2,1,0:T(8,128)(2,1)S(1)}, u32[]{:S(2)}, u32[]{:S(2)}) async-start(bf16[8,8,3072]{2,1,0:T(8,128)(2,1)} %pad_maximum_fusion.1), calls=%async_computation | async-start | bytes 786432 | tf_op jit(solution)/shard_map/gather_z/all_to_all | solution.py:22
  34.6 13.1 %all-to-all-start.1 = ((bf16[4,64,1280]{2,1,0:T(8,128)(2,1)}), bf16[4,64,1280]{2,1,0:T(8,128)(2,1)S(1)}, u32[]{:S(2)}, u32[]{:S(2)}) async-start(bf16[4,64,1280]{2,1,0:T(8,128)(2,1)} %pad_maximum_fusion), calls=%async_computation.1 | async-start | bytes 1310720 | tf_op jit(solution)/shard_map/gather_inputs/all_to_all | solution.py:22
  38.8 48.3 %all-gather.2.cloned.1.call-start = ((), (), s32[]{:S(2)}) async-start(), calls=%async_computation.8 | async-start | bytes 4718592 | tf_op jit(solution)/shard_map/gather_targets/all_gather | solution.py:457
  38.8 12.6 %collective-permute-start.8 = (bf16[64,1024]{1,0:T(8,128)(2,1)S(1)}, bf16[64,1024]{1,0:T(8,128)(2,1)S(1)}, u32[]{:S(2)}, u32[]{:S(2)}) collective-permute-start(bf16[64,1024]{1,0:T(8,128)(2,1)S(1)} %get-tuple-element.51.refs_0_), channel_id=1, source_target_pairs={{0,192},{64,128},{128,64},{192,0},{1,193},{65,129},{129,65},{193,1... | collective-permute-start | bytes 393224 | tf_op jit(solution)/shard_map/gather_targets/ppermute | solution.py:34
  41.4 9.9 %collective-permute-start.7 = (bf16[64,1024]{1,0:T(8,128)(2,1)S(1)}, bf16[64,1024]{1,0:T(8,128)(2,1)S(1)}, u32[]{:S(2)}, u32[]{:S(2)}) collective-permute-start(bf16[64,1024]{1,0:T(8,128)(2,1)S(1)} %get-tuple-element.51.refs_0_), channel_id=1, source_target_pairs={{0,128},{64,192},{128,0},{192,64},{1,129},{65,193},{129,1},{193,65... | collective-permute-start | bytes 393224 | tf_op jit(solution)/shard_map/gather_targets/ppermute | solution.py:34
  42.0 10.1 %collective-permute-start.6 = (bf16[64,1024]{1,0:T(8,128)(2,1)S(1)}, bf16[64,1024]{1,0:T(8,128)(2,1)S(1)}, u32[]{:S(2)}, u32[]{:S(2)}) collective-permute-start(bf16[64,1024]{1,0:T(8,128)(2,1)S(1)} %get-tuple-element.51.refs_0_), channel_id=1, source_target_pairs={{0,64},{64,0},{128,192},{192,128},{1,65},{65,1},{129,193},{193,129... | collective-permute-start | bytes 393224 | tf_op jit(solution)/shard_map/gather_targets/ppermute | solution.py:34
  52.9 14.7 %all-to-all-start.2 = ((f32[8,32,256]{2,1,0:T(8,128)}), f32[8,32,256]{2,1,0:T(8,128)S(1)}, u32[]{:S(2)}, u32[]{:S(2)}) async-start(f32[8,32,256]{2,1,0:T(8,128)} %bitcast.10), calls=%async_computation.2 | async-start | bytes 524288 | tf_op jit(solution)/shard_map/head/all_to_all | solution.py:22
  77.9 6.5 %collective-permute-start.1 = (bf16[16,2048]{1,0:T(8,128)(2,1)S(1)}, bf16[16,2048]{1,0:T(8,128)(2,1)S(1)}, u32[]{:S(2)}, u32[]{:S(2)}) collective-permute-start(bf16[16,2048]{1,0:T(8,128)(2,1)S(1)} %bitcast.39), channel_id=1, source_target_pairs={{0,192},{64,128},{128,64},{192,0},{1,193},{65,129},{129,65},{193,1... | collective-permute-start | bytes 196616 | tf_op jit(solution)/shard_map/gather_heads/ppermute | solution.py:34
  87.1 7.0 %collective-permute-start.11 = (bf16[16,8192]{1,0:T(8,128)(2,1)S(1)}, bf16[16,8192]{1,0:T(8,128)(2,1)S(1)}, u32[]{:S(2)}, u32[]{:S(2)}) collective-permute-start(bf16[16,8192]{1,0:T(8,128)(2,1)S(1)} %get-tuple-element.25.refs_0_), channel_id=1, source_target_pairs={{0,2},{2,0},{4,6},{6,4},{1,3},{3,1},{5,7},{7,5},{8,10},{10,8},{12,... | collective-permute-start | bytes 786440 | tf_op jit(solution)/shard_map/gather_heads/ppermute | solution.py:34
  88.2 12.9 %collective-permute-start.10 = (bf16[16,8192]{1,0:T(8,128)(2,1)S(1)}, bf16[16,8192]{1,0:T(8,128)(2,1)S(1)}, u32[]{:S(2)}, u32[]{:S(2)}) collective-permute-start(bf16[16,8192]{1,0:T(8,128)(2,1)S(1)} %get-tuple-element.25.refs_0_), channel_id=1, source_target_pairs={{0,6},{2,4},{4,2},{6,0},{1,7},{3,5},{5,3},{7,1},{8,14},{10,12},{12... | collective-permute-start | bytes 786440 | tf_op jit(solution)/shard_map/gather_heads/ppermute | solution.py:34
  89.4 11.6 %collective-permute-start.9 = (bf16[16,8192]{1,0:T(8,128)(2,1)S(1)}, bf16[16,8192]{1,0:T(8,128)(2,1)S(1)}, u32[]{:S(2)}, u32[]{:S(2)}) collective-permute-start(bf16[16,8192]{1,0:T(8,128)(2,1)S(1)} %get-tuple-element.25.refs_0_), channel_id=1, source_target_pairs={{0,4},{2,6},{4,0},{6,2},{1,5},{3,7},{5,1},{7,3},{8,12},{10,14},{12... | collective-permute-start | bytes 786440 | tf_op jit(solution)/shard_map/gather_heads/ppermute | solution.py:34
  90.5 10.6 %collective-permute-start.14 = (bf16[64,2048]{1,0:T(8,128)(2,1)S(1)}, bf16[64,2048]{1,0:T(8,128)(2,1)S(1)}, u32[]{:S(2)}, u32[]{:S(2)}) collective-permute-start(bf16[64,2048]{1,0:T(8,128)(2,1)S(1)} %get-tuple-element.26.refs_4_), channel_id=1, source_target_pairs={{0,64},{64,0},{128,192},{192,128},{1,65},{65,1},{129,193},{193,129... | collective-permute-start | bytes 786440 | tf_op jit(solution)/shard_map/gather_heads/ppermute | solution.py:34
  91.8 9.3 %collective-permute-start.13 = (bf16[64,2048]{1,0:T(8,128)(2,1)S(1)}, bf16[64,2048]{1,0:T(8,128)(2,1)S(1)}, u32[]{:S(2)}, u32[]{:S(2)}) collective-permute-start(bf16[64,2048]{1,0:T(8,128)(2,1)S(1)} %get-tuple-element.26.refs_4_), channel_id=1, source_target_pairs={{0,192},{64,128},{128,64},{192,0},{1,193},{65,129},{129,65},{193,1... | collective-permute-start | bytes 786440 | tf_op jit(solution)/shard_map/gather_heads/ppermute | solution.py:34
  94.1 9.9 %collective-permute-start.12 = (bf16[64,2048]{1,0:T(8,128)(2,1)S(1)}, bf16[64,2048]{1,0:T(8,128)(2,1)S(1)}, u32[]{:S(2)}, u32[]{:S(2)}) collective-permute-start(bf16[64,2048]{1,0:T(8,128)(2,1)S(1)} %get-tuple-element.26.refs_4_), channel_id=1, source_target_pairs={{0,128},{64,192},{128,0},{192,64},{1,129},{65,193},{129,1},{193,65... | collective-permute-start | bytes 786440 | tf_op jit(solution)/shard_map/gather_heads/ppermute | solution.py:34
  143.5 5.8 %collective-permute-start.23 = (bf16[128,8192]{1,0:T(8,128)(2,1)S(1)}, bf16[128,8192]{1,0:T(8,128)(2,1)S(1)}, u32[]{:S(2)}, u32[]{:S(2)}) collective-permute-start(bf16[128,8192]{1,0:T(8,128)(2,1)S(1)} %grad.3), channel_id=1, source_target_pairs={{0,1},{1,0},{2,3},{3,2},{4,5},{5,4},{6,7},{7,6},{8,9},{9,8},{10,11... | collective-permute-start | bytes 6291464 | tf_op jit(solution)/shard_map/reduce_grad/ppermute | solution.py:34
  149.9 7.6 %collective-permute-start.30 = (bf16[64,2048]{1,0:T(8,128)(2,1)S(1)}, bf16[64,2048]{1,0:T(8,128)(2,1)S(1)}, u32[]{:S(2)}, u32[]{:S(2)}) collective-permute-start(bf16[64,2048]{1,0:T(8,128)(2,1)S(1)} %get-tuple-element.48), channel_id=1, source_target_pairs={{0,64},{64,0},{128,192},{192,128},{1,65},{65,1},{129,193},{193,129... | collective-permute-start | bytes 786440 | tf_op jit(solution)/shard_map/reduce_grad/ppermute | solution.py:34
  150.3 9.0 %collective-permute-start.32 = (bf16[64,2048]{1,0:T(8,128)(2,1)S(1)}, bf16[64,2048]{1,0:T(8,128)(2,1)S(1)}, u32[]{:S(2)}, u32[]{:S(2)}) collective-permute-start(bf16[64,2048]{1,0:T(8,128)(2,1)S(1)} %get-tuple-element.49), channel_id=1, source_target_pairs={{0,192},{64,128},{128,64},{192,0},{1,193},{65,129},{129,65},{193,1... | collective-permute-start | bytes 786440 | tf_op jit(solution)/shard_map/reduce_grad/ppermute | solution.py:34
  151.3 12.5 %collective-permute-start.31 = (bf16[64,2048]{1,0:T(8,128)(2,1)S(1)}, bf16[64,2048]{1,0:T(8,128)(2,1)S(1)}, u32[]{:S(2)}, u32[]{:S(2)}) collective-permute-start(bf16[64,2048]{1,0:T(8,128)(2,1)S(1)} %get-tuple-element.50), channel_id=1, source_target_pairs={{0,128},{64,192},{128,0},{192,64},{1,129},{65,193},{129,1},{193,65... | collective-permute-start | bytes 786440 | tf_op jit(solution)/shard_map/reduce_grad/ppermute | solution.py:34
  153.3 11.8 %collective-permute-start.24 = (bf16[16,8192]{1,0:T(8,128)(2,1)S(1)}, bf16[16,8192]{1,0:T(8,128)(2,1)S(1)}, u32[]{:S(2)}, u32[]{:S(2)}) collective-permute-start(bf16[16,8192]{1,0:T(8,128)(2,1)S(1)} %get-tuple-element.45), channel_id=1, source_target_pairs={{0,2},{2,0},{4,6},{6,4},{1,3},{3,1},{5,7},{7,5},{8,10},{10,8},{12,... | collective-permute-start | bytes 786440 | tf_op jit(solution)/shard_map/reduce_grad/ppermute | solution.py:34
  153.7 13.5 %collective-permute-start.26 = (bf16[16,8192]{1,0:T(8,128)(2,1)S(1)}, bf16[16,8192]{1,0:T(8,128)(2,1)S(1)}, u32[]{:S(2)}, u32[]{:S(2)}) collective-permute-start(bf16[16,8192]{1,0:T(8,128)(2,1)S(1)} %get-tuple-element.46), channel_id=1, source_target_pairs={{0,6},{2,4},{4,2},{6,0},{1,7},{3,5},{5,3},{7,1},{8,14},{10,12},{12... | collective-permute-start | bytes 786440 | tf_op jit(solution)/shard_map/reduce_grad/ppermute | solution.py:34
  157.5 9.7 %collective-permute-start.25 = (bf16[16,8192]{1,0:T(8,128)(2,1)S(1)}, bf16[16,8192]{1,0:T(8,128)(2,1)S(1)}, u32[]{:S(2)}, u32[]{:S(2)}) collective-permute-start(bf16[16,8192]{1,0:T(8,128)(2,1)S(1)} %get-tuple-element.47), channel_id=1, source_target_pairs={{0,4},{2,6},{4,0},{6,2},{1,5},{3,7},{5,1},{7,3},{8,12},{10,14},{12... | collective-permute-start | bytes 786440 | tf_op jit(solution)/shard_map/reduce_grad/ppermute | solution.py:34
  164.3 6.4 %collective-permute-start.35 = (bf16[16,2048]{1,0:T(8,128)(2,1)S(1)}, bf16[16,2048]{1,0:T(8,128)(2,1)S(1)}, u32[]{:S(2)}, u32[]{:S(2)}) collective-permute-start(bf16[16,2048]{1,0:T(8,128)(2,1)S(1)} %get-tuple-element.58), channel_id=1, source_target_pairs={{0,6},{2,4},{4,2},{6,0},{1,7},{3,5},{5,3},{7,1},{8,14},{10,12},{12... | collective-permute-start | bytes 196616 | tf_op jit(solution)/shard_map/reduce_grad/ppermute | solution.py:34
  165.1 5.7 %collective-permute-start.34 = (bf16[16,2048]{1,0:T(8,128)(2,1)S(1)}, bf16[16,2048]{1,0:T(8,128)(2,1)S(1)}, u32[]{:S(2)}, u32[]{:S(2)}) collective-permute-start(bf16[16,2048]{1,0:T(8,128)(2,1)S(1)} %get-tuple-element.59), channel_id=1, source_target_pairs={{0,4},{2,6},{4,0},{6,2},{1,5},{3,7},{5,1},{7,3},{8,12},{10,14},{12... | collective-permute-start | bytes 196616 | tf_op jit(solution)/shard_map/reduce_grad/ppermute | solution.py:34
  185.2 13.8 %all-to-all-start.7 = ((bf16[8,48,256]{2,1,0:T(8,128)(2,1)}), bf16[8,48,256]{2,1,0:T(8,128)(2,1)S(1)}, u32[]{:S(2)}, u32[]{:S(2)}) async-start(bf16[8,48,256]{2,1,0:T(8,128)(2,1)} %finish.1), calls=%async_computation.7 | async-start | bytes 393216 | tf_op jit(solution)/shard_map/finish/all_to_all | solution.py:22
  (25 other events, 173.6 us)
Sparse Core Ops, SparseCore 0:
  53.0 33.8 all-gather.1

commit v11 on v10

--- a/solution.py
+++ b/solution.py
@@ -14,7 +14,7 @@
 CHUNKS = 4
 PADDED = 512
 LIMIT = 14 * 1024 * 1024
-HEADS_COST = 60_000_000_000
+HEADS_COST = 110_000_000_000
 SIZES = {"y": 4, "z": 8, "x": 4, "c": 2}
 
 
@@ -71,6 +71,43 @@
 
 def shape(*sizes, dtype=F32):
     return jax.ShapeDtypeStruct(sizes, dtype)
+
+
+def taken_kernel(in_width, out_width, voc, positions, offsets, log_ref, out_ref):
+    own, rows = positions.shape[0], log_ref.shape[0]
+    row = lax.broadcasted_iota(jnp.int32, (own, rows), 0)
+    column = lax.broadcasted_iota(jnp.int32, (own, rows), 1)
+    source = jnp.zeros((own, rows), jnp.int32)
+    target = source
+    for at in range(own):
+        source = jnp.where(row == at, positions[at], source)
+        target = jnp.where(row == at, positions[at] + offsets[at], target)
+    source = jnp.where(source == column, 1.0, 0.0).astype(BF16)
+    target = jnp.where(target == column, 1.0, 0.0).astype(BF16)
+    block = log_ref[:, pl.ds(pl.multiple_of(voc[0] * in_width, in_width), in_width)]
+    inputs = jnp.dot(source, block, preferred_element_type=F32)
+    targets = jnp.dot(target, block, preferred_element_type=F32)
+    every = jnp.dot(source, log_ref[...], preferred_element_type=F32)
+    parts = []
+    for z in range(8):
+        starts = [(y * 8 + z) * out_width for y in range(4)]
+        parts.append(jnp.concatenate([every[:, at : at + out_width] for at in starts], axis=1))
+    out_ref[:, :in_width] = jnp.concatenate([inputs] * 8, axis=0).astype(BF16)
+    out_ref[:, in_width : 2 * in_width] = jnp.concatenate([targets] * 8, axis=0).astype(BF16)
+    out_ref[:, 2 * in_width :] = jnp.concatenate(parts, axis=0).astype(BF16)
+
+
+def taken(voc, positions, offsets, log_hidden, in_width, out_width):
+    own = positions.shape[0]
+    smem, vmem = (pl.BlockSpec(memory_space=kind) for kind in (pltpu.SMEM, pltpu.VMEM))
+    return pl.pallas_call(
+        functools.partial(taken_kernel, in_width, out_width),
+        in_specs=[smem, smem, smem, vmem],
+        out_specs=vmem,
+        out_shape=shape(8 * own, 2 * in_width + 4 * out_width, dtype=BF16),
+        compiler_params=pltpu.CompilerParams(vmem_limit_bytes=8 * 1024 * 1024),
+        cost_estimate=cost(4 * own * log_hidden.size, 2 * log_hidden.size),
+    )(voc, positions, offsets, log_hidden)
 
 
 def prepare_kernel(place, vocab_ref, down_ref, done_ref, wide):
@@ -414,9 +451,6 @@
     rows = count // vocs
     at_x, at_y, at_c = lax.axis_index("x"), lax.axis_index("y"), lax.axis_index("c")
     voc_index = at_x * 2 + at_c
-    taken = jnp.concatenate([positions, positions + offsets])
-    taken = jnp.take(log_hidden, taken, axis=0, mode="clip")
-    inputs = taken[:own]
     steps = jnp.arange(16)
     order = ((at_x ^ (steps % 4)) * 2 + (at_c ^ (steps // 8))) * 2 + (steps // 4) % 2
     target_order = (order // 4 ^ at_y) * 4 + order % 4
@@ -424,18 +458,8 @@
     with jax.named_scope("prepare"):
         stored, done = prepare(place, vocab_head)
     with jax.named_scope("gather_z"):
-        blocks = lax.dynamic_slice_in_dim(
-            taken.reshape(2, own, -1), voc_index * in_width, in_width, 2
-        )
-        input_cols = inputs.reshape(own, 4, 8, out_width).transpose(2, 0, 1, 3)
-        sent = jnp.concatenate(
-            [
-                jnp.broadcast_to(blocks[0], (8, own, in_width)),
-                jnp.broadcast_to(blocks[1], (8, own, in_width)),
-                input_cols.reshape(8, own, -1),
-            ],
-            axis=2,
-        )
+        sent = taken(voc_index[None], positions, offsets, log_hidden, in_width, out_width)
+        sent = sent.reshape(8, own, -1)
         (lines,) = settled([exchange(sent, "z")], done)
         lines = lines.reshape(8 * own, -1)
         input_lines, target_lines = lines[:, :in_width], lines[:, in_width : 2 * in_width]

time: 210 us -> 217 us (1.033)
  waiting for transfers between devices: 43.7 us -> 51.1 us
  other arithmetic: 5.26 us -> 3.01 us
    all_gather x1, waiting for transfers between devices: 0.01 us -> 9.18 us  [shards(): target_all = lax.all_gather(target_rows, VOC, axis=1, tiled=True)]
    unnamed x17 -> x21, local copies, waits for them, and re-layouts: 6.69 us -> 9.27 us
    ppermute x36, starting transfers between devices: 39.6 us -> 37.4 us  [swap(): lax.ppermute(block, axis, [(i, i ^ step) for i in range(SIZES[axis])])]
  transfers between devices with their start and end apart: 41 -> 41, of which waited for: 18 -> 17; matrix products, arithmetic and copies ran while one was open for 1% -> 1% of each run, Pallas kernels for 5% -> 6%
where the time goes in v11:
time: 217 us; the launch traced here: 216 us
  starting transfers between devices  68.5 us (32%)
  waiting for transfers between devices  51.1 us (24%)
  blocking collectives  46.7 us (22%)
  Pallas kernels  18.7 us (9%)
  between operations  16.2 us (7%)
  local copies, waits for them, and re-layouts  9.68 us (4%)
  other arithmetic  3.01 us (1%)
  matrix products  2.33 us (1%)
    all_to_all x4, blocking collectives, exchange(): return lax.all_to_all(blocks, axis, split_axis=0, concat_axis=0, tiled=True)  46.7 us
    ppermute x36, starting transfers between devices, swap(): lax.ppermute(block, axis, [(i, i ^ step) for i in range(SIZES[axis])])  37.4 us
    all_to_all x4, starting transfers between devices, exchange(): return lax.all_to_all(blocks, axis, split_axis=0, concat_axis=0, tiled=True)  31.1 us
    ppermute x36, waiting for transfers between devices, swap(): lax.ppermute(block, axis, [(i, i ^ step) for i in range(SIZES[axis])])  21.8 us
    all_to_all x4, waiting for transfers between devices, exchange(): return lax.all_to_all(blocks, axis, split_axis=0, concat_axis=0, tiled=True)  20.1 us
    pallas_call x9, Pallas kernels, call(): pl.pallas_call(kernel, in_specs=specs, out_specs=jax.tree.map(lambda _: p...  11.5 us
    unnamed x21, local copies, waits for them, and re-layouts  9.27 us
    all_gather x1, waiting for transfers between devices, shards(): target_all = lax.all_gather(target_rows, VOC, axis=1, tiled=True)  9.18 us
  transfers between devices with their start and end apart: 41, of which 17 were waited for; matrix products, arithmetic and copies ran while one was open for 1% of the time, Pallas kernels for 6%

profile of v11, /device:TPU:1, one launch (start us, length us, event | category | flops | bytes accessed | tf_op | source)
XLA Modules:
  0.0 216.2 jit_solution(6094469846075151274)
XLA Ops:
  11.4 9.0 %all-to-all-start = ((bf16[8,8,3072]{2,1,0:T(8,128)(2,1)}), bf16[8,8,3072]{2,1,0:T(8,128)(2,1)S(1)}, u32[]{:S(2)}, u32[]{:S(2)}) async-start(bf16[8,8,3072]{2,1,0:T(8,128)(2,1)} %bitcast.2), calls=%async_computation | async-start | bytes 786432 | tf_op jit(solution)/shard_map/gather_z/all_to_all | solution.py:22
  20.5 3.3 %copy-done.1 = bf16[501,8192]{1,0:T(8,128)(2,1)S(1)} copy-done((bf16[501,8192]{1,0:T(8,128)(2,1)S(1)}, bf16[501,8192]{1,0:T(8,128)(2,1)}, u32[]{:S(2)}) %copy-start.1) | copy-done | bytes 8208408
  23.8 3.2 %prepare.1 = (bf16[8192,512]{1,0:T(8,128)(2,1)S(1)}, f32[8,128]{1,0:T(8,128)S(1)}) custom-call(s32[33]{0:T(128)S(1)} %pad_add_fusion.place, bf16[501,8192]{1,0:T(8,128)(2,1)S(1)} %copy-done.1), custom_call_target="tpu_custom_call" | custom-call | bytes 16777216 | tf_op jit(solution)/shard_map/prepare/pallas_call | solution.py:59
  27.0 3.3 %copy-done.3 = bf16[8192,512]{1,0:T(8,128)(2,1)} copy-done((bf16[8192,512]{1,0:T(8,128)(2,1)}, bf16[8192,512]{1,0:T(8,128)(2,1)S(1)}, u32[]{:S(2)}) %copy-start.3) | copy-done | bytes 8388632
  30.3 4.3 %all-to-all-done.refs_0_ = bf16[8,8,3072]{2,1,0:T(8,128)(2,1)S(1)} async-done(((bf16[8,8,3072]{2,1,0:T(8,128)(2,1)}), bf16[8,8,3072]{2,1,0:T(8,128)(2,1)S(1)}, u32[]{:S(2)}, u32[]{:S(2)}) %all-to-all-start) | async-done | bytes 393248 | tf_op jit(solution)/shard_map/gather_z/all_to_all | solution.py:22
  35.7 4.2 %all-to-all-start.1 = ((bf16[4,64,1280]{2,1,0:T(8,128)(2,1)}), bf16[4,64,1280]{2,1,0:T(8,128)(2,1)S(1)}, u32[]{:S(2)}, u32[]{:S(2)}) async-start(bf16[4,64,1280]{2,1,0:T(8,128)(2,1)} %pad_maximum_fusion), calls=%async_computation.1 | async-start | bytes 1310720 | tf_op jit(solution)/shard_map/gather_inputs/all_to_all | solution.py:22
  39.8 2.7 %collective-permute-start.8 = (bf16[64,1024]{1,0:T(8,128)(2,1)S(1)}, bf16[64,1024]{1,0:T(8,128)(2,1)S(1)}, u32[]{:S(2)}, u32[]{:S(2)}) collective-permute-start(bf16[64,1024]{1,0:T(8,128)(2,1)S(1)} %get-tuple-element.51.refs_0_), channel_id=1, source_target_pairs={{0,192},{64,128},{128,64},{192,0},{1,193},{65,129},{129,65},{193,1... | collective-permute-start | bytes 393224 | tf_op jit(solution)/shard_map/gather_targets/ppermute | solution.py:34
  43.1 5.6 %all-to-all-done.1 = bf16[4,64,1280]{2,1,0:T(8,128)(2,1)S(1)} async-done(((bf16[4,64,1280]{2,1,0:T(8,128)(2,1)}), bf16[4,64,1280]{2,1,0:T(8,128)(2,1)S(1)}, u32[]{:S(2)}, u32[]{:S(2)}) %all-to-all-start.1) | async-done | bytes 655392 | tf_op jit(solution)/shard_map/gather_inputs/all_to_all | solution.py:22
  49.8 10.0 %all-to-all-start.2 = ((f32[8,32,256]{2,1,0:T(8,128)}), f32[8,32,256]{2,1,0:T(8,128)S(1)}, u32[]{:S(2)}, u32[]{:S(2)}) async-start(f32[8,32,256]{2,1,0:T(8,128)} %bitcast.6), calls=%async_computation.2 | async-start | bytes 524288 | tf_op jit(solution)/shard_map/head/all_to_all | solution.py:22
  60.8 5.6 %all-to-all-done.2.parts_ref = f32[8,32,256]{2,1,0:T(8,128)S(1)} async-done(((f32[8,32,256]{2,1,0:T(8,128)}), f32[8,32,256]{2,1,0:T(8,128)S(1)}, u32[]{:S(2)}, u32[]{:S(2)}) %all-to-all-start.2) | async-done | bytes 262176 | tf_op jit(solution)/shard_map/head/all_to_all | solution.py:22
  66.4 10.4 %all_to_all.40 = bf16[8,32,256]{2,1,0:T(8,128)(2,1)S(1)} all-to-all(bf16[8,32,256]{2,1,0:T(8,128)(2,1)S(1)} %get-tuple-element.24), channel_id=1, replica_groups=mesh['y'=4,'z'=8,'x'=4,'c'=2] {'z'}, dimensions={0} | all-to-all | bytes 262144 | tf_op jit(solution)/shard_map/gather_heads/all_to_all | solution.py:22
  81.2 2.3 %collective-permute-start.3 = (bf16[16,2048]{1,0:T(8,128)(2,1)S(1)}, bf16[16,2048]{1,0:T(8,128)(2,1)S(1)}, u32[]{:S(2)}, u32[]{:S(2)}) collective-permute-start(bf16[16,2048]{1,0:T(8,128)(2,1)S(1)} %bitcast.37), channel_id=1, source_target_pairs={{0,4},{2,6},{4,0},{6,2},{1,5},{3,7},{5,1},{7,3},{8,12},{10,14},{12... | collective-permute-start | bytes 196616 | tf_op jit(solution)/shard_map/gather_heads/ppermute | solution.py:34
  87.6 9.2 %all-gather.2.cloned.1.call-done.refs_8_.target_ref = bf16[256,8192]{1,0:T(8,128)(2,1)} async-done(((bf16[256,1024]{1,0:T(8,128)(2,1)}), bf16[256,8192]{1,0:T(8,128)(2,1)}) %all-gather.2.cloned.1.call-update) | async-done | bytes 4194320 | tf_op jit(solution)/shard_map/gather_targets/all_gather | solution.py:481
  104.6 2.7 %collective-permute-start.12 = (bf16[64,2048]{1,0:T(8,128)(2,1)S(1)}, bf16[64,2048]{1,0:T(8,128)(2,1)S(1)}, u32[]{:S(2)}, u32[]{:S(2)}) collective-permute-start(bf16[64,2048]{1,0:T(8,128)(2,1)S(1)} %get-tuple-element.26.refs_4_), channel_id=1, source_target_pairs={{0,128},{64,192},{128,0},{192,64},{1,129},{65,193},{129,1},{193,65... | collective-permute-start | bytes 786440 | tf_op jit(solution)/shard_map/gather_heads/ppermute | solution.py:34
  107.3 4.8 %teacher.1 = (f32[256,512]{1,0:T(8,128)S(1)}, bf16[8192,512]{1,0:T(8,128)(2,1)S(1)}) custom-call(s32[33]{0:T(128)S(1)} %pad_add_fusion.place, bf16[256,8192]{1,0:T(8,128)(2,1)S(1)} %copy-done.2, bf16[8192,512]{1,0:T(8,128)(2,1)} %copy-done.3), custom_call_target="tpu_custom_call" | custom-call | flops 2147483648 | bytes 12582912 | tf_op jit(solution)/shard_map/teacher/pallas_call | solution.py:160
  112.1 2.6 %collective-permute-done.12.refs_5_ = bf16[64,2048]{1,0:T(8,128)(2,1)S(1)} collective-permute-done((bf16[64,2048]{1,0:T(8,128)(2,1)S(1)}, bf16[64,2048]{1,0:T(8,128)(2,1)S(1)}, u32[]{:S(2)}, u32[]{:S(2)}) %collective-permute-start.12) | collective-permute-done | bytes 262176 | tf_op jit(solution)/shard_map/gather_heads/ppermute | solution.py:34
  114.7 2.2 %collective-permute-start.15 = (bf16[16,8192]{1,0:T(8,128)(2,1)S(1)}, bf16[16,8192]{1,0:T(8,128)(2,1)S(1)}, u32[]{:S(2)}, u32[]{:S(2)}) collective-permute-start(bf16[16,8192]{1,0:T(8,128)(2,1)S(1)} %get-tuple-element.29.refs_0_), channel_id=1, source_target_pairs={{0,1},{1,0},{2,3},{3,2},{4,5},{5,4},{6,7},{7,6},{8,9},{9,8},{10,11... | collective-permute-start | bytes 786440 | tf_op jit(solution)/shard_map/gather_heads/ppermute | solution.py:34
  122.7 12.4 %all_to_all.41.parts_ref = f32[32,8,128]{2,1,0:T(8,128)S(1)} all-to-all(f32[32,8,128]{2,1,0:T(8,128)S(1)} %get-tuple-element.39), channel_id=1, replica_groups=mesh['y'=4,'z'=8,'x'=4,'c'=2] {'y','x','c'}, dimensions={0} | all-to-all | bytes 262144 | tf_op jit(solution)/shard_map/totals/all_to_all | solution.py:22
  135.2 13.5 %all_to_all.42.parts_ref = f32[8,8,128]{2,1,0:T(8,128)S(1)} all-to-all(f32[8,8,128]{2,1,0:T(8,128)S(1)} %totals.2), channel_id=1, replica_groups=mesh['y'=4,'z'=8,'x'=4,'c'=2] {'z'}, dimensions={0} | all-to-all | bytes 65536 | tf_op jit(solution)/shard_map/totals/all_to_all | solution.py:22
  161.8 3.0 %collective-permute-done.30 = bf16[64,2048]{1,0:T(8,128)(2,1)S(1)} collective-permute-done((bf16[64,2048]{1,0:T(8,128)(2,1)S(1)}, bf16[64,2048]{1,0:T(8,128)(2,1)S(1)}, u32[]{:S(2)}, u32[]{:S(2)}) %collective-permute-start.30) | collective-permute-done | bytes 262176 | tf_op jit(solution)/shard_map/reduce_grad/ppermute | solution.py:34
  166.6 4.4 %collective-permute-done.31 = bf16[64,2048]{1,0:T(8,128)(2,1)S(1)} collective-permute-done((bf16[64,2048]{1,0:T(8,128)(2,1)S(1)}, bf16[64,2048]{1,0:T(8,128)(2,1)S(1)}, u32[]{:S(2)}, u32[]{:S(2)}) %collective-permute-start.31) | collective-permute-done | bytes 262176 | tf_op jit(solution)/shard_map/reduce_grad/ppermute | solution.py:34
  181.4 10.3 %all_to_all.43.parts_ref = bf16[8,32,256]{2,1,0:T(8,128)(2,1)S(1)} all-to-all(bf16[8,32,256]{2,1,0:T(8,128)(2,1)S(1)} %bitcast.45), channel_id=1, replica_groups=mesh['y'=4,'z'=8,'x'=4,'c'=2] {'z'}, dimensions={0} | all-to-all | bytes 262144 | tf_op jit(solution)/shard_map/reduce_grad/all_to_all | solution.py:22
  192.5 7.9 %all-to-all-start.7 = ((bf16[8,48,256]{2,1,0:T(8,128)(2,1)}), bf16[8,48,256]{2,1,0:T(8,128)(2,1)S(1)}, u32[]{:S(2)}, u32[]{:S(2)}) async-start(bf16[8,48,256]{2,1,0:T(8,128)(2,1)} %finish.1), calls=%async_computation.7 | async-start | bytes 393216 | tf_op jit(solution)/shard_map/finish/all_to_all | solution.py:22
  201.7 4.7 %all-to-all-done.7 = bf16[8,48,256]{2,1,0:T(8,128)(2,1)S(1)} async-done(((bf16[8,48,256]{2,1,0:T(8,128)(2,1)}), bf16[8,48,256]{2,1,0:T(8,128)(2,1)S(1)}, u32[]{:S(2)}, u32[]{:S(2)}) %all-to-all-start.7) | async-done | bytes 196640 | tf_op jit(solution)/shard_map/finish/all_to_all | solution.py:22
  (128 shorter events, 58.4 us)
Async XLA Ops:
  11.4 23.2 %all-to-all-start = ((bf16[8,8,3072]{2,1,0:T(8,128)(2,1)}), bf16[8,8,3072]{2,1,0:T(8,128)(2,1)S(1)}, u32[]{:S(2)}, u32[]{:S(2)}) async-start(bf16[8,8,3072]{2,1,0:T(8,128)(2,1)} %bitcast.2), calls=%async_computation | async-start | bytes 786432 | tf_op jit(solution)/shard_map/gather_z/all_to_all | solution.py:22
  35.7 13.1 %all-to-all-start.1 = ((bf16[4,64,1280]{2,1,0:T(8,128)(2,1)}), bf16[4,64,1280]{2,1,0:T(8,128)(2,1)S(1)}, u32[]{:S(2)}, u32[]{:S(2)}) async-start(bf16[4,64,1280]{2,1,0:T(8,128)(2,1)} %pad_maximum_fusion), calls=%async_computation.1 | async-start | bytes 1310720 | tf_op jit(solution)/shard_map/gather_inputs/all_to_all | solution.py:22
  39.8 20.0 %collective-permute-start.8 = (bf16[64,1024]{1,0:T(8,128)(2,1)S(1)}, bf16[64,1024]{1,0:T(8,128)(2,1)S(1)}, u32[]{:S(2)}, u32[]{:S(2)}) collective-permute-start(bf16[64,1024]{1,0:T(8,128)(2,1)S(1)} %get-tuple-element.51.refs_0_), channel_id=1, source_target_pairs={{0,192},{64,128},{128,64},{192,0},{1,193},{65,129},{129,65},{193,1... | collective-permute-start | bytes 393224 | tf_op jit(solution)/shard_map/gather_targets/ppermute | solution.py:34
  42.5 17.3 %collective-permute-start.7 = (bf16[64,1024]{1,0:T(8,128)(2,1)S(1)}, bf16[64,1024]{1,0:T(8,128)(2,1)S(1)}, u32[]{:S(2)}, u32[]{:S(2)}) collective-permute-start(bf16[64,1024]{1,0:T(8,128)(2,1)S(1)} %get-tuple-element.51.refs_0_), channel_id=1, source_target_pairs={{0,128},{64,192},{128,0},{192,64},{1,129},{65,193},{129,1},{193,65... | collective-permute-start | bytes 393224 | tf_op jit(solution)/shard_map/gather_targets/ppermute | solution.py:34
  43.1 16.8 %collective-permute-start.6 = (bf16[64,1024]{1,0:T(8,128)(2,1)S(1)}, bf16[64,1024]{1,0:T(8,128)(2,1)S(1)}, u32[]{:S(2)}, u32[]{:S(2)}) collective-permute-start(bf16[64,1024]{1,0:T(8,128)(2,1)S(1)} %get-tuple-element.51.refs_0_), channel_id=1, source_target_pairs={{0,64},{64,0},{128,192},{192,128},{1,65},{65,1},{129,193},{193,129... | collective-permute-start | bytes 393224 | tf_op jit(solution)/shard_map/gather_targets/ppermute | solution.py:34
  49.8 16.5 %all-to-all-start.2 = ((f32[8,32,256]{2,1,0:T(8,128)}), f32[8,32,256]{2,1,0:T(8,128)S(1)}, u32[]{:S(2)}, u32[]{:S(2)}) async-start(f32[8,32,256]{2,1,0:T(8,128)} %bitcast.6), calls=%async_computation.2 | async-start | bytes 524288 | tf_op jit(solution)/shard_map/head/all_to_all | solution.py:22
  59.8 36.9 %all-gather.2.cloned.1.call-start = ((), (), s32[]{:S(2)}) async-start(), calls=%async_computation.8 | async-start | bytes 4718592 | tf_op jit(solution)/shard_map/gather_targets/all_gather | solution.py:481
  76.9 6.5 %collective-permute-start.1 = (bf16[16,2048]{1,0:T(8,128)(2,1)S(1)}, bf16[16,2048]{1,0:T(8,128)(2,1)S(1)}, u32[]{:S(2)}, u32[]{:S(2)}) collective-permute-start(bf16[16,2048]{1,0:T(8,128)(2,1)S(1)} %bitcast.32), channel_id=1, source_target_pairs={{0,192},{64,128},{128,64},{192,0},{1,193},{65,129},{129,65},{193,1... | collective-permute-start | bytes 196616 | tf_op jit(solution)/shard_map/gather_heads/ppermute | solution.py:34
  80.5 6.5 %collective-permute-start.4 = (bf16[16,2048]{1,0:T(8,128)(2,1)S(1)}, bf16[16,2048]{1,0:T(8,128)(2,1)S(1)}, u32[]{:S(2)}, u32[]{:S(2)}) collective-permute-start(bf16[16,2048]{1,0:T(8,128)(2,1)S(1)} %bitcast.36), channel_id=1, source_target_pairs={{0,6},{2,4},{4,2},{6,0},{1,7},{3,5},{5,3},{7,1},{8,14},{10,12},{12... | collective-permute-start | bytes 196616 | tf_op jit(solution)/shard_map/gather_heads/ppermute | solution.py:34
  81.2 6.4 %collective-permute-start.3 = (bf16[16,2048]{1,0:T(8,128)(2,1)S(1)}, bf16[16,2048]{1,0:T(8,128)(2,1)S(1)}, u32[]{:S(2)}, u32[]{:S(2)}) collective-permute-start(bf16[16,2048]{1,0:T(8,128)(2,1)S(1)} %bitcast.37), channel_id=1, source_target_pairs={{0,4},{2,6},{4,0},{6,2},{1,5},{3,7},{5,1},{7,3},{8,12},{10,14},{12... | collective-permute-start | bytes 196616 | tf_op jit(solution)/shard_map/gather_heads/ppermute | solution.py:34
  96.8 7.7 %collective-permute-start.11 = (bf16[16,8192]{1,0:T(8,128)(2,1)S(1)}, bf16[16,8192]{1,0:T(8,128)(2,1)S(1)}, u32[]{:S(2)}, u32[]{:S(2)}) collective-permute-start(bf16[16,8192]{1,0:T(8,128)(2,1)S(1)} %get-tuple-element.25.refs_0_), channel_id=1, source_target_pairs={{0,2},{2,0},{4,6},{6,4},{1,3},{3,1},{5,7},{7,5},{8,10},{10,8},{12,... | collective-permute-start | bytes 786440 | tf_op jit(solution)/shard_map/gather_heads/ppermute | solution.py:34
  97.1 15.0 %collective-permute-start.10 = (bf16[16,8192]{1,0:T(8,128)(2,1)S(1)}, bf16[16,8192]{1,0:T(8,128)(2,1)S(1)}, u32[]{:S(2)}, u32[]{:S(2)}) collective-permute-start(bf16[16,8192]{1,0:T(8,128)(2,1)S(1)} %get-tuple-element.25.refs_0_), channel_id=1, source_target_pairs={{0,6},{2,4},{4,2},{6,0},{1,7},{3,5},{5,3},{7,1},{8,14},{10,12},{12... | collective-permute-start | bytes 786440 | tf_op jit(solution)/shard_map/gather_heads/ppermute | solution.py:34
  98.6 13.5 %collective-permute-start.9 = (bf16[16,8192]{1,0:T(8,128)(2,1)S(1)}, bf16[16,8192]{1,0:T(8,128)(2,1)S(1)}, u32[]{:S(2)}, u32[]{:S(2)}) collective-permute-start(bf16[16,8192]{1,0:T(8,128)(2,1)S(1)} %get-tuple-element.25.refs_0_), channel_id=1, source_target_pairs={{0,4},{2,6},{4,0},{6,2},{1,5},{3,7},{5,1},{7,3},{8,12},{10,14},{12... | collective-permute-start | bytes 786440 | tf_op jit(solution)/shard_map/gather_heads/ppermute | solution.py:34
  100.2 11.9 %collective-permute-start.14 = (bf16[64,2048]{1,0:T(8,128)(2,1)S(1)}, bf16[64,2048]{1,0:T(8,128)(2,1)S(1)}, u32[]{:S(2)}, u32[]{:S(2)}) collective-permute-start(bf16[64,2048]{1,0:T(8,128)(2,1)S(1)} %get-tuple-element.26.refs_4_), channel_id=1, source_target_pairs={{0,64},{64,0},{128,192},{192,128},{1,65},{65,1},{129,193},{193,129... | collective-permute-start | bytes 786440 | tf_op jit(solution)/shard_map/gather_heads/ppermute | solution.py:34
  101.4 10.7 %collective-permute-start.13 = (bf16[64,2048]{1,0:T(8,128)(2,1)S(1)}, bf16[64,2048]{1,0:T(8,128)(2,1)S(1)}, u32[]{:S(2)}, u32[]{:S(2)}) collective-permute-start(bf16[64,2048]{1,0:T(8,128)(2,1)S(1)} %get-tuple-element.26.refs_4_), channel_id=1, source_target_pairs={{0,192},{64,128},{128,64},{192,0},{1,193},{65,129},{129,65},{193,1... | collective-permute-start | bytes 786440 | tf_op jit(solution)/shard_map/gather_heads/ppermute | solution.py:34
  104.6 10.1 %collective-permute-start.12 = (bf16[64,2048]{1,0:T(8,128)(2,1)S(1)}, bf16[64,2048]{1,0:T(8,128)(2,1)S(1)}, u32[]{:S(2)}, u32[]{:S(2)}) collective-permute-start(bf16[64,2048]{1,0:T(8,128)(2,1)S(1)} %get-tuple-element.26.refs_4_), channel_id=1, source_target_pairs={{0,128},{64,192},{128,0},{192,64},{1,129},{65,193},{129,1},{193,65... | collective-permute-start | bytes 786440 | tf_op jit(solution)/shard_map/gather_heads/ppermute | solution.py:34
  157.2 7.6 %collective-permute-start.30 = (bf16[64,2048]{1,0:T(8,128)(2,1)S(1)}, bf16[64,2048]{1,0:T(8,128)(2,1)S(1)}, u32[]{:S(2)}, u32[]{:S(2)}) collective-permute-start(bf16[64,2048]{1,0:T(8,128)(2,1)S(1)} %get-tuple-element.48), channel_id=1, source_target_pairs={{0,64},{64,0},{128,192},{192,128},{1,65},{65,1},{129,193},{193,129... | collective-permute-start | bytes 786440 | tf_op jit(solution)/shard_map/reduce_grad/ppermute | solution.py:34
  157.6 9.0 %collective-permute-start.32 = (bf16[64,2048]{1,0:T(8,128)(2,1)S(1)}, bf16[64,2048]{1,0:T(8,128)(2,1)S(1)}, u32[]{:S(2)}, u32[]{:S(2)}) collective-permute-start(bf16[64,2048]{1,0:T(8,128)(2,1)S(1)} %get-tuple-element.49), channel_id=1, source_target_pairs={{0,192},{64,128},{128,64},{192,0},{1,193},{65,129},{129,65},{193,1... | collective-permute-start | bytes 786440 | tf_op jit(solution)/shard_map/reduce_grad/ppermute | solution.py:34
  158.5 12.5 %collective-permute-start.31 = (bf16[64,2048]{1,0:T(8,128)(2,1)S(1)}, bf16[64,2048]{1,0:T(8,128)(2,1)S(1)}, u32[]{:S(2)}, u32[]{:S(2)}) collective-permute-start(bf16[64,2048]{1,0:T(8,128)(2,1)S(1)} %get-tuple-element.50), channel_id=1, source_target_pairs={{0,128},{64,192},{128,0},{192,64},{1,129},{65,193},{129,1},{193,65... | collective-permute-start | bytes 786440 | tf_op jit(solution)/shard_map/reduce_grad/ppermute | solution.py:34
  160.6 11.8 %collective-permute-start.24 = (bf16[16,8192]{1,0:T(8,128)(2,1)S(1)}, bf16[16,8192]{1,0:T(8,128)(2,1)S(1)}, u32[]{:S(2)}, u32[]{:S(2)}) collective-permute-start(bf16[16,8192]{1,0:T(8,128)(2,1)S(1)} %get-tuple-element.45), channel_id=1, source_target_pairs={{0,2},{2,0},{4,6},{6,4},{1,3},{3,1},{5,7},{7,5},{8,10},{10,8},{12,... | collective-permute-start | bytes 786440 | tf_op jit(solution)/shard_map/reduce_grad/ppermute | solution.py:34
  161.0 13.5 %collective-permute-start.26 = (bf16[16,8192]{1,0:T(8,128)(2,1)S(1)}, bf16[16,8192]{1,0:T(8,128)(2,1)S(1)}, u32[]{:S(2)}, u32[]{:S(2)}) collective-permute-start(bf16[16,8192]{1,0:T(8,128)(2,1)S(1)} %get-tuple-element.46), channel_id=1, source_target_pairs={{0,6},{2,4},{4,2},{6,0},{1,7},{3,5},{5,3},{7,1},{8,14},{10,12},{12... | collective-permute-start | bytes 786440 | tf_op jit(solution)/shard_map/reduce_grad/ppermute | solution.py:34
  164.8 9.7 %collective-permute-start.25 = (bf16[16,8192]{1,0:T(8,128)(2,1)S(1)}, bf16[16,8192]{1,0:T(8,128)(2,1)S(1)}, u32[]{:S(2)}, u32[]{:S(2)}) collective-permute-start(bf16[16,8192]{1,0:T(8,128)(2,1)S(1)} %get-tuple-element.47), channel_id=1, source_target_pairs={{0,4},{2,6},{4,0},{6,2},{1,5},{3,7},{5,1},{7,3},{8,12},{10,14},{12... | collective-permute-start | bytes 786440 | tf_op jit(solution)/shard_map/reduce_grad/ppermute | solution.py:34
  171.6 6.4 %collective-permute-start.35 = (bf16[16,2048]{1,0:T(8,128)(2,1)S(1)}, bf16[16,2048]{1,0:T(8,128)(2,1)S(1)}, u32[]{:S(2)}, u32[]{:S(2)}) collective-permute-start(bf16[16,2048]{1,0:T(8,128)(2,1)S(1)} %get-tuple-element.58), channel_id=1, source_target_pairs={{0,6},{2,4},{4,2},{6,0},{1,7},{3,5},{5,3},{7,1},{8,14},{10,12},{12... | collective-permute-start | bytes 196616 | tf_op jit(solution)/shard_map/reduce_grad/ppermute | solution.py:34
  192.5 13.8 %all-to-all-start.7 = ((bf16[8,48,256]{2,1,0:T(8,128)(2,1)}), bf16[8,48,256]{2,1,0:T(8,128)(2,1)S(1)}, u32[]{:S(2)}, u32[]{:S(2)}) async-start(bf16[8,48,256]{2,1,0:T(8,128)(2,1)} %finish.1), calls=%async_computation.7 | async-start | bytes 393216 | tf_op jit(solution)/shard_map/finish/all_to_all | solution.py:22
  (27 other events, 199.7 us)
Sparse Core Ops, SparseCore 0:
  63.1 33.6 all-gather.1

commit v12 on v10

--- a/solution.py
+++ b/solution.py
@@ -339,8 +339,8 @@
 def stack_kernel(*refs):
     blocks, out_ref = refs[:4], refs[-1]
     rows = blocks[0].shape[0]
-    for at, block in enumerate(blocks):
-        out_ref[at * rows : (at + 1) * rows] = block[...]
+    for peer, block in zip(PEERS, blocks):
+        out_ref[peer * rows : (peer + 1) * rows] = block[...]
 
 
 def stacked(blocks, awaited):
@@ -352,7 +352,7 @@
         out_shape=shape(4 * rows, across, dtype=BF16),
         compiler_params=pltpu.CompilerParams(vmem_limit_bytes=4 * 1024 * 1024),
         cost_estimate=cost(0, 16 * rows * across),
-    )(*blocks, awaited)
+    )(*[blocks[peer] for peer in PEERS], awaited)
 
 
 def heads_kernel(parts_ref, residual_ref, bias_ref, heads_ref, preact_ref):

time: 210 us -> 210 us (level)
  transfers between devices with their start and end apart: 41 -> 41, of which waited for: 18 -> 17; matrix products, arithmetic and copies ran while one was open for 1% -> 1% of each run, Pallas kernels for 5% -> 5%
where the time goes in v12:
time: 210 us; the launch traced here: 209 us
  starting transfers between devices  70 us (33%)
  blocking collectives  48 us (23%)
  waiting for transfers between devices  42.2 us (20%)
  Pallas kernels  17.1 us (8%)
  between operations  16.2 us (8%)
  local copies, waits for them, and re-layouts  7.87 us (4%)
  other arithmetic  5.26 us (3%)
  matrix products  2.33 us (1%)
    all_to_all x4, blocking collectives, exchange(): return lax.all_to_all(blocks, axis, split_axis=0, concat_axis=0, tiled=True)  48 us
    ppermute x36, starting transfers between devices, swap(): lax.ppermute(block, axis, [(i, i ^ step) for i in range(SIZES[axis])])  41.6 us
    all_to_all x4, starting transfers between devices, exchange(): return lax.all_to_all(blocks, axis, split_axis=0, concat_axis=0, tiled=True)  28.4 us
    ppermute x36, waiting for transfers between devices, swap(): lax.ppermute(block, axis, [(i, i ^ step) for i in range(SIZES[axis])])  21.8 us
    all_to_all x4, waiting for transfers between devices, exchange(): return lax.all_to_all(blocks, axis, split_axis=0, concat_axis=0, tiled=True)  20.5 us
    pallas_call x9, Pallas kernels, call(): pl.pallas_call(kernel, in_specs=specs, out_specs=jax.tree.map(lambda _: p...  11.5 us
    unnamed x17, local copies, waits for them, and re-layouts  6.69 us
    pallas_call x1, Pallas kernels, teacher_logits(): pl.pallas_call(teacher_kernel, in_specs=[pl.BlockSpec(memory_space=pltpu....  4.78 us
  transfers between devices with their start and end apart: 41, of which 17 were waited for; matrix products, arithmetic and copies ran while one was open for 1% of the time, Pallas kernels for 5%

profile of v12, /device:TPU:1, one launch (start us, length us, event | category | flops | bytes accessed | tf_op | source)
XLA Modules:
  0.0 209.0 jit_solution(15426813413639436239)
XLA Ops:
  10.3 9.0 %all-to-all-start = ((bf16[8,8,3072]{2,1,0:T(8,128)(2,1)}), bf16[8,8,3072]{2,1,0:T(8,128)(2,1)S(1)}, u32[]{:S(2)}, u32[]{:S(2)}) async-start(bf16[8,8,3072]{2,1,0:T(8,128)(2,1)} %pad_maximum_fusion.1), calls=%async_computation | async-start | bytes 786432 | tf_op jit(solution)/shard_map/gather_z/all_to_all | solution.py:22
  19.4 3.3 %copy-done.1 = bf16[501,8192]{1,0:T(8,128)(2,1)S(1)} copy-done((bf16[501,8192]{1,0:T(8,128)(2,1)S(1)}, bf16[501,8192]{1,0:T(8,128)(2,1)}, u32[]{:S(2)}) %copy-start.1) | copy-done | bytes 8208408
  22.7 3.2 %prepare.1 = (bf16[8192,512]{1,0:T(8,128)(2,1)S(1)}, f32[8,128]{1,0:T(8,128)S(1)}) custom-call(s32[33]{0:T(128)S(1)} %pad_add_fusion.place, bf16[501,8192]{1,0:T(8,128)(2,1)S(1)} %copy-done.1), custom_call_target="tpu_custom_call" | custom-call | bytes 16777216 | tf_op jit(solution)/shard_map/prepare/pallas_call | solution.py:59
  25.9 3.3 %copy-done.3 = bf16[8192,512]{1,0:T(8,128)(2,1)} copy-done((bf16[8192,512]{1,0:T(8,128)(2,1)}, bf16[8192,512]{1,0:T(8,128)(2,1)S(1)}, u32[]{:S(2)}) %copy-start.3) | copy-done | bytes 8388632
  29.2 4.3 %all-to-all-done.refs_0_ = bf16[8,8,3072]{2,1,0:T(8,128)(2,1)S(1)} async-done(((bf16[8,8,3072]{2,1,0:T(8,128)(2,1)}), bf16[8,8,3072]{2,1,0:T(8,128)(2,1)S(1)}, u32[]{:S(2)}, u32[]{:S(2)}) %all-to-all-start) | async-done | bytes 393248 | tf_op jit(solution)/shard_map/gather_z/all_to_all | solution.py:22
  34.6 4.2 %all-to-all-start.1 = ((bf16[4,64,1280]{2,1,0:T(8,128)(2,1)}), bf16[4,64,1280]{2,1,0:T(8,128)(2,1)S(1)}, u32[]{:S(2)}, u32[]{:S(2)}) async-start(bf16[4,64,1280]{2,1,0:T(8,128)(2,1)} %pad_maximum_fusion), calls=%async_computation.1 | async-start | bytes 1310720 | tf_op jit(solution)/shard_map/gather_inputs/all_to_all | solution.py:22
  42.6 5.0 %all-to-all-done.1 = bf16[4,64,1280]{2,1,0:T(8,128)(2,1)S(1)} async-done(((bf16[4,64,1280]{2,1,0:T(8,128)(2,1)}), bf16[4,64,1280]{2,1,0:T(8,128)(2,1)S(1)}, u32[]{:S(2)}, u32[]{:S(2)}) %all-to-all-start.1) | async-done | bytes 655392 | tf_op jit(solution)/shard_map/gather_inputs/all_to_all | solution.py:22
  49.3 4.0 %collective-permute-done.6.refs_1_ = bf16[64,1024]{1,0:T(8,128)(2,1)S(1)} collective-permute-done((bf16[64,1024]{1,0:T(8,128)(2,1)S(1)}, bf16[64,1024]{1,0:T(8,128)(2,1)S(1)}, u32[]{:S(2)}, u32[]{:S(2)}) %collective-permute-start.6) | collective-permute-done | bytes 131104 | tf_op jit(solution)/shard_map/gather_targets/ppermute | solution.py:34
  54.1 7.2 %all-to-all-start.2 = ((f32[8,32,256]{2,1,0:T(8,128)}), f32[8,32,256]{2,1,0:T(8,128)S(1)}, u32[]{:S(2)}, u32[]{:S(2)}) async-start(f32[8,32,256]{2,1,0:T(8,128)} %bitcast.10), calls=%async_computation.2 | async-start | bytes 524288 | tf_op jit(solution)/shard_map/head/all_to_all | solution.py:22
  61.4 6.5 %all-to-all-done.2.parts_ref = f32[8,32,256]{2,1,0:T(8,128)S(1)} async-done(((f32[8,32,256]{2,1,0:T(8,128)}), f32[8,32,256]{2,1,0:T(8,128)S(1)}, u32[]{:S(2)}, u32[]{:S(2)}) %all-to-all-start.2) | async-done | bytes 262176 | tf_op jit(solution)/shard_map/head/all_to_all | solution.py:22
  67.9 10.2 %all_to_all.40 = bf16[8,32,256]{2,1,0:T(8,128)(2,1)S(1)} all-to-all(bf16[8,32,256]{2,1,0:T(8,128)(2,1)S(1)} %get-tuple-element.24), channel_id=1, replica_groups=mesh['y'=4,'z'=8,'x'=4,'c'=2] {'z'}, dimensions={0} | all-to-all | bytes 262144 | tf_op jit(solution)/shard_map/gather_heads/all_to_all | solution.py:22
  79.2 2.3 %collective-permute-start = (bf16[16,2048]{1,0:T(8,128)(2,1)S(1)}, bf16[16,2048]{1,0:T(8,128)(2,1)S(1)}, u32[]{:S(2)}, u32[]{:S(2)}) collective-permute-start(bf16[16,2048]{1,0:T(8,128)(2,1)S(1)} %bitcast.40), channel_id=1, source_target_pairs={{0,128},{64,192},{128,0},{192,64},{1,129},{65,193},{129,1},{193,65... | collective-permute-start | bytes 196616 | tf_op jit(solution)/shard_map/gather_heads/ppermute | solution.py:34
  82.5 2.2 %collective-permute-start.3 = (bf16[16,2048]{1,0:T(8,128)(2,1)S(1)}, bf16[16,2048]{1,0:T(8,128)(2,1)S(1)}, u32[]{:S(2)}, u32[]{:S(2)}) collective-permute-start(bf16[16,2048]{1,0:T(8,128)(2,1)S(1)} %bitcast.44), channel_id=1, source_target_pairs={{0,4},{2,6},{4,0},{6,2},{1,5},{3,7},{5,1},{7,3},{8,12},{10,14},{12... | collective-permute-start | bytes 196616 | tf_op jit(solution)/shard_map/gather_heads/ppermute | solution.py:34
  91.5 2.8 %collective-permute-start.13 = (bf16[64,2048]{1,0:T(8,128)(2,1)S(1)}, bf16[64,2048]{1,0:T(8,128)(2,1)S(1)}, u32[]{:S(2)}, u32[]{:S(2)}) collective-permute-start(bf16[64,2048]{1,0:T(8,128)(2,1)S(1)} %get-tuple-element.26.refs_4_), channel_id=1, source_target_pairs={{0,192},{64,128},{128,64},{192,0},{1,193},{65,129},{129,65},{193,1... | collective-permute-start | bytes 786440 | tf_op jit(solution)/shard_map/gather_heads/ppermute | solution.py:34
  94.3 2.7 %collective-permute-start.12 = (bf16[64,2048]{1,0:T(8,128)(2,1)S(1)}, bf16[64,2048]{1,0:T(8,128)(2,1)S(1)}, u32[]{:S(2)}, u32[]{:S(2)}) collective-permute-start(bf16[64,2048]{1,0:T(8,128)(2,1)S(1)} %get-tuple-element.26.refs_4_), channel_id=1, source_target_pairs={{0,128},{64,192},{128,0},{192,64},{1,129},{65,193},{129,1},{193,65... | collective-permute-start | bytes 786440 | tf_op jit(solution)/shard_map/gather_heads/ppermute | solution.py:34
  96.9 4.8 %teacher.1 = (f32[256,512]{1,0:T(8,128)S(1)}, bf16[8192,512]{1,0:T(8,128)(2,1)S(1)}) custom-call(s32[33]{0:T(128)S(1)} %pad_add_fusion.place, bf16[256,8192]{1,0:T(8,128)(2,1)S(1)} %copy-done.2, bf16[8192,512]{1,0:T(8,128)(2,1)} %copy-done.3), custom_call_target="tpu_custom_call" | custom-call | flops 2147483648 | bytes 12582912 | tf_op jit(solution)/shard_map/teacher/pallas_call | solution.py:123
  102.8 5.4 %collective-permute-start.15 = (bf16[16,8192]{1,0:T(8,128)(2,1)S(1)}, bf16[16,8192]{1,0:T(8,128)(2,1)S(1)}, u32[]{:S(2)}, u32[]{:S(2)}) collective-permute-start(bf16[16,8192]{1,0:T(8,128)(2,1)S(1)} %get-tuple-element.29.refs_0_), channel_id=1, source_target_pairs={{0,1},{1,0},{2,3},{3,2},{4,5},{5,4},{6,7},{7,6},{8,9},{9,8},{10,11... | collective-permute-start | bytes 786440 | tf_op jit(solution)/shard_map/gather_heads/ppermute | solution.py:34
  113.9 13.4 %all_to_all.41.parts_ref = f32[32,8,128]{2,1,0:T(8,128)S(1)} all-to-all(f32[32,8,128]{2,1,0:T(8,128)S(1)} %get-tuple-element.39), channel_id=1, replica_groups=mesh['y'=4,'z'=8,'x'=4,'c'=2] {'y','x','c'}, dimensions={0} | all-to-all | bytes 262144 | tf_op jit(solution)/shard_map/totals/all_to_all | solution.py:22
  127.3 14.1 %all_to_all.42.parts_ref = f32[8,8,128]{2,1,0:T(8,128)S(1)} all-to-all(f32[8,8,128]{2,1,0:T(8,128)S(1)} %totals.2), channel_id=1, replica_groups=mesh['y'=4,'z'=8,'x'=4,'c'=2] {'z'}, dimensions={0} | all-to-all | bytes 65536 | tf_op jit(solution)/shard_map/totals/all_to_all | solution.py:22
  154.5 3.0 %collective-permute-done.30 = bf16[64,2048]{1,0:T(8,128)(2,1)S(1)} collective-permute-done((bf16[64,2048]{1,0:T(8,128)(2,1)S(1)}, bf16[64,2048]{1,0:T(8,128)(2,1)S(1)}, u32[]{:S(2)}, u32[]{:S(2)}) %collective-permute-start.30) | collective-permute-done | bytes 262176 | tf_op jit(solution)/shard_map/reduce_grad/ppermute | solution.py:34
  159.4 4.4 %collective-permute-done.31 = bf16[64,2048]{1,0:T(8,128)(2,1)S(1)} collective-permute-done((bf16[64,2048]{1,0:T(8,128)(2,1)S(1)}, bf16[64,2048]{1,0:T(8,128)(2,1)S(1)}, u32[]{:S(2)}, u32[]{:S(2)}) %collective-permute-start.31) | collective-permute-done | bytes 262176 | tf_op jit(solution)/shard_map/reduce_grad/ppermute | solution.py:34
  174.2 10.3 %all_to_all.43.parts_ref = bf16[8,32,256]{2,1,0:T(8,128)(2,1)S(1)} all-to-all(bf16[8,32,256]{2,1,0:T(8,128)(2,1)S(1)} %bitcast.53), channel_id=1, replica_groups=mesh['y'=4,'z'=8,'x'=4,'c'=2] {'z'}, dimensions={0} | all-to-all | bytes 262144 | tf_op jit(solution)/shard_map/reduce_grad/all_to_all | solution.py:22
  185.2 7.9 %all-to-all-start.7 = ((bf16[8,48,256]{2,1,0:T(8,128)(2,1)}), bf16[8,48,256]{2,1,0:T(8,128)(2,1)S(1)}, u32[]{:S(2)}, u32[]{:S(2)}) async-start(bf16[8,48,256]{2,1,0:T(8,128)(2,1)} %finish.1), calls=%async_computation.7 | async-start | bytes 393216 | tf_op jit(solution)/shard_map/finish/all_to_all | solution.py:22
  194.4 4.7 %all-to-all-done.7 = bf16[8,48,256]{2,1,0:T(8,128)(2,1)S(1)} async-done(((bf16[8,48,256]{2,1,0:T(8,128)(2,1)}), bf16[8,48,256]{2,1,0:T(8,128)(2,1)S(1)}, u32[]{:S(2)}, u32[]{:S(2)}) %all-to-all-start.7) | async-done | bytes 196640 | tf_op jit(solution)/shard_map/finish/all_to_all | solution.py:22
  (132 shorter events, 54.7 us)
Async XLA Ops:
  10.3 23.2 %all-to-all-start = ((bf16[8,8,3072]{2,1,0:T(8,128)(2,1)}), bf16[8,8,3072]{2,1,0:T(8,128)(2,1)S(1)}, u32[]{:S(2)}, u32[]{:S(2)}) async-start(bf16[8,8,3072]{2,1,0:T(8,128)(2,1)} %pad_maximum_fusion.1), calls=%async_computation | async-start | bytes 786432 | tf_op jit(solution)/shard_map/gather_z/all_to_all | solution.py:22
  34.6 13.1 %all-to-all-start.1 = ((bf16[4,64,1280]{2,1,0:T(8,128)(2,1)}), bf16[4,64,1280]{2,1,0:T(8,128)(2,1)S(1)}, u32[]{:S(2)}, u32[]{:S(2)}) async-start(bf16[4,64,1280]{2,1,0:T(8,128)(2,1)} %pad_maximum_fusion), calls=%async_computation.1 | async-start | bytes 1310720 | tf_op jit(solution)/shard_map/gather_inputs/all_to_all | solution.py:22
  38.8 48.5 %all-gather.2.cloned.1.call-start = ((), (), s32[]{:S(2)}) async-start(), calls=%async_computation.8 | async-start | bytes 4718592 | tf_op jit(solution)/shard_map/gather_targets/all_gather | solution.py:457
  38.8 10.5 %collective-permute-start.8 = (bf16[64,1024]{1,0:T(8,128)(2,1)S(1)}, bf16[64,1024]{1,0:T(8,128)(2,1)S(1)}, u32[]{:S(2)}, u32[]{:S(2)}) collective-permute-start(bf16[64,1024]{1,0:T(8,128)(2,1)S(1)} %get-tuple-element.51.refs_0_), channel_id=1, source_target_pairs={{0,64},{64,0},{128,192},{192,128},{1,65},{65,1},{129,193},{193,129... | collective-permute-start | bytes 393224 | tf_op jit(solution)/shard_map/gather_targets/ppermute | solution.py:34
  40.2 9.0 %collective-permute-start.7 = (bf16[64,1024]{1,0:T(8,128)(2,1)S(1)}, bf16[64,1024]{1,0:T(8,128)(2,1)S(1)}, u32[]{:S(2)}, u32[]{:S(2)}) collective-permute-start(bf16[64,1024]{1,0:T(8,128)(2,1)S(1)} %get-tuple-element.51.refs_0_), channel_id=1, source_target_pairs={{0,192},{64,128},{128,64},{192,0},{1,193},{65,129},{129,65},{193,1... | collective-permute-start | bytes 393224 | tf_op jit(solution)/shard_map/gather_targets/ppermute | solution.py:34
  42.0 11.3 %collective-permute-start.6 = (bf16[64,1024]{1,0:T(8,128)(2,1)S(1)}, bf16[64,1024]{1,0:T(8,128)(2,1)S(1)}, u32[]{:S(2)}, u32[]{:S(2)}) collective-permute-start(bf16[64,1024]{1,0:T(8,128)(2,1)S(1)} %get-tuple-element.51.refs_0_), channel_id=1, source_target_pairs={{0,128},{64,192},{128,0},{192,64},{1,129},{65,193},{129,1},{193,65... | collective-permute-start | bytes 393224 | tf_op jit(solution)/shard_map/gather_targets/ppermute | solution.py:34
  54.1 13.8 %all-to-all-start.2 = ((f32[8,32,256]{2,1,0:T(8,128)}), f32[8,32,256]{2,1,0:T(8,128)S(1)}, u32[]{:S(2)}, u32[]{:S(2)}) async-start(f32[8,32,256]{2,1,0:T(8,128)} %bitcast.10), calls=%async_computation.2 | async-start | bytes 524288 | tf_op jit(solution)/shard_map/head/all_to_all | solution.py:22
  78.5 6.2 %collective-permute-start.1 = (bf16[16,2048]{1,0:T(8,128)(2,1)S(1)}, bf16[16,2048]{1,0:T(8,128)(2,1)S(1)}, u32[]{:S(2)}, u32[]{:S(2)}) collective-permute-start(bf16[16,2048]{1,0:T(8,128)(2,1)S(1)} %bitcast.39), channel_id=1, source_target_pairs={{0,192},{64,128},{128,64},{192,0},{1,193},{65,129},{129,65},{193,1... | collective-permute-start | bytes 196616 | tf_op jit(solution)/shard_map/gather_heads/ppermute | solution.py:34
  87.3 7.0 %collective-permute-start.11 = (bf16[16,8192]{1,0:T(8,128)(2,1)S(1)}, bf16[16,8192]{1,0:T(8,128)(2,1)S(1)}, u32[]{:S(2)}, u32[]{:S(2)}) collective-permute-start(bf16[16,8192]{1,0:T(8,128)(2,1)S(1)} %get-tuple-element.25.refs_0_), channel_id=1, source_target_pairs={{0,2},{2,0},{4,6},{6,4},{1,3},{3,1},{5,7},{7,5},{8,10},{10,8},{12,... | collective-permute-start | bytes 786440 | tf_op jit(solution)/shard_map/gather_heads/ppermute | solution.py:34
  88.6 13.1 %collective-permute-start.10 = (bf16[16,8192]{1,0:T(8,128)(2,1)S(1)}, bf16[16,8192]{1,0:T(8,128)(2,1)S(1)}, u32[]{:S(2)}, u32[]{:S(2)}) collective-permute-start(bf16[16,8192]{1,0:T(8,128)(2,1)S(1)} %get-tuple-element.25.refs_0_), channel_id=1, source_target_pairs={{0,6},{2,4},{4,2},{6,0},{1,7},{3,5},{5,3},{7,1},{8,14},{10,12},{12... | collective-permute-start | bytes 786440 | tf_op jit(solution)/shard_map/gather_heads/ppermute | solution.py:34
  89.8 12.0 %collective-permute-start.9 = (bf16[16,8192]{1,0:T(8,128)(2,1)S(1)}, bf16[16,8192]{1,0:T(8,128)(2,1)S(1)}, u32[]{:S(2)}, u32[]{:S(2)}) collective-permute-start(bf16[16,8192]{1,0:T(8,128)(2,1)S(1)} %get-tuple-element.25.refs_0_), channel_id=1, source_target_pairs={{0,4},{2,6},{4,0},{6,2},{1,5},{3,7},{5,1},{7,3},{8,12},{10,14},{12... | collective-permute-start | bytes 786440 | tf_op jit(solution)/shard_map/gather_heads/ppermute | solution.py:34
  90.6 11.1 %collective-permute-start.14 = (bf16[64,2048]{1,0:T(8,128)(2,1)S(1)}, bf16[64,2048]{1,0:T(8,128)(2,1)S(1)}, u32[]{:S(2)}, u32[]{:S(2)}) collective-permute-start(bf16[64,2048]{1,0:T(8,128)(2,1)S(1)} %get-tuple-element.26.refs_4_), channel_id=1, source_target_pairs={{0,64},{64,0},{128,192},{192,128},{1,65},{65,1},{129,193},{193,129... | collective-permute-start | bytes 786440 | tf_op jit(solution)/shard_map/gather_heads/ppermute | solution.py:34
  91.5 10.3 %collective-permute-start.13 = (bf16[64,2048]{1,0:T(8,128)(2,1)S(1)}, bf16[64,2048]{1,0:T(8,128)(2,1)S(1)}, u32[]{:S(2)}, u32[]{:S(2)}) collective-permute-start(bf16[64,2048]{1,0:T(8,128)(2,1)S(1)} %get-tuple-element.26.refs_4_), channel_id=1, source_target_pairs={{0,192},{64,128},{128,64},{192,0},{1,193},{65,129},{129,65},{193,1... | collective-permute-start | bytes 786440 | tf_op jit(solution)/shard_map/gather_heads/ppermute | solution.py:34
  94.3 8.5 %collective-permute-start.12 = (bf16[64,2048]{1,0:T(8,128)(2,1)S(1)}, bf16[64,2048]{1,0:T(8,128)(2,1)S(1)}, u32[]{:S(2)}, u32[]{:S(2)}) collective-permute-start(bf16[64,2048]{1,0:T(8,128)(2,1)S(1)} %get-tuple-element.26.refs_4_), channel_id=1, source_target_pairs={{0,128},{64,192},{128,0},{192,64},{1,129},{65,193},{129,1},{193,65... | collective-permute-start | bytes 786440 | tf_op jit(solution)/shard_map/gather_heads/ppermute | solution.py:34
  102.8 6.5 %collective-permute-start.15 = (bf16[16,8192]{1,0:T(8,128)(2,1)S(1)}, bf16[16,8192]{1,0:T(8,128)(2,1)S(1)}, u32[]{:S(2)}, u32[]{:S(2)}) collective-permute-start(bf16[16,8192]{1,0:T(8,128)(2,1)S(1)} %get-tuple-element.29.refs_0_), channel_id=1, source_target_pairs={{0,1},{1,0},{2,3},{3,2},{4,5},{5,4},{6,7},{7,6},{8,9},{9,8},{10,11... | collective-permute-start | bytes 786440 | tf_op jit(solution)/shard_map/gather_heads/ppermute | solution.py:34
  143.5 5.8 %collective-permute-start.23 = (bf16[128,8192]{1,0:T(8,128)(2,1)S(1)}, bf16[128,8192]{1,0:T(8,128)(2,1)S(1)}, u32[]{:S(2)}, u32[]{:S(2)}) collective-permute-start(bf16[128,8192]{1,0:T(8,128)(2,1)S(1)} %grad.3), channel_id=1, source_target_pairs={{0,1},{1,0},{2,3},{3,2},{4,5},{5,4},{6,7},{7,6},{8,9},{9,8},{10,11... | collective-permute-start | bytes 6291464 | tf_op jit(solution)/shard_map/reduce_grad/ppermute | solution.py:34
  149.9 7.6 %collective-permute-start.30 = (bf16[64,2048]{1,0:T(8,128)(2,1)S(1)}, bf16[64,2048]{1,0:T(8,128)(2,1)S(1)}, u32[]{:S(2)}, u32[]{:S(2)}) collective-permute-start(bf16[64,2048]{1,0:T(8,128)(2,1)S(1)} %get-tuple-element.48), channel_id=1, source_target_pairs={{0,64},{64,0},{128,192},{192,128},{1,65},{65,1},{129,193},{193,129... | collective-permute-start | bytes 786440 | tf_op jit(solution)/shard_map/reduce_grad/ppermute | solution.py:34
  150.3 9.0 %collective-permute-start.32 = (bf16[64,2048]{1,0:T(8,128)(2,1)S(1)}, bf16[64,2048]{1,0:T(8,128)(2,1)S(1)}, u32[]{:S(2)}, u32[]{:S(2)}) collective-permute-start(bf16[64,2048]{1,0:T(8,128)(2,1)S(1)} %get-tuple-element.49), channel_id=1, source_target_pairs={{0,192},{64,128},{128,64},{192,0},{1,193},{65,129},{129,65},{193,1... | collective-permute-start | bytes 786440 | tf_op jit(solution)/shard_map/reduce_grad/ppermute | solution.py:34
  151.3 12.5 %collective-permute-start.31 = (bf16[64,2048]{1,0:T(8,128)(2,1)S(1)}, bf16[64,2048]{1,0:T(8,128)(2,1)S(1)}, u32[]{:S(2)}, u32[]{:S(2)}) collective-permute-start(bf16[64,2048]{1,0:T(8,128)(2,1)S(1)} %get-tuple-element.50), channel_id=1, source_target_pairs={{0,128},{64,192},{128,0},{192,64},{1,129},{65,193},{129,1},{193,65... | collective-permute-start | bytes 786440 | tf_op jit(solution)/shard_map/reduce_grad/ppermute | solution.py:34
  153.3 11.8 %collective-permute-start.24 = (bf16[16,8192]{1,0:T(8,128)(2,1)S(1)}, bf16[16,8192]{1,0:T(8,128)(2,1)S(1)}, u32[]{:S(2)}, u32[]{:S(2)}) collective-permute-start(bf16[16,8192]{1,0:T(8,128)(2,1)S(1)} %get-tuple-element.45), channel_id=1, source_target_pairs={{0,2},{2,0},{4,6},{6,4},{1,3},{3,1},{5,7},{7,5},{8,10},{10,8},{12,... | collective-permute-start | bytes 786440 | tf_op jit(solution)/shard_map/reduce_grad/ppermute | solution.py:34
  153.7 13.5 %collective-permute-start.26 = (bf16[16,8192]{1,0:T(8,128)(2,1)S(1)}, bf16[16,8192]{1,0:T(8,128)(2,1)S(1)}, u32[]{:S(2)}, u32[]{:S(2)}) collective-permute-start(bf16[16,8192]{1,0:T(8,128)(2,1)S(1)} %get-tuple-element.46), channel_id=1, source_target_pairs={{0,6},{2,4},{4,2},{6,0},{1,7},{3,5},{5,3},{7,1},{8,14},{10,12},{12... | collective-permute-start | bytes 786440 | tf_op jit(solution)/shard_map/reduce_grad/ppermute | solution.py:34
  157.5 9.7 %collective-permute-start.25 = (bf16[16,8192]{1,0:T(8,128)(2,1)S(1)}, bf16[16,8192]{1,0:T(8,128)(2,1)S(1)}, u32[]{:S(2)}, u32[]{:S(2)}) collective-permute-start(bf16[16,8192]{1,0:T(8,128)(2,1)S(1)} %get-tuple-element.47), channel_id=1, source_target_pairs={{0,4},{2,6},{4,0},{6,2},{1,5},{3,7},{5,1},{7,3},{8,12},{10,14},{12... | collective-permute-start | bytes 786440 | tf_op jit(solution)/shard_map/reduce_grad/ppermute | solution.py:34
  164.3 6.4 %collective-permute-start.35 = (bf16[16,2048]{1,0:T(8,128)(2,1)S(1)}, bf16[16,2048]{1,0:T(8,128)(2,1)S(1)}, u32[]{:S(2)}, u32[]{:S(2)}) collective-permute-start(bf16[16,2048]{1,0:T(8,128)(2,1)S(1)} %get-tuple-element.58), channel_id=1, source_target_pairs={{0,6},{2,4},{4,2},{6,0},{1,7},{3,5},{5,3},{7,1},{8,14},{10,12},{12... | collective-permute-start | bytes 196616 | tf_op jit(solution)/shard_map/reduce_grad/ppermute | solution.py:34
  185.2 13.8 %all-to-all-start.7 = ((bf16[8,48,256]{2,1,0:T(8,128)(2,1)}), bf16[8,48,256]{2,1,0:T(8,128)(2,1)S(1)}, u32[]{:S(2)}, u32[]{:S(2)}) async-start(bf16[8,48,256]{2,1,0:T(8,128)(2,1)} %finish.1), calls=%async_computation.7 | async-start | bytes 393216 | tf_op jit(solution)/shard_map/finish/all_to_all | solution.py:22
  (25 other events, 175.5 us)
Sparse Core Ops, SparseCore 0:
  54.3 32.8 all-gather.1
